TPU v7x, 128 devices: a whole 4x4x4 slice. The times are simulated.
128 devices in a mesh: row: 16 (over x, z_hi, core), col: 8 (over z_lo, y).
Axes of the slice: x: 4, y: 4, z: 4 (z_hi: 2, z_lo: 2; z = z_hi * 2 + z_lo), core: 2. Of those that a mesh axis runs over, the one named last changes fastest.
Arguments:
- scene: bfloat16 [1024, 2048, 128], P('row', 'col'), may hold values from -6 to 6
- conv_first: bfloat16 [3, 3, 128, 128], replicated, may hold values from -0.1875 to 0.1875
- conv_second: bfloat16 [3, 3, 128, 128], replicated, may hold values from -0.1875 to 0.1875
- embed_weight: bfloat16 [8192, 768], P('row'), may hold values from -0.0625 to 0.0625
- router_weight: bfloat16 [768, 16], replicated, may hold values from -0.21875 to 0.21875
- expert_ids: int32 [16, 8, 256, 1], P('row', 'col'), may hold values from 0 to 15; in each aligned block of 256 rows (0 to 255, 256 to 511, ..., all dimensions but the last counted through in order) at most 48 rows name the same one
- expert_up: bfloat16 [16, 768, 3072], P('col'), may hold values from -0.21875 to 0.21875
- expert_down: bfloat16 [16, 3072, 768], P('col'), may hold values from -0.109375 to 0.109375
Outputs:
- mixed: bfloat16 [16, 8, 256, 768], P('row', 'col')
Inputs may be any that keep to these rules, and one draw needn't show every extreme that they name: `expert_ids`: within the tokens of one block (a, b), no expert is named by more than 48 tokens, a bound that some block reaches.
All inputs are finite; a program needn't handle non-finite values.
Results may differ from a plain program's by a relative error of at most 0.014.
Values may be sent and summed in bfloat16 or wider, within the bound.
No kernel may reach another device: no remote copies, remote signals or barrier semaphores. Data moves between devices by JAX's collectives and lax.ppermute only.
A program may use at most 128 MiB of HBM per device.

v0:
```python
import functools

import jax
import jax.numpy as jnp
from jax import lax
from jax.experimental import pallas as pl
from jax.experimental.pallas import tpu as pltpu
from jax.sharding import PartitionSpec as P

ROWS, COLS, CH = 64, 256, 128
WIDE = 272
DIM, FF, CAP, TOK = 768, 3072, 48, 256
SLOTS = 8 * CAP
FIRST = 5
F32, BF16 = jnp.float32, jnp.bfloat16
ANY = pl.BlockSpec(memory_space=pl.ANY)
VMEM = pl.BlockSpec(memory_space=pltpu.VMEM)
SMEM = pl.BlockSpec(memory_space=pltpu.SMEM)


def params():
    return pltpu.CompilerParams(vmem_limit_bytes=56 * 2**20)


def hop(dx=0, dy=0, dh=0, dl=0, dc=0):
    pairs = []
    for x in range(4):
        for h in range(2):
            for c in range(2):
                for low in range(2):
                    for y in range(4):
                        here = (x * 4 + h * 2 + c) * 8 + low * 4 + y
                        there = (
                            ((x + dx) % 4 * 4 + (h + dh) % 2 * 2 + (c + dc) % 2) * 8
                            + (low + dl) % 2 * 4
                            + (y + dy) % 4
                        )
                        pairs.append((here, there))
    return pairs


def send(value, **step):
    return lax.ppermute(value, ("row", "col"), hop(**step))


def pair_weights(source, target):
    zero = jnp.zeros((CH, CH), BF16)
    for j in range(4):
        for dx in range(3):
            rows = pl.ds(j * CH, CH)
            target[rows, pl.ds(dx * 256, CH)] = source[j, dx] if j < 3 else zero
            target[rows, pl.ds(dx * 256 + CH, CH)] = source[j - 1, dx] if j > 0 else zero


def pair_conv(source, weights, pair):
    taps = jnp.concatenate([source[2 * pair + j] for j in range(4)], axis=1)
    parts = jnp.dot(taps, weights[...], preferred_element_type=F32)
    left = pltpu.roll(parts[:, 0:256], 1, 0)
    right = pltpu.roll(parts[:, 512:768], WIDE - 1, 0)
    return left + parts[:, 256:512] + right


def conv_kernel(
    start, steps, place, scene, top, bottom, strip, first, second, keep, other,
    block, hidden, rows, w1, w2, sems,
):
    step = pl.program_id(0)
    height = 8 * steps + 4
    base = 8 * start - 2
    chunks = []
    for k in range(steps):
        lo, hi = (0, 12) if k == 0 else (4 + 8 * k, 12 + 8 * k)
        copies = []
        if base + lo < 0:
            copies.append((top, block.at[0:2, 0:COLS]))
        a, b = max(base + lo, 0), min(base + hi, ROWS)
        copies.append((scene.at[a:b], block.at[a - base : b - base, 0:COLS]))
        if base + hi > ROWS:
            copies.append((bottom, block.at[height - 2 : height, 0:COLS]))
        copies.append((strip.at[base + lo + 2 : base + hi + 2], block.at[lo:hi, COLS:WIDE]))
        chunks.append(
            [pltpu.make_async_copy(s, d, sems.at[k, n]) for n, (s, d) in enumerate(copies)]
        )
    place_row, place_col, core = place[0], place[1], place[2]
    tail = lax.broadcasted_iota(jnp.int32, (16, 256), 0)
    cut = ((place_col == 0) & (tail >= 8)) | ((place_col == 7) & (tail < 8))
    edge = jnp.where(cut, 0.0, 1.0).astype(F32)

    def conv_first(pair):
        value = jnp.maximum(pair_conv(block, w1, pair), 0.0)
        body, ends = value[0:COLS].astype(BF16), (value[COLS:WIDE] * edge).astype(BF16)
        for i in range(2):
            hidden[2 * pair + i, 0:COLS] = body[:, i * CH : (i + 1) * CH]
            hidden[2 * pair + i, COLS:WIDE] = ends[:, i * CH : (i + 1) * CH]

    @pl.when(step == 0)
    def _():
        for chunk in chunks:
            for copy in chunk:
                copy.start()
        pair_weights(first, w1)
        pair_weights(second, w2)
        for copy in chunks[0]:
            copy.wait()
        conv_first(0)
        if start == 0:

            @pl.when(place_row == 0)
            def _():
                hidden[0] = jnp.zeros((WIDE, CH), BF16)

    for k in range(1, steps):

        @pl.when(step == k)
        def _(k=k):
            for copy in chunks[k]:
                copy.wait()

    for i in range(4):
        conv_first(4 * step + 1 + i)
    if 8 * (start + steps) == ROWS:

        @pl.when((step == steps - 1) & (place_row == 15))
        def _():
            hidden[8 * steps + 1] = jnp.zeros((WIDE, CH), BF16)

    for i in range(4):
        pair = 4 * step + i
        value = pair_conv(hidden, w2, pair)[0:COLS]
        for n in range(2):
            cells = block[2 * pair + 2 + n, 0:COLS].astype(F32)
            rows[pl.ds((2 * i + n) * COLS, COLS), :] = value[:, n * CH : (n + 1) * CH] + cells
    for dy in range(8):
        for j in range(4):
            low = rows[pl.ds(dy * COLS + j, 32, stride=8), :]
            high = rows[pl.ds(dy * COLS + 4 + j, 32, stride=8), :]
            lanes = pl.ds(j * CH, CH)
            keep[dy, :, lanes] = jnp.where(core == 0, low, high).astype(BF16)
            other[dy, :, lanes] = jnp.where(core == 0, high, low).astype(BF16)


def conv_call(start, steps, *args):
    shape = jax.ShapeDtypeStruct((8, 32 * steps, 512), BF16)
    out = pl.BlockSpec((8, 32, 512), lambda i: (0, i, 0))
    return pl.pallas_call(
        functools.partial(conv_kernel, start, steps),
        grid=(steps,),
        in_specs=[SMEM, ANY, ANY, ANY, ANY, VMEM, VMEM],
        out_specs=[out, out],
        out_shape=[shape, shape],
        scratch_shapes=[
            pltpu.VMEM((8 * steps + 4, WIDE, CH), BF16),
            pltpu.VMEM((8 * steps + 2, WIDE, CH), BF16),
            pltpu.VMEM((8 * COLS, CH), F32),
            pltpu.VMEM((512, 768), BF16),
            pltpu.VMEM((512, 768), BF16),
            pltpu.SemaphoreType.DMA((steps, 4)),
        ],
        compiler_params=params(),
        name=f"convs_{start}",
    )(*args)


def embed_kernel(layout, has_sum, order, *refs):
    tokens, pieces = refs[0:4], refs[4 : 4 + len(layout)]
    rest = refs[4 + len(layout) :]
    given, rest = (rest[0:2], rest[2:]) if has_sum else ((), rest)
    own, partner, lhs, rhs, lhs_sems, rhs_sems = rest
    copies = []
    for n, (which, offset, depth) in enumerate(layout):
        k = order[which]
        here, at = [], 0
        for m, source in enumerate(tokens):
            count = source.shape[1]
            here.append(
                pltpu.make_async_copy(
                    source.at[k, :, pl.ds(offset, depth)],
                    lhs.at[n, pl.ds(at, count), pl.ds(0, depth)],
                    lhs_sems.at[n, m],
                )
            )
            at += count
        here.append(
            pltpu.make_async_copy(pieces[n], rhs.at[n, pl.ds(0, depth)], rhs_sems.at[n])
        )
        copies.append(here)
    for here in copies:
        for copy in here:
            copy.start()
    for n, (which, offset, depth) in enumerate(layout):
        for copy in copies[n]:
            copy.wait()
        for target, at, base in ((partner, TOK, 1), (own, 0, 0)):
            part = jnp.dot(
                lhs[n, pl.ds(at, TOK), 0:depth], rhs[n, 0:depth], preferred_element_type=F32
            )
            if n == 0 and not has_sum:
                target[...] = part
            elif n == 0:
                target[...] = given[base][...] + part
            else:
                target[...] += part


def embed_call(name, order, tokens, pieces, sums=()):
    layout = tuple((which, offset, array.shape[0]) for array, which, offset in pieces)
    count = len(pieces)
    shape = jax.ShapeDtypeStruct((TOK, DIM), F32)
    return pl.pallas_call(
        functools.partial(embed_kernel, layout, bool(sums)),
        in_specs=[SMEM] + [ANY] * (4 + count) + [VMEM] * len(sums),
        out_specs=[VMEM, VMEM],
        out_shape=[shape, shape],
        scratch_shapes=[
            pltpu.VMEM((count, 2 * TOK, 512), BF16),
            pltpu.VMEM((count, 512, DIM), BF16),
            pltpu.SemaphoreType.DMA((count, 4)),
            pltpu.SemaphoreType.DMA((count,)),
        ],
        compiler_params=params(),
        name=name,
    )(order, *tokens, *[array for array, _, _ in pieces], *sums)


def route_kernel(own, came, router, ids_row, ids_col, embedded, out0, out1, gate, place):
    value = (own[...] + came[...]).astype(BF16)
    embedded[...] = value
    wide = value.astype(F32)
    scale = lax.rsqrt(jnp.mean(wide * wide, axis=-1, keepdims=True) + 1e-06)
    normed = (wide * scale).astype(BF16)
    scores = jnp.dot(normed, router[...], preferred_element_type=F32)
    across = lax.broadcasted_iota(jnp.int32, (TOK, TOK), 1)
    down = lax.broadcasted_iota(jnp.int32, (TOK, TOK), 0)
    col, row = ids_col[...], ids_row[...]
    hot = jnp.where(col == lax.broadcasted_iota(jnp.int32, (TOK, 16), 1), 1.0, 0.0)
    gate[...] = jax.nn.sigmoid(jnp.sum(scores * hot, axis=-1, keepdims=True))
    earlier = jnp.where(across < down, 1.0, 0.0).astype(BF16)
    counts = jnp.dot(earlier, hot.astype(BF16), preferred_element_type=F32)
    rank = jnp.sum(counts * hot, axis=-1, keepdims=True).astype(jnp.int32)
    place[...] = (col & 1) * SLOTS + (col >> 1) * CAP + rank
    hot_t = jnp.where(row == lax.broadcasted_iota(jnp.int32, (16, TOK), 0), 1.0, 0.0)
    later = jnp.where(down < across, 1.0, 0.0).astype(BF16)
    counts_t = jnp.dot(hot_t.astype(BF16), later, preferred_element_type=F32)
    rank_t = jnp.sum(counts_t * hot_t, axis=0, keepdims=True).astype(jnp.int32)
    place_t = (row & 1) * SLOTS + (row >> 1) * CAP + rank_t
    slot = lax.broadcasted_iota(jnp.int32, (SLOTS, TOK), 0)
    for n, out in enumerate((out0, out1)):
        pick = jnp.where(slot + n * SLOTS == place_t, 1.0, 0.0).astype(BF16)
        out[...] = jnp.dot(pick, normed, preferred_element_type=F32).astype(BF16)


def route_call(*args):
    shapes = [((TOK, DIM), BF16), ((SLOTS, DIM), BF16), ((SLOTS, DIM), BF16)]
    shapes += [((TOK, 1), F32), ((TOK, 1), jnp.int32)]
    return pl.pallas_call(
        route_kernel,
        in_specs=[VMEM] * 5,
        out_specs=[VMEM] * 5,
        out_shape=[jax.ShapeDtypeStruct(*shape) for shape in shapes],
        compiler_params=params(),
        name="route",
    )(*args)


def expert_kernel(rows, up, down, out, total):
    step = pl.program_id(0)
    z = jnp.dot(rows[...], up[...], preferred_element_type=F32)
    act = 0.5 * z * (1.0 + jnp.tanh(0.7978845608028654 * (z + 0.044715 * (z * z * z))))
    part = jnp.dot(act.astype(BF16), down[...], preferred_element_type=F32)

    @pl.when(step == 0)
    def _():
        total[...] = part

    @pl.when(step > 0)
    def _():
        total[...] += part

    @pl.when(step == pl.num_programs(0) - 1)
    def _():
        out[...] = total[...].astype(BF16)


def expert_call(which, rows, up, down, width=768):
    whole = pl.BlockSpec((SLOTS, DIM), lambda i: (0, 0))
    return pl.pallas_call(
        expert_kernel,
        grid=(FF // width,),
        in_specs=[
            whole,
            pl.BlockSpec((None, DIM, width), lambda i: (which, 0, i)),
            pl.BlockSpec((None, width, DIM), lambda i: (which, i, 0)),
        ],
        out_specs=whole,
        out_shape=jax.ShapeDtypeStruct((SLOTS, DIM), BF16),
        scratch_shapes=[pltpu.VMEM((SLOTS, DIM), F32)],
        compiler_params=params(),
        name=f"expert_{which}",
    )(rows, up, down)


def mix_kernel(embedded, gate, place, back0, back1, out):
    slot = lax.broadcasted_iota(jnp.int32, (TOK, SLOTS), 1)
    result = None
    for n, back in enumerate((back0, back1)):
        pick = jnp.where(slot + n * SLOTS == place[...], 1.0, 0.0).astype(BF16)
        part = jnp.dot(pick, back[...], preferred_element_type=F32)
        result = part if result is None else result + part
    out[...] = (embedded[...].astype(F32) + gate[...] * result).astype(BF16)


def mix_call(*args):
    return pl.pallas_call(
        mix_kernel,
        in_specs=[VMEM] * 5,
        out_specs=VMEM,
        out_shape=jax.ShapeDtypeStruct((TOK, DIM), BF16),
        compiler_params=params(),
        name="mix",
    )(*args)


def neighbours(value, axis, ahead):
    count = lax.axis_size(axis)
    pairs = [(i, i + 1) for i in range(count - 1)]
    return lax.ppermute(value, axis, pairs if ahead else [(j, i) for i, j in pairs])


def exchange(value):
    value = value.reshape(8, CAP, DIM)
    return lax.all_to_all(value, "col", 0, 0, tiled=True).reshape(SLOTS, DIM)


def local(
    scene, conv_first, conv_second, embed_weight, router_weight, expert_ids, expert_up, expert_down
):
    row, col = lax.axis_index("row"), lax.axis_index("col")
    x, high, core = row // 4, row // 2 % 2, row % 2
    place = jnp.stack([row, col, core]).astype(jnp.int32)

    top = neighbours(scene[ROWS - 2 :], "row", True)
    bottom = neighbours(scene[:2], "row", False)
    left_own = jnp.concatenate([top[:, :2], scene[:, :2], bottom[:, :2]], axis=0)
    right_own = jnp.concatenate([top[:, -2:], scene[:, -2:], bottom[:, -2:]], axis=0)
    left = neighbours(right_own, "col", True)
    right = neighbours(left_own, "col", False)
    strip = jnp.concatenate([right, jnp.zeros((ROWS + 4, 12, CH), BF16), left], axis=1)

    w = embed_weight
    w_minus, w_plus, w_high = send(w, dx=1), send(w, dx=-1), send(w, dh=1, dl=1)
    scene_args = (place, scene, top, bottom, strip, conv_first, conv_second)
    keep0, other0 = conv_call(0, FIRST, *scene_args)
    keep0, other0, w_minus, w_plus, w_high = lax.optimization_barrier(
        (keep0, other0, w_minus, w_plus, w_high)
    )
    w_far0, w_far1 = send(w_minus[:256], dx=1), send(w_plus[256:], dx=-1)
    w_high_minus, w_high_plus = send(w_high, dx=1), send(w_high, dx=-1)
    came0 = send(other0, dc=1)
    keep1, other1 = conv_call(FIRST, 8 - FIRST, *scene_args)
    came1 = send(other1, dc=1)
    w_high_far0, w_high_far1 = send(w_far0, dh=1, dl=1), send(w_far1, dh=1, dl=1)

    shards = [(a % 4) * 2 + (b % 2) for b in (high, high + 1) for a in (x, x - 1, x + 1, x + 2)]
    order = jnp.stack(shards).astype(jnp.int32)
    tokens = (keep0, keep1, came0, came1)
    sums = embed_call(
        "embed_a", order, tokens, [(w, 0, 0), (w_minus, 1, 0), (w_plus, 2, 0), (w_high, 4, 0)]
    )
    sums = embed_call(
        "embed_b",
        order,
        tokens,
        [(w_far0, 3, 0), (w_far1, 3, 256), (w_high_minus, 5, 0), (w_high_plus, 6, 0)],
        sums,
    )
    own, partner = embed_call(
        "embed_c", order, tokens, [(w_high_far0, 7, 0), (w_high_far1, 7, 256)], sums
    )
    came = send(partner, dc=1)
    embedded, out0, out1, gate, slots = route_call(
        own, came, router_weight, expert_ids.reshape(1, TOK), expert_ids.reshape(TOK, 1)
    )
    in0, in1 = exchange(out0), exchange(out1)
    back0 = exchange(expert_call(0, in0, expert_up, expert_down))
    back1 = exchange(expert_call(1, in1, expert_up, expert_down))
    return mix_call(embedded, gate, slots, back0, back1).reshape(1, 1, TOK, DIM)


def solution(mesh):
    return jax.shard_map(
        local,
        mesh=mesh,
        in_specs=(
            P("row", "col", None),
            P(),
            P(),
            P("row", None),
            P(),
            P("row", "col", None, None),
            P("col", None, None),
            P("col", None, None),
        ),
        out_specs=P("row", "col", None, None),
        check_vma=False,
    )
```

profile of v0, /device:TPU:0, one launch (start us, length us, event | category | flops | bytes accessed | tf_op | source)
XLA Modules:
  0.0 184.1 jit_solution(13394766495854599083)
XLA Ops:
  0.0 1.6 collective-permute-start.4
  1.6 1.7 collective-permute-start.5
  3.2 4.1 %collective-permute-start.6 = (bf16[512,768]{1,0:T(8,128)(2,1)}, bf16[512,768]{1,0:T(8,128)(2,1)}, u32[]{:S(2)}, u32[]{:S(2)}) collective-permute-start(bf16[512,768]{1,0:T(8,128)(2,1)} %refs_4_.1), channel_id=1, source_target_pairs={{0,20},{1,21},{2,22},{3,23},{4,16},{5,17},{6,18},{7,19},{8,28},{9,... | collective-permute-start | bytes 2359304 | tf_op jit(solution)/shard_map/ppermute | solution.py:43
  7.4 1.0 fusion.1
  8.3 1.3 collective-permute-start
  9.7 1.3 collective-permute-start.1
  11.0 1.0 fusion
  12.0 1.0 collective-permute-done.1.bottom
  13.1 0.1 pad_maximum_fusion.1
  13.1 1.3 collective-permute-start.2
  14.5 4.5 %collective-permute-start.3 = (bf16[68,2,128]{2,1,0:T(2,128)(2,1)S(1)}, bf16[68,2,128]{2,1,0:T(2,128)(2,1)S(1)}, u32[]{:S(2)}, u32[]{:S(2)}) collective-permute-start(bf16[68,2,128]{2,1,0:T(2,128)(2,1)S(1)} %pad_maximum_fusion.2), channel_id=1, source_target_pairs={{0,1},{1,2},{2,3},{3,4},{4,5},{5,6},{6,7},{8,9},{9,10},{10,11},{11... | collective-permute-start | bytes 104456 | tf_op jit(solution)/shard_map/ppermute | solution.py:326
  19.1 0.6 pad_add_fusion.place
  19.7 0.1 pad.1.clone
  19.7 0.9 collective-permute-done.3
  20.7 0.8 pad_maximum_fusion.strip
  21.5 10.2 %convs_5.1 = (bf16[8,96,512]{2,1,0:T(8,128)(2,1)}, bf16[8,96,512]{2,1,0:T(8,128)(2,1)}) custom-call(s32[3]{0:T(128)} %pad_add_fusion.place, bf16[64,256,128]{2,1,0:T(8,128)(2,1)} %scene.3, bf16[2,256,128]{2,1,0:T(8,128)(2,1)} %copy-done.7, bf16[2,256,128]{2,1,0:T(8,128)(2,1)} %copy-done.8, bf16[68,16,128]{2,1,0:T(8,128)(2,1)} %pad_maximum_fusion.strip, ...), custom_call_target="tpu_custom_call" | custom-call | tf_op jit(solution)/shard_map/convs_5/pallas_call | solution.py:145
  31.7 4.1 %collective-permute-start.8 = (bf16[8,96,512]{2,1,0:T(8,128)(2,1)}, bf16[8,96,512]{2,1,0:T(8,128)(2,1)S(1)}, u32[]{:S(2)}, u32[]{:S(2)}) collective-permute-start(bf16[8,96,512]{2,1,0:T(8,128)(2,1)} %get-tuple-element.30), channel_id=1, source_target_pairs={{0,8},{1,9},{2,10},{3,11},{4,12},{5,13},{6,14},{7,15},{8,0},{9,1},... | collective-permute-start | bytes 2359304 | tf_op jit(solution)/shard_map/ppermute | solution.py:43
  35.8 14.0 %convs_0.1 = (bf16[8,160,512]{2,1,0:T(8,128)(2,1)}, bf16[8,160,512]{2,1,0:T(8,128)(2,1)}) custom-call(s32[3]{0:T(128)} %pad_add_fusion.place, bf16[64,256,128]{2,1,0:T(8,128)(2,1)} %scene.3, bf16[2,256,128]{2,1,0:T(8,128)(2,1)} %copy-done.7, bf16[2,256,128]{2,1,0:T(8,128)(2,1)} %copy-done.8, bf16[68,16,128]{2,1,0:T(8,128)(2,1)} %pad_maximum_fusion.strip, ...), custom_call_target="tpu_custom_call" | custom-call | tf_op jit(solution)/shard_map/convs_0/pallas_call | solution.py:145
  49.8 0.9 copy-done.5
  50.8 9.3 %collective-permute-start.13 = (bf16[512,768]{1,0:T(8,128)(2,1)}, bf16[512,768]{1,0:T(8,128)(2,1)}, u32[]{:S(2)}, u32[]{:S(2)}) collective-permute-start(bf16[512,768]{1,0:T(8,128)(2,1)} %collective-permute-done.6.refs_7_), channel_id=1, source_target_pairs={{0,32},{1,33},{2,34},{3,35},{4,36},{5,37},{6,38},{7,39},{8,40},{9,... | collective-permute-start | bytes 2359304 | tf_op jit(solution)/shard_map/ppermute | solution.py:43
  60.1 1.3 collective-permute-start.14
  61.4 1.0 slice.39
  62.4 0.8 collective-permute-start.9
  63.2 2.5 %collective-permute-start.11 = (bf16[256,768]{1,0:T(8,128)(2,1)S(1)}, bf16[256,768]{1,0:T(8,128)(2,1)}, u32[]{:S(2)}, u32[]{:S(2)}) collective-permute-start(bf16[256,768]{1,0:T(8,128)(2,1)S(1)} %slice.39), channel_id=1, source_target_pairs={{0,96},{1,97},{2,98},{3,99},{4,100},{5,101},{6,102},{7,103},{8,104... | collective-permute-start | bytes 1179656 | tf_op jit(solution)/shard_map/ppermute | solution.py:43
  65.7 22.0 %collective-permute-done.9.refs_4_ = bf16[256,768]{1,0:T(8,128)(2,1)S(1)} collective-permute-done((bf16[256,768]{1,0:T(8,128)(2,1)S(1)}, bf16[256,768]{1,0:T(8,128)(2,1)S(1)}, u32[]{:S(2)}, u32[]{:S(2)}) %collective-permute-start.9) | collective-permute-done | bytes 393248 | tf_op jit(solution)/shard_map/ppermute | solution.py:43
  87.8 4.7 %collective-permute-start.10 = (bf16[256,768]{1,0:T(8,128)(2,1)S(1)}, bf16[256,768]{1,0:T(8,128)(2,1)}, u32[]{:S(2)}, u32[]{:S(2)}) collective-permute-start(bf16[256,768]{1,0:T(8,128)(2,1)S(1)} %collective-permute-done.9.refs_4_), channel_id=1, source_target_pairs={{0,20},{1,21},{2,22},{3,23},{4,16},{5,17},{6,18},{7,19},{8,28},{9,... | collective-permute-start | bytes 1179656 | tf_op jit(solution)/shard_map/ppermute | solution.py:43
  92.5 0.3 collective-permute-start.12
  92.8 0.6 stack.47.order
  93.4 1.1 copy-done
  94.5 5.6 %embed_a.1 = (f32[256,768]{1,0:T(8,128)}, f32[256,768]{1,0:T(8,128)}) custom-call(s32[8]{0:T(128)} %stack.47.order, bf16[8,160,512]{2,1,0:T(8,128)(2,1)} %get-tuple-element.27.refs_0_, bf16[8,96,512]{2,1,0:T(8,128)(2,1)} %get-tuple-element.28.refs_1_, bf16[8,160,512]{2,1,0:T(8,128)(2,1)} %copy-done, bf16[8,96,512]{2,1,0:T(8,128)(2,1)} %copy-done.1, ...), custom_call_target="tpu_custom_call" | custom-call | tf_op jit(solution)/shard_map/embed_a/pallas_call | solution.py:209
  100.1 5.7 %embed_b.1 = (f32[256,768]{1,0:T(8,128)}, f32[256,768]{1,0:T(8,128)}) custom-call(s32[8]{0:T(128)} %stack.47.order, bf16[8,160,512]{2,1,0:T(8,128)(2,1)} %get-tuple-element.27.refs_0_, bf16[8,96,512]{2,1,0:T(8,128)(2,1)} %get-tuple-element.28.refs_1_, bf16[8,160,512]{2,1,0:T(8,128)(2,1)} %copy-done, bf16[8,96,512]{2,1,0:T(8,128)(2,1)} %copy-done.1, ...), custom_call_target="tpu_custom_call" | custom-call | tf_op jit(solution)/shard_map/embed_b/pallas_call | solution.py:209
  105.8 4.1 %collective-permute-done.12.refs_5_ = bf16[256,768]{1,0:T(8,128)(2,1)} collective-permute-done((bf16[256,768]{1,0:T(8,128)(2,1)}, bf16[256,768]{1,0:T(8,128)(2,1)}, u32[]{:S(2)}, u32[]{:S(2)}) %collective-permute-start.12) | collective-permute-done | bytes 393248 | tf_op jit(solution)/shard_map/ppermute | solution.py:43
  110.0 4.5 %embed_c.1 = (f32[256,768]{1,0:T(8,128)}, f32[256,768]{1,0:T(8,128)}) custom-call(s32[8]{0:T(128)} %stack.47.order, bf16[8,160,512]{2,1,0:T(8,128)(2,1)} %get-tuple-element.27.refs_0_, bf16[8,96,512]{2,1,0:T(8,128)(2,1)} %get-tuple-element.28.refs_1_, bf16[8,160,512]{2,1,0:T(8,128)(2,1)} %copy-done, bf16[8,96,512]{2,1,0:T(8,128)(2,1)} %copy-done.1, ...), custom_call_target="tpu_custom_call" | custom-call | tf_op jit(solution)/shard_map/embed_c/pallas_call | solution.py:209
  114.5 0.1 collective-permute-start.15
  114.6 0.8 copy.10.router
  115.4 0.8 copy.11.ids_col
  116.2 0.9 collective-permute-done.15.came
  117.1 0.9 copy-done.6
  117.9 3.3 %route.1 = (bf16[256,768]{1,0:T(8,128)(2,1)}, bf16[384,768]{1,0:T(8,128)(2,1)}, bf16[384,768]{1,0:T(8,128)(2,1)}, f32[256,1]{1,0:T(8,128)}, s32[256,1]{1,0:T(8,128)}) custom-call(f32[256,768]{1,0:T(8,128)} %get-tuple-element.38.own, f32[256,768]{1,0:T(8,128)} %copy-done.6, bf16[768,16]{1,0:T(8,128)(2,1)} %copy.10.router, s32[1,256]{1,0:T(1,128)} %bitcast.30, ...), custom_call_target="tpu_custom_call" | custom-call | tf_op jit(solution)/shard_map/route/pallas_call | solution.py:255
  121.3 16.3 %all_to_all.20 = bf16[8,48,768]{2,1,0:T(8,128)(2,1)} all-to-all(bf16[8,48,768]{2,1,0:T(8,128)(2,1)} %bitcast.29), channel_id=1, replica_groups=mesh['row'=16,'col'=8] {'col'}, dimensions={0} | all-to-all | bytes 1179648 | tf_op jit(solution)/shard_map/all_to_all | solution.py:331
  137.5 3.5 %all-to-all-start.2 = ((bf16[8,48,768]{2,1,0:T(8,128)(2,1)}), bf16[8,48,768]{2,1,0:T(8,128)(2,1)S(1)}, u32[]{:S(2)}, u32[]{:S(2)}) async-start(bf16[8,48,768]{2,1,0:T(8,128)(2,1)} %bitcast.28), calls=%async_computation.2 | async-start | bytes 1179648 | tf_op jit(solution)/shard_map/all_to_all | solution.py:331
  141.1 8.8 %expert_0.1 = bf16[384,768]{1,0:T(8,128)(2,1)} custom-call(bf16[384,768]{1,0:T(8,128)(2,1)} %bitcast.24, bf16[2,768,3072]{2,1,0:T(8,128)(2,1)} %up.3, bf16[2,3072,768]{2,1,0:T(8,128)(2,1)} %down.3), custom_call_target="tpu_custom_call" | custom-call | tf_op jit(solution)/shard_map/expert_0/pallas_call | solution.py:286
  149.9 1.7 all-to-all-done.2
  151.7 3.9 %all-to-all-start.1 = ((bf16[8,48,768]{2,1,0:T(8,128)(2,1)}), bf16[8,48,768]{2,1,0:T(8,128)(2,1)S(1)}, u32[]{:S(2)}, u32[]{:S(2)}) async-start(bf16[8,48,768]{2,1,0:T(8,128)(2,1)} %bitcast.23), calls=%async_computation.1 | async-start | bytes 1179648 | tf_op jit(solution)/shard_map/all_to_all | solution.py:331
  155.6 8.5 %expert_1.1 = bf16[384,768]{1,0:T(8,128)(2,1)} custom-call(bf16[384,768]{1,0:T(8,128)(2,1)} %bitcast.22, bf16[2,768,3072]{2,1,0:T(8,128)(2,1)} %up.3, bf16[2,3072,768]{2,1,0:T(8,128)(2,1)} %down.3), custom_call_target="tpu_custom_call" | custom-call | tf_op jit(solution)/shard_map/expert_1/pallas_call | solution.py:286
  164.0 2.0 %all-to-all-done.1 = bf16[8,48,768]{2,1,0:T(8,128)(2,1)S(1)} async-done(((bf16[8,48,768]{2,1,0:T(8,128)(2,1)}), bf16[8,48,768]{2,1,0:T(8,128)(2,1)S(1)}, u32[]{:S(2)}, u32[]{:S(2)}) %all-to-all-start.1) | async-done | bytes 589856 | tf_op jit(solution)/shard_map/all_to_all | solution.py:331
  166.0 15.2 %all_to_all.21 = bf16[8,48,768]{2,1,0:T(8,128)(2,1)} all-to-all(bf16[8,48,768]{2,1,0:T(8,128)(2,1)} %bitcast.25), channel_id=1, replica_groups=mesh['row'=16,'col'=8] {'col'}, dimensions={0} | all-to-all | bytes 1179648 | tf_op jit(solution)/shard_map/all_to_all | solution.py:331
  181.2 2.9 %mix.1 = bf16[256,768]{1,0:T(8,128)(2,1)} custom-call(bf16[256,768]{1,0:T(8,128)(2,1)} %get-tuple-element.40.embedded, f32[256,1]{1,0:T(8,128)} %get-tuple-element.41.gate, s32[256,1]{1,0:T(8,128)} %get-tuple-element.42.place, bf16[384,768]{1,0:T(8,128)(2,1)} %bitcast.26, bf16[384,768]{1,0:T(8,128)(2,1)} %bitcast.27), custom_call_target="tpu_custom_call" | custom-call | tf_op jit(solution)/shard_map/mix/pallas_call | solution.py:313
  (38 shorter events, 0.2 us)
Async XLA Ops:
  0.0 49.8 %collective-permute-start.4 = (bf16[512,768]{1,0:T(8,128)(2,1)}, bf16[512,768]{1,0:T(8,128)(2,1)S(1)}, u32[]{:S(2)}, u32[]{:S(2)}) collective-permute-start(bf16[512,768]{1,0:T(8,128)(2,1)} %refs_4_.1), channel_id=1, source_target_pairs={{0,32},{1,33},{2,34},{3,35},{4,36},{5,37},{6,38},{7,39},{8,40},{9,... | collective-permute-start | bytes 2359304 | tf_op jit(solution)/shard_map/ppermute | solution.py:43
  1.6 48.2 %collective-permute-start.5 = (bf16[512,768]{1,0:T(8,128)(2,1)}, bf16[512,768]{1,0:T(8,128)(2,1)S(1)}, u32[]{:S(2)}, u32[]{:S(2)}) collective-permute-start(bf16[512,768]{1,0:T(8,128)(2,1)} %refs_4_.1), channel_id=1, source_target_pairs={{0,96},{1,97},{2,98},{3,99},{4,100},{5,101},{6,102},{7,103},{8,104... | collective-permute-start | bytes 2359304 | tf_op jit(solution)/shard_map/ppermute | solution.py:43
  3.2 46.6 %collective-permute-start.6 = (bf16[512,768]{1,0:T(8,128)(2,1)}, bf16[512,768]{1,0:T(8,128)(2,1)}, u32[]{:S(2)}, u32[]{:S(2)}) collective-permute-start(bf16[512,768]{1,0:T(8,128)(2,1)} %refs_4_.1), channel_id=1, source_target_pairs={{0,20},{1,21},{2,22},{3,23},{4,16},{5,17},{6,18},{7,19},{8,28},{9,... | collective-permute-start | bytes 2359304 | tf_op jit(solution)/shard_map/ppermute | solution.py:43
  8.3 3.7 %collective-permute-start = (bf16[2,256,128]{2,1,0:T(8,128)(2,1)S(1)}, bf16[2,256,128]{2,1,0:T(8,128)(2,1)S(1)}, u32[]{:S(2)}, u32[]{:S(2)}) collective-permute-start(bf16[2,256,128]{2,1,0:T(8,128)(2,1)S(1)} %get-tuple-element.48), channel_id=1, source_target_pairs={{0,8},{8,16},{16,24},{24,32},{32,40},{40,48},{48,56},{56,64},{64,7... | collective-permute-start | bytes 393224 | tf_op jit(solution)/shard_map/ppermute | solution.py:326
  9.7 3.4 %collective-permute-start.1 = (bf16[2,256,128]{2,1,0:T(8,128)(2,1)S(1)}, bf16[2,256,128]{2,1,0:T(8,128)(2,1)S(1)}, u32[]{:S(2)}, u32[]{:S(2)}) collective-permute-start(bf16[2,256,128]{2,1,0:T(8,128)(2,1)S(1)} %get-tuple-element.47), channel_id=1, source_target_pairs={{8,0},{16,8},{24,16},{32,24},{40,32},{48,40},{56,48},{64,56},{72,6... | collective-permute-start | bytes 393224 | tf_op jit(solution)/shard_map/ppermute | solution.py:326
  12.0 9.5 %copy-start.7 = (bf16[2,256,128]{2,1,0:T(8,128)(2,1)}, bf16[2,256,128]{2,1,0:T(8,128)(2,1)S(1)}, u32[]{:S(2)}) copy-start(bf16[2,256,128]{2,1,0:T(8,128)(2,1)S(1)} %collective-permute-done.top) | copy-start | bytes 393220
  13.1 8.4 %copy-start.8 = (bf16[2,256,128]{2,1,0:T(8,128)(2,1)}, bf16[2,256,128]{2,1,0:T(8,128)(2,1)S(1)}, u32[]{:S(2)}) copy-start(bf16[2,256,128]{2,1,0:T(8,128)(2,1)S(1)} %collective-permute-done.1.bottom) | copy-start | bytes 393220
  13.1 6.6 %collective-permute-start.2 = (bf16[68,2,128]{2,1,0:T(2,128)(2,1)S(1)}, bf16[68,2,128]{2,1,0:T(2,128)(2,1)S(1)}, u32[]{:S(2)}, u32[]{:S(2)}) collective-permute-start(bf16[68,2,128]{2,1,0:T(2,128)(2,1)S(1)} %pad_maximum_fusion.1), channel_id=1, source_target_pairs={{1,0},{2,1},{3,2},{4,3},{5,4},{6,5},{7,6},{9,8},{10,9},{11,10},{12... | collective-permute-start | bytes 104456 | tf_op jit(solution)/shard_map/ppermute | solution.py:326
  14.5 6.2 %collective-permute-start.3 = (bf16[68,2,128]{2,1,0:T(2,128)(2,1)S(1)}, bf16[68,2,128]{2,1,0:T(2,128)(2,1)S(1)}, u32[]{:S(2)}, u32[]{:S(2)}) collective-permute-start(bf16[68,2,128]{2,1,0:T(2,128)(2,1)S(1)} %pad_maximum_fusion.2), channel_id=1, source_target_pairs={{0,1},{1,2},{2,3},{3,4},{4,5},{5,6},{6,7},{8,9},{9,10},{10,11},{11... | collective-permute-start | bytes 104456 | tf_op jit(solution)/shard_map/ppermute | solution.py:326
  31.7 31.5 %collective-permute-start.8 = (bf16[8,96,512]{2,1,0:T(8,128)(2,1)}, bf16[8,96,512]{2,1,0:T(8,128)(2,1)S(1)}, u32[]{:S(2)}, u32[]{:S(2)}) collective-permute-start(bf16[8,96,512]{2,1,0:T(8,128)(2,1)} %get-tuple-element.30), channel_id=1, source_target_pairs={{0,8},{1,9},{2,10},{3,11},{4,12},{5,13},{6,14},{7,15},{8,0},{9,1},... | collective-permute-start | bytes 2359304 | tf_op jit(solution)/shard_map/ppermute | solution.py:43
  49.8 43.6 %copy-start.4 = (bf16[512,768]{1,0:T(8,128)(2,1)}, bf16[512,768]{1,0:T(8,128)(2,1)S(1)}, u32[]{:S(2)}) copy-start(bf16[512,768]{1,0:T(8,128)(2,1)S(1)} %collective-permute-done.4.refs_5_) | copy-start | bytes 2359300
  49.8 0.9 copy-start.5
  50.7 42.7 %collective-permute-start.7 = (bf16[8,160,512]{2,1,0:T(8,128)(2,1)}, bf16[8,160,512]{2,1,0:T(8,128)(2,1)S(1)}, u32[]{:S(2)}, u32[]{:S(2)}) collective-permute-start(bf16[8,160,512]{2,1,0:T(8,128)(2,1)} %get-tuple-element.29), channel_id=1, source_target_pairs={{0,8},{1,9},{2,10},{3,11},{4,12},{5,13},{6,14},{7,15},{8,0},{9,1},... | collective-permute-start | bytes 3932168 | tf_op jit(solution)/shard_map/ppermute | solution.py:43
  50.8 49.3 %collective-permute-start.13 = (bf16[512,768]{1,0:T(8,128)(2,1)}, bf16[512,768]{1,0:T(8,128)(2,1)}, u32[]{:S(2)}, u32[]{:S(2)}) collective-permute-start(bf16[512,768]{1,0:T(8,128)(2,1)} %collective-permute-done.6.refs_7_), channel_id=1, source_target_pairs={{0,32},{1,33},{2,34},{3,35},{4,36},{5,37},{6,38},{7,39},{8,40},{9,... | collective-permute-start | bytes 2359304 | tf_op jit(solution)/shard_map/ppermute | solution.py:43
  60.1 40.0 %collective-permute-start.14 = (bf16[512,768]{1,0:T(8,128)(2,1)}, bf16[512,768]{1,0:T(8,128)(2,1)}, u32[]{:S(2)}, u32[]{:S(2)}) collective-permute-start(bf16[512,768]{1,0:T(8,128)(2,1)} %collective-permute-done.6.refs_7_), channel_id=1, source_target_pairs={{0,96},{1,97},{2,98},{3,99},{4,100},{5,101},{6,102},{7,103},{8,104... | collective-permute-start | bytes 2359304 | tf_op jit(solution)/shard_map/ppermute | solution.py:43
  62.4 25.3 %collective-permute-start.9 = (bf16[256,768]{1,0:T(8,128)(2,1)S(1)}, bf16[256,768]{1,0:T(8,128)(2,1)S(1)}, u32[]{:S(2)}, u32[]{:S(2)}) collective-permute-start(bf16[256,768]{1,0:T(8,128)(2,1)S(1)} %slice.38), channel_id=1, source_target_pairs={{0,32},{1,33},{2,34},{3,35},{4,36},{5,37},{6,38},{7,39},{8,40},{9,... | collective-permute-start | bytes 1179656 | tf_op jit(solution)/shard_map/ppermute | solution.py:43
  63.2 30.2 %copy-start.1 = (bf16[8,96,512]{2,1,0:T(8,128)(2,1)}, bf16[8,96,512]{2,1,0:T(8,128)(2,1)S(1)}, u32[]{:S(2)}) copy-start(bf16[8,96,512]{2,1,0:T(8,128)(2,1)S(1)} %collective-permute-done.8.refs_3_) | copy-start | bytes 2359300
  63.2 29.3 %collective-permute-start.11 = (bf16[256,768]{1,0:T(8,128)(2,1)S(1)}, bf16[256,768]{1,0:T(8,128)(2,1)}, u32[]{:S(2)}, u32[]{:S(2)}) collective-permute-start(bf16[256,768]{1,0:T(8,128)(2,1)S(1)} %slice.39), channel_id=1, source_target_pairs={{0,96},{1,97},{2,98},{3,99},{4,100},{5,101},{6,102},{7,103},{8,104... | collective-permute-start | bytes 1179656 | tf_op jit(solution)/shard_map/ppermute | solution.py:43
  87.7 12.3 %copy-start.9 = (bf16[256,768]{1,0:T(8,128)(2,1)}, bf16[256,768]{1,0:T(8,128)(2,1)S(1)}, u32[]{:S(2)}) copy-start(bf16[256,768]{1,0:T(8,128)(2,1)S(1)} %collective-permute-done.9.refs_4_) | copy-start | bytes 1179652
  87.8 18.1 %collective-permute-start.10 = (bf16[256,768]{1,0:T(8,128)(2,1)S(1)}, bf16[256,768]{1,0:T(8,128)(2,1)}, u32[]{:S(2)}, u32[]{:S(2)}) collective-permute-start(bf16[256,768]{1,0:T(8,128)(2,1)S(1)} %collective-permute-done.9.refs_4_), channel_id=1, source_target_pairs={{0,20},{1,21},{2,22},{3,23},{4,16},{5,17},{6,18},{7,19},{8,28},{9,... | collective-permute-start | bytes 1179656 | tf_op jit(solution)/shard_map/ppermute | solution.py:43
  92.5 17.5 %collective-permute-start.12 = (bf16[256,768]{1,0:T(8,128)(2,1)}, bf16[256,768]{1,0:T(8,128)(2,1)}, u32[]{:S(2)}, u32[]{:S(2)}) collective-permute-start(bf16[256,768]{1,0:T(8,128)(2,1)} %collective-permute-done.11.refs_5_), channel_id=1, source_target_pairs={{0,20},{1,21},{2,22},{3,23},{4,16},{5,17},{6,18},{7,19},{8,28},{9,... | collective-permute-start | bytes 1179656 | tf_op jit(solution)/shard_map/ppermute | solution.py:43
  93.4 1.1 copy-start
  105.8 8.8 %copy-start.10 = (bf16[768,16]{0,1:T(8,128)(2,1)S(1)}, bf16[768,16]{0,1:T(8,128)(2,1)}, u32[]{:S(2)}) copy-start(bf16[768,16]{0,1:T(8,128)(2,1)} %param.12) | copy-start | bytes 73732
  105.8 9.6 %copy-start.11 = (s32[1,1,256,1]{2,3,1,0:T(1,128)S(1)}, s32[1,1,256,1]{2,3,1,0:T(1,128)}, u32[]{:S(2)}) copy-start(s32[1,1,256,1]{2,3,1,0:T(1,128)} %param.13) | copy-start | bytes 3076
  114.5 2.6 %collective-permute-start.15 = (f32[256,768]{1,0:T(8,128)}, f32[256,768]{1,0:T(8,128)S(1)}, u32[]{:S(2)}, u32[]{:S(2)}) collective-permute-start(f32[256,768]{1,0:T(8,128)} %get-tuple-element.39), channel_id=1, source_target_pairs={{0,8},{1,9},{2,10},{3,11},{4,12},{5,13},{6,14},{7,15},{8,0},{9,1},... | collective-permute-start | bytes 2359304 | tf_op jit(solution)/shard_map/ppermute | solution.py:43
  117.1 0.9 copy-start.6
  137.5 14.1 %all-to-all-start.2 = ((bf16[8,48,768]{2,1,0:T(8,128)(2,1)}), bf16[8,48,768]{2,1,0:T(8,128)(2,1)S(1)}, u32[]{:S(2)}, u32[]{:S(2)}) async-start(bf16[8,48,768]{2,1,0:T(8,128)(2,1)} %bitcast.28), calls=%async_computation.2 | async-start | bytes 1179648 | tf_op jit(solution)/shard_map/all_to_all | solution.py:331
  151.7 3.9 %copy-start.2 = (bf16[8,48,768]{2,1,0:T(8,128)(2,1)}, bf16[8,48,768]{2,1,0:T(8,128)(2,1)S(1)}, u32[]{:S(2)}) copy-start(bf16[8,48,768]{2,1,0:T(8,128)(2,1)S(1)} %all-to-all-done.2) | copy-start | bytes 1769476
  151.7 14.4 %all-to-all-start.1 = ((bf16[8,48,768]{2,1,0:T(8,128)(2,1)}), bf16[8,48,768]{2,1,0:T(8,128)(2,1)S(1)}, u32[]{:S(2)}, u32[]{:S(2)}) async-start(bf16[8,48,768]{2,1,0:T(8,128)(2,1)} %bitcast.23), calls=%async_computation.1 | async-start | bytes 1179648 | tf_op jit(solution)/shard_map/all_to_all | solution.py:331
  166.0 15.2 %copy-start.3 = (bf16[8,48,768]{2,1,0:T(8,128)(2,1)}, bf16[8,48,768]{2,1,0:T(8,128)(2,1)S(1)}, u32[]{:S(2)}) copy-start(bf16[8,48,768]{2,1,0:T(8,128)(2,1)S(1)} %all-to-all-done.1) | copy-start | bytes 1769476
where the time goes:
time: 185 us; the launch traced here: 184 us
  Pallas kernels  63.4 us (34%)
  starting transfers between devices  46.4 us (25%)
  waiting for transfers between devices  32.7 us (18%)
  blocking collectives  31.4 us (17%)
  local copies, waits for them, and re-layouts  8.29 us (4%)
    all_to_all x2, blocking collectives, exchange(): return lax.all_to_all(value, 'col', 0, 0, tiled=True).reshape(SLOTS, DIM)  31.4 us
    ppermute x12, starting transfers between devices, send(): return lax.ppermute(value, ('row', 'col'), hop(**step))  30.5 us
    ppermute x12, waiting for transfers between devices, send(): return lax.ppermute(value, ('row', 'col'), hop(**step))  27 us
    pallas_call x2, Pallas kernels, conv_call(): pl.pallas_call(functools.partial(conv_kernel, start, steps), grid=(steps,...  24.1 us
    pallas_call x2, Pallas kernels, expert_call(): pl.pallas_call(expert_kernel, grid=(FF // width,), in_specs=[whole, pl.Bl...  17.3 us
    pallas_call x3, Pallas kernels, embed_call(): pl.pallas_call(functools.partial(embed_kernel, layout, bool(sums)), in_sp...  15.8 us
    ppermute x4, starting transfers between devices, neighbours(): lax.ppermute(value, axis, pairs if ahead else [(j, i) for i, j in pairs])  8.43 us
    all_to_all x2, starting transfers between devices, exchange(): return lax.all_to_all(value, 'col', 0, 0, tiled=True).reshape(SLOTS, DIM)  7.43 us
  transfers between devices with their start and end apart: 18, of which 7 were waited for; matrix products, arithmetic and copies ran while one was open for 4% of the time, Pallas kernels for 29%

commit v1 on v0

--- a/solution.py
+++ b/solution.py
@@ -11,15 +11,19 @@
 WIDE = 272
 DIM, FF, CAP, TOK = 768, 3072, 48, 256
 SLOTS = 8 * CAP
-FIRST = 5
+FIRST = 4
 F32, BF16 = jnp.float32, jnp.bfloat16
 ANY = pl.BlockSpec(memory_space=pl.ANY)
 VMEM = pl.BlockSpec(memory_space=pltpu.VMEM)
 SMEM = pl.BlockSpec(memory_space=pltpu.SMEM)
 
 
-def params():
-    return pltpu.CompilerParams(vmem_limit_bytes=56 * 2**20)
+def params(mib):
+    return pltpu.CompilerParams(vmem_limit_bytes=mib * 2**20)
+
+
+def cost(micros):
+    return pl.CostEstimate(flops=int(micros * 1.15e9), bytes_accessed=0, transcendentals=0)
 
 
 def hop(dx=0, dy=0, dh=0, dl=0, dc=0):
@@ -60,10 +64,8 @@
     return left + parts[:, 256:512] + right
 
 
-def conv_kernel(
-    start, steps, place, scene, top, bottom, strip, first, second, keep, other,
-    block, hidden, rows, w1, w2, sems,
-):
+def conv_kernel(start, steps, place, scene, top, bottom, strip, first, second, *refs):
+    patches, block, hidden, rows, w1, w2, sems = refs[-7:]
     step = pl.program_id(0)
     height = 8 * steps + 4
     base = 8 * start - 2
@@ -81,7 +83,7 @@
         chunks.append(
             [pltpu.make_async_copy(s, d, sems.at[k, n]) for n, (s, d) in enumerate(copies)]
         )
-    place_row, place_col, core = place[0], place[1], place[2]
+    place_row, place_col = place[0], place[1]
     tail = lax.broadcasted_iota(jnp.int32, (16, 256), 0)
     cut = ((place_col == 0) & (tail >= 8)) | ((place_col == 7) & (tail < 8))
     edge = jnp.where(cut, 0.0, 1.0).astype(F32)
@@ -131,23 +133,19 @@
             cells = block[2 * pair + 2 + n, 0:COLS].astype(F32)
             rows[pl.ds((2 * i + n) * COLS, COLS), :] = value[:, n * CH : (n + 1) * CH] + cells
     for dy in range(8):
-        for j in range(4):
-            low = rows[pl.ds(dy * COLS + j, 32, stride=8), :]
-            high = rows[pl.ds(dy * COLS + 4 + j, 32, stride=8), :]
-            lanes = pl.ds(j * CH, CH)
-            keep[dy, :, lanes] = jnp.where(core == 0, low, high).astype(BF16)
-            other[dy, :, lanes] = jnp.where(core == 0, high, low).astype(BF16)
+        for j in range(8):
+            cells = rows[pl.ds(dy * COLS + j, 32, stride=8), :]
+            patches[j // 4, dy, :, pl.ds(j % 4 * CH, CH)] = cells.astype(BF16)
 
 
 def conv_call(start, steps, *args):
-    shape = jax.ShapeDtypeStruct((8, 32 * steps, 512), BF16)
-    out = pl.BlockSpec((8, 32, 512), lambda i: (0, i, 0))
+    given = len(args) - 7
     return pl.pallas_call(
         functools.partial(conv_kernel, start, steps),
         grid=(steps,),
-        in_specs=[SMEM, ANY, ANY, ANY, ANY, VMEM, VMEM],
-        out_specs=[out, out],
-        out_shape=[shape, shape],
+        in_specs=[SMEM, ANY, ANY, ANY, ANY, VMEM, VMEM] + [ANY] * given,
+        out_specs=pl.BlockSpec((2, 8, 32, 512), lambda i: (0, 0, start + i, 0)),
+        out_shape=jax.ShapeDtypeStruct((2, 8, TOK, 512), BF16),
         scratch_shapes=[
             pltpu.VMEM((8 * steps + 4, WIDE, CH), BF16),
             pltpu.VMEM((8 * steps + 2, WIDE, CH), BF16),
@@ -156,70 +154,72 @@
             pltpu.VMEM((512, 768), BF16),
             pltpu.SemaphoreType.DMA((steps, 4)),
         ],
-        compiler_params=params(),
+        input_output_aliases={7: 0} if given else {},
+        compiler_params=params(20),
+        cost_estimate=cost(12),
         name=f"convs_{start}",
     )(*args)
 
 
-def embed_kernel(layout, has_sum, order, *refs):
-    tokens, pieces = refs[0:4], refs[4 : 4 + len(layout)]
-    rest = refs[4 + len(layout) :]
+def embed_kernel(layout, has_sum, order, tokens, *refs):
+    count = sum(len(parts) for _, parts in layout)
+    pieces, rest = refs[:count], refs[count:]
     given, rest = (rest[0:2], rest[2:]) if has_sum else ((), rest)
     own, partner, lhs, rhs, lhs_sems, rhs_sems = rest
-    copies = []
-    for n, (which, offset, depth) in enumerate(layout):
+    copies, at = [], 0
+    for n, (which, parts) in enumerate(layout):
         k = order[which]
-        here, at = [], 0
-        for m, source in enumerate(tokens):
-            count = source.shape[1]
-            here.append(
-                pltpu.make_async_copy(
-                    source.at[k, :, pl.ds(offset, depth)],
-                    lhs.at[n, pl.ds(at, count), pl.ds(0, depth)],
-                    lhs_sems.at[n, m],
-                )
+        here = [
+            pltpu.make_async_copy(
+                tokens.at[order[12 + m], k], lhs.at[n, pl.ds(m * TOK, TOK)], lhs_sems.at[n, m]
             )
-            at += count
-        here.append(
-            pltpu.make_async_copy(pieces[n], rhs.at[n, pl.ds(0, depth)], rhs_sems.at[n])
-        )
+            for m in range(2)
+        ]
+        for m, (first, quarter) in enumerate(parts):
+            if quarter is None:
+                source, target = pieces[at], rhs.at[n]
+            else:
+                target = rhs.at[n, pl.ds(pl.multiple_of(order[quarter] * 128, 128), 128)]
+                source = pieces[at].at[first : first + 128]
+            here.append(pltpu.make_async_copy(source, target, rhs_sems.at[n, m]))
+            at += 1
         copies.append(here)
     for here in copies:
         for copy in here:
             copy.start()
-    for n, (which, offset, depth) in enumerate(layout):
+    for n in range(len(layout)):
         for copy in copies[n]:
             copy.wait()
-        for target, at, base in ((partner, TOK, 1), (own, 0, 0)):
-            part = jnp.dot(
-                lhs[n, pl.ds(at, TOK), 0:depth], rhs[n, 0:depth], preferred_element_type=F32
-            )
+        for m, target in ((1, partner), (0, own)):
+            part = jnp.dot(lhs[n, pl.ds(m * TOK, TOK)], rhs[n], preferred_element_type=F32)
             if n == 0 and not has_sum:
                 target[...] = part
             elif n == 0:
-                target[...] = given[base][...] + part
+                target[...] = given[m][...] + part
             else:
                 target[...] += part
 
 
-def embed_call(name, order, tokens, pieces, sums=()):
-    layout = tuple((which, offset, array.shape[0]) for array, which, offset in pieces)
-    count = len(pieces)
+def embed_call(name, order, tokens, shards, sums=()):
+    layout = tuple((which, tuple(part[1:] for part in parts)) for which, parts in shards)
+    arrays = [part[0] for _, parts in shards for part in parts]
     shape = jax.ShapeDtypeStruct((TOK, DIM), F32)
+    count = len(shards)
     return pl.pallas_call(
         functools.partial(embed_kernel, layout, bool(sums)),
-        in_specs=[SMEM] + [ANY] * (4 + count) + [VMEM] * len(sums),
+        in_specs=[SMEM] + [ANY] * (1 + len(arrays)) + [VMEM] * len(sums),
         out_specs=[VMEM, VMEM],
         out_shape=[shape, shape],
         scratch_shapes=[
             pltpu.VMEM((count, 2 * TOK, 512), BF16),
             pltpu.VMEM((count, 512, DIM), BF16),
+            pltpu.SemaphoreType.DMA((count, 2)),
             pltpu.SemaphoreType.DMA((count, 4)),
-            pltpu.SemaphoreType.DMA((count,)),
         ],
-        compiler_params=params(),
+        compiler_params=params(20),
+        cost_estimate=cost(4),
         name=name,
-    )(order, *tokens, *[array for array, _, _ in pieces], *sums)
+    )(order, tokens, *arrays, *sums)
 
 
 def route_kernel(own, came, router, ids_row, ids_col, embedded, out0, out1, gate, place):
@@ -257,44 +257,29 @@
         in_specs=[VMEM] * 5,
         out_specs=[VMEM] * 5,
         out_shape=[jax.ShapeDtypeStruct(*shape) for shape in shapes],
-        compiler_params=params(),
+        compiler_params=params(16),
+        cost_estimate=cost(3),
         name="route",
     )(*args)
 
 
-def expert_kernel(rows, up, down, out, total):
-    step = pl.program_id(0)
-    z = jnp.dot(rows[...], up[...], preferred_element_type=F32)
-    act = 0.5 * z * (1.0 + jnp.tanh(0.7978845608028654 * (z + 0.044715 * (z * z * z))))
-    part = jnp.dot(act.astype(BF16), down[...], preferred_element_type=F32)
-
-    @pl.when(step == 0)
-    def _():
-        total[...] = part
-
-    @pl.when(step > 0)
-    def _():
-        total[...] += part
-
-    @pl.when(step == pl.num_programs(0) - 1)
-    def _():
-        out[...] = total[...].astype(BF16)
-
-
-def expert_call(which, rows, up, down, width=768):
-    whole = pl.BlockSpec((SLOTS, DIM), lambda i: (0, 0))
-    return pl.pallas_call(
-        expert_kernel,
-        grid=(FF // width,),
-        in_specs=[
-            whole,
-            pl.BlockSpec((None, DIM, width), lambda i: (which, 0, i)),
-            pl.BlockSpec((None, width, DIM), lambda i: (which, i, 0)),
-        ],
-        out_specs=whole,
+def expert_kernel(which, rows, up, down, out, hidden):
+    for at in range(0, FF, 512):
+        z = jnp.dot(rows[...], up[which, :, at : at + 512], preferred_element_type=F32)
+        act = 0.5 * z * (1.0 + jnp.tanh(0.7978845608028654 * (z + 0.044715 * (z * z * z))))
+        hidden[:, at : at + 512] = act.astype(BF16)
+    out[...] = jnp.dot(hidden[...], down[which], preferred_element_type=F32).astype(BF16)
+
+
+def expert_call(which, rows, up, down):
+    return pl.pallas_call(
+        functools.partial(expert_kernel, which),
+        in_specs=[VMEM] * 3,
+        out_specs=VMEM,
         out_shape=jax.ShapeDtypeStruct((SLOTS, DIM), BF16),
-        scratch_shapes=[pltpu.VMEM((SLOTS, DIM), F32)],
-        compiler_params=params(),
+        scratch_shapes=[pltpu.VMEM((SLOTS, FF), BF16)],
+        compiler_params=params(30),
+        cost_estimate=cost(5),
         name=f"expert_{which}",
     )(rows, up, down)
 
@@ -315,7 +300,8 @@
         in_specs=[VMEM] * 5,
         out_specs=VMEM,
         out_shape=jax.ShapeDtypeStruct((TOK, DIM), BF16),
-        compiler_params=params(),
+        compiler_params=params(12),
+        cost_estimate=cost(2),
         name="mix",
     )(*args)
 
@@ -335,8 +321,8 @@
     scene, conv_first, conv_second, embed_weight, router_weight, expert_ids, expert_up, expert_down
 ):
     row, col = lax.axis_index("row"), lax.axis_index("col")
-    x, high, core = row // 4, row // 2 % 2, row % 2
-    place = jnp.stack([row, col, core]).astype(jnp.int32)
+    x, high, core = row >> 2, (row >> 1) & 1, row & 1
+    place = jnp.stack([row, col]).astype(jnp.int32)
 
     top = neighbours(scene[ROWS - 2 :], "row", True)
     bottom = neighbours(scene[:2], "row", False)
@@ -346,36 +332,34 @@
     right = neighbours(left_own, "col", False)
     strip = jnp.concatenate([right, jnp.zeros((ROWS + 4, 12, CH), BF16), left], axis=1)
 
-    w = embed_weight
+    w, y = embed_weight, col & 3
     w_minus, w_plus, w_high = send(w, dx=1), send(w, dx=-1), send(w, dh=1, dl=1)
+    later, strip = lax.optimization_barrier((w, strip))
+    quarter = lax.dynamic_slice_in_dim(later, y * 128, 128, 0)
+    far, high_far = send(quarter, dx=2), send(quarter, dx=2, dh=1, dl=1)
     scene_args = (place, scene, top, bottom, strip, conv_first, conv_second)
-    keep0, other0 = conv_call(0, FIRST, *scene_args)
-    keep0, other0, w_minus, w_plus, w_high = lax.optimization_barrier(
-        (keep0, other0, w_minus, w_plus, w_high)
+    patches = conv_call(0, FIRST, *scene_args)
+    patches, w_minus, w_plus, w_high, far, high_far = lax.optimization_barrier(
+        (patches, w_minus, w_plus, w_high, far, high_far)
     )
-    w_far0, w_far1 = send(w_minus[:256], dx=1), send(w_plus[256:], dx=-1)
-    w_high_minus, w_high_plus = send(w_high, dx=1), send(w_high, dx=-1)
-    came0 = send(other0, dc=1)
-    keep1, other1 = conv_call(FIRST, 8 - FIRST, *scene_args)
-    came1 = send(other1, dc=1)
-    w_high_far0, w_high_far1 = send(w_far0, dh=1, dl=1), send(w_far1, dh=1, dl=1)
-
-    shards = [(a % 4) * 2 + (b % 2) for b in (high, high + 1) for a in (x, x - 1, x + 1, x + 2)]
-    order = jnp.stack(shards).astype(jnp.int32)
-    tokens = (keep0, keep1, came0, came1)
-    sums = embed_call(
-        "embed_a", order, tokens, [(w, 0, 0), (w_minus, 1, 0), (w_plus, 2, 0), (w_high, 4, 0)]
-    )
-    sums = embed_call(
-        "embed_b",
-        order,
-        tokens,
-        [(w_far0, 3, 0), (w_far1, 3, 256), (w_high_minus, 5, 0), (w_high_plus, 6, 0)],
-        sums,
-    )
-    own, partner = embed_call(
-        "embed_c", order, tokens, [(w_high_far0, 7, 0), (w_high_far1, 7, 256)], sums
-    )
+    w_high_minus, w_high_plus = send(w_minus, dh=1, dl=1), send(w_high, dx=-1)
+    fars = jnp.concatenate([far, high_far], axis=0)
+    fars = (fars, send(fars, dy=1), send(fars, dy=-1), send(fars, dy=2))
+    patches = conv_call(FIRST, 8 - FIRST, *scene_args, patches)
+    pairs = [[i, i + 1] for i in range(0, 16, 2)]
+    patches = lax.all_to_all(patches, "row", 0, 0, axis_index_groups=pairs, tiled=True)
+
+    shards = [(a & 3) * 2 + (b & 1) for b in (high, high + 1) for a in (x, x - 1, x + 1, x + 2)]
+    order = shards + [y, (y + 3) & 3, (y + 1) & 3, (y + 2) & 3, core, 1 - core]
+    order = jnp.stack(order).astype(jnp.int32)
+    whole = [(0, w), (1, w_minus), (2, w_plus), (4, w_high), (5, w_high_minus), (6, w_high_plus)]
+    whole = [(which, [(array, 0, None)]) for which, array in whole]
+    parts = [
+        (which, [(array, first, 8 + n) for n, array in enumerate(fars)])
+        for which, first in ((3, 0), (7, 128))
+    ]
+    sums = embed_call("embed_a", order, patches, whole[:4])
+    own, partner = embed_call("embed_b", order, patches, parts + whole[4:], sums)
     came = send(partner, dc=1)
     embedded, out0, out1, gate, slots = route_call(
         own, came, router_weight, expert_ids.reshape(1, TOK), expert_ids.reshape(TOK, 1)

time: 185 us -> 161 us (0.87)
  waiting for transfers between devices: 32.7 us -> 4.2 us
  Pallas kernels: 63.4 us -> 40.9 us
  local copies, waits for them, and re-layouts: 8.29 us -> 22.4 us
  blocking collectives: 31.4 us -> 39.9 us
  starting transfers between devices: 46.4 us -> 51.8 us
    ppermute x12 -> x11, waiting for transfers between devices: 27 us -> 1.8 us  [send(): return lax.ppermute(value, ('row', 'col'), hop(**step))]
    unnamed x25 -> x24, local copies, waits for them, and re-layouts: 3.71 us -> 19 us
    pallas_call x2, Pallas kernels: 17.3 us -> 9.05 us  [expert_call(): pl.pallas_call(functools.partial(expert_kernel, which), in_specs=[VMEM] *...]
    pallas_call x3 -> x2, Pallas kernels: 15.8 us -> 8.32 us  [embed_call(): pl.pallas_call(functools.partial(embed_kernel, layout, bool(sums)), in_sp...]
    all_to_all x0 -> x1, blocking collectives: none -> 7.23 us  [local(): lax.all_to_all(patches, 'row', 0, 0, axis_index_groups=pairs, tiled=True)]
    pallas_call x2, Pallas kernels: 24.1 us -> 20.4 us  [conv_call(): pl.pallas_call(functools.partial(conv_kernel, start, steps), grid=(steps,...]
    all_to_all x2, waiting for transfers between devices: 3.73 us -> 0.01 us  [exchange(): return lax.all_to_all(value, 'col', 0, 0, tiled=True).reshape(SLOTS, DIM)]
    ppermute x12 -> x11, starting transfers between devices: 30.5 us -> 34.2 us  [send(): return lax.ppermute(value, ('row', 'col'), hop(**step))]
  transfers between devices with their start and end apart: 18 -> 17, of which waited for: 7 -> 3; matrix products, arithmetic and copies ran while one was open for 4% -> 2% of each run, Pallas kernels for 29% -> 20%
where the time goes in v1:
time: 161 us; the launch traced here: 160 us
  starting transfers between devices  51.8 us (32%)
  Pallas kernels  40.9 us (25%)
  blocking collectives  39.9 us (25%)
  local copies, waits for them, and re-layouts  22.4 us (14%)
  waiting for transfers between devices  4.2 us (3%)
    ppermute x11, starting transfers between devices, send(): return lax.ppermute(value, ('row', 'col'), hop(**step))  34.2 us
    all_to_all x2, blocking collectives, exchange(): return lax.all_to_all(value, 'col', 0, 0, tiled=True).reshape(SLOTS, DIM)  32.7 us
    pallas_call x2, Pallas kernels, conv_call(): pl.pallas_call(functools.partial(conv_kernel, start, steps), grid=(steps,...  20.4 us
    unnamed x24, local copies, waits for them, and re-layouts  19 us
    all_to_all x2, starting transfers between devices, exchange(): return lax.all_to_all(value, 'col', 0, 0, tiled=True).reshape(SLOTS, DIM)  9.16 us
    pallas_call x2, Pallas kernels, expert_call(): pl.pallas_call(functools.partial(expert_kernel, which), in_specs=[VMEM] *...  9.05 us
    ppermute x4, starting transfers between devices, neighbours(): lax.ppermute(value, axis, pairs if ahead else [(j, i) for i, j in pairs])  8.43 us
    pallas_call x2, Pallas kernels, embed_call(): pl.pallas_call(functools.partial(embed_kernel, layout, bool(sums)), in_sp...  8.32 us
  transfers between devices with their start and end apart: 17, of which 3 were waited for; matrix products, arithmetic and copies ran while one was open for 2% of the time, Pallas kernels for 20%

profile of v1, /device:TPU:0, one launch (start us, length us, event | category | flops | bytes accessed | tf_op | source)
XLA Modules:
  0.0 159.8 jit_solution(8702239518276580108)
XLA Ops:
  0.0 1.6 collective-permute-start.4
  1.6 1.7 %collective-permute-start.5 = (bf16[512,768]{1,0:T(8,128)(2,1)}, bf16[512,768]{1,0:T(8,128)(2,1)S(1)}, u32[]{:S(2)}, u32[]{:S(2)}) collective-permute-start(bf16[512,768]{1,0:T(8,128)(2,1)} %refs_0_.1), channel_id=1, source_target_pairs={{0,96},{1,97},{2,98},{3,99},{4,100},{5,101},{6,102},{7,103},{8,104... | collective-permute-start | bytes 2359304 | tf_op jit(solution)/shard_map/ppermute | solution.py:47
  3.2 4.1 %collective-permute-start.6 = (bf16[512,768]{1,0:T(8,128)(2,1)}, bf16[512,768]{1,0:T(8,128)(2,1)S(1)}, u32[]{:S(2)}, u32[]{:S(2)}) collective-permute-start(bf16[512,768]{1,0:T(8,128)(2,1)} %refs_0_.1), channel_id=1, source_target_pairs={{0,20},{1,21},{2,22},{3,23},{4,16},{5,17},{6,18},{7,19},{8,28},{9,... | collective-permute-start | bytes 2359304 | tf_op jit(solution)/shard_map/ppermute | solution.py:47
  7.4 1.0 fusion.1
  8.3 1.3 collective-permute-start
  9.7 1.3 collective-permute-start.1
  11.0 1.0 fusion
  12.0 1.1 collective-permute-done.1.bottom
  13.1 0.1 pad_maximum_fusion.1
  13.1 1.3 collective-permute-start.2
  14.4 0.1 pad_maximum_fusion.2
  14.5 4.5 %collective-permute-start.3 = (bf16[68,2,128]{2,1,0:T(2,128)(2,1)S(1)}, bf16[68,2,128]{2,1,0:T(2,128)(2,1)S(1)}, u32[]{:S(2)}, u32[]{:S(2)}) collective-permute-start(bf16[68,2,128]{2,1,0:T(2,128)(2,1)S(1)} %pad_maximum_fusion.2), channel_id=1, source_target_pairs={{0,1},{1,2},{2,3},{3,4},{4,5},{5,6},{6,7},{8,9},{9,10},{10,11},{11... | collective-permute-start | bytes 104456 | tf_op jit(solution)/shard_map/ppermute | solution.py:312
  19.1 0.1 pad_add_fusion.place
  19.1 0.1 pad.1.clone
  19.2 0.1 stack.68.order
  19.3 1.3 collective-permute-done.3
  20.7 0.1 pad_maximum_fusion.strip
  20.8 0.0 copy-start.8
  20.8 1.0 constant_dynamic-slice_fusion
  21.8 14.5 %collective-permute-start.7 = (bf16[128,768]{1,0:T(8,128)(2,1)S(1)}, bf16[128,768]{1,0:T(8,128)(2,1)S(1)}, u32[]{:S(2)}, u32[]{:S(2)}) collective-permute-start(bf16[128,768]{1,0:T(8,128)(2,1)S(1)} %constant_dynamic-slice_fusion), channel_id=1, source_target_pairs={{0,64},{1,65},{2,66},{3,67},{4,68},{5,69},{6,70},{7,71},{8,72},{9,... | collective-permute-start | bytes 589832 | tf_op jit(solution)/shard_map/ppermute | solution.py:47
  36.2 2.2 %copy-done.1 = bf16[64,256,128]{2,1,0:T(8,128)(2,1)S(1)} copy-done((bf16[64,256,128]{2,1,0:T(8,128)(2,1)S(1)}, bf16[64,256,128]{2,1,0:T(8,128)(2,1)}, u32[]{:S(2)}) %copy-start.1) | copy-done | bytes 4194328
  38.4 1.0 copy-done.7
  39.4 1.0 copy-done.9
  40.4 9.9 %convs_0.1.refs_0_ = bf16[2,8,256,512]{3,2,1,0:T(8,128)(2,1)S(1)} custom-call(s32[2]{0:T(128)S(1)} %pad_add_fusion.place, bf16[64,256,128]{2,1,0:T(8,128)(2,1)S(1)} %copy-done.1, bf16[2,256,128]{2,1,0:T(8,128)(2,1)S(1)} %collective-permute-done.top, bf16[2,256,128]{2,1,0:T(8,128)(2,1)S(1)} %collective-permute-done.1.bottom, ...), custom_call_target="tpu_custom_call" | custom-call | flops 13799999488 | tf_op jit(solution)/shard_map/convs_0/pallas_call | solution.py:143
  50.3 5.2 %collective-permute-start.10 = (bf16[256,768]{1,0:T(8,128)(2,1)S(1)}, bf16[256,768]{1,0:T(8,128)(2,1)S(1)}, u32[]{:S(2)}, u32[]{:S(2)}) collective-permute-start(bf16[256,768]{1,0:T(8,128)(2,1)S(1)} %constant_dynamic-update-slice_fusion.refs_0_.refs_4_), channel_id=1, source_target_pairs={{0,3},{1,0},{2,1},{3,2},{4,7},{5,4},{6,5},{7,6},{8,11},{9,8},{10,9... | collective-permute-start | bytes 1179656 | tf_op jit(solution)/shard_map/ppermute | solution.py:47
  55.5 0.9 collective-permute-start.9
  56.5 2.8 %collective-permute-start.12 = (bf16[512,768]{1,0:T(8,128)(2,1)S(1)}, bf16[512,768]{1,0:T(8,128)(2,1)S(1)}, u32[]{:S(2)}, u32[]{:S(2)}) collective-permute-start(bf16[512,768]{1,0:T(8,128)(2,1)S(1)} %collective-permute-done.4.refs_1_), channel_id=1, source_target_pairs={{0,20},{1,21},{2,22},{3,23},{4,16},{5,17},{6,18},{7,19},{8,28},{9,... | collective-permute-start | bytes 2359304 | tf_op jit(solution)/shard_map/ppermute | solution.py:47
  59.2 3.2 %collective-permute-start.13 = (bf16[512,768]{1,0:T(8,128)(2,1)S(1)}, bf16[512,768]{1,0:T(8,128)(2,1)S(1)}, u32[]{:S(2)}, u32[]{:S(2)}) collective-permute-start(bf16[512,768]{1,0:T(8,128)(2,1)S(1)} %collective-permute-done.6.refs_3_), channel_id=1, source_target_pairs={{0,96},{1,97},{2,98},{3,99},{4,100},{5,101},{6,102},{7,103},{8,104... | collective-permute-start | bytes 2359304 | tf_op jit(solution)/shard_map/ppermute | solution.py:47
  62.4 10.5 %convs_4.1 = bf16[2,8,256,512]{3,2,1,0:T(8,128)(2,1)S(1)} custom-call(s32[2]{0:T(128)S(1)} %pad_add_fusion.place, bf16[64,256,128]{2,1,0:T(8,128)(2,1)S(1)} %copy-done.1, bf16[2,256,128]{2,1,0:T(8,128)(2,1)S(1)} %collective-permute-done.top, bf16[2,256,128]{2,1,0:T(8,128)(2,1)S(1)} %collective-permute-done.1.bottom, ...), custom_call_target="tpu_custom_call", output_to_operand_aliasing={{}: (7, {})} | custom-call | flops 13799999488 | tf_op jit(solution)/shard_map/convs_4/pallas_call | solution.py:143
  73.0 7.2 %all_to_all.25.tokens = bf16[2,8,256,512]{3,2,1,0:T(8,128)(2,1)S(1)} all-to-all(bf16[2,8,256,512]{3,2,1,0:T(8,128)(2,1)S(1)} %convs_4.1), channel_id=1, replica_groups={{0,8},{16,24},{32,40},{48,56},{64,72},{80,88},{96,104},{112,120},{1,9},..., dimensions={0} | all-to-all | bytes 8388608 | tf_op jit(solution)/shard_map/all_to_all | solution.py:350
  80.2 3.1 %embed_a.1 = (f32[256,768]{1,0:T(8,128)S(1)}, f32[256,768]{1,0:T(8,128)S(1)}) custom-call(s32[14]{0:T(128)S(1)} %stack.68.order, bf16[2,8,256,512]{3,2,1,0:T(8,128)(2,1)S(1)} %all_to_all.25.tokens, bf16[512,768]{1,0:T(8,128)(2,1)S(1)} %copy-done, bf16[512,768]{1,0:T(8,128)(2,1)S(1)} %collective-permute-done.4.refs_1_, ...), custom_call_target="tpu_custom_call" | custom-call | flops 4600000000 | tf_op jit(solution)/shard_map/embed_a/pallas_call | solution.py:208
  83.4 5.2 %embed_b.1 = (f32[256,768]{1,0:T(8,128)S(1)}, f32[256,768]{1,0:T(8,128)S(1)}) custom-call(s32[14]{0:T(128)S(1)} %stack.68.order, bf16[2,8,256,512]{3,2,1,0:T(8,128)(2,1)S(1)} %all_to_all.25.tokens, bf16[256,768]{1,0:T(8,128)(2,1)S(1)} %constant_dynamic-update-slice_fusion.refs_0_.refs_4_, bf16[256,768]{1,0:T(8,128)(2,1)S(1)} %collective-permute-done.9.refs_1_.refs_5_, ...), custom_call_target="tpu_custom_call" | custom-call | flops 4600000000 | tf_op jit(solution)/shard_map/embed_b/pallas_call | solution.py:208
  88.6 0.3 collective-permute-start.14
  88.9 0.2 copy.11.router
  89.1 0.1 copy.12.ids_col
  89.2 1.8 %collective-permute-done.14.came = f32[256,768]{1,0:T(8,128)S(1)} collective-permute-done((f32[256,768]{1,0:T(8,128)S(1)}, f32[256,768]{1,0:T(8,128)S(1)}, u32[]{:S(2)}, u32[]{:S(2)}) %collective-permute-start.14) | collective-permute-done | bytes 786464 | tf_op jit(solution)/shard_map/ppermute | solution.py:47
  91.0 1.7 %route.1 = (bf16[256,768]{1,0:T(8,128)(2,1)S(1)}, bf16[384,768]{1,0:T(8,128)(2,1)S(1)}, bf16[384,768]{1,0:T(8,128)(2,1)}, f32[256,1]{1,0:T(8,128)S(1)}, s32[256,1]{1,0:T(8,128)S(1)}) custom-call(f32[256,768]{1,0:T(8,128)S(1)} %get-tuple-element.32.own, f32[256,768]{1,0:T(8,128)S(1)} %collective-permute-done.14.came, bf16[768,16]{1,0:T(8,128)(2,1)S(1)} %copy.11.router, ...), custom_call_target="tpu_custom_call" | custom-call | flops 3449999872 | tf_op jit(solution)/shard_map/route/pallas_call | solution.py:255
  92.7 17.5 %all_to_all.26 = bf16[8,48,768]{2,1,0:T(8,128)(2,1)S(1)} all-to-all(bf16[8,48,768]{2,1,0:T(8,128)(2,1)S(1)} %bitcast.29), channel_id=1, replica_groups=mesh['row'=16,'col'=8] {'col'}, dimensions={0} | all-to-all | bytes 1179648 | tf_op jit(solution)/shard_map/all_to_all | solution.py:317
  110.3 3.5 %all-to-all-start.3 = ((bf16[8,48,768]{2,1,0:T(8,128)(2,1)}), bf16[8,48,768]{2,1,0:T(8,128)(2,1)S(1)}, u32[]{:S(2)}, u32[]{:S(2)}) async-start(bf16[8,48,768]{2,1,0:T(8,128)(2,1)} %bitcast.22), calls=%async_computation.3 | async-start | bytes 1179648 | tf_op jit(solution)/shard_map/all_to_all | solution.py:317
  113.8 3.7 %copy-done.3 = bf16[2,768,3072]{2,1,0:T(8,128)(2,1)S(1)} copy-done((bf16[2,768,3072]{2,1,0:T(8,128)(2,1)S(1)}, bf16[2,768,3072]{2,1,0:T(8,128)(2,1)}, u32[]{:S(2)}) %copy-start.3) | copy-done | bytes 9437208
  117.5 3.7 %copy-done.5 = bf16[2,3072,768]{2,1,0:T(8,128)(2,1)S(1)} copy-done((bf16[2,3072,768]{2,1,0:T(8,128)(2,1)S(1)}, bf16[2,3072,768]{2,1,0:T(8,128)(2,1)}, u32[]{:S(2)}) %copy-start.5) | copy-done | bytes 9437208
  121.2 5.0 %expert_0.1 = bf16[384,768]{1,0:T(8,128)(2,1)} custom-call(bf16[384,768]{1,0:T(8,128)(2,1)S(1)} %bitcast.30, bf16[2,768,3072]{2,1,0:T(8,128)(2,1)S(1)} %copy-done.3, bf16[2,3072,768]{2,1,0:T(8,128)(2,1)S(1)} %copy-done.5), custom_call_target="tpu_custom_call" | custom-call | flops 5750000128 | tf_op jit(solution)/shard_map/expert_0/pallas_call | solution.py:275
  126.1 5.6 %all-to-all-start.2 = ((bf16[8,48,768]{2,1,0:T(8,128)(2,1)}), bf16[8,48,768]{2,1,0:T(8,128)(2,1)S(1)}, u32[]{:S(2)}, u32[]{:S(2)}) async-start(bf16[8,48,768]{2,1,0:T(8,128)(2,1)} %bitcast.20), calls=%async_computation.2 | async-start | bytes 1179648 | tf_op jit(solution)/shard_map/all_to_all | solution.py:317
  131.8 3.7 %copy-done.4 = bf16[2,768,3072]{2,1,0:T(8,128)(2,1)S(1)} copy-done((bf16[2,768,3072]{2,1,0:T(8,128)(2,1)S(1)}, bf16[2,768,3072]{2,1,0:T(8,128)(2,1)}, u32[]{:S(2)}) %copy-start.4) | copy-done | bytes 9437208
  135.5 3.7 %copy-done.6 = bf16[2,3072,768]{2,1,0:T(8,128)(2,1)S(1)} copy-done((bf16[2,3072,768]{2,1,0:T(8,128)(2,1)S(1)}, bf16[2,3072,768]{2,1,0:T(8,128)(2,1)}, u32[]{:S(2)}) %copy-start.6) | copy-done | bytes 9437208
  139.1 4.1 %expert_1.1 = bf16[384,768]{1,0:T(8,128)(2,1)S(1)} custom-call(bf16[384,768]{1,0:T(8,128)(2,1)S(1)} %bitcast.28, bf16[2,768,3072]{2,1,0:T(8,128)(2,1)S(1)} %copy-done.4, bf16[2,3072,768]{2,1,0:T(8,128)(2,1)S(1)} %copy-done.6), custom_call_target="tpu_custom_call" | custom-call | flops 5750000128 | tf_op jit(solution)/shard_map/expert_1/pallas_call | solution.py:275
  143.2 15.1 %all_to_all.27 = bf16[8,48,768]{2,1,0:T(8,128)(2,1)S(1)} all-to-all(bf16[8,48,768]{2,1,0:T(8,128)(2,1)S(1)} %bitcast.31), channel_id=1, replica_groups=mesh['row'=16,'col'=8] {'col'}, dimensions={0} | all-to-all | bytes 1179648 | tf_op jit(solution)/shard_map/all_to_all | solution.py:317
  158.4 1.4 mix.1
  (35 shorter events, 0.1 us)
Async XLA Ops:
  0.0 50.3 %collective-permute-start.4 = (bf16[512,768]{1,0:T(8,128)(2,1)}, bf16[512,768]{1,0:T(8,128)(2,1)S(1)}, u32[]{:S(2)}, u32[]{:S(2)}) collective-permute-start(bf16[512,768]{1,0:T(8,128)(2,1)} %refs_0_.1), channel_id=1, source_target_pairs={{0,32},{1,33},{2,34},{3,35},{4,36},{5,37},{6,38},{7,39},{8,40},{9,... | collective-permute-start | bytes 2359304 | tf_op jit(solution)/shard_map/ppermute | solution.py:47
  1.6 48.7 %collective-permute-start.5 = (bf16[512,768]{1,0:T(8,128)(2,1)}, bf16[512,768]{1,0:T(8,128)(2,1)S(1)}, u32[]{:S(2)}, u32[]{:S(2)}) collective-permute-start(bf16[512,768]{1,0:T(8,128)(2,1)} %refs_0_.1), channel_id=1, source_target_pairs={{0,96},{1,97},{2,98},{3,99},{4,100},{5,101},{6,102},{7,103},{8,104... | collective-permute-start | bytes 2359304 | tf_op jit(solution)/shard_map/ppermute | solution.py:47
  3.2 47.1 %collective-permute-start.6 = (bf16[512,768]{1,0:T(8,128)(2,1)}, bf16[512,768]{1,0:T(8,128)(2,1)S(1)}, u32[]{:S(2)}, u32[]{:S(2)}) collective-permute-start(bf16[512,768]{1,0:T(8,128)(2,1)} %refs_0_.1), channel_id=1, source_target_pairs={{0,20},{1,21},{2,22},{3,23},{4,16},{5,17},{6,18},{7,19},{8,28},{9,... | collective-permute-start | bytes 2359304 | tf_op jit(solution)/shard_map/ppermute | solution.py:47
  8.3 3.6 %collective-permute-start = (bf16[2,256,128]{2,1,0:T(8,128)(2,1)S(1)}, bf16[2,256,128]{2,1,0:T(8,128)(2,1)S(1)}, u32[]{:S(2)}, u32[]{:S(2)}) collective-permute-start(bf16[2,256,128]{2,1,0:T(8,128)(2,1)S(1)} %get-tuple-element.42), channel_id=1, source_target_pairs={{0,8},{8,16},{16,24},{24,32},{32,40},{40,48},{48,56},{56,64},{64,7... | collective-permute-start | bytes 393224 | tf_op jit(solution)/shard_map/ppermute | solution.py:312
  9.7 3.4 %collective-permute-start.1 = (bf16[2,256,128]{2,1,0:T(8,128)(2,1)S(1)}, bf16[2,256,128]{2,1,0:T(8,128)(2,1)S(1)}, u32[]{:S(2)}, u32[]{:S(2)}) collective-permute-start(bf16[2,256,128]{2,1,0:T(8,128)(2,1)S(1)} %get-tuple-element.41), channel_id=1, source_target_pairs={{8,0},{16,8},{24,16},{32,24},{40,32},{48,40},{56,48},{64,56},{72,6... | collective-permute-start | bytes 393224 | tf_op jit(solution)/shard_map/ppermute | solution.py:312
  13.1 6.2 %collective-permute-start.2 = (bf16[68,2,128]{2,1,0:T(2,128)(2,1)S(1)}, bf16[68,2,128]{2,1,0:T(2,128)(2,1)S(1)}, u32[]{:S(2)}, u32[]{:S(2)}) collective-permute-start(bf16[68,2,128]{2,1,0:T(2,128)(2,1)S(1)} %pad_maximum_fusion.1), channel_id=1, source_target_pairs={{1,0},{2,1},{3,2},{4,3},{5,4},{6,5},{7,6},{9,8},{10,9},{11,10},{12... | collective-permute-start | bytes 104456 | tf_op jit(solution)/shard_map/ppermute | solution.py:312
  14.5 6.2 %collective-permute-start.3 = (bf16[68,2,128]{2,1,0:T(2,128)(2,1)S(1)}, bf16[68,2,128]{2,1,0:T(2,128)(2,1)S(1)}, u32[]{:S(2)}, u32[]{:S(2)}) collective-permute-start(bf16[68,2,128]{2,1,0:T(2,128)(2,1)S(1)} %pad_maximum_fusion.2), channel_id=1, source_target_pairs={{0,1},{1,2},{2,3},{3,4},{4,5},{5,6},{6,7},{8,9},{9,10},{10,11},{11... | collective-permute-start | bytes 104456 | tf_op jit(solution)/shard_map/ppermute | solution.py:312
  20.8 41.7 %copy-start.8 = (bf16[3,3,128,128]{3,2,1,0:T(8,128)(2,1)S(1)}, bf16[3,3,128,128]{3,2,1,0:T(8,128)(2,1)}, u32[]{:S(2)}) copy-start(bf16[3,3,128,128]{3,2,1,0:T(8,128)(2,1)} %first.3) | copy-start | bytes 884740
  21.8 28.5 %collective-permute-start.7 = (bf16[128,768]{1,0:T(8,128)(2,1)S(1)}, bf16[128,768]{1,0:T(8,128)(2,1)S(1)}, u32[]{:S(2)}, u32[]{:S(2)}) collective-permute-start(bf16[128,768]{1,0:T(8,128)(2,1)S(1)} %constant_dynamic-slice_fusion), channel_id=1, source_target_pairs={{0,64},{1,65},{2,66},{3,67},{4,68},{5,69},{6,70},{7,71},{8,72},{9,... | collective-permute-start | bytes 589832 | tf_op jit(solution)/shard_map/ppermute | solution.py:47
  36.2 14.0 %collective-permute-start.8 = (bf16[128,768]{1,0:T(8,128)(2,1)S(1)}, bf16[128,768]{1,0:T(8,128)(2,1)S(1)}, u32[]{:S(2)}, u32[]{:S(2)}) collective-permute-start(bf16[128,768]{1,0:T(8,128)(2,1)S(1)} %constant_dynamic-slice_fusion), channel_id=1, source_target_pairs={{0,84},{1,85},{2,86},{3,87},{4,80},{5,81},{6,82},{7,83},{8,92},{9,... | collective-permute-start | bytes 589832 | tf_op jit(solution)/shard_map/ppermute | solution.py:47
  36.2 2.2 %copy-start.1 = (bf16[64,256,128]{2,1,0:T(8,128)(2,1)S(1)}, bf16[64,256,128]{2,1,0:T(8,128)(2,1)}, u32[]{:S(2)}) copy-start(bf16[64,256,128]{2,1,0:T(8,128)(2,1)} %scene.3) | copy-start | bytes 12582916
  38.4 1.0 copy-start.7
  39.4 1.0 copy-start.9
  50.3 33.0 %collective-permute-start.10 = (bf16[256,768]{1,0:T(8,128)(2,1)S(1)}, bf16[256,768]{1,0:T(8,128)(2,1)S(1)}, u32[]{:S(2)}, u32[]{:S(2)}) collective-permute-start(bf16[256,768]{1,0:T(8,128)(2,1)S(1)} %constant_dynamic-update-slice_fusion.refs_0_.refs_4_), channel_id=1, source_target_pairs={{0,3},{1,0},{2,1},{3,2},{4,7},{5,4},{6,5},{7,6},{8,11},{9,8},{10,9... | collective-permute-start | bytes 1179656 | tf_op jit(solution)/shard_map/ppermute | solution.py:47
  55.5 27.8 %collective-permute-start.11 = (bf16[256,768]{1,0:T(8,128)(2,1)S(1)}, bf16[256,768]{1,0:T(8,128)(2,1)S(1)}, u32[]{:S(2)}, u32[]{:S(2)}) collective-permute-start(bf16[256,768]{1,0:T(8,128)(2,1)S(1)} %constant_dynamic-update-slice_fusion.refs_0_.refs_4_), channel_id=1, source_target_pairs={{0,2},{1,3},{2,0},{3,1},{4,6},{5,7},{6,4},{7,5},{8,10},{9,11},{10,... | collective-permute-start | bytes 1179656 | tf_op jit(solution)/shard_map/ppermute | solution.py:47
  55.5 27.8 %collective-permute-start.9 = (bf16[256,768]{1,0:T(8,128)(2,1)S(1)}, bf16[256,768]{1,0:T(8,128)(2,1)S(1)}, u32[]{:S(2)}, u32[]{:S(2)}) collective-permute-start(bf16[256,768]{1,0:T(8,128)(2,1)S(1)} %constant_dynamic-update-slice_fusion.refs_0_.refs_4_), channel_id=1, source_target_pairs={{0,1},{1,2},{2,3},{3,0},{4,5},{5,6},{6,7},{7,4},{8,9},{9,10},{10,1... | collective-permute-start | bytes 1179656 | tf_op jit(solution)/shard_map/ppermute | solution.py:47
  56.5 26.9 %collective-permute-start.12 = (bf16[512,768]{1,0:T(8,128)(2,1)S(1)}, bf16[512,768]{1,0:T(8,128)(2,1)S(1)}, u32[]{:S(2)}, u32[]{:S(2)}) collective-permute-start(bf16[512,768]{1,0:T(8,128)(2,1)S(1)} %collective-permute-done.4.refs_1_), channel_id=1, source_target_pairs={{0,20},{1,21},{2,22},{3,23},{4,16},{5,17},{6,18},{7,19},{8,28},{9,... | collective-permute-start | bytes 2359304 | tf_op jit(solution)/shard_map/ppermute | solution.py:47
  59.2 24.1 %collective-permute-start.13 = (bf16[512,768]{1,0:T(8,128)(2,1)S(1)}, bf16[512,768]{1,0:T(8,128)(2,1)S(1)}, u32[]{:S(2)}, u32[]{:S(2)}) collective-permute-start(bf16[512,768]{1,0:T(8,128)(2,1)S(1)} %collective-permute-done.6.refs_3_), channel_id=1, source_target_pairs={{0,96},{1,97},{2,98},{3,99},{4,100},{5,101},{6,102},{7,103},{8,104... | collective-permute-start | bytes 2359304 | tf_op jit(solution)/shard_map/ppermute | solution.py:47
  73.0 7.2 %copy-start = (bf16[512,768]{1,0:T(8,128)(2,1)S(1)}, bf16[512,768]{1,0:T(8,128)(2,1)}, u32[]{:S(2)}) copy-start(bf16[512,768]{1,0:T(8,128)(2,1)} %refs_0_.1) | copy-start | bytes 2359300
  83.4 5.5 %copy-start.10 = (bf16[768,16]{0,1:T(8,128)(2,1)S(1)}, bf16[768,16]{0,1:T(8,128)(2,1)}, u32[]{:S(2)}) copy-start(bf16[768,16]{0,1:T(8,128)(2,1)} %param.12) | copy-start | bytes 73732
  83.4 5.7 %copy-start.2 = (s32[1,1,256,1]{2,3,1,0:T(1,128)S(1)}, s32[1,1,256,1]{2,3,1,0:T(1,128)}, u32[]{:S(2)}) copy-start(s32[1,1,256,1]{2,3,1,0:T(1,128)} %param.13) | copy-start | bytes 3076
  88.6 2.4 %collective-permute-start.14 = (f32[256,768]{1,0:T(8,128)S(1)}, f32[256,768]{1,0:T(8,128)S(1)}, u32[]{:S(2)}, u32[]{:S(2)}) collective-permute-start(f32[256,768]{1,0:T(8,128)S(1)} %get-tuple-element.33), channel_id=1, source_target_pairs={{0,8},{1,9},{2,10},{3,11},{4,12},{5,13},{6,14},{7,15},{8,0},{9,1},... | collective-permute-start | bytes 2359304 | tf_op jit(solution)/shard_map/ppermute | solution.py:47
  110.3 15.9 %all-to-all-start.3 = ((bf16[8,48,768]{2,1,0:T(8,128)(2,1)}), bf16[8,48,768]{2,1,0:T(8,128)(2,1)S(1)}, u32[]{:S(2)}, u32[]{:S(2)}) async-start(bf16[8,48,768]{2,1,0:T(8,128)(2,1)} %bitcast.22), calls=%async_computation.3 | async-start | bytes 1179648 | tf_op jit(solution)/shard_map/all_to_all | solution.py:317
  113.8 3.7 %copy-start.3 = (bf16[2,768,3072]{2,1,0:T(8,128)(2,1)S(1)}, bf16[2,768,3072]{2,1,0:T(8,128)(2,1)}, u32[]{:S(2)}) copy-start(bf16[2,768,3072]{2,1,0:T(8,128)(2,1)} %up.3) | copy-start | bytes 28311556
  117.5 3.7 %copy-start.5 = (bf16[2,3072,768]{2,1,0:T(8,128)(2,1)S(1)}, bf16[2,3072,768]{2,1,0:T(8,128)(2,1)}, u32[]{:S(2)}) copy-start(bf16[2,3072,768]{2,1,0:T(8,128)(2,1)} %down.3) | copy-start | bytes 28311556
  126.1 17.1 %all-to-all-start.2 = ((bf16[8,48,768]{2,1,0:T(8,128)(2,1)}), bf16[8,48,768]{2,1,0:T(8,128)(2,1)S(1)}, u32[]{:S(2)}, u32[]{:S(2)}) async-start(bf16[8,48,768]{2,1,0:T(8,128)(2,1)} %bitcast.20), calls=%async_computation.2 | async-start | bytes 1179648 | tf_op jit(solution)/shard_map/all_to_all | solution.py:317
  131.8 3.7 %copy-start.4 = (bf16[2,768,3072]{2,1,0:T(8,128)(2,1)S(1)}, bf16[2,768,3072]{2,1,0:T(8,128)(2,1)}, u32[]{:S(2)}) copy-start(bf16[2,768,3072]{2,1,0:T(8,128)(2,1)} %up.3) | copy-start | bytes 28311556
  135.4 3.7 %copy-start.6 = (bf16[2,3072,768]{2,1,0:T(8,128)(2,1)S(1)}, bf16[2,3072,768]{2,1,0:T(8,128)(2,1)}, u32[]{:S(2)}) copy-start(bf16[2,3072,768]{2,1,0:T(8,128)(2,1)} %down.3) | copy-start | bytes 28311556

commit v2 on v1

--- a/solution.py
+++ b/solution.py
@@ -11,11 +11,12 @@
 WIDE = 272
 DIM, FF, CAP, TOK = 768, 3072, 48, 256
 SLOTS = 8 * CAP
-FIRST = 4
+STEPS = ROWS // 8
 F32, BF16 = jnp.float32, jnp.bfloat16
 ANY = pl.BlockSpec(memory_space=pl.ANY)
 VMEM = pl.BlockSpec(memory_space=pltpu.VMEM)
 SMEM = pl.BlockSpec(memory_space=pltpu.SMEM)
+HBM = pl.BlockSpec(memory_space=pltpu.HBM)
 
 
 def params(mib):
@@ -64,25 +65,28 @@
     return left + parts[:, 256:512] + right
 
 
-def conv_kernel(start, steps, place, scene, top, bottom, strip, first, second, *refs):
-    patches, block, hidden, rows, w1, w2, sems = refs[-7:]
+def conv_kernel(
+    place, scene, top, bottom, strip, first, second, patches,
+    block, hidden, rows, w1, w2, first_in, second_in, sems, weight_sems,
+):
     step = pl.program_id(0)
-    height = 8 * steps + 4
-    base = 8 * start - 2
     chunks = []
-    for k in range(steps):
+    for k in range(STEPS):
         lo, hi = (0, 12) if k == 0 else (4 + 8 * k, 12 + 8 * k)
-        copies = []
-        if base + lo < 0:
+        a, b = max(lo - 2, 0), min(hi - 2, ROWS)
+        copies = [(scene.at[a:b], block.at[a + 2 : b + 2, 0:COLS])]
+        if k == 0:
             copies.append((top, block.at[0:2, 0:COLS]))
-        a, b = max(base + lo, 0), min(base + hi, ROWS)
-        copies.append((scene.at[a:b], block.at[a - base : b - base, 0:COLS]))
-        if base + hi > ROWS:
-            copies.append((bottom, block.at[height - 2 : height, 0:COLS]))
-        copies.append((strip.at[base + lo + 2 : base + hi + 2], block.at[lo:hi, COLS:WIDE]))
+        if k == STEPS - 1:
+            copies.append((bottom, block.at[ROWS + 2 : ROWS + 4, 0:COLS]))
+        copies.append((strip.at[lo:hi], block.at[lo:hi, COLS:WIDE]))
         chunks.append(
             [pltpu.make_async_copy(s, d, sems.at[k, n]) for n, (s, d) in enumerate(copies)]
         )
+    weights = [
+        pltpu.make_async_copy(first, first_in, weight_sems.at[0]),
+        pltpu.make_async_copy(second, second_in, weight_sems.at[1]),
+    ]
     place_row, place_col = place[0], place[1]
     tail = lax.broadcasted_iota(jnp.int32, (16, 256), 0)
     cut = ((place_col == 0) & (tail >= 8)) | ((place_col == 7) & (tail < 8))
@@ -97,21 +101,22 @@
 
     @pl.when(step == 0)
     def _():
-        for chunk in chunks:
+        for chunk in [chunks[0], weights] + chunks[1:]:
             for copy in chunk:
                 copy.start()
-        pair_weights(first, w1)
-        pair_weights(second, w2)
+        for copy in weights:
+            copy.wait()
+        pair_weights(first_in, w1)
+        pair_weights(second_in, w2)
         for copy in chunks[0]:
             copy.wait()
         conv_first(0)
-        if start == 0:
-
-            @pl.when(place_row == 0)
-            def _():
-                hidden[0] = jnp.zeros((WIDE, CH), BF16)
-
-    for k in range(1, steps):
+
+        @pl.when(place_row == 0)
+        def _():
+            hidden[0] = jnp.zeros((WIDE, CH), BF16)
+
+    for k in range(1, STEPS):
 
         @pl.when(step == k)
         def _(k=k):
@@ -120,11 +125,10 @@
 
     for i in range(4):
         conv_first(4 * step + 1 + i)
-    if 8 * (start + steps) == ROWS:
-
-        @pl.when((step == steps - 1) & (place_row == 15))
-        def _():
-            hidden[8 * steps + 1] = jnp.zeros((WIDE, CH), BF16)
+
+    @pl.when((step == STEPS - 1) & (place_row == 15))
+    def _():
+        hidden[ROWS + 1] = jnp.zeros((WIDE, CH), BF16)
 
     for i in range(4):
         pair = 4 * step + i
@@ -138,26 +142,27 @@
             patches[j // 4, dy, :, pl.ds(j % 4 * CH, CH)] = cells.astype(BF16)
 
 
-def conv_call(start, steps, *args):
-    given = len(args) - 7
+def conv_call(*args):
     return pl.pallas_call(
-        functools.partial(conv_kernel, start, steps),
-        grid=(steps,),
-        in_specs=[SMEM, ANY, ANY, ANY, ANY, VMEM, VMEM] + [ANY] * given,
-        out_specs=pl.BlockSpec((2, 8, 32, 512), lambda i: (0, 0, start + i, 0)),
+        conv_kernel,
+        grid=(STEPS,),
+        in_specs=[SMEM, HBM, ANY, ANY, ANY, HBM, HBM],
+        out_specs=pl.BlockSpec((2, 8, 32, 512), lambda i: (0, 0, i, 0)),
         out_shape=jax.ShapeDtypeStruct((2, 8, TOK, 512), BF16),
         scratch_shapes=[
-            pltpu.VMEM((8 * steps + 4, WIDE, CH), BF16),
-            pltpu.VMEM((8 * steps + 2, WIDE, CH), BF16),
+            pltpu.VMEM((ROWS + 4, WIDE, CH), BF16),
+            pltpu.VMEM((ROWS + 2, WIDE, CH), BF16),
             pltpu.VMEM((8 * COLS, CH), F32),
             pltpu.VMEM((512, 768), BF16),
             pltpu.VMEM((512, 768), BF16),
-            pltpu.SemaphoreType.DMA((steps, 4)),
+            pltpu.VMEM((3, 3, CH, CH), BF16),
+            pltpu.VMEM((3, 3, CH, CH), BF16),
+            pltpu.SemaphoreType.DMA((STEPS, 4)),
+            pltpu.SemaphoreType.DMA((2,)),
         ],
-        input_output_aliases={7: 0} if given else {},
-        compiler_params=params(20),
-        cost_estimate=cost(12),
-        name=f"convs_{start}",
+        compiler_params=params(60),
+        cost_estimate=cost(20),
+        name="convs",
     )(*args)
 
 
@@ -171,17 +176,13 @@
         k = order[which]
         here = [
             pltpu.make_async_copy(
-                tokens.at[order[12 + m], k], lhs.at[n, pl.ds(m * TOK, TOK)], lhs_sems.at[n, m]
+                tokens.at[order[8 + m], k], lhs.at[n, pl.ds(m * TOK, TOK)], lhs_sems.at[n, m]
             )
             for m in range(2)
         ]
-        for m, (first, quarter) in enumerate(parts):
-            if quarter is None:
-                source, target = pieces[at], rhs.at[n]
-            else:
-                target = rhs.at[n, pl.ds(pl.multiple_of(order[quarter] * 128, 128), 128)]
-                source = pieces[at].at[first : first + 128]
-            here.append(pltpu.make_async_copy(source, target, rhs_sems.at[n, m]))
+        for m, (first, count) in enumerate(parts):
+            target = rhs.at[n, pl.ds(first, count)]
+            here.append(pltpu.make_async_copy(pieces[at], target, rhs_sems.at[n, m]))
             at += 1
         copies.append(here)
     for here in copies:
@@ -201,8 +202,11 @@
 
 
 def embed_call(name, order, tokens, shards, sums=()):
-    layout = tuple((which, tuple(part[1:] for part in parts)) for which, parts in shards)
-    arrays = [part[0] for _, parts in shards for part in parts]
+    layout, arrays = [], []
+    for which, parts in shards:
+        heights = [part.shape[0] for part in parts]
+        layout.append((which, [(sum(heights[:m]), count) for m, count in enumerate(heights)]))
+        arrays.extend(parts)
     shape = jax.ShapeDtypeStruct((TOK, DIM), F32)
     count = len(shards)
     return pl.pallas_call(
@@ -263,22 +267,43 @@
     )(*args)
 
 
-def expert_kernel(which, rows, up, down, out, hidden):
-    for at in range(0, FF, 512):
-        z = jnp.dot(rows[...], up[which, :, at : at + 512], preferred_element_type=F32)
+def expert_kernel(which, width, rows, up, down, out, up_in, down_in, sems):
+    copies = []
+    for n, at in enumerate(range(0, FF, width)):
+        part = pl.ds(at, width)
+        copies.append(
+            (
+                pltpu.make_async_copy(up.at[which, :, part], up_in.at[n], sems.at[0, n]),
+                pltpu.make_async_copy(down.at[which, part], down_in.at[n], sems.at[1, n]),
+            )
+        )
+    for pair in copies:
+        for copy in pair:
+            copy.start()
+    total = None
+    for n, (up_copy, down_copy) in enumerate(copies):
+        up_copy.wait()
+        z = jnp.dot(rows[...], up_in[n], preferred_element_type=F32)
         act = 0.5 * z * (1.0 + jnp.tanh(0.7978845608028654 * (z + 0.044715 * (z * z * z))))
-        hidden[:, at : at + 512] = act.astype(BF16)
-    out[...] = jnp.dot(hidden[...], down[which], preferred_element_type=F32).astype(BF16)
-
-
-def expert_call(which, rows, up, down):
+        down_copy.wait()
+        part = jnp.dot(act.astype(BF16), down_in[n], preferred_element_type=F32)
+        total = part if total is None else total + part
+    out[...] = total.astype(BF16)
+
+
+def expert_call(which, rows, up, down, width=512):
+    count = FF // width
     return pl.pallas_call(
-        functools.partial(expert_kernel, which),
-        in_specs=[VMEM] * 3,
+        functools.partial(expert_kernel, which, width),
+        in_specs=[VMEM, HBM, HBM],
         out_specs=VMEM,
         out_shape=jax.ShapeDtypeStruct((SLOTS, DIM), BF16),
-        scratch_shapes=[pltpu.VMEM((SLOTS, FF), BF16)],
-        compiler_params=params(30),
+        scratch_shapes=[
+            pltpu.VMEM((count, DIM, width), BF16),
+            pltpu.VMEM((count, width, DIM), BF16),
+            pltpu.SemaphoreType.DMA((2, count)),
+        ],
+        compiler_params=params(56),
         cost_estimate=cost(5),
         name=f"expert_{which}",
     )(rows, up, down)
@@ -332,34 +357,28 @@
     right = neighbours(left_own, "col", False)
     strip = jnp.concatenate([right, jnp.zeros((ROWS + 4, 12, CH), BF16), left], axis=1)
 
-    w, y = embed_weight, col & 3
+    w = embed_weight
     w_minus, w_plus, w_high = send(w, dx=1), send(w, dx=-1), send(w, dh=1, dl=1)
-    later, strip = lax.optimization_barrier((w, strip))
-    quarter = lax.dynamic_slice_in_dim(later, y * 128, 128, 0)
-    far, high_far = send(quarter, dx=2), send(quarter, dx=2, dh=1, dl=1)
-    scene_args = (place, scene, top, bottom, strip, conv_first, conv_second)
-    patches = conv_call(0, FIRST, *scene_args)
-    patches, w_minus, w_plus, w_high, far, high_far = lax.optimization_barrier(
-        (patches, w_minus, w_plus, w_high, far, high_far)
+    strip, w_minus, w_plus, w_high = lax.optimization_barrier((strip, w_minus, w_plus, w_high))
+    w_far, w_high_plus = send(w_minus, dx=1), send(w_high, dx=-1)
+    w_high_minus = send(w_minus, dh=1, dl=1)
+    patches = conv_call(place, scene, top, bottom, strip, conv_first, conv_second)
+    patches, w_far, w_high_plus, w_high_minus = lax.optimization_barrier(
+        (patches, w_far, w_high_plus, w_high_minus)
     )
-    w_high_minus, w_high_plus = send(w_minus, dh=1, dl=1), send(w_high, dx=-1)
-    fars = jnp.concatenate([far, high_far], axis=0)
-    fars = (fars, send(fars, dy=1), send(fars, dy=-1), send(fars, dy=2))
-    patches = conv_call(FIRST, 8 - FIRST, *scene_args, patches)
+    last = [
+        send(w_high_plus[:176], dx=-1),
+        send(w_high_minus[176:352], dx=1),
+        send(w_far[352:], dh=1, dl=1),
+    ]
     pairs = [[i, i + 1] for i in range(0, 16, 2)]
     patches = lax.all_to_all(patches, "row", 0, 0, axis_index_groups=pairs, tiled=True)
 
-    shards = [(a & 3) * 2 + (b & 1) for b in (high, high + 1) for a in (x, x - 1, x + 1, x + 2)]
-    order = shards + [y, (y + 3) & 3, (y + 1) & 3, (y + 2) & 3, core, 1 - core]
-    order = jnp.stack(order).astype(jnp.int32)
-    whole = [(0, w), (1, w_minus), (2, w_plus), (4, w_high), (5, w_high_minus), (6, w_high_plus)]
-    whole = [(which, [(array, 0, None)]) for which, array in whole]
-    parts = [
-        (which, [(array, first, 8 + n) for n, array in enumerate(fars)])
-        for which, first in ((3, 0), (7, 128))
-    ]
-    sums = embed_call("embed_a", order, patches, whole[:4])
-    own, partner = embed_call("embed_b", order, patches, parts + whole[4:], sums)
+    order = [(a & 3) * 2 + (b & 1) for b in (high, high + 1) for a in (x, x - 1, x + 1, x + 2)]
+    order = jnp.stack(order + [core, 1 - core]).astype(jnp.int32)
+    whole = [w, w_minus, w_plus, w_far, w_high, w_high_minus, w_high_plus]
+    sums = embed_call("embed_a", order, patches, [(n, [a]) for n, a in enumerate(whole)])
+    own, partner = embed_call("embed_b", order, patches, [(7, last)], sums)
     came = send(partner, dc=1)
     embedded, out0, out1, gate, slots = route_call(
         own, came, router_weight, expert_ids.reshape(1, TOK), expert_ids.reshape(TOK, 1)

time: 161 us -> 152 us (0.944)
  local copies, waits for them, and re-layouts: 22.4 us -> 6.71 us
  Pallas kernels: 40.9 us -> 54 us
  blocking collectives: 39.9 us -> 33.4 us
  starting transfers between devices: 51.8 us -> 45.8 us
  waiting for transfers between devices: 4.2 us -> 8.99 us
    unnamed x24 -> x17, local copies, waits for them, and re-layouts: 19 us -> 2.22 us
    pallas_call x4 -> x3, Pallas kernels: 29.5 us -> 43.1 us  [the longest x1 22.8 us: conv_call(): pl.pallas_call(conv_kernel, grid=(STEPS,), in_specs=[SMEM, HBM, ANY, ANY,...]
    ppermute x11 -> x10, starting transfers between devices: 34.2 us -> 22.7 us  [send(): return lax.ppermute(value, ('row', 'col'), hop(**step))]
    all_to_all x1 -> x0, blocking collectives: 7.23 us -> none  [local(): lax.all_to_all(patches, 'row', 0, 0, axis_index_groups=pairs, tiled=True)]
    all_to_all x0 -> x1, starting transfers between devices: none -> 5.76 us  [local(): lax.all_to_all(patches, 'row', 0, 0, axis_index_groups=pairs, tiled=True)]
    ppermute x11 -> x10, waiting for transfers between devices: 1.8 us -> 6.18 us  [send(): return lax.ppermute(value, ('row', 'col'), hop(**step))]
    slice x0 -> x3, local copies, waits for them, and re-layouts: none -> 2.16 us  [the longest x1 0.73 us: local(): w_high_minus[176:352]]
  transfers between devices with their start and end apart: 17 -> 17, of which waited for: 3 -> 6; matrix products, arithmetic and copies ran while one was open for 2% -> 4% of each run, Pallas kernels for 20% -> 32%
where the time goes in v2:
time: 152 us; the launch traced here: 151 us
  Pallas kernels  54 us (36%)
  starting transfers between devices  45.8 us (30%)
  blocking collectives  33.4 us (22%)
  waiting for transfers between devices  8.99 us (6%)
  local copies, waits for them, and re-layouts  6.71 us (4%)
  other arithmetic  1.59 us (1%)
    all_to_all x2, blocking collectives, exchange(): return lax.all_to_all(value, 'col', 0, 0, tiled=True).reshape(SLOTS, DIM)  33.4 us
    pallas_call x1, Pallas kernels, conv_call(): pl.pallas_call(conv_kernel, grid=(STEPS,), in_specs=[SMEM, HBM, ANY, ANY,...  22.8 us
    ppermute x10, starting transfers between devices, send(): return lax.ppermute(value, ('row', 'col'), hop(**step))  22.7 us
    pallas_call x2, Pallas kernels, expert_call(): pl.pallas_call(functools.partial(expert_kernel, which, width), in_specs=[...  20.3 us
    all_to_all x2, starting transfers between devices, exchange(): return lax.all_to_all(value, 'col', 0, 0, tiled=True).reshape(SLOTS, DIM)  8.97 us
    ppermute x4, starting transfers between devices, neighbours(): lax.ppermute(value, axis, pairs if ahead else [(j, i) for i, j in pairs])  8.43 us
    pallas_call x2, Pallas kernels, embed_call(): pl.pallas_call(functools.partial(embed_kernel, layout, bool(sums)), in_sp...  7.72 us
    ppermute x10, waiting for transfers between devices, send(): return lax.ppermute(value, ('row', 'col'), hop(**step))  6.18 us
  transfers between devices with their start and end apart: 17, of which 6 were waited for; matrix products, arithmetic and copies ran while one was open for 4% of the time, Pallas kernels for 32%

profile of v2, /device:TPU:0, one launch (start us, length us, event | category | flops | bytes accessed | tf_op | source)
XLA Modules:
  0.0 150.8 jit_solution(6529692429797404610)
XLA Ops:
  0.0 1.6 %collective-permute-start.4 = (bf16[512,768]{1,0:T(8,128)(2,1)}, bf16[512,768]{1,0:T(8,128)(2,1)}, u32[]{:S(2)}, u32[]{:S(2)}) collective-permute-start(bf16[512,768]{1,0:T(8,128)(2,1)} %refs_0_.1), channel_id=1, source_target_pairs={{0,32},{1,33},{2,34},{3,35},{4,36},{5,37},{6,38},{7,39},{8,40},{9,... | collective-permute-start | bytes 2359304 | tf_op jit(solution)/shard_map/ppermute | solution.py:48
  1.6 1.7 %collective-permute-start.5 = (bf16[512,768]{1,0:T(8,128)(2,1)}, bf16[512,768]{1,0:T(8,128)(2,1)S(1)}, u32[]{:S(2)}, u32[]{:S(2)}) collective-permute-start(bf16[512,768]{1,0:T(8,128)(2,1)} %refs_0_.1), channel_id=1, source_target_pairs={{0,96},{1,97},{2,98},{3,99},{4,100},{5,101},{6,102},{7,103},{8,104... | collective-permute-start | bytes 2359304 | tf_op jit(solution)/shard_map/ppermute | solution.py:48
  3.2 4.1 %collective-permute-start.6 = (bf16[512,768]{1,0:T(8,128)(2,1)}, bf16[512,768]{1,0:T(8,128)(2,1)}, u32[]{:S(2)}, u32[]{:S(2)}) collective-permute-start(bf16[512,768]{1,0:T(8,128)(2,1)} %refs_0_.1), channel_id=1, source_target_pairs={{0,20},{1,21},{2,22},{3,23},{4,16},{5,17},{6,18},{7,19},{8,28},{9,... | collective-permute-start | bytes 2359304 | tf_op jit(solution)/shard_map/ppermute | solution.py:48
  7.4 1.0 fusion.1
  8.3 1.3 collective-permute-start
  9.7 1.3 collective-permute-start.1
  11.0 1.0 fusion
  12.0 1.0 collective-permute-done.1.bottom
  13.1 0.1 pad_maximum_fusion.1
  13.1 1.3 collective-permute-start.2
  14.4 0.1 pad_maximum_fusion.2
  14.5 4.5 %collective-permute-start.3 = (bf16[68,2,128]{2,1,0:T(2,128)(2,1)S(1)}, bf16[68,2,128]{2,1,0:T(2,128)(2,1)S(1)}, u32[]{:S(2)}, u32[]{:S(2)}) collective-permute-start(bf16[68,2,128]{2,1,0:T(2,128)(2,1)S(1)} %pad_maximum_fusion.2), channel_id=1, source_target_pairs={{0,1},{1,2},{2,3},{3,4},{4,5},{5,6},{6,7},{8,9},{9,10},{10,11},{11... | collective-permute-start | bytes 104456 | tf_op jit(solution)/shard_map/ppermute | solution.py:337
  19.1 0.7 pad_add_fusion.place
  19.7 0.1 pad.1.clone
  19.8 0.1 stack.52.order
  19.9 0.8 collective-permute-done.3
  20.7 0.8 pad_maximum_fusion.strip
  21.5 0.9 copy-done.2
  22.4 4.3 %collective-permute-done.6.refs_4_ = bf16[512,768]{1,0:T(8,128)(2,1)} collective-permute-done((bf16[512,768]{1,0:T(8,128)(2,1)}, bf16[512,768]{1,0:T(8,128)(2,1)}, u32[]{:S(2)}, u32[]{:S(2)}) %collective-permute-start.6) | collective-permute-done | bytes 786464 | tf_op jit(solution)/shard_map/ppermute | solution.py:48
  26.7 8.5 %collective-permute-start.7 = (bf16[512,768]{1,0:T(8,128)(2,1)}, bf16[512,768]{1,0:T(8,128)(2,1)S(1)}, u32[]{:S(2)}, u32[]{:S(2)}) collective-permute-start(bf16[512,768]{1,0:T(8,128)(2,1)} %collective-permute-done.4.refs_1_), channel_id=1, source_target_pairs={{0,32},{1,33},{2,34},{3,35},{4,36},{5,37},{6,38},{7,39},{8,40},{9,... | collective-permute-start | bytes 2359304 | tf_op jit(solution)/shard_map/ppermute | solution.py:48
  35.2 1.4 collective-permute-start.8
  36.6 22.8 %convs.1 = bf16[2,8,256,512]{3,2,1,0:T(8,128)(2,1)} custom-call(s32[2]{0:T(128)} %pad_add_fusion.place, bf16[64,256,128]{2,1,0:T(8,128)(2,1)} %scene.1, bf16[2,256,128]{2,1,0:T(8,128)(2,1)} %copy-done.6, bf16[2,256,128]{2,1,0:T(8,128)(2,1)} %copy-done.7, bf16[68,16,128]{2,1,0:T(8,128)(2,1)} %pad_maximum_fusion.strip, bf16[3,3,128,128]{3,2,1,0:T(8,128)(2,1)} %first.1, ...), custom_call_target="tpu_custom_call" | custom-call | flops 23000000512 | tf_op jit(solution)/shard_map/convs/pallas_call | solution.py:146
  59.4 5.8 %all-to-all-start = ((bf16[2,8,256,512]{3,2,1,0:T(8,128)(2,1)}), bf16[2,8,256,512]{3,2,1,0:T(8,128)(2,1)}, u32[]{:S(2)}, u32[]{:S(2)}) async-start(bf16[2,8,256,512]{3,2,1,0:T(8,128)(2,1)} %convs.1), calls=%async_computation | async-start | bytes 8388608 | tf_op jit(solution)/shard_map/all_to_all | solution.py:375
  65.2 0.7 slice.41
  65.9 1.9 %collective-permute-start.10 = (bf16[176,768]{1,0:T(8,128)(2,1)}, bf16[176,768]{1,0:T(8,128)(2,1)S(1)}, u32[]{:S(2)}, u32[]{:S(2)}) collective-permute-start(bf16[176,768]{1,0:T(8,128)(2,1)} %slice.41), channel_id=1, source_target_pairs={{0,96},{1,97},{2,98},{3,99},{4,100},{5,101},{6,102},{7,103},{8,104... | collective-permute-start | bytes 811016 | tf_op jit(solution)/shard_map/ppermute | solution.py:48
  67.9 0.7 slice.42
  68.6 0.1 collective-permute-start.11
  68.7 0.7 slice.43
  69.4 3.2 %collective-permute-start.12 = (bf16[160,768]{1,0:T(8,128)(2,1)}, bf16[160,768]{1,0:T(8,128)(2,1)}, u32[]{:S(2)}, u32[]{:S(2)}) collective-permute-start(bf16[160,768]{1,0:T(8,128)(2,1)} %slice.43), channel_id=1, source_target_pairs={{0,20},{1,21},{2,22},{3,23},{4,16},{5,17},{6,18},{7,19},{8,28},{9,... | collective-permute-start | bytes 737288 | tf_op jit(solution)/shard_map/ppermute | solution.py:48
  72.6 0.8 all-to-all-done.tokens
  73.3 1.1 copy-done.3
  74.5 5.3 %embed_a.1 = (f32[256,768]{1,0:T(8,128)S(1)}, f32[256,768]{1,0:T(8,128)S(1)}) custom-call(s32[10]{0:T(128)S(1)} %stack.52.order, bf16[2,8,256,512]{3,2,1,0:T(8,128)(2,1)} %all-to-all-done.tokens, bf16[512,768]{1,0:T(8,128)(2,1)S(1)} %copy-done.1, bf16[512,768]{1,0:T(8,128)(2,1)} %collective-permute-done.4.refs_1_, bf16[512,768]{1,0:T(8,128)(2,1)S(1)} %copy-done.3, ...), custom_call_target="tpu_custom_call" | custom-call | flops 4600000000 | tf_op jit(solution)/shard_map/embed_a/pallas_call | solution.py:212
  79.9 0.0 copy-start.5
  79.9 0.0 copy-start
  79.9 2.4 %embed_b.1 = (f32[256,768]{1,0:T(8,128)S(1)}, f32[256,768]{1,0:T(8,128)S(1)}) custom-call(s32[10]{0:T(128)S(1)} %stack.52.order, bf16[2,8,256,512]{3,2,1,0:T(8,128)(2,1)} %all-to-all-done.tokens, bf16[176,768]{1,0:T(8,128)(2,1)S(1)} %collective-permute-done.10.refs_0_, bf16[176,768]{1,0:T(8,128)(2,1)} %collective-permute-done.11.refs_1_, ...), custom_call_target="tpu_custom_call" | custom-call | flops 4600000000 | tf_op jit(solution)/shard_map/embed_b/pallas_call | solution.py:212
  82.3 0.2 collective-permute-start.13
  82.5 0.2 copy.10.router
  82.7 0.1 copy.11.ids_col
  82.8 1.8 %collective-permute-done.13.came = f32[256,768]{1,0:T(8,128)S(1)} collective-permute-done((f32[256,768]{1,0:T(8,128)S(1)}, f32[256,768]{1,0:T(8,128)S(1)}, u32[]{:S(2)}, u32[]{:S(2)}) %collective-permute-start.13) | collective-permute-done | bytes 786464 | tf_op jit(solution)/shard_map/ppermute | solution.py:48
  84.6 1.8 %route.1 = (bf16[256,768]{1,0:T(8,128)(2,1)S(1)}, bf16[384,768]{1,0:T(8,128)(2,1)S(1)}, bf16[384,768]{1,0:T(8,128)(2,1)}, f32[256,1]{1,0:T(8,128)S(1)}, s32[256,1]{1,0:T(8,128)S(1)}) custom-call(f32[256,768]{1,0:T(8,128)S(1)} %get-tuple-element.32.own, f32[256,768]{1,0:T(8,128)S(1)} %collective-permute-done.13.came, bf16[768,16]{1,0:T(8,128)(2,1)S(1)} %copy.10.router, ...), custom_call_target="tpu_custom_call" | custom-call | flops 3449999872 | tf_op jit(solution)/shard_map/route/pallas_call | solution.py:259
  86.4 18.1 %all_to_all.25 = bf16[8,48,768]{2,1,0:T(8,128)(2,1)} all-to-all(bf16[8,48,768]{2,1,0:T(8,128)(2,1)S(1)} %bitcast.24), channel_id=1, replica_groups=mesh['row'=16,'col'=8] {'col'}, dimensions={0} | all-to-all | bytes 1179648 | tf_op jit(solution)/shard_map/all_to_all | solution.py:342
  104.5 3.7 %all-to-all-start.3 = ((bf16[8,48,768]{2,1,0:T(8,128)(2,1)}), bf16[8,48,768]{2,1,0:T(8,128)(2,1)S(1)}, u32[]{:S(2)}, u32[]{:S(2)}) async-start(bf16[8,48,768]{2,1,0:T(8,128)(2,1)} %bitcast.18), calls=%async_computation.3 | async-start | bytes 1179648 | tf_op jit(solution)/shard_map/all_to_all | solution.py:342
  108.2 10.1 %expert_0.1 = bf16[384,768]{1,0:T(8,128)(2,1)} custom-call(bf16[384,768]{1,0:T(8,128)(2,1)} %bitcast.30, bf16[2,768,3072]{2,1,0:T(8,128)(2,1)} %up.3, bf16[2,3072,768]{2,1,0:T(8,128)(2,1)} %down.3), custom_call_target="tpu_custom_call" | custom-call | flops 5750000128 | tf_op jit(solution)/shard_map/expert_0/pallas_call | solution.py:296
  118.4 0.2 all-to-all-done.3
  118.6 5.3 %all-to-all-start.2 = ((bf16[8,48,768]{2,1,0:T(8,128)(2,1)}), bf16[8,48,768]{2,1,0:T(8,128)(2,1)S(1)}, u32[]{:S(2)}, u32[]{:S(2)}) async-start(bf16[8,48,768]{2,1,0:T(8,128)(2,1)} %bitcast.29), calls=%async_computation.2 | async-start | bytes 1179648 | tf_op jit(solution)/shard_map/all_to_all | solution.py:342
  123.8 10.2 %expert_1.1 = bf16[384,768]{1,0:T(8,128)(2,1)} custom-call(bf16[384,768]{1,0:T(8,128)(2,1)} %bitcast.28, bf16[2,768,3072]{2,1,0:T(8,128)(2,1)} %up.3, bf16[2,3072,768]{2,1,0:T(8,128)(2,1)} %down.3), custom_call_target="tpu_custom_call" | custom-call | flops 5750000128 | tf_op jit(solution)/shard_map/expert_1/pallas_call | solution.py:296
  134.0 15.3 %all_to_all.26 = bf16[8,48,768]{2,1,0:T(8,128)(2,1)S(1)} all-to-all(bf16[8,48,768]{2,1,0:T(8,128)(2,1)} %bitcast.31), channel_id=1, replica_groups=mesh['row'=16,'col'=8] {'col'}, dimensions={0} | all-to-all | bytes 1179648 | tf_op jit(solution)/shard_map/all_to_all | solution.py:342
  149.4 1.4 mix.1
  (27 shorter events, 0.1 us)
Async XLA Ops:
  0.0 21.5 %collective-permute-start.4 = (bf16[512,768]{1,0:T(8,128)(2,1)}, bf16[512,768]{1,0:T(8,128)(2,1)}, u32[]{:S(2)}, u32[]{:S(2)}) collective-permute-start(bf16[512,768]{1,0:T(8,128)(2,1)} %refs_0_.1), channel_id=1, source_target_pairs={{0,32},{1,33},{2,34},{3,35},{4,36},{5,37},{6,38},{7,39},{8,40},{9,... | collective-permute-start | bytes 2359304 | tf_op jit(solution)/shard_map/ppermute | solution.py:48
  1.6 19.9 %collective-permute-start.5 = (bf16[512,768]{1,0:T(8,128)(2,1)}, bf16[512,768]{1,0:T(8,128)(2,1)S(1)}, u32[]{:S(2)}, u32[]{:S(2)}) collective-permute-start(bf16[512,768]{1,0:T(8,128)(2,1)} %refs_0_.1), channel_id=1, source_target_pairs={{0,96},{1,97},{2,98},{3,99},{4,100},{5,101},{6,102},{7,103},{8,104... | collective-permute-start | bytes 2359304 | tf_op jit(solution)/shard_map/ppermute | solution.py:48
  3.2 23.5 %collective-permute-start.6 = (bf16[512,768]{1,0:T(8,128)(2,1)}, bf16[512,768]{1,0:T(8,128)(2,1)}, u32[]{:S(2)}, u32[]{:S(2)}) collective-permute-start(bf16[512,768]{1,0:T(8,128)(2,1)} %refs_0_.1), channel_id=1, source_target_pairs={{0,20},{1,21},{2,22},{3,23},{4,16},{5,17},{6,18},{7,19},{8,28},{9,... | collective-permute-start | bytes 2359304 | tf_op jit(solution)/shard_map/ppermute | solution.py:48
  8.3 3.6 %collective-permute-start = (bf16[2,256,128]{2,1,0:T(8,128)(2,1)S(1)}, bf16[2,256,128]{2,1,0:T(8,128)(2,1)S(1)}, u32[]{:S(2)}, u32[]{:S(2)}) collective-permute-start(bf16[2,256,128]{2,1,0:T(8,128)(2,1)S(1)} %get-tuple-element.42), channel_id=1, source_target_pairs={{0,8},{8,16},{16,24},{24,32},{32,40},{40,48},{48,56},{56,64},{64,7... | collective-permute-start | bytes 393224 | tf_op jit(solution)/shard_map/ppermute | solution.py:337
  9.7 3.4 %collective-permute-start.1 = (bf16[2,256,128]{2,1,0:T(8,128)(2,1)S(1)}, bf16[2,256,128]{2,1,0:T(8,128)(2,1)S(1)}, u32[]{:S(2)}, u32[]{:S(2)}) collective-permute-start(bf16[2,256,128]{2,1,0:T(8,128)(2,1)S(1)} %get-tuple-element.41), channel_id=1, source_target_pairs={{8,0},{16,8},{24,16},{32,24},{40,32},{48,40},{56,48},{64,56},{72,6... | collective-permute-start | bytes 393224 | tf_op jit(solution)/shard_map/ppermute | solution.py:337
  12.0 24.6 %copy-start.6 = (bf16[2,256,128]{2,1,0:T(8,128)(2,1)}, bf16[2,256,128]{2,1,0:T(8,128)(2,1)S(1)}, u32[]{:S(2)}) copy-start(bf16[2,256,128]{2,1,0:T(8,128)(2,1)S(1)} %collective-permute-done.top) | copy-start | bytes 393220
  13.1 23.6 %copy-start.7 = (bf16[2,256,128]{2,1,0:T(8,128)(2,1)}, bf16[2,256,128]{2,1,0:T(8,128)(2,1)S(1)}, u32[]{:S(2)}) copy-start(bf16[2,256,128]{2,1,0:T(8,128)(2,1)S(1)} %collective-permute-done.1.bottom) | copy-start | bytes 393220
  13.1 6.7 %collective-permute-start.2 = (bf16[68,2,128]{2,1,0:T(2,128)(2,1)S(1)}, bf16[68,2,128]{2,1,0:T(2,128)(2,1)S(1)}, u32[]{:S(2)}, u32[]{:S(2)}) collective-permute-start(bf16[68,2,128]{2,1,0:T(2,128)(2,1)S(1)} %pad_maximum_fusion.1), channel_id=1, source_target_pairs={{1,0},{2,1},{3,2},{4,3},{5,4},{6,5},{7,6},{9,8},{10,9},{11,10},{12... | collective-permute-start | bytes 104456 | tf_op jit(solution)/shard_map/ppermute | solution.py:337
  14.5 6.2 %collective-permute-start.3 = (bf16[68,2,128]{2,1,0:T(2,128)(2,1)S(1)}, bf16[68,2,128]{2,1,0:T(2,128)(2,1)S(1)}, u32[]{:S(2)}, u32[]{:S(2)}) collective-permute-start(bf16[68,2,128]{2,1,0:T(2,128)(2,1)S(1)} %pad_maximum_fusion.2), channel_id=1, source_target_pairs={{0,1},{1,2},{2,3},{3,4},{4,5},{5,6},{6,7},{8,9},{9,10},{10,11},{11... | collective-permute-start | bytes 104456 | tf_op jit(solution)/shard_map/ppermute | solution.py:337
  21.5 0.9 copy-start.2
  26.7 32.7 %collective-permute-start.7 = (bf16[512,768]{1,0:T(8,128)(2,1)}, bf16[512,768]{1,0:T(8,128)(2,1)S(1)}, u32[]{:S(2)}, u32[]{:S(2)}) collective-permute-start(bf16[512,768]{1,0:T(8,128)(2,1)} %collective-permute-done.4.refs_1_), channel_id=1, source_target_pairs={{0,32},{1,33},{2,34},{3,35},{4,36},{5,37},{6,38},{7,39},{8,40},{9,... | collective-permute-start | bytes 2359304 | tf_op jit(solution)/shard_map/ppermute | solution.py:48
  35.2 24.2 %collective-permute-start.9 = (bf16[512,768]{1,0:T(8,128)(2,1)}, bf16[512,768]{1,0:T(8,128)(2,1)S(1)}, u32[]{:S(2)}, u32[]{:S(2)}) collective-permute-start(bf16[512,768]{1,0:T(8,128)(2,1)} %collective-permute-done.4.refs_1_), channel_id=1, source_target_pairs={{0,20},{1,21},{2,22},{3,23},{4,16},{5,17},{6,18},{7,19},{8,28},{9,... | collective-permute-start | bytes 2359304 | tf_op jit(solution)/shard_map/ppermute | solution.py:48
  35.2 24.2 %collective-permute-start.8 = (bf16[512,768]{1,0:T(8,128)(2,1)}, bf16[512,768]{1,0:T(8,128)(2,1)S(1)}, u32[]{:S(2)}, u32[]{:S(2)}) collective-permute-start(bf16[512,768]{1,0:T(8,128)(2,1)} %collective-permute-done.6.refs_4_), channel_id=1, source_target_pairs={{0,96},{1,97},{2,98},{3,99},{4,100},{5,101},{6,102},{7,103},{8,104... | collective-permute-start | bytes 2359304 | tf_op jit(solution)/shard_map/ppermute | solution.py:48
  59.4 13.9 %copy-start.1 = (bf16[512,768]{1,0:T(8,128)(2,1)S(1)}, bf16[512,768]{1,0:T(8,128)(2,1)}, u32[]{:S(2)}) copy-start(bf16[512,768]{1,0:T(8,128)(2,1)} %refs_0_.1) | copy-start | bytes 2359300
  59.4 13.9 %all-to-all-start = ((bf16[2,8,256,512]{3,2,1,0:T(8,128)(2,1)}), bf16[2,8,256,512]{3,2,1,0:T(8,128)(2,1)}, u32[]{:S(2)}, u32[]{:S(2)}) async-start(bf16[2,8,256,512]{3,2,1,0:T(8,128)(2,1)} %convs.1), calls=%async_computation | async-start | bytes 8388608 | tf_op jit(solution)/shard_map/all_to_all | solution.py:375
  65.9 13.9 %collective-permute-start.10 = (bf16[176,768]{1,0:T(8,128)(2,1)}, bf16[176,768]{1,0:T(8,128)(2,1)S(1)}, u32[]{:S(2)}, u32[]{:S(2)}) collective-permute-start(bf16[176,768]{1,0:T(8,128)(2,1)} %slice.41), channel_id=1, source_target_pairs={{0,96},{1,97},{2,98},{3,99},{4,100},{5,101},{6,102},{7,103},{8,104... | collective-permute-start | bytes 811016 | tf_op jit(solution)/shard_map/ppermute | solution.py:48
  68.6 11.2 %collective-permute-start.11 = (bf16[176,768]{1,0:T(8,128)(2,1)}, bf16[176,768]{1,0:T(8,128)(2,1)}, u32[]{:S(2)}, u32[]{:S(2)}) collective-permute-start(bf16[176,768]{1,0:T(8,128)(2,1)} %slice.42), channel_id=1, source_target_pairs={{0,32},{1,33},{2,34},{3,35},{4,36},{5,37},{6,38},{7,39},{8,40},{9,... | collective-permute-start | bytes 811016 | tf_op jit(solution)/shard_map/ppermute | solution.py:48
  69.4 10.4 %collective-permute-start.12 = (bf16[160,768]{1,0:T(8,128)(2,1)}, bf16[160,768]{1,0:T(8,128)(2,1)}, u32[]{:S(2)}, u32[]{:S(2)}) collective-permute-start(bf16[160,768]{1,0:T(8,128)(2,1)} %slice.43), channel_id=1, source_target_pairs={{0,20},{1,21},{2,22},{3,23},{4,16},{5,17},{6,18},{7,19},{8,28},{9,... | collective-permute-start | bytes 737288 | tf_op jit(solution)/shard_map/ppermute | solution.py:48
  73.3 1.1 copy-start.3
  79.9 2.6 %copy-start.5 = (bf16[768,16]{0,1:T(8,128)(2,1)S(1)}, bf16[768,16]{0,1:T(8,128)(2,1)}, u32[]{:S(2)}) copy-start(bf16[768,16]{0,1:T(8,128)(2,1)} %param.12) | copy-start | bytes 73732
  79.9 2.8 %copy-start = (s32[1,1,256,1]{2,3,1,0:T(1,128)S(1)}, s32[1,1,256,1]{2,3,1,0:T(1,128)}, u32[]{:S(2)}) copy-start(s32[1,1,256,1]{2,3,1,0:T(1,128)} %param.13) | copy-start | bytes 3076
  82.3 2.4 %collective-permute-start.13 = (f32[256,768]{1,0:T(8,128)S(1)}, f32[256,768]{1,0:T(8,128)S(1)}, u32[]{:S(2)}, u32[]{:S(2)}) collective-permute-start(f32[256,768]{1,0:T(8,128)S(1)} %get-tuple-element.33), channel_id=1, source_target_pairs={{0,8},{1,9},{2,10},{3,11},{4,12},{5,13},{6,14},{7,15},{8,0},{9,1},... | collective-permute-start | bytes 2359304 | tf_op jit(solution)/shard_map/ppermute | solution.py:48
  104.5 14.1 %all-to-all-start.3 = ((bf16[8,48,768]{2,1,0:T(8,128)(2,1)}), bf16[8,48,768]{2,1,0:T(8,128)(2,1)S(1)}, u32[]{:S(2)}, u32[]{:S(2)}) async-start(bf16[8,48,768]{2,1,0:T(8,128)(2,1)} %bitcast.18), calls=%async_computation.3 | async-start | bytes 1179648 | tf_op jit(solution)/shard_map/all_to_all | solution.py:342
  118.6 5.3 %copy-start.4 = (bf16[8,48,768]{2,1,0:T(8,128)(2,1)}, bf16[8,48,768]{2,1,0:T(8,128)(2,1)S(1)}, u32[]{:S(2)}) copy-start(bf16[8,48,768]{2,1,0:T(8,128)(2,1)S(1)} %all-to-all-done.3) | copy-start | bytes 1769476
  118.6 15.5 %all-to-all-start.2 = ((bf16[8,48,768]{2,1,0:T(8,128)(2,1)}), bf16[8,48,768]{2,1,0:T(8,128)(2,1)S(1)}, u32[]{:S(2)}, u32[]{:S(2)}) async-start(bf16[8,48,768]{2,1,0:T(8,128)(2,1)} %bitcast.29), calls=%async_computation.2 | async-start | bytes 1179648 | tf_op jit(solution)/shard_map/all_to_all | solution.py:342

commit v3 on v2

--- a/solution.py
+++ b/solution.py
@@ -11,7 +11,7 @@
 WIDE = 272
 DIM, FF, CAP, TOK = 768, 3072, 48, 256
 SLOTS = 8 * CAP
-STEPS = ROWS // 8
+STEPS, BAND = 4, 2
 F32, BF16 = jnp.float32, jnp.bfloat16
 ANY = pl.BlockSpec(memory_space=pl.ANY)
 VMEM = pl.BlockSpec(memory_space=pltpu.VMEM)
@@ -66,13 +66,14 @@
 
 
 def conv_kernel(
-    place, scene, top, bottom, strip, first, second, patches,
+    place, scene, top, bottom, strip, first, second, keep, other,
     block, hidden, rows, w1, w2, first_in, second_in, sems, weight_sems,
 ):
     step = pl.program_id(0)
     chunks = []
     for k in range(STEPS):
-        lo, hi = (0, 12) if k == 0 else (4 + 8 * k, 12 + 8 * k)
+        hi = 8 * BAND * (k + 1) + 4
+        lo = 0 if k == 0 else hi - 8 * BAND
         a, b = max(lo - 2, 0), min(hi - 2, ROWS)
         copies = [(scene.at[a:b], block.at[a + 2 : b + 2, 0:COLS])]
         if k == 0:
@@ -87,7 +88,7 @@
         pltpu.make_async_copy(first, first_in, weight_sems.at[0]),
         pltpu.make_async_copy(second, second_in, weight_sems.at[1]),
     ]
-    place_row, place_col = place[0], place[1]
+    place_row, place_col, core = place[0], place[1], place[2]
     tail = lax.broadcasted_iota(jnp.int32, (16, 256), 0)
     cut = ((place_col == 0) & (tail >= 8)) | ((place_col == 7) & (tail < 8))
     edge = jnp.where(cut, 0.0, 1.0).astype(F32)
@@ -101,7 +102,7 @@
 
     @pl.when(step == 0)
     def _():
-        for chunk in [chunks[0], weights] + chunks[1:]:
+        for chunk in (chunks[0], weights, chunks[1]):
             for copy in chunk:
                 copy.start()
         for copy in weights:
@@ -122,24 +123,30 @@
         def _(k=k):
             for copy in chunks[k]:
                 copy.wait()
-
-    for i in range(4):
-        conv_first(4 * step + 1 + i)
+            for copy in chunks[k + 1] if k + 1 < STEPS else ():
+                copy.start()
+
+    for i in range(4 * BAND):
+        conv_first(4 * BAND * step + 1 + i)
 
     @pl.when((step == STEPS - 1) & (place_row == 15))
     def _():
         hidden[ROWS + 1] = jnp.zeros((WIDE, CH), BF16)
 
-    for i in range(4):
-        pair = 4 * step + i
+    for i in range(4 * BAND):
+        pair = 4 * BAND * step + i
         value = pair_conv(hidden, w2, pair)[0:COLS]
         for n in range(2):
             cells = block[2 * pair + 2 + n, 0:COLS].astype(F32)
             rows[pl.ds((2 * i + n) * COLS, COLS), :] = value[:, n * CH : (n + 1) * CH] + cells
-    for dy in range(8):
-        for j in range(8):
-            cells = rows[pl.ds(dy * COLS + j, 32, stride=8), :]
-            patches[j // 4, dy, :, pl.ds(j % 4 * CH, CH)] = cells.astype(BF16)
+    for line in range(8 * BAND):
+        dy, at = line % 8, pl.ds(line // 8 * 32, 32)
+        for j in range(4):
+            low = rows[pl.ds(line * COLS + j, 32, stride=8), :]
+            high = rows[pl.ds(line * COLS + 4 + j, 32, stride=8), :]
+            lanes = pl.ds(j * CH, CH)
+            keep[dy, at, lanes] = jnp.where(core == 0, low, high).astype(BF16)
+            other[dy, at, lanes] = jnp.where(core == 0, high, low).astype(BF16)
 
 
 def conv_call(*args):
@@ -147,12 +154,12 @@
         conv_kernel,
         grid=(STEPS,),
         in_specs=[SMEM, HBM, ANY, ANY, ANY, HBM, HBM],
-        out_specs=pl.BlockSpec((2, 8, 32, 512), lambda i: (0, 0, i, 0)),
-        out_shape=jax.ShapeDtypeStruct((2, 8, TOK, 512), BF16),
+        out_specs=[pl.BlockSpec((8, 32 * BAND, 512), lambda i: (0, i, 0))] * 2,
+        out_shape=[jax.ShapeDtypeStruct((8, TOK, 512), BF16)] * 2,
         scratch_shapes=[
             pltpu.VMEM((ROWS + 4, WIDE, CH), BF16),
             pltpu.VMEM((ROWS + 2, WIDE, CH), BF16),
-            pltpu.VMEM((8 * COLS, CH), F32),
+            pltpu.VMEM((8 * BAND * COLS, CH), F32),
             pltpu.VMEM((512, 768), BF16),
             pltpu.VMEM((512, 768), BF16),
             pltpu.VMEM((3, 3, CH, CH), BF16),
@@ -160,34 +167,41 @@
             pltpu.SemaphoreType.DMA((STEPS, 4)),
             pltpu.SemaphoreType.DMA((2,)),
         ],
-        compiler_params=params(60),
+        compiler_params=params(56),
         cost_estimate=cost(20),
         name="convs",
     )(*args)
 
 
-def embed_kernel(layout, has_sum, order, tokens, *refs):
+def embed_kernel(layout, has_sum, fetched, order, keep, came, *refs):
     count = sum(len(parts) for _, parts in layout)
-    pieces, rest = refs[:count], refs[count:]
-    given, rest = (rest[0:2], rest[2:]) if has_sum else ((), rest)
-    own, partner, lhs, rhs, lhs_sems, rhs_sems = rest
+    pieces, refs = refs[:count], refs[count:]
+    sources, refs = refs[:fetched], refs[fetched:]
+    given, refs = (refs[0:2], refs[2:]) if has_sum else ((), refs)
+    own, partner, refs = refs[0], refs[1], refs[2:]
+    targets, refs = refs[: 2 * fetched], refs[2 * fetched :]
+    lhs, rhs, lhs_sems, rhs_sems, fetch_sems = refs
     copies, at = [], 0
     for n, (which, parts) in enumerate(layout):
         k = order[which]
         here = [
-            pltpu.make_async_copy(
-                tokens.at[order[8 + m], k], lhs.at[n, pl.ds(m * TOK, TOK)], lhs_sems.at[n, m]
-            )
-            for m in range(2)
+            pltpu.make_async_copy(source.at[k], lhs.at[n, pl.ds(m * TOK, TOK)], lhs_sems.at[n, m])
+            for m, source in enumerate((keep, came))
         ]
-        for m, (first, count) in enumerate(parts):
-            target = rhs.at[n, pl.ds(first, count)]
+        for m, (first, rows) in enumerate(parts):
+            target = rhs.at[n, pl.ds(first, rows)]
             here.append(pltpu.make_async_copy(pieces[at], target, rhs_sems.at[n, m]))
             at += 1
         copies.append(here)
+    fetches = [
+        pltpu.make_async_copy(sources[n // 2].at[n % 2], target, fetch_sems.at[n])
+        for n, target in enumerate(targets)
+    ]
     for here in copies:
         for copy in here:
             copy.start()
+    for copy in fetches:
+        copy.start()
     for n in range(len(layout)):
         for copy in copies[n]:
             copy.wait()
@@ -199,31 +213,35 @@
                 target[...] = given[m][...] + part
             else:
                 target[...] += part
-
-
-def embed_call(name, order, tokens, shards, sums=()):
+    for copy in fetches:
+        copy.wait()
+
+
+def embed_call(name, order, keep, came, shards, sums=(), fetch=()):
     layout, arrays = [], []
     for which, parts in shards:
         heights = [part.shape[0] for part in parts]
-        layout.append((which, [(sum(heights[:m]), count) for m, count in enumerate(heights)]))
+        layout.append((which, [(sum(heights[:m]), rows) for m, rows in enumerate(heights)]))
         arrays.extend(parts)
     shape = jax.ShapeDtypeStruct((TOK, DIM), F32)
+    halves = [jax.ShapeDtypeStruct(a.shape[1:], a.dtype) for a in fetch for _ in range(2)]
     count = len(shards)
     return pl.pallas_call(
-        functools.partial(embed_kernel, layout, bool(sums)),
-        in_specs=[SMEM] + [ANY] * (1 + len(arrays)) + [VMEM] * len(sums),
-        out_specs=[VMEM, VMEM],
-        out_shape=[shape, shape],
+        functools.partial(embed_kernel, layout, bool(sums), len(fetch)),
+        in_specs=[SMEM] + [ANY] * (2 + len(arrays)) + [HBM] * len(fetch) + [VMEM] * len(sums),
+        out_specs=[VMEM, VMEM] + [ANY] * len(halves),
+        out_shape=[shape, shape] + halves,
         scratch_shapes=[
             pltpu.VMEM((count, 2 * TOK, 512), BF16),
             pltpu.VMEM((count, 512, DIM), BF16),
             pltpu.SemaphoreType.DMA((count, 2)),
             pltpu.SemaphoreType.DMA((count, 4)),
+            pltpu.SemaphoreType.DMA((4,)),
         ],
-        compiler_params=params(20),
+        compiler_params=params(34 if fetch else 16),
         cost_estimate=cost(4),
         name=name,
-    )(order, tokens, *arrays, *sums)
+    )(order, keep, came, *arrays, *fetch, *sums)
 
 
 def route_kernel(own, came, router, ids_row, ids_col, embedded, out0, out1, gate, place):
@@ -267,45 +285,25 @@
     )(*args)
 
 
-def expert_kernel(which, width, rows, up, down, out, up_in, down_in, sems):
-    copies = []
-    for n, at in enumerate(range(0, FF, width)):
-        part = pl.ds(at, width)
-        copies.append(
-            (
-                pltpu.make_async_copy(up.at[which, :, part], up_in.at[n], sems.at[0, n]),
-                pltpu.make_async_copy(down.at[which, part], down_in.at[n], sems.at[1, n]),
-            )
-        )
-    for pair in copies:
-        for copy in pair:
-            copy.start()
-    total = None
-    for n, (up_copy, down_copy) in enumerate(copies):
-        up_copy.wait()
-        z = jnp.dot(rows[...], up_in[n], preferred_element_type=F32)
+def expert_kernel(rows, up, down, out, hidden):
+    for at in range(0, FF, 512):
+        part = pl.ds(at, 512)
+        z = jnp.dot(rows[...], up[:, part], preferred_element_type=F32)
         act = 0.5 * z * (1.0 + jnp.tanh(0.7978845608028654 * (z + 0.044715 * (z * z * z))))
-        down_copy.wait()
-        part = jnp.dot(act.astype(BF16), down_in[n], preferred_element_type=F32)
-        total = part if total is None else total + part
-    out[...] = total.astype(BF16)
-
-
-def expert_call(which, rows, up, down, width=512):
-    count = FF // width
+        hidden[:, part] = act.astype(BF16)
+    out[...] = jnp.dot(hidden[...], down[...], preferred_element_type=F32).astype(BF16)
+
+
+def expert_call(name, rows, up, down):
     return pl.pallas_call(
-        functools.partial(expert_kernel, which, width),
-        in_specs=[VMEM, HBM, HBM],
+        expert_kernel,
+        in_specs=[VMEM] * 3,
         out_specs=VMEM,
         out_shape=jax.ShapeDtypeStruct((SLOTS, DIM), BF16),
-        scratch_shapes=[
-            pltpu.VMEM((count, DIM, width), BF16),
-            pltpu.VMEM((count, width, DIM), BF16),
-            pltpu.SemaphoreType.DMA((2, count)),
-        ],
-        compiler_params=params(56),
+        scratch_shapes=[pltpu.VMEM((SLOTS, FF), BF16)],
+        compiler_params=params(12),
         cost_estimate=cost(5),
-        name=f"expert_{which}",
+        name=name,
     )(rows, up, down)
 
 
@@ -337,6 +335,10 @@
     return lax.ppermute(value, axis, pairs if ahead else [(j, i) for i, j in pairs])
 
 
+def columns(top, scene, bottom, first):
+    return jnp.concatenate([a[:, first : first + 2] for a in (top, scene, bottom)], axis=0)
+
+
 def exchange(value):
     value = value.reshape(8, CAP, DIM)
     return lax.all_to_all(value, "col", 0, 0, tiled=True).reshape(SLOTS, DIM)
@@ -347,45 +349,48 @@
 ):
     row, col = lax.axis_index("row"), lax.axis_index("col")
     x, high, core = row >> 2, (row >> 1) & 1, row & 1
-    place = jnp.stack([row, col]).astype(jnp.int32)
+    place = jnp.stack([row, col, core]).astype(jnp.int32)
 
     top = neighbours(scene[ROWS - 2 :], "row", True)
     bottom = neighbours(scene[:2], "row", False)
-    left_own = jnp.concatenate([top[:, :2], scene[:, :2], bottom[:, :2]], axis=0)
-    right_own = jnp.concatenate([top[:, -2:], scene[:, -2:], bottom[:, -2:]], axis=0)
-    left = neighbours(right_own, "col", True)
-    right = neighbours(left_own, "col", False)
+    w, top, bottom = lax.optimization_barrier((embed_weight, top, bottom))
+    w_minus, w_plus, w_high = send(w, dx=1), send(w, dx=-1), send(w, dh=1, dl=1)
+    left = neighbours(columns(top, scene, bottom, COLS - 2), "col", True)
+    right = neighbours(columns(top, scene, bottom, 0), "col", False)
     strip = jnp.concatenate([right, jnp.zeros((ROWS + 4, 12, CH), BF16), left], axis=1)
-
-    w = embed_weight
-    w_minus, w_plus, w_high = send(w, dx=1), send(w, dx=-1), send(w, dh=1, dl=1)
-    strip, w_minus, w_plus, w_high = lax.optimization_barrier((strip, w_minus, w_plus, w_high))
+    keep, other = conv_call(place, scene, top, bottom, strip, conv_first, conv_second)
+    keep, other, w_minus, w_plus, w_high = lax.optimization_barrier(
+        (keep, other, w_minus, w_plus, w_high)
+    )
+    came = send(other, dc=1)
     w_far, w_high_plus = send(w_minus, dx=1), send(w_high, dx=-1)
     w_high_minus = send(w_minus, dh=1, dl=1)
-    patches = conv_call(place, scene, top, bottom, strip, conv_first, conv_second)
-    patches, w_far, w_high_plus, w_high_minus = lax.optimization_barrier(
-        (patches, w_far, w_high_plus, w_high_minus)
+    order = [(a & 3) * 2 + (b & 1) for b in (high, high + 1) for a in (x, x - 1, x + 1, x + 2)]
+    order = jnp.stack(order).astype(jnp.int32)
+    shards = [(n, [a]) for n, a in zip((0, 1, 2, 4), (w, w_minus, w_plus, w_high))]
+    *sums, up0, up1, down0, down1 = embed_call(
+        "embed_a", order, keep, came, shards, fetch=(expert_up, expert_down)
+    )
+    *sums, w_far, w_high_plus, w_high_minus = lax.optimization_barrier(
+        (*sums, w_far, w_high_plus, w_high_minus)
+    )
+    far = [w_far, w_high_minus, w_high_plus]
+    sums = embed_call(
+        "embed_b", order, keep, came, [(n, [a]) for n, a in zip((3, 5, 6), far)], sums
     )
     last = [
         send(w_high_plus[:176], dx=-1),
         send(w_high_minus[176:352], dx=1),
         send(w_far[352:], dh=1, dl=1),
     ]
-    pairs = [[i, i + 1] for i in range(0, 16, 2)]
-    patches = lax.all_to_all(patches, "row", 0, 0, axis_index_groups=pairs, tiled=True)
-
-    order = [(a & 3) * 2 + (b & 1) for b in (high, high + 1) for a in (x, x - 1, x + 1, x + 2)]
-    order = jnp.stack(order + [core, 1 - core]).astype(jnp.int32)
-    whole = [w, w_minus, w_plus, w_far, w_high, w_high_minus, w_high_plus]
-    sums = embed_call("embed_a", order, patches, [(n, [a]) for n, a in enumerate(whole)])
-    own, partner = embed_call("embed_b", order, patches, [(7, last)], sums)
+    own, partner = embed_call("embed_c", order, keep, came, [(7, last)], sums)
     came = send(partner, dc=1)
     embedded, out0, out1, gate, slots = route_call(
         own, came, router_weight, expert_ids.reshape(1, TOK), expert_ids.reshape(TOK, 1)
     )
     in0, in1 = exchange(out0), exchange(out1)
-    back0 = exchange(expert_call(0, in0, expert_up, expert_down))
-    back1 = exchange(expert_call(1, in1, expert_up, expert_down))
+    back0 = exchange(expert_call("expert_0", in0, up0, down0))
+    back1 = exchange(expert_call("expert_1", in1, up1, down1))
     return mix_call(embedded, gate, slots, back0, back1).reshape(1, 1, TOK, DIM)
 
 

time: 152 us -> 427 us (2.81)
  Pallas kernels: 54 us -> 327 us
  local copies, waits for them, and re-layouts: 6.71 us -> 20.8 us
  starting transfers between devices: 45.8 us -> 35 us
    pallas_call x4 -> x5, Pallas kernels: 28.1 us -> 303 us  [the longest x3 294 us: embed_call(): pl.pallas_call(functools.partial(embed_kernel, layout, bool(sums), len(fe...]
    unnamed x17 -> x33, local copies, waits for them, and re-layouts: 2.22 us -> 15.2 us
    all_to_all x1 -> x0, starting transfers between devices: 5.76 us -> none  [local(): lax.all_to_all(patches, 'row', 0, 0, axis_index_groups=pairs, tiled=True)]
    ppermute x10 -> x11, starting transfers between devices: 22.7 us -> 18.4 us  [send(): return lax.ppermute(value, ('row', 'col'), hop(**step))]
  transfers between devices with their start and end apart: 17 -> 17, of which waited for: 6 -> 5; matrix products, arithmetic and copies ran while one was open for 4% -> 1% of each run, Pallas kernels for 32% -> 75%
where the time goes in v3:
time: 427 us; the launch traced here: 426 us
  Pallas kernels  327 us (77%)
  starting transfers between devices  35 us (8%)
  blocking collectives  29.5 us (7%)
  local copies, waits for them, and re-layouts  20.8 us (5%)
  waiting for transfers between devices  12.4 us (3%)
    pallas_call x3, Pallas kernels, embed_call(): pl.pallas_call(functools.partial(embed_kernel, layout, bool(sums), len(fe...  294 us
    all_to_all x2, blocking collectives, exchange(): return lax.all_to_all(value, 'col', 0, 0, tiled=True).reshape(SLOTS, DIM)  29.5 us
    pallas_call x1, Pallas kernels, conv_call(): pl.pallas_call(conv_kernel, grid=(STEPS,), in_specs=[SMEM, HBM, ANY, ANY,...  20.8 us
    ppermute x11, starting transfers between devices, send(): return lax.ppermute(value, ('row', 'col'), hop(**step))  18.4 us
    unnamed x33, local copies, waits for them, and re-layouts  15.2 us
    pallas_call x2, Pallas kernels, expert_call(): pl.pallas_call(expert_kernel, in_specs=[VMEM] * 3, out_specs=VMEM, out_sh...  9.02 us
  transfers between devices with their start and end apart: 17, of which 5 were waited for; matrix products, arithmetic and copies ran while one was open for 1% of the time, Pallas kernels for 75%

profile of v3, /device:TPU:0, one launch (start us, length us, event | category | flops | bytes accessed | tf_op | source)
XLA Modules:
  0.0 426.3 jit_solution(775441103976129618)
XLA Ops:
  0.0 1.0 fusion.1
  1.0 1.3 collective-permute-start
  2.3 1.3 collective-permute-start.1
  3.6 1.0 fusion
  4.7 5.1 %collective-permute-done.1.bottom = bf16[2,256,128]{2,1,0:T(8,128)(2,1)S(1)} collective-permute-done((bf16[2,256,128]{2,1,0:T(8,128)(2,1)S(1)}, bf16[2,256,128]{2,1,0:T(8,128)(2,1)S(1)}, u32[]{:S(2)}, u32[]{:S(2)}) %collective-permute-start.1) | collective-permute-done | bytes 131104 | tf_op jit(solution)/shard_map/ppermute | solution.py:335
  9.8 1.3 collective-permute-start.2
  11.2 4.5 %collective-permute-start.3 = (bf16[68,2,128]{2,1,0:T(2,128)(2,1)S(1)}, bf16[68,2,128]{2,1,0:T(2,128)(2,1)S(1)}, u32[]{:S(2)}, u32[]{:S(2)}) collective-permute-start(bf16[68,2,128]{2,1,0:T(2,128)(2,1)S(1)} %pad_maximum_fusion.2), channel_id=1, source_target_pairs={{0,1},{1,2},{2,3},{3,4},{4,5},{5,6},{6,7},{8,9},{9,10},{10,11},{11... | collective-permute-start | bytes 104456 | tf_op jit(solution)/shard_map/ppermute | solution.py:335
  15.7 0.6 pad_add_fusion.place
  16.4 3.3 collective-permute-start.4
  19.7 1.4 collective-permute-start.5
  21.1 4.4 %collective-permute-start.6 = (bf16[512,768]{1,0:T(8,128)(2,1)}, bf16[512,768]{1,0:T(8,128)(2,1)}, u32[]{:S(2)}, u32[]{:S(2)}) collective-permute-start(bf16[512,768]{1,0:T(8,128)(2,1)} %refs_0_), channel_id=1, source_target_pairs={{0,20},{1,21},{2,22},{3,23},{4,16},{5,17},{6,18},{7,19},{8,28},{9,... | collective-permute-start | bytes 2359304 | tf_op jit(solution)/shard_map/ppermute | solution.py:48
  25.5 0.8 pad_maximum_fusion.strip
  26.3 20.8 %convs.1 = (bf16[8,256,512]{2,1,0:T(8,128)(2,1)}, bf16[8,256,512]{2,1,0:T(8,128)(2,1)}) custom-call(s32[3]{0:T(128)} %pad_add_fusion.place, bf16[64,256,128]{2,1,0:T(8,128)(2,1)} %scene.1, bf16[2,256,128]{2,1,0:T(8,128)(2,1)} %copy-done.14, bf16[2,256,128]{2,1,0:T(8,128)(2,1)} %copy-done.15, bf16[68,16,128]{2,1,0:T(8,128)(2,1)} %pad_maximum_fusion.strip, ...), custom_call_target="tpu_custom_call" | custom-call | flops 23000000512 | tf_op jit(solution)/shard_map/convs/pallas_call | solution.py:153
  47.1 0.9 copy-done.2
  48.0 0.6 collective-permute-start.7
  48.6 1.8 collective-permute-start.10
  50.4 1.5 collective-permute-start.8
  51.9 1.8 collective-permute-start.9
  53.7 1.6 copy-done
  55.3 1.1 copy-done.3
  56.5 288.0 %embed_a.1 = (f32[256,768]{1,0:T(8,128)S(1)}, f32[256,768]{1,0:T(8,128)S(1)}, bf16[768,3072]{1,0:T(8,128)(2,1)S(1)}, bf16[768,3072]{1,0:T(8,128)(2,1)S(1)}, bf16...) custom-call(s32[8]{0:T(128)S(1)} %stack.47.order, bf16[8,256,512]{2,1,0:T(8,128)(2,1)S(1)} %copy-done, ...), custom_call_target="tpu_custom_call" | custom-call | flops 4600000000 | tf_op jit(solution)/shard_map/embed_a/pallas_call | solution.py:229
  344.5 1.2 slice.41
  345.7 1.3 collective-permute-start.11
  347.0 1.2 slice.42
  348.2 0.7 collective-permute-start.12
  348.9 1.0 slice.43
  349.9 1.7 collective-permute-start.13
  351.6 3.5 embed_b.1
  355.1 2.9 collective-permute-done.13.refs_2_
  358.0 2.4 embed_c.1
  360.4 0.9 copy-done.11
  361.3 0.2 copy.10.router
  361.6 2.2 collective-permute-done.14.came
  363.8 1.1 copy-done.12
  364.9 1.6 route.1
  366.6 15.7 %all_to_all.20 = bf16[8,48,768]{2,1,0:T(8,128)(2,1)S(1)} all-to-all(bf16[8,48,768]{2,1,0:T(8,128)(2,1)S(1)} %bitcast.24), channel_id=1, replica_groups=mesh['row'=16,'col'=8] {'col'}, dimensions={0} | all-to-all | bytes 1179648 | tf_op jit(solution)/shard_map/all_to_all | solution.py:344
  382.3 3.5 all-to-all-start
  385.8 2.3 copy-done.9
  388.1 2.3 copy-done.10
  390.5 4.9 %expert_1.1 = bf16[384,768]{1,0:T(8,128)(2,1)} custom-call(bf16[384,768]{1,0:T(8,128)(2,1)S(1)} %bitcast.25, bf16[768,3072]{1,0:T(8,128)(2,1)S(1)} %copy-done.9, bf16[3072,768]{1,0:T(8,128)(2,1)S(1)} %copy-done.10), custom_call_target="tpu_custom_call" | custom-call | flops 5750000128 | tf_op jit(solution)/shard_map/expert_1/pallas_call | solution.py:298
  395.4 1.0 all-to-all-done
  396.4 4.7 %all-to-all-start.3 = ((bf16[8,48,768]{2,1,0:T(8,128)(2,1)}), bf16[8,48,768]{2,1,0:T(8,128)(2,1)S(1)}, u32[]{:S(2)}, u32[]{:S(2)}) async-start(bf16[8,48,768]{2,1,0:T(8,128)(2,1)} %bitcast.19), calls=%async_computation.3 | async-start | bytes 1179648 | tf_op jit(solution)/shard_map/all_to_all | solution.py:344
  401.0 2.3 copy-done.6
  403.4 2.3 copy-done.7
  405.7 4.1 expert_0.1
  409.8 1.3 all-to-all-done.3
  411.1 13.8 %all_to_all.21 = bf16[8,48,768]{2,1,0:T(8,128)(2,1)S(1)} all-to-all(bf16[8,48,768]{2,1,0:T(8,128)(2,1)S(1)} %bitcast.26), channel_id=1, replica_groups=mesh['row'=16,'col'=8] {'col'}, dimensions={0} | all-to-all | bytes 1179648 | tf_op jit(solution)/shard_map/all_to_all | solution.py:344
  425.0 1.4 mix.1
  (43 shorter events, 0.5 us)
Async XLA Ops:
  1.0 3.6 collective-permute-start
  2.3 7.4 %collective-permute-start.1 = (bf16[2,256,128]{2,1,0:T(8,128)(2,1)S(1)}, bf16[2,256,128]{2,1,0:T(8,128)(2,1)S(1)}, u32[]{:S(2)}, u32[]{:S(2)}) collective-permute-start(bf16[2,256,128]{2,1,0:T(8,128)(2,1)S(1)} %get-tuple-element.67), channel_id=1, source_target_pairs={{8,0},{16,8},{24,16},{32,24},{40,32},{48,40},{56,48},{64,56},{72,6... | collective-permute-start | bytes 393224 | tf_op jit(solution)/shard_map/ppermute | solution.py:335
  4.6 21.7 %copy-start.14 = (bf16[2,256,128]{2,1,0:T(8,128)(2,1)}, bf16[2,256,128]{2,1,0:T(8,128)(2,1)S(1)}, u32[]{:S(2)}) copy-start(bf16[2,256,128]{2,1,0:T(8,128)(2,1)S(1)} %collective-permute-done.top) | copy-start | bytes 393220
  9.7 16.6 %copy-start.15 = (bf16[2,256,128]{2,1,0:T(8,128)(2,1)}, bf16[2,256,128]{2,1,0:T(8,128)(2,1)S(1)}, u32[]{:S(2)}) copy-start(bf16[2,256,128]{2,1,0:T(8,128)(2,1)S(1)} %collective-permute-done.1.bottom) | copy-start | bytes 393220
  9.8 15.7 %collective-permute-start.2 = (bf16[68,2,128]{2,1,0:T(2,128)(2,1)S(1)}, bf16[68,2,128]{2,1,0:T(2,128)(2,1)S(1)}, u32[]{:S(2)}, u32[]{:S(2)}) collective-permute-start(bf16[68,2,128]{2,1,0:T(2,128)(2,1)S(1)} %pad_maximum_fusion.1), channel_id=1, source_target_pairs={{1,0},{2,1},{3,2},{4,3},{5,4},{6,5},{7,6},{9,8},{10,9},{11,10},{12... | collective-permute-start | bytes 104456 | tf_op jit(solution)/shard_map/ppermute | solution.py:335
  11.2 14.3 %collective-permute-start.3 = (bf16[68,2,128]{2,1,0:T(2,128)(2,1)S(1)}, bf16[68,2,128]{2,1,0:T(2,128)(2,1)S(1)}, u32[]{:S(2)}, u32[]{:S(2)}) collective-permute-start(bf16[68,2,128]{2,1,0:T(2,128)(2,1)S(1)} %pad_maximum_fusion.2), channel_id=1, source_target_pairs={{0,1},{1,2},{2,3},{3,4},{4,5},{5,6},{6,7},{8,9},{9,10},{10,11},{11... | collective-permute-start | bytes 104456 | tf_op jit(solution)/shard_map/ppermute | solution.py:335
  16.4 30.7 %collective-permute-start.4 = (bf16[512,768]{1,0:T(8,128)(2,1)}, bf16[512,768]{1,0:T(8,128)(2,1)}, u32[]{:S(2)}, u32[]{:S(2)}) collective-permute-start(bf16[512,768]{1,0:T(8,128)(2,1)} %refs_0_), channel_id=1, source_target_pairs={{0,32},{1,33},{2,34},{3,35},{4,36},{5,37},{6,38},{7,39},{8,40},{9,... | collective-permute-start | bytes 2359304 | tf_op jit(solution)/shard_map/ppermute | solution.py:48
  19.7 27.4 %collective-permute-start.5 = (bf16[512,768]{1,0:T(8,128)(2,1)}, bf16[512,768]{1,0:T(8,128)(2,1)S(1)}, u32[]{:S(2)}, u32[]{:S(2)}) collective-permute-start(bf16[512,768]{1,0:T(8,128)(2,1)} %refs_0_), channel_id=1, source_target_pairs={{0,96},{1,97},{2,98},{3,99},{4,100},{5,101},{6,102},{7,103},{8,104... | collective-permute-start | bytes 2359304 | tf_op jit(solution)/shard_map/ppermute | solution.py:48
  21.1 26.9 %collective-permute-start.6 = (bf16[512,768]{1,0:T(8,128)(2,1)}, bf16[512,768]{1,0:T(8,128)(2,1)}, u32[]{:S(2)}, u32[]{:S(2)}) collective-permute-start(bf16[512,768]{1,0:T(8,128)(2,1)} %refs_0_), channel_id=1, source_target_pairs={{0,20},{1,21},{2,22},{3,23},{4,16},{5,17},{6,18},{7,19},{8,28},{9,... | collective-permute-start | bytes 2359304 | tf_op jit(solution)/shard_map/ppermute | solution.py:48
  26.3 27.4 %copy-start.1 = (bf16[512,768]{1,0:T(8,128)(2,1)S(1)}, bf16[512,768]{1,0:T(8,128)(2,1)}, u32[]{:S(2)}) copy-start(bf16[512,768]{1,0:T(8,128)(2,1)} %refs_0_) | copy-start | bytes 2359300
  47.1 0.9 copy-start.2
  48.0 5.7 %collective-permute-start.7 = (bf16[8,256,512]{2,1,0:T(8,128)(2,1)}, bf16[8,256,512]{2,1,0:T(8,128)(2,1)S(1)}, u32[]{:S(2)}, u32[]{:S(2)}) collective-permute-start(bf16[8,256,512]{2,1,0:T(8,128)(2,1)} %get-tuple-element.41), channel_id=1, source_target_pairs={{0,8},{1,9},{2,10},{3,11},{4,12},{5,13},{6,14},{7,15},{8,0},{9,1},... | collective-permute-start | bytes 6291464 | tf_op jit(solution)/shard_map/ppermute | solution.py:48
  48.6 295.9 %collective-permute-start.10 = (bf16[512,768]{1,0:T(8,128)(2,1)}, bf16[512,768]{1,0:T(8,128)(2,1)}, u32[]{:S(2)}, u32[]{:S(2)}) collective-permute-start(bf16[512,768]{1,0:T(8,128)(2,1)} %collective-permute-done.4.refs_1_), channel_id=1, source_target_pairs={{0,20},{1,21},{2,22},{3,23},{4,16},{5,17},{6,18},{7,19},{8,28},{9,... | collective-permute-start | bytes 2359304 | tf_op jit(solution)/shard_map/ppermute | solution.py:48
  50.4 294.1 %collective-permute-start.8 = (bf16[512,768]{1,0:T(8,128)(2,1)}, bf16[512,768]{1,0:T(8,128)(2,1)}, u32[]{:S(2)}, u32[]{:S(2)}) collective-permute-start(bf16[512,768]{1,0:T(8,128)(2,1)} %collective-permute-done.4.refs_1_), channel_id=1, source_target_pairs={{0,32},{1,33},{2,34},{3,35},{4,36},{5,37},{6,38},{7,39},{8,40},{9,... | collective-permute-start | bytes 2359304 | tf_op jit(solution)/shard_map/ppermute | solution.py:48
  51.9 292.7 %collective-permute-start.9 = (bf16[512,768]{1,0:T(8,128)(2,1)}, bf16[512,768]{1,0:T(8,128)(2,1)}, u32[]{:S(2)}, u32[]{:S(2)}) collective-permute-start(bf16[512,768]{1,0:T(8,128)(2,1)} %collective-permute-done.6.refs_3_), channel_id=1, source_target_pairs={{0,96},{1,97},{2,98},{3,99},{4,100},{5,101},{6,102},{7,103},{8,104... | collective-permute-start | bytes 2359304 | tf_op jit(solution)/shard_map/ppermute | solution.py:48
  53.7 1.6 copy-start
  55.3 1.1 copy-start.3
  344.5 10.6 %copy-start.5 = (bf16[768,3072]{1,0:T(8,128)(2,1)}, bf16[768,3072]{1,0:T(8,128)(2,1)S(1)}, u32[]{:S(2)}) copy-start(bf16[768,3072]{1,0:T(8,128)(2,1)S(1)} %get-tuple-element.60.up) | copy-start | bytes 14155780
  344.5 10.6 %copy-start.8 = (bf16[768,3072]{1,0:T(8,128)(2,1)}, bf16[768,3072]{1,0:T(8,128)(2,1)S(1)}, u32[]{:S(2)}) copy-start(bf16[768,3072]{1,0:T(8,128)(2,1)S(1)} %get-tuple-element.63.up) | copy-start | bytes 14155780
  345.7 12.3 %collective-permute-start.11 = (bf16[176,768]{1,0:T(8,128)(2,1)S(1)}, bf16[176,768]{1,0:T(8,128)(2,1)S(1)}, u32[]{:S(2)}, u32[]{:S(2)}) collective-permute-start(bf16[176,768]{1,0:T(8,128)(2,1)S(1)} %slice.41), channel_id=1, source_target_pairs={{0,96},{1,97},{2,98},{3,99},{4,100},{5,101},{6,102},{7,103},{8,104... | collective-permute-start | bytes 811016 | tf_op jit(solution)/shard_map/ppermute | solution.py:48
  348.2 9.8 %collective-permute-start.12 = (bf16[176,768]{1,0:T(8,128)(2,1)S(1)}, bf16[176,768]{1,0:T(8,128)(2,1)S(1)}, u32[]{:S(2)}, u32[]{:S(2)}) collective-permute-start(bf16[176,768]{1,0:T(8,128)(2,1)S(1)} %slice.42), channel_id=1, source_target_pairs={{0,32},{1,33},{2,34},{3,35},{4,36},{5,37},{6,38},{7,39},{8,40},{9,... | collective-permute-start | bytes 811016 | tf_op jit(solution)/shard_map/ppermute | solution.py:48
  349.9 8.1 %collective-permute-start.13 = (bf16[160,768]{1,0:T(8,128)(2,1)S(1)}, bf16[160,768]{1,0:T(8,128)(2,1)S(1)}, u32[]{:S(2)}, u32[]{:S(2)}) collective-permute-start(bf16[160,768]{1,0:T(8,128)(2,1)S(1)} %slice.43), channel_id=1, source_target_pairs={{0,20},{1,21},{2,22},{3,23},{4,16},{5,17},{6,18},{7,19},{8,28},{9,... | collective-permute-start | bytes 737288 | tf_op jit(solution)/shard_map/ppermute | solution.py:48
  358.0 3.3 copy-start.13
  358.0 3.5 copy-start.4
  360.4 0.9 copy-start.11
  361.3 2.5 collective-permute-start.14
  363.8 1.1 copy-start.12
  382.3 14.1 %all-to-all-start = ((bf16[8,48,768]{2,1,0:T(8,128)(2,1)}), bf16[8,48,768]{2,1,0:T(8,128)(2,1)S(1)}, u32[]{:S(2)}, u32[]{:S(2)}) async-start(bf16[8,48,768]{2,1,0:T(8,128)(2,1)} %bitcast.13), calls=%async_computation | async-start | bytes 1179648 | tf_op jit(solution)/shard_map/all_to_all | solution.py:344
  385.8 2.3 copy-start.9
  388.1 2.3 copy-start.10
  396.4 14.7 %all-to-all-start.3 = ((bf16[8,48,768]{2,1,0:T(8,128)(2,1)}), bf16[8,48,768]{2,1,0:T(8,128)(2,1)S(1)}, u32[]{:S(2)}, u32[]{:S(2)}) async-start(bf16[8,48,768]{2,1,0:T(8,128)(2,1)} %bitcast.19), calls=%async_computation.3 | async-start | bytes 1179648 | tf_op jit(solution)/shard_map/all_to_all | solution.py:344
  401.0 2.3 copy-start.6
  403.4 2.3 copy-start.7

commit v4 on v3

--- a/solution.py
+++ b/solution.py
@@ -11,7 +11,7 @@
 WIDE = 272
 DIM, FF, CAP, TOK = 768, 3072, 48, 256
 SLOTS = 8 * CAP
-STEPS, BAND = 4, 2
+STEPS, BAND = 2, 2
 F32, BF16 = jnp.float32, jnp.bfloat16
 ANY = pl.BlockSpec(memory_space=pl.ANY)
 VMEM = pl.BlockSpec(memory_space=pltpu.VMEM)
@@ -44,6 +44,14 @@
     return pairs
 
 
+def in_hbm(value):
+    return pltpu.with_memory_space_constraint(value, pltpu.HBM)
+
+
+def in_vmem(value):
+    return pltpu.with_memory_space_constraint(value, pltpu.VMEM)
+
+
 def send(value, **step):
     return lax.ppermute(value, ("row", "col"), hop(**step))
 
@@ -65,25 +73,31 @@
     return left + parts[:, 256:512] + right
 
 
-def conv_kernel(
-    place, scene, top, bottom, strip, first, second, keep, other,
-    block, hidden, rows, w1, w2, first_in, second_in, sems, weight_sems,
-):
+def conv_kernel(start, fetched, place, scene, top, bottom, strip, first, second, *refs):
+    sources, refs = refs[:fetched], refs[-11 - 2 * fetched :]
+    keep, other, targets, refs = refs[0], refs[1], refs[2 : 2 + 2 * fetched], refs[2 + 2 * fetched :]
+    block, hidden, rows, w1, w2, first_in, second_in, sems, weight_sems = refs
     step = pl.program_id(0)
+    base = start * 8 * BAND - 2
+    height = 8 * BAND * STEPS + 4
     chunks = []
     for k in range(STEPS):
         hi = 8 * BAND * (k + 1) + 4
         lo = 0 if k == 0 else hi - 8 * BAND
-        a, b = max(lo - 2, 0), min(hi - 2, ROWS)
-        copies = [(scene.at[a:b], block.at[a + 2 : b + 2, 0:COLS])]
-        if k == 0:
+        a, b = max(lo + base, 0), min(hi + base, ROWS)
+        copies = [(scene.at[a:b], block.at[a - base : b - base, 0:COLS])]
+        if lo + base < 0:
             copies.append((top, block.at[0:2, 0:COLS]))
-        if k == STEPS - 1:
-            copies.append((bottom, block.at[ROWS + 2 : ROWS + 4, 0:COLS]))
-        copies.append((strip.at[lo:hi], block.at[lo:hi, COLS:WIDE]))
+        if hi + base > ROWS:
+            copies.append((bottom, block.at[height - 2 : height, 0:COLS]))
+        copies.append((strip.at[lo + base + 2 : hi + base + 2], block.at[lo:hi, COLS:WIDE]))
         chunks.append(
             [pltpu.make_async_copy(s, d, sems.at[k, n]) for n, (s, d) in enumerate(copies)]
         )
+    fetches = [
+        pltpu.make_async_copy(sources[n // 2].at[n % 2], target, weight_sems.at[2 + n])
+        for n, target in enumerate(targets)
+    ]
     weights = [
         pltpu.make_async_copy(first, first_in, weight_sems.at[0]),
         pltpu.make_async_copy(second, second_in, weight_sems.at[1]),
@@ -105,6 +119,8 @@
         for chunk in (chunks[0], weights, chunks[1]):
             for copy in chunk:
                 copy.start()
+        for copy in fetches:
+            copy.start()
         for copy in weights:
             copy.wait()
         pair_weights(first_in, w1)
@@ -112,10 +128,11 @@
         for copy in chunks[0]:
             copy.wait()
         conv_first(0)
-
-        @pl.when(place_row == 0)
-        def _():
-            hidden[0] = jnp.zeros((WIDE, CH), BF16)
+        if start == 0:
+
+            @pl.when(place_row == 0)
+            def _():
+                hidden[0] = jnp.zeros((WIDE, CH), BF16)
 
     for k in range(1, STEPS):
 
@@ -128,10 +145,11 @@
 
     for i in range(4 * BAND):
         conv_first(4 * BAND * step + 1 + i)
-
-    @pl.when((step == STEPS - 1) & (place_row == 15))
-    def _():
-        hidden[ROWS + 1] = jnp.zeros((WIDE, CH), BF16)
+    if base + height > ROWS:
+
+        @pl.when((step == STEPS - 1) & (place_row == 15))
+        def _():
+            hidden[height - 3] = jnp.zeros((WIDE, CH), BF16)
 
     for i in range(4 * BAND):
         pair = 4 * BAND * step + i
@@ -149,103 +167,94 @@
             other[dy, at, lanes] = jnp.where(core == 0, high, low).astype(BF16)
 
 
-def conv_call(*args):
+    if fetches:
+
+        @pl.when(step == STEPS - 1)
+        def _():
+            for copy in fetches:
+                copy.wait()
+
+
+def conv_call(start, args, fetch=(), given=()):
+    shape = jax.ShapeDtypeStruct((8, TOK, 512), BF16)
+    halves = [pltpu.VMEM(a.shape[1:], a.dtype) for a in fetch for _ in range(2)]
+    height = 8 * BAND * STEPS
     return pl.pallas_call(
-        conv_kernel,
+        functools.partial(conv_kernel, start, len(fetch)),
         grid=(STEPS,),
-        in_specs=[SMEM, HBM, ANY, ANY, ANY, HBM, HBM],
-        out_specs=[pl.BlockSpec((8, 32 * BAND, 512), lambda i: (0, i, 0))] * 2,
-        out_shape=[jax.ShapeDtypeStruct((8, TOK, 512), BF16)] * 2,
+        in_specs=[SMEM, HBM, ANY, ANY, ANY, HBM, HBM] + [HBM] * len(fetch) + [ANY] * len(given),
+        out_specs=[pl.BlockSpec((8, 32 * BAND, 512), lambda i: (0, start + i, 0))] * 2
+        + [ANY] * len(halves),
+        out_shape=[shape, shape] + halves,
         scratch_shapes=[
-            pltpu.VMEM((ROWS + 4, WIDE, CH), BF16),
-            pltpu.VMEM((ROWS + 2, WIDE, CH), BF16),
+            pltpu.VMEM((height + 4, WIDE, CH), BF16),
+            pltpu.VMEM((height + 2, WIDE, CH), BF16),
             pltpu.VMEM((8 * BAND * COLS, CH), F32),
             pltpu.VMEM((512, 768), BF16),
             pltpu.VMEM((512, 768), BF16),
             pltpu.VMEM((3, 3, CH, CH), BF16),
             pltpu.VMEM((3, 3, CH, CH), BF16),
             pltpu.SemaphoreType.DMA((STEPS, 4)),
-            pltpu.SemaphoreType.DMA((2,)),
+            pltpu.SemaphoreType.DMA((6,)),
         ],
-        compiler_params=params(56),
-        cost_estimate=cost(20),
-        name="convs",
-    )(*args)
-
-
-def embed_kernel(layout, has_sum, fetched, order, keep, came, *refs):
+        input_output_aliases={7 + len(fetch) + n: n for n in range(len(given))},
+        compiler_params=params(28),
+        cost_estimate=cost(11),
+        name=f"convs_{start}",
+    )(*args, *fetch, *given)
+
+
+def embed_kernel(layout, has_sum, order, tokens, *refs):
     count = sum(len(parts) for _, parts in layout)
     pieces, refs = refs[:count], refs[count:]
-    sources, refs = refs[:fetched], refs[fetched:]
-    given, refs = (refs[0:2], refs[2:]) if has_sum else ((), refs)
-    own, partner, refs = refs[0], refs[1], refs[2:]
-    targets, refs = refs[: 2 * fetched], refs[2 * fetched :]
-    lhs, rhs, lhs_sems, rhs_sems, fetch_sems = refs
+    given, refs = (refs[0], refs[1:]) if has_sum else (None, refs)
+    total, lhs, rhs, lhs_sems, rhs_sems = refs
     copies, at = [], 0
     for n, (which, parts) in enumerate(layout):
-        k = order[which]
-        here = [
-            pltpu.make_async_copy(source.at[k], lhs.at[n, pl.ds(m * TOK, TOK)], lhs_sems.at[n, m])
-            for m, source in enumerate((keep, came))
-        ]
+        here = [pltpu.make_async_copy(tokens.at[order[which]], lhs.at[n], lhs_sems.at[n])]
         for m, (first, rows) in enumerate(parts):
             target = rhs.at[n, pl.ds(first, rows)]
             here.append(pltpu.make_async_copy(pieces[at], target, rhs_sems.at[n, m]))
             at += 1
         copies.append(here)
-    fetches = [
-        pltpu.make_async_copy(sources[n // 2].at[n % 2], target, fetch_sems.at[n])
-        for n, target in enumerate(targets)
-    ]
     for here in copies:
         for copy in here:
             copy.start()
-    for copy in fetches:
-        copy.start()
+    result = given[...] if has_sum else None
     for n in range(len(layout)):
         for copy in copies[n]:
             copy.wait()
-        for m, target in ((1, partner), (0, own)):
-            part = jnp.dot(lhs[n, pl.ds(m * TOK, TOK)], rhs[n], preferred_element_type=F32)
-            if n == 0 and not has_sum:
-                target[...] = part
-            elif n == 0:
-                target[...] = given[m][...] + part
-            else:
-                target[...] += part
-    for copy in fetches:
-        copy.wait()
-
-
-def embed_call(name, order, keep, came, shards, sums=(), fetch=()):
+        part = jnp.dot(lhs[n], rhs[n], preferred_element_type=F32)
+        result = part if result is None else result + part
+    total[...] = result.astype(total.dtype)
+
+
+def embed_call(name, order, tokens, shards, sums=(), dtype=F32, micros=3):
     layout, arrays = [], []
     for which, parts in shards:
         heights = [part.shape[0] for part in parts]
         layout.append((which, [(sum(heights[:m]), rows) for m, rows in enumerate(heights)]))
         arrays.extend(parts)
-    shape = jax.ShapeDtypeStruct((TOK, DIM), F32)
-    halves = [jax.ShapeDtypeStruct(a.shape[1:], a.dtype) for a in fetch for _ in range(2)]
     count = len(shards)
     return pl.pallas_call(
-        functools.partial(embed_kernel, layout, bool(sums), len(fetch)),
-        in_specs=[SMEM] + [ANY] * (2 + len(arrays)) + [HBM] * len(fetch) + [VMEM] * len(sums),
-        out_specs=[VMEM, VMEM] + [ANY] * len(halves),
-        out_shape=[shape, shape] + halves,
+        functools.partial(embed_kernel, layout, bool(sums)),
+        in_specs=[SMEM] + [ANY] * (1 + len(arrays)) + [VMEM] * len(sums),
+        out_specs=VMEM,
+        out_shape=jax.ShapeDtypeStruct((TOK, DIM), dtype),
         scratch_shapes=[
-            pltpu.VMEM((count, 2 * TOK, 512), BF16),
+            pltpu.VMEM((count, TOK, 512), BF16),
             pltpu.VMEM((count, 512, DIM), BF16),
-            pltpu.SemaphoreType.DMA((count, 2)),
+            pltpu.SemaphoreType.DMA((count,)),
             pltpu.SemaphoreType.DMA((count, 4)),
-            pltpu.SemaphoreType.DMA((4,)),
         ],
-        compiler_params=params(34 if fetch else 16),
-        cost_estimate=cost(4),
+        compiler_params=params(20),
+        cost_estimate=cost(micros),
         name=name,
-    )(order, keep, came, *arrays, *fetch, *sums)
+    )(order, tokens, *arrays, *sums)
 
 
 def route_kernel(own, came, router, ids_row, ids_col, embedded, out0, out1, gate, place):
-    value = (own[...] + came[...]).astype(BF16)
+    value = (own[...] + came[...].astype(F32)).astype(BF16)
     embedded[...] = value
     wide = value.astype(F32)
     scale = lax.rsqrt(jnp.mean(wide * wide, axis=-1, keepdims=True) + 1e-06)
@@ -353,44 +362,46 @@
 
     top = neighbours(scene[ROWS - 2 :], "row", True)
     bottom = neighbours(scene[:2], "row", False)
-    w, top, bottom = lax.optimization_barrier((embed_weight, top, bottom))
+    w = embed_weight
     w_minus, w_plus, w_high = send(w, dx=1), send(w, dx=-1), send(w, dh=1, dl=1)
     left = neighbours(columns(top, scene, bottom, COLS - 2), "col", True)
     right = neighbours(columns(top, scene, bottom, 0), "col", False)
     strip = jnp.concatenate([right, jnp.zeros((ROWS + 4, 12, CH), BF16), left], axis=1)
-    keep, other = conv_call(place, scene, top, bottom, strip, conv_first, conv_second)
+    conv_args = (place, in_hbm(scene), top, bottom, strip, in_hbm(conv_first), in_hbm(conv_second))
+    keep, other = conv_call(0, conv_args)
     keep, other, w_minus, w_plus, w_high = lax.optimization_barrier(
         (keep, other, w_minus, w_plus, w_high)
     )
-    came = send(other, dc=1)
     w_far, w_high_plus = send(w_minus, dx=1), send(w_high, dx=-1)
     w_high_minus = send(w_minus, dh=1, dl=1)
-    order = [(a & 3) * 2 + (b & 1) for b in (high, high + 1) for a in (x, x - 1, x + 1, x + 2)]
-    order = jnp.stack(order).astype(jnp.int32)
-    shards = [(n, [a]) for n, a in zip((0, 1, 2, 4), (w, w_minus, w_plus, w_high))]
-    *sums, up0, up1, down0, down1 = embed_call(
-        "embed_a", order, keep, came, shards, fetch=(expert_up, expert_down)
+    keep, other, up0, up1, down0, down1 = conv_call(
+        STEPS, conv_args, (in_hbm(expert_up), in_hbm(expert_down)), (keep, other)
     )
-    *sums, w_far, w_high_plus, w_high_minus = lax.optimization_barrier(
-        (*sums, w_far, w_high_plus, w_high_minus)
-    )
-    far = [w_far, w_high_minus, w_high_plus]
-    sums = embed_call(
-        "embed_b", order, keep, came, [(n, [a]) for n, a in zip((3, 5, 6), far)], sums
+    came = send(other, dc=1)
+    keep, w_far, w_high_plus, w_high_minus = lax.optimization_barrier(
+        (keep, w_far, w_high_plus, w_high_minus)
     )
     last = [
         send(w_high_plus[:176], dx=-1),
         send(w_high_minus[176:352], dx=1),
         send(w_far[352:], dh=1, dl=1),
     ]
-    own, partner = embed_call("embed_c", order, keep, came, [(7, last)], sums)
+    order = [(a & 3) * 2 + (b & 1) for b in (high, high + 1) for a in (x, x - 1, x + 1, x + 2)]
+    order = jnp.stack(order).astype(jnp.int32)
+    shards = [w, w_minus, w_plus, w_far, w_high, w_high_minus, w_high_plus]
+    shards = [(n, [a]) for n, a in enumerate(shards)]
+    own = embed_call("embed_own", order, keep, shards, micros=40)
+    own, came = lax.optimization_barrier((own, came))
+    partner = embed_call("embed_partner", order, came, shards)
+    partner = embed_call("embed_partner_last", order, came, [(7, last)], [partner], BF16)
     came = send(partner, dc=1)
+    own = embed_call("embed_own_last", order, keep, [(7, last)], [own])
     embedded, out0, out1, gate, slots = route_call(
         own, came, router_weight, expert_ids.reshape(1, TOK), expert_ids.reshape(TOK, 1)
     )
     in0, in1 = exchange(out0), exchange(out1)
-    back0 = exchange(expert_call("expert_0", in0, up0, down0))
-    back1 = exchange(expert_call("expert_1", in1, up1, down1))
+    back0 = exchange(expert_call("expert_0", in0, in_vmem(up0), in_vmem(down0)))
+    back1 = exchange(expert_call("expert_1", in1, in_vmem(up1), in_vmem(down1)))
     return mix_call(embedded, gate, slots, back0, back1).reshape(1, 1, TOK, DIM)
 
 

time: 427 us -> 146 us (0.34)
  Pallas kernels: 327 us -> 45.2 us
  starting transfers between devices: 35 us -> 47.7 us
  local copies, waits for them, and re-layouts: 20.8 us -> 14.4 us
    pallas_call x4 -> x6, Pallas kernels: 315 us -> 32.9 us  [the longest x2 22.2 us: conv_call(): pl.pallas_call(functools.partial(conv_kernel, start, len(fetch)), grid=(S...]
    ppermute x11, starting transfers between devices: 18.4 us -> 31 us  [send(): return lax.ppermute(value, ('row', 'col'), hop(**step))]
    unnamed x33 -> x31, local copies, waits for them, and re-layouts: 15.2 us -> 12.1 us
  transfers between devices with their start and end apart: 17 -> 17, of which waited for: 5 -> 5; matrix products, arithmetic and copies ran while one was open for 1% -> 2% of each run, Pallas kernels for 75% -> 28%
where the time goes in v4:
time: 146 us; the launch traced here: 145 us
  starting transfers between devices  47.7 us (33%)
  Pallas kernels  45.2 us (31%)
  blocking collectives  28.2 us (19%)
  local copies, waits for them, and re-layouts  14.4 us (10%)
  waiting for transfers between devices  8.79 us (6%)
    ppermute x11, starting transfers between devices, send(): return lax.ppermute(value, ('row', 'col'), hop(**step))  31 us
    all_to_all x2, blocking collectives, exchange(): return lax.all_to_all(value, 'col', 0, 0, tiled=True).reshape(SLOTS, DIM)  28.2 us
    pallas_call x2, Pallas kernels, conv_call(): pl.pallas_call(functools.partial(conv_kernel, start, len(fetch)), grid=(S...  22.2 us
    unnamed x31, local copies, waits for them, and re-layouts  12.1 us
    pallas_call x4, Pallas kernels, embed_call(): pl.pallas_call(functools.partial(embed_kernel, layout, bool(sums)), in_sp...  10.8 us
    pallas_call x2, Pallas kernels, expert_call(): pl.pallas_call(expert_kernel, in_specs=[VMEM] * 3, out_specs=VMEM, out_sh...  9.22 us
    ppermute x4, starting transfers between devices, neighbours(): lax.ppermute(value, axis, pairs if ahead else [(j, i) for i, j in pairs])  8.43 us
    all_to_all x2, starting transfers between devices, exchange(): return lax.all_to_all(value, 'col', 0, 0, tiled=True).reshape(SLOTS, DIM)  8.31 us
  transfers between devices with their start and end apart: 17, of which 5 were waited for; matrix products, arithmetic and copies ran while one was open for 2% of the time, Pallas kernels for 28%

profile of v4, /device:TPU:0, one launch (start us, length us, event | category | flops | bytes accessed | tf_op | source)
XLA Modules:
  0.0 145.0 jit_solution(13492401472460791704)
XLA Ops:
  0.0 1.6 %collective-permute-start.4 = (bf16[512,768]{1,0:T(8,128)(2,1)}, bf16[512,768]{1,0:T(8,128)(2,1)S(1)}, u32[]{:S(2)}, u32[]{:S(2)}) collective-permute-start(bf16[512,768]{1,0:T(8,128)(2,1)} %refs_0_.5), channel_id=1, source_target_pairs={{0,32},{1,33},{2,34},{3,35},{4,36},{5,37},{6,38},{7,39},{8,40},{9,... | collective-permute-start | bytes 2359304 | tf_op jit(solution)/shard_map/ppermute | solution.py:56
  1.6 1.7 %collective-permute-start.5 = (bf16[512,768]{1,0:T(8,128)(2,1)}, bf16[512,768]{1,0:T(8,128)(2,1)S(1)}, u32[]{:S(2)}, u32[]{:S(2)}) collective-permute-start(bf16[512,768]{1,0:T(8,128)(2,1)} %refs_0_.5), channel_id=1, source_target_pairs={{0,96},{1,97},{2,98},{3,99},{4,100},{5,101},{6,102},{7,103},{8,104... | collective-permute-start | bytes 2359304 | tf_op jit(solution)/shard_map/ppermute | solution.py:56
  3.2 4.1 %collective-permute-start.6 = (bf16[512,768]{1,0:T(8,128)(2,1)}, bf16[512,768]{1,0:T(8,128)(2,1)S(1)}, u32[]{:S(2)}, u32[]{:S(2)}) collective-permute-start(bf16[512,768]{1,0:T(8,128)(2,1)} %refs_0_.5), channel_id=1, source_target_pairs={{0,20},{1,21},{2,22},{3,23},{4,16},{5,17},{6,18},{7,19},{8,28},{9,... | collective-permute-start | bytes 2359304 | tf_op jit(solution)/shard_map/ppermute | solution.py:56
  7.4 1.0 fusion.1
  8.3 1.3 collective-permute-start
  9.7 1.3 collective-permute-start.1
  11.0 1.0 fusion
  12.0 1.1 collective-permute-done.1.bottom
  13.1 1.3 collective-permute-start.2
  14.4 0.1 pad_maximum_fusion.2
  14.5 4.5 %collective-permute-start.3 = (bf16[68,2,128]{2,1,0:T(2,128)(2,1)S(1)}, bf16[68,2,128]{2,1,0:T(2,128)(2,1)S(1)}, u32[]{:S(2)}, u32[]{:S(2)}) collective-permute-start(bf16[68,2,128]{2,1,0:T(2,128)(2,1)S(1)} %pad_maximum_fusion.2), channel_id=1, source_target_pairs={{0,1},{1,2},{2,3},{3,4},{4,5},{5,6},{6,7},{8,9},{9,10},{10,11},{11... | collective-permute-start | bytes 104456 | tf_op jit(solution)/shard_map/ppermute | solution.py:344
  19.1 0.1 pad_add_fusion.place
  19.1 0.1 pad.1.clone
  19.2 0.1 stack.47.order
  19.3 1.3 collective-permute-done.3
  20.7 0.1 pad_maximum_fusion.strip
  20.8 10.9 %convs_0.1 = (bf16[8,256,512]{2,1,0:T(8,128)(2,1)S(1)}, bf16[8,256,512]{2,1,0:T(8,128)(2,1)S(1)}) custom-call(s32[3]{0:T(128)S(1)} %pad_add_fusion.place, bf16[64,256,128]{2,1,0:T(8,128)(2,1)} %scene.3, bf16[2,256,128]{2,1,0:T(8,128)(2,1)S(1)} %collective-permute-done.top, bf16[2,256,128]{2,1,0:T(8,128)(2,1)S(1)} %collective-permute-done.1.bottom, ...), custom_call_target="tpu_custom_call" | custom-call | flops 12650000384 | tf_op jit(solution)/shard_map/convs_0/pallas_call | solution.py:182
  31.7 12.9 %collective-permute-start.7 = (bf16[512,768]{1,0:T(8,128)(2,1)S(1)}, bf16[512,768]{1,0:T(8,128)(2,1)S(1)}, u32[]{:S(2)}, u32[]{:S(2)}) collective-permute-start(bf16[512,768]{1,0:T(8,128)(2,1)S(1)} %collective-permute-done.4.refs_1_), channel_id=1, source_target_pairs={{0,32},{1,33},{2,34},{3,35},{4,36},{5,37},{6,38},{7,39},{8,40},{9,... | collective-permute-start | bytes 2359304 | tf_op jit(solution)/shard_map/ppermute | solution.py:56
  44.6 1.5 %collective-permute-start.8 = (bf16[512,768]{1,0:T(8,128)(2,1)S(1)}, bf16[512,768]{1,0:T(8,128)(2,1)S(1)}, u32[]{:S(2)}, u32[]{:S(2)}) collective-permute-start(bf16[512,768]{1,0:T(8,128)(2,1)S(1)} %collective-permute-done.6.refs_4_), channel_id=1, source_target_pairs={{0,96},{1,97},{2,98},{3,99},{4,100},{5,101},{6,102},{7,103},{8,104... | collective-permute-start | bytes 2359304 | tf_op jit(solution)/shard_map/ppermute | solution.py:56
  46.1 11.3 %convs_2.1 = (bf16[8,256,512]{2,1,0:T(8,128)(2,1)S(1)}, bf16[8,256,512]{2,1,0:T(8,128)(2,1)S(1)}, bf16[768,3072]{1,0:T(8,128)(2,1)S(1)}, bf16[768,3072]{1,0:T(8,...) custom-call(s32[3]{0:T(128)S(1)} %pad_add_fusion.place, ...), custom_call_target="tpu_custom_call", output_to_operand_aliasing={{0}: (9, {}), {1}: (10, {})} | custom-call | flops 12650000384 | tf_op jit(solution)/shard_map/convs_2/pallas_call | solution.py:182
  57.4 4.2 %collective-permute-start.13 = (bf16[8,256,512]{2,1,0:T(8,128)(2,1)S(1)}, bf16[8,256,512]{2,1,0:T(8,128)(2,1)S(1)}, u32[]{:S(2)}, u32[]{:S(2)}) collective-permute-start(bf16[8,256,512]{2,1,0:T(8,128)(2,1)S(1)} %get-tuple-element.41), channel_id=1, source_target_pairs={{0,8},{1,9},{2,10},{3,11},{4,12},{5,13},{6,14},{7,15},{8,0},{9,1},... | collective-permute-start | bytes 6291464 | tf_op jit(solution)/shard_map/ppermute | solution.py:56
  61.6 4.3 %collective-permute-done.9.refs_5_ = bf16[512,768]{1,0:T(8,128)(2,1)S(1)} collective-permute-done((bf16[512,768]{1,0:T(8,128)(2,1)S(1)}, bf16[512,768]{1,0:T(8,128)(2,1)S(1)}, u32[]{:S(2)}, u32[]{:S(2)}) %collective-permute-start.9) | collective-permute-done | bytes 786464 | tf_op jit(solution)/shard_map/ppermute | solution.py:56
  65.9 1.1 collective-permute-start.10
  67.0 1.3 collective-permute-start.11
  68.3 2.6 %collective-permute-start.12 = (bf16[160,768]{1,0:T(8,128)(2,1)S(1)}, bf16[160,768]{1,0:T(8,128)(2,1)S(1)}, u32[]{:S(2)}, u32[]{:S(2)}) collective-permute-start(bf16[160,768]{1,0:T(8,128)(2,1)S(1)} %slice.43), channel_id=1, source_target_pairs={{0,20},{1,21},{2,22},{3,23},{4,16},{5,17},{6,18},{7,19},{8,28},{9,... | collective-permute-start | bytes 737288 | tf_op jit(solution)/shard_map/ppermute | solution.py:56
  70.9 4.0 %embed_own.1.refs_3_ = f32[256,768]{1,0:T(8,128)S(1)} custom-call(s32[8]{0:T(128)S(1)} %stack.47.order, bf16[8,256,512]{2,1,0:T(8,128)(2,1)S(1)} %get-tuple-element.36.tokens, bf16[512,768]{1,0:T(8,128)(2,1)S(1)} %copy-done.1, bf16[512,768]{1,0:T(8,128)(2,1)S(1)} %collective-permute-done.4.refs_1_, bf16[512,768]{1,0:T(8,128)(2,1)S(1)} %collective-permute-done.5.refs_2_, ...), custom_call_target="tpu_custom_call" | custom-call | flops 46000001024 | tf_op jit(solution)/shard_map/embed_own/pallas_call | solution.py:239
  75.0 0.9 copy-done.12
  75.9 4.0 %embed_partner.1.refs_3_ = f32[256,768]{1,0:T(8,128)S(1)} custom-call(s32[8]{0:T(128)S(1)} %stack.47.order, bf16[8,256,512]{2,1,0:T(8,128)(2,1)S(1)} %collective-permute-done.13.tokens, bf16[512,768]{1,0:T(8,128)(2,1)S(1)} %copy-done.1, bf16[512,768]{1,0:T(8,128)(2,1)S(1)} %collective-permute-done.4.refs_1_, ...), custom_call_target="tpu_custom_call" | custom-call | flops 3449999872 | tf_op jit(solution)/shard_map/embed_partner/pallas_call | solution.py:239
  80.0 1.4 embed_partner_last.1
  81.4 0.1 collective-permute-start.14
  81.5 0.2 copy.12.router
  81.7 0.1 copy.13.ids_col
  81.8 1.6 %copy-done.11 = bf16[8,256,512]{2,1,0:T(8,128)(2,1)S(1)} copy-done((bf16[8,256,512]{2,1,0:T(8,128)(2,1)S(1)}, bf16[8,256,512]{2,1,0:T(8,128)(2,1)}, u32[]{:S(2)}) %copy-start.11) | copy-done | bytes 2097176
  83.4 1.4 embed_own_last.1.own
  84.8 1.7 %route.1 = (bf16[256,768]{1,0:T(8,128)(2,1)S(1)}, bf16[384,768]{1,0:T(8,128)(2,1)}, bf16[384,768]{1,0:T(8,128)(2,1)S(1)}, f32[256,1]{1,0:T(8,128)S(1)}, s32[256,1]{1,0:T(8,128)S(1)}) custom-call(f32[256,768]{1,0:T(8,128)S(1)} %embed_own_last.1.own, bf16[256,768]{1,0:T(8,128)(2,1)S(1)} %collective-permute-done.14.came, bf16[768,16]{1,0:T(8,128)(2,1)S(1)} %copy.12.router, ...), custom_call_target="tpu_custom_call" | custom-call | flops 3449999872 | tf_op jit(solution)/shard_map/route/pallas_call | solution.py:286
  86.5 14.3 %all_to_all.20 = bf16[8,48,768]{2,1,0:T(8,128)(2,1)S(1)} all-to-all(bf16[8,48,768]{2,1,0:T(8,128)(2,1)S(1)} %bitcast.24), channel_id=1, replica_groups=mesh['row'=16,'col'=8] {'col'}, dimensions={0} | all-to-all | bytes 1179648 | tf_op jit(solution)/shard_map/all_to_all | solution.py:353
  100.7 3.5 %all-to-all-start = ((bf16[8,48,768]{2,1,0:T(8,128)(2,1)}), bf16[8,48,768]{2,1,0:T(8,128)(2,1)S(1)}, u32[]{:S(2)}, u32[]{:S(2)}) async-start(bf16[8,48,768]{2,1,0:T(8,128)(2,1)} %bitcast.13), calls=%async_computation | async-start | bytes 1179648 | tf_op jit(solution)/shard_map/all_to_all | solution.py:353
  104.3 2.3 %copy-done.7 = bf16[768,3072]{1,0:T(8,128)(2,1)S(1)} copy-done((bf16[768,3072]{1,0:T(8,128)(2,1)S(1)}, bf16[768,3072]{1,0:T(8,128)(2,1)}, u32[]{:S(2)}) %copy-start.7) | copy-done | bytes 4718616
  106.6 2.3 %copy-done.9 = bf16[3072,768]{1,0:T(8,128)(2,1)S(1)} copy-done((bf16[3072,768]{1,0:T(8,128)(2,1)S(1)}, bf16[3072,768]{1,0:T(8,128)(2,1)}, u32[]{:S(2)}) %copy-start.9) | copy-done | bytes 4718616
  109.0 5.0 %expert_1.1 = bf16[384,768]{1,0:T(8,128)(2,1)} custom-call(bf16[384,768]{1,0:T(8,128)(2,1)S(1)} %bitcast.25, bf16[768,3072]{1,0:T(8,128)(2,1)S(1)} %copy-done.7, bf16[3072,768]{1,0:T(8,128)(2,1)S(1)} %copy-done.9), custom_call_target="tpu_custom_call" | custom-call | flops 5750000128 | tf_op jit(solution)/shard_map/expert_1/pallas_call | solution.py:307
  114.0 0.9 all-to-all-done
  114.9 4.8 %all-to-all-start.3 = ((bf16[8,48,768]{2,1,0:T(8,128)(2,1)}), bf16[8,48,768]{2,1,0:T(8,128)(2,1)S(1)}, u32[]{:S(2)}, u32[]{:S(2)}) async-start(bf16[8,48,768]{2,1,0:T(8,128)(2,1)} %bitcast.19), calls=%async_computation.3 | async-start | bytes 1179648 | tf_op jit(solution)/shard_map/all_to_all | solution.py:353
  119.6 2.3 %copy-done.3 = bf16[768,3072]{1,0:T(8,128)(2,1)S(1)} copy-done((bf16[768,3072]{1,0:T(8,128)(2,1)S(1)}, bf16[768,3072]{1,0:T(8,128)(2,1)}, u32[]{:S(2)}) %copy-start.3) | copy-done | bytes 4718616
  122.0 2.3 %copy-done.5 = bf16[3072,768]{1,0:T(8,128)(2,1)S(1)} copy-done((bf16[3072,768]{1,0:T(8,128)(2,1)S(1)}, bf16[3072,768]{1,0:T(8,128)(2,1)}, u32[]{:S(2)}) %copy-start.5) | copy-done | bytes 4718616
  124.3 4.2 %expert_0.1 = bf16[384,768]{1,0:T(8,128)(2,1)S(1)} custom-call(bf16[384,768]{1,0:T(8,128)(2,1)S(1)} %bitcast.22, bf16[768,3072]{1,0:T(8,128)(2,1)S(1)} %copy-done.3, bf16[3072,768]{1,0:T(8,128)(2,1)S(1)} %copy-done.5), custom_call_target="tpu_custom_call" | custom-call | flops 5750000128 | tf_op jit(solution)/shard_map/expert_0/pallas_call | solution.py:307
  128.5 1.2 all-to-all-done.3
  129.7 13.9 %all_to_all.21 = bf16[8,48,768]{2,1,0:T(8,128)(2,1)S(1)} all-to-all(bf16[8,48,768]{2,1,0:T(8,128)(2,1)S(1)} %bitcast.26), channel_id=1, replica_groups=mesh['row'=16,'col'=8] {'col'}, dimensions={0} | all-to-all | bytes 1179648 | tf_op jit(solution)/shard_map/all_to_all | solution.py:353
  143.6 1.4 mix.1
  (44 shorter events, 0.2 us)
Async XLA Ops:
  0.0 31.7 %collective-permute-start.4 = (bf16[512,768]{1,0:T(8,128)(2,1)}, bf16[512,768]{1,0:T(8,128)(2,1)S(1)}, u32[]{:S(2)}, u32[]{:S(2)}) collective-permute-start(bf16[512,768]{1,0:T(8,128)(2,1)} %refs_0_.5), channel_id=1, source_target_pairs={{0,32},{1,33},{2,34},{3,35},{4,36},{5,37},{6,38},{7,39},{8,40},{9,... | collective-permute-start | bytes 2359304 | tf_op jit(solution)/shard_map/ppermute | solution.py:56
  1.6 30.1 %collective-permute-start.5 = (bf16[512,768]{1,0:T(8,128)(2,1)}, bf16[512,768]{1,0:T(8,128)(2,1)S(1)}, u32[]{:S(2)}, u32[]{:S(2)}) collective-permute-start(bf16[512,768]{1,0:T(8,128)(2,1)} %refs_0_.5), channel_id=1, source_target_pairs={{0,96},{1,97},{2,98},{3,99},{4,100},{5,101},{6,102},{7,103},{8,104... | collective-permute-start | bytes 2359304 | tf_op jit(solution)/shard_map/ppermute | solution.py:56
  3.2 28.5 %collective-permute-start.6 = (bf16[512,768]{1,0:T(8,128)(2,1)}, bf16[512,768]{1,0:T(8,128)(2,1)S(1)}, u32[]{:S(2)}, u32[]{:S(2)}) collective-permute-start(bf16[512,768]{1,0:T(8,128)(2,1)} %refs_0_.5), channel_id=1, source_target_pairs={{0,20},{1,21},{2,22},{3,23},{4,16},{5,17},{6,18},{7,19},{8,28},{9,... | collective-permute-start | bytes 2359304 | tf_op jit(solution)/shard_map/ppermute | solution.py:56
  8.3 3.6 %collective-permute-start = (bf16[2,256,128]{2,1,0:T(8,128)(2,1)S(1)}, bf16[2,256,128]{2,1,0:T(8,128)(2,1)S(1)}, u32[]{:S(2)}, u32[]{:S(2)}) collective-permute-start(bf16[2,256,128]{2,1,0:T(8,128)(2,1)S(1)} %get-tuple-element.56), channel_id=1, source_target_pairs={{0,8},{8,16},{16,24},{24,32},{32,40},{40,48},{48,56},{56,64},{64,7... | collective-permute-start | bytes 393224 | tf_op jit(solution)/shard_map/ppermute | solution.py:344
  9.7 3.4 %collective-permute-start.1 = (bf16[2,256,128]{2,1,0:T(8,128)(2,1)S(1)}, bf16[2,256,128]{2,1,0:T(8,128)(2,1)S(1)}, u32[]{:S(2)}, u32[]{:S(2)}) collective-permute-start(bf16[2,256,128]{2,1,0:T(8,128)(2,1)S(1)} %get-tuple-element.55), channel_id=1, source_target_pairs={{8,0},{16,8},{24,16},{32,24},{40,32},{48,40},{56,48},{64,56},{72,6... | collective-permute-start | bytes 393224 | tf_op jit(solution)/shard_map/ppermute | solution.py:344
  13.1 6.2 %collective-permute-start.2 = (bf16[68,2,128]{2,1,0:T(2,128)(2,1)S(1)}, bf16[68,2,128]{2,1,0:T(2,128)(2,1)S(1)}, u32[]{:S(2)}, u32[]{:S(2)}) collective-permute-start(bf16[68,2,128]{2,1,0:T(2,128)(2,1)S(1)} %pad_maximum_fusion.1), channel_id=1, source_target_pairs={{1,0},{2,1},{3,2},{4,3},{5,4},{6,5},{7,6},{9,8},{10,9},{11,10},{12... | collective-permute-start | bytes 104456 | tf_op jit(solution)/shard_map/ppermute | solution.py:344
  14.5 6.2 %collective-permute-start.3 = (bf16[68,2,128]{2,1,0:T(2,128)(2,1)S(1)}, bf16[68,2,128]{2,1,0:T(2,128)(2,1)S(1)}, u32[]{:S(2)}, u32[]{:S(2)}) collective-permute-start(bf16[68,2,128]{2,1,0:T(2,128)(2,1)S(1)} %pad_maximum_fusion.2), channel_id=1, source_target_pairs={{0,1},{1,2},{2,3},{3,4},{4,5},{5,6},{6,7},{8,9},{9,10},{10,11},{11... | collective-permute-start | bytes 104456 | tf_op jit(solution)/shard_map/ppermute | solution.py:344
  31.7 39.2 %copy-start.1 = (bf16[512,768]{1,0:T(8,128)(2,1)S(1)}, bf16[512,768]{1,0:T(8,128)(2,1)}, u32[]{:S(2)}) copy-start(bf16[512,768]{1,0:T(8,128)(2,1)} %refs_0_.5) | copy-start | bytes 2359300
  31.7 29.9 %collective-permute-start.7 = (bf16[512,768]{1,0:T(8,128)(2,1)S(1)}, bf16[512,768]{1,0:T(8,128)(2,1)S(1)}, u32[]{:S(2)}, u32[]{:S(2)}) collective-permute-start(bf16[512,768]{1,0:T(8,128)(2,1)S(1)} %collective-permute-done.4.refs_1_), channel_id=1, source_target_pairs={{0,32},{1,33},{2,34},{3,35},{4,36},{5,37},{6,38},{7,39},{8,40},{9,... | collective-permute-start | bytes 2359304 | tf_op jit(solution)/shard_map/ppermute | solution.py:56
  44.6 21.2 %collective-permute-start.9 = (bf16[512,768]{1,0:T(8,128)(2,1)S(1)}, bf16[512,768]{1,0:T(8,128)(2,1)S(1)}, u32[]{:S(2)}, u32[]{:S(2)}) collective-permute-start(bf16[512,768]{1,0:T(8,128)(2,1)S(1)} %collective-permute-done.4.refs_1_), channel_id=1, source_target_pairs={{0,20},{1,21},{2,22},{3,23},{4,16},{5,17},{6,18},{7,19},{8,28},{9,... | collective-permute-start | bytes 2359304 | tf_op jit(solution)/shard_map/ppermute | solution.py:56
  44.6 21.2 %collective-permute-start.8 = (bf16[512,768]{1,0:T(8,128)(2,1)S(1)}, bf16[512,768]{1,0:T(8,128)(2,1)S(1)}, u32[]{:S(2)}, u32[]{:S(2)}) collective-permute-start(bf16[512,768]{1,0:T(8,128)(2,1)S(1)} %collective-permute-done.6.refs_4_), channel_id=1, source_target_pairs={{0,96},{1,97},{2,98},{3,99},{4,100},{5,101},{6,102},{7,103},{8,104... | collective-permute-start | bytes 2359304 | tf_op jit(solution)/shard_map/ppermute | solution.py:56
  57.4 17.5 %copy-start.2 = (bf16[768,3072]{1,0:T(8,128)(2,1)}, bf16[768,3072]{1,0:T(8,128)(2,1)S(1)}, u32[]{:S(2)}) copy-start(bf16[768,3072]{1,0:T(8,128)(2,1)S(1)} %get-tuple-element.48.up) | copy-start | bytes 14155780
  57.4 17.5 %copy-start.4 = (bf16[3072,768]{1,0:T(8,128)(2,1)}, bf16[3072,768]{1,0:T(8,128)(2,1)S(1)}, u32[]{:S(2)}) copy-start(bf16[3072,768]{1,0:T(8,128)(2,1)S(1)} %get-tuple-element.49.down) | copy-start | bytes 14155780
  57.4 17.5 %copy-start.6 = (bf16[768,3072]{1,0:T(8,128)(2,1)}, bf16[768,3072]{1,0:T(8,128)(2,1)S(1)}, u32[]{:S(2)}) copy-start(bf16[768,3072]{1,0:T(8,128)(2,1)S(1)} %get-tuple-element.51.up) | copy-start | bytes 14155780
  57.4 17.5 %copy-start.8 = (bf16[3072,768]{1,0:T(8,128)(2,1)}, bf16[3072,768]{1,0:T(8,128)(2,1)S(1)}, u32[]{:S(2)}) copy-start(bf16[3072,768]{1,0:T(8,128)(2,1)S(1)} %get-tuple-element.52.down) | copy-start | bytes 14155780
  57.4 17.5 %copy-start.10 = (bf16[8,256,512]{2,1,0:T(8,128)(2,1)}, bf16[8,256,512]{2,1,0:T(8,128)(2,1)S(1)}, u32[]{:S(2)}) copy-start(bf16[8,256,512]{2,1,0:T(8,128)(2,1)S(1)} %get-tuple-element.36.tokens) | copy-start | bytes 6291460
  57.4 18.5 %collective-permute-start.13 = (bf16[8,256,512]{2,1,0:T(8,128)(2,1)S(1)}, bf16[8,256,512]{2,1,0:T(8,128)(2,1)S(1)}, u32[]{:S(2)}, u32[]{:S(2)}) collective-permute-start(bf16[8,256,512]{2,1,0:T(8,128)(2,1)S(1)} %get-tuple-element.41), channel_id=1, source_target_pairs={{0,8},{1,9},{2,10},{3,11},{4,12},{5,13},{6,14},{7,15},{8,0},{9,1},... | collective-permute-start | bytes 6291464 | tf_op jit(solution)/shard_map/ppermute | solution.py:56
  65.9 14.0 %collective-permute-start.10 = (bf16[176,768]{1,0:T(8,128)(2,1)S(1)}, bf16[176,768]{1,0:T(8,128)(2,1)S(1)}, u32[]{:S(2)}, u32[]{:S(2)}) collective-permute-start(bf16[176,768]{1,0:T(8,128)(2,1)S(1)} %slice.41), channel_id=1, source_target_pairs={{0,96},{1,97},{2,98},{3,99},{4,100},{5,101},{6,102},{7,103},{8,104... | collective-permute-start | bytes 811016 | tf_op jit(solution)/shard_map/ppermute | solution.py:56
  67.0 13.0 %collective-permute-start.11 = (bf16[176,768]{1,0:T(8,128)(2,1)S(1)}, bf16[176,768]{1,0:T(8,128)(2,1)S(1)}, u32[]{:S(2)}, u32[]{:S(2)}) collective-permute-start(bf16[176,768]{1,0:T(8,128)(2,1)S(1)} %slice.42), channel_id=1, source_target_pairs={{0,32},{1,33},{2,34},{3,35},{4,36},{5,37},{6,38},{7,39},{8,40},{9,... | collective-permute-start | bytes 811016 | tf_op jit(solution)/shard_map/ppermute | solution.py:56
  68.3 11.7 %collective-permute-start.12 = (bf16[160,768]{1,0:T(8,128)(2,1)S(1)}, bf16[160,768]{1,0:T(8,128)(2,1)S(1)}, u32[]{:S(2)}, u32[]{:S(2)}) collective-permute-start(bf16[160,768]{1,0:T(8,128)(2,1)S(1)} %slice.43), channel_id=1, source_target_pairs={{0,20},{1,21},{2,22},{3,23},{4,16},{5,17},{6,18},{7,19},{8,28},{9,... | collective-permute-start | bytes 737288 | tf_op jit(solution)/shard_map/ppermute | solution.py:56
  75.0 0.9 copy-start.12
  79.9 1.6 %copy-start.14 = (bf16[768,16]{0,1:T(8,128)(2,1)S(1)}, bf16[768,16]{0,1:T(8,128)(2,1)}, u32[]{:S(2)}) copy-start(bf16[768,16]{0,1:T(8,128)(2,1)} %param.12) | copy-start | bytes 73732
  79.9 1.7 %copy-start = (s32[1,1,256,1]{2,3,1,0:T(1,128)S(1)}, s32[1,1,256,1]{2,3,1,0:T(1,128)}, u32[]{:S(2)}) copy-start(s32[1,1,256,1]{2,3,1,0:T(1,128)} %param.13) | copy-start | bytes 3076
  79.9 1.9 %copy-start.13 = (f32[256,768]{1,0:T(8,128)S(1)}, f32[256,768]{1,0:T(8,128)}, u32[]{:S(2)}) copy-start(f32[256,768]{1,0:T(8,128)} %copy-done.12) | copy-start | bytes 2359300
  81.4 3.4 %collective-permute-start.14 = (bf16[256,768]{1,0:T(8,128)(2,1)S(1)}, bf16[256,768]{1,0:T(8,128)(2,1)S(1)}, u32[]{:S(2)}, u32[]{:S(2)}) collective-permute-start(bf16[256,768]{1,0:T(8,128)(2,1)S(1)} %embed_partner_last.1), channel_id=1, source_target_pairs={{0,8},{1,9},{2,10},{3,11},{4,12},{5,13},{6,14},{7,15},{8,0},{9,1},... | collective-permute-start | bytes 1179656 | tf_op jit(solution)/shard_map/ppermute | solution.py:56
  81.8 1.6 %copy-start.11 = (bf16[8,256,512]{2,1,0:T(8,128)(2,1)S(1)}, bf16[8,256,512]{2,1,0:T(8,128)(2,1)}, u32[]{:S(2)}) copy-start(bf16[8,256,512]{2,1,0:T(8,128)(2,1)} %copy-done.10) | copy-start | bytes 6291460
  100.7 14.1 %all-to-all-start = ((bf16[8,48,768]{2,1,0:T(8,128)(2,1)}), bf16[8,48,768]{2,1,0:T(8,128)(2,1)S(1)}, u32[]{:S(2)}, u32[]{:S(2)}) async-start(bf16[8,48,768]{2,1,0:T(8,128)(2,1)} %bitcast.13), calls=%async_computation | async-start | bytes 1179648 | tf_op jit(solution)/shard_map/all_to_all | solution.py:353
  104.3 2.3 %copy-start.7 = (bf16[768,3072]{1,0:T(8,128)(2,1)S(1)}, bf16[768,3072]{1,0:T(8,128)(2,1)}, u32[]{:S(2)}) copy-start(bf16[768,3072]{1,0:T(8,128)(2,1)} %copy-done.6) | copy-start | bytes 14155780
  106.6 2.3 %copy-start.9 = (bf16[3072,768]{1,0:T(8,128)(2,1)S(1)}, bf16[3072,768]{1,0:T(8,128)(2,1)}, u32[]{:S(2)}) copy-start(bf16[3072,768]{1,0:T(8,128)(2,1)} %copy-done.8) | copy-start | bytes 14155780
  114.9 14.8 %all-to-all-start.3 = ((bf16[8,48,768]{2,1,0:T(8,128)(2,1)}), bf16[8,48,768]{2,1,0:T(8,128)(2,1)S(1)}, u32[]{:S(2)}, u32[]{:S(2)}) async-start(bf16[8,48,768]{2,1,0:T(8,128)(2,1)} %bitcast.19), calls=%async_computation.3 | async-start | bytes 1179648 | tf_op jit(solution)/shard_map/all_to_all | solution.py:353
  119.6 2.3 %copy-start.3 = (bf16[768,3072]{1,0:T(8,128)(2,1)S(1)}, bf16[768,3072]{1,0:T(8,128)(2,1)}, u32[]{:S(2)}) copy-start(bf16[768,3072]{1,0:T(8,128)(2,1)} %copy-done.2) | copy-start | bytes 14155780
  122.0 2.3 %copy-start.5 = (bf16[3072,768]{1,0:T(8,128)(2,1)S(1)}, bf16[3072,768]{1,0:T(8,128)(2,1)}, u32[]{:S(2)}) copy-start(bf16[3072,768]{1,0:T(8,128)(2,1)} %copy-done.4) | copy-start | bytes 14155780

commit v5 on v4

--- a/solution.py
+++ b/solution.py
@@ -10,7 +10,7 @@
 ROWS, COLS, CH = 64, 256, 128
 WIDE = 272
 DIM, FF, CAP, TOK = 768, 3072, 48, 256
-SLOTS = 8 * CAP
+PAIR = 2 * CAP
 STEPS, BAND = 2, 2
 F32, BF16 = jnp.float32, jnp.bfloat16
 ANY = pl.BlockSpec(memory_space=pl.ANY)
@@ -204,27 +204,19 @@
     )(*args, *fetch, *given)
 
 
-def embed_kernel(layout, has_sum, order, tokens, *refs):
+def embed_kernel(layout, order, tokens, *refs):
     count = sum(len(parts) for _, parts in layout)
-    pieces, refs = refs[:count], refs[count:]
-    given, refs = (refs[0], refs[1:]) if has_sum else (None, refs)
-    total, lhs, rhs, lhs_sems, rhs_sems = refs
-    copies, at = [], 0
-    for n, (which, parts) in enumerate(layout):
-        here = [pltpu.make_async_copy(tokens.at[order[which]], lhs.at[n], lhs_sems.at[n])]
-        for m, (first, rows) in enumerate(parts):
-            target = rhs.at[n, pl.ds(first, rows)]
-            here.append(pltpu.make_async_copy(pieces[at], target, rhs_sems.at[n, m]))
-            at += 1
-        copies.append(here)
-    for here in copies:
-        for copy in here:
-            copy.start()
-    result = given[...] if has_sum else None
-    for n in range(len(layout)):
-        for copy in copies[n]:
-            copy.wait()
-        part = jnp.dot(lhs[n], rhs[n], preferred_element_type=F32)
+    pieces, given, total, whole = refs[:count], refs[count:-2], refs[-2], refs[-1]
+    result = given[0][...] if given else None
+    at = 0
+    for which, parts in layout:
+        shard = pieces[at]
+        if len(parts) > 1:
+            shard = whole
+            for m, (first, rows) in enumerate(parts):
+                whole[pl.ds(first, rows)] = pieces[at + m][...]
+        at += len(parts)
+        part = jnp.dot(tokens[order[which]], shard[...], preferred_element_type=F32)
         result = part if result is None else result + part
     total[...] = result.astype(total.dtype)
 
@@ -235,58 +227,55 @@
         heights = [part.shape[0] for part in parts]
         layout.append((which, [(sum(heights[:m]), rows) for m, rows in enumerate(heights)]))
         arrays.extend(parts)
-    count = len(shards)
     return pl.pallas_call(
-        functools.partial(embed_kernel, layout, bool(sums)),
-        in_specs=[SMEM] + [ANY] * (1 + len(arrays)) + [VMEM] * len(sums),
+        functools.partial(embed_kernel, layout),
+        in_specs=[SMEM] + [VMEM] * (1 + len(arrays) + len(sums)),
         out_specs=VMEM,
         out_shape=jax.ShapeDtypeStruct((TOK, DIM), dtype),
-        scratch_shapes=[
-            pltpu.VMEM((count, TOK, 512), BF16),
-            pltpu.VMEM((count, 512, DIM), BF16),
-            pltpu.SemaphoreType.DMA((count,)),
-            pltpu.SemaphoreType.DMA((count, 4)),
-        ],
-        compiler_params=params(20),
+        scratch_shapes=[pltpu.VMEM((512, DIM), BF16)],
+        compiler_params=params(12),
         cost_estimate=cost(micros),
         name=name,
     )(order, tokens, *arrays, *sums)
 
 
-def route_kernel(own, came, router, ids_row, ids_col, embedded, out0, out1, gate, place):
+def route_kernel(where, own, came, router, ids_row, ids_col, embedded, gate, place, *outs):
     value = (own[...] + came[...].astype(F32)).astype(BF16)
     embedded[...] = value
     wide = value.astype(F32)
     scale = lax.rsqrt(jnp.mean(wide * wide, axis=-1, keepdims=True) + 1e-06)
     normed = (wide * scale).astype(BF16)
-    scores = jnp.dot(normed, router[...], preferred_element_type=F32)
+    scores = lax.dot_general(
+        normed, router[...], (((1,), (1,)), ((), ())), preferred_element_type=F32
+    )
     across = lax.broadcasted_iota(jnp.int32, (TOK, TOK), 1)
     down = lax.broadcasted_iota(jnp.int32, (TOK, TOK), 0)
-    col, row = ids_col[...], ids_row[...]
+    col, row, me = ids_col[...], ids_row[...], where[1]
     hot = jnp.where(col == lax.broadcasted_iota(jnp.int32, (TOK, 16), 1), 1.0, 0.0)
     gate[...] = jax.nn.sigmoid(jnp.sum(scores * hot, axis=-1, keepdims=True))
     earlier = jnp.where(across < down, 1.0, 0.0).astype(BF16)
     counts = jnp.dot(earlier, hot.astype(BF16), preferred_element_type=F32)
     rank = jnp.sum(counts * hot, axis=-1, keepdims=True).astype(jnp.int32)
-    place[...] = (col & 1) * SLOTS + (col >> 1) * CAP + rank
+    place[...] = ((col >> 1) ^ me) * PAIR + (col & 1) * CAP + rank
     hot_t = jnp.where(row == lax.broadcasted_iota(jnp.int32, (16, TOK), 0), 1.0, 0.0)
     later = jnp.where(down < across, 1.0, 0.0).astype(BF16)
     counts_t = jnp.dot(hot_t.astype(BF16), later, preferred_element_type=F32)
     rank_t = jnp.sum(counts_t * hot_t, axis=0, keepdims=True).astype(jnp.int32)
-    place_t = (row & 1) * SLOTS + (row >> 1) * CAP + rank_t
-    slot = lax.broadcasted_iota(jnp.int32, (SLOTS, TOK), 0)
-    for n, out in enumerate((out0, out1)):
-        pick = jnp.where(slot + n * SLOTS == place_t, 1.0, 0.0).astype(BF16)
-        out[...] = jnp.dot(pick, normed, preferred_element_type=F32).astype(BF16)
+    place_t = ((row >> 1) ^ me) * PAIR + (row & 1) * CAP + rank_t
+    slot = lax.broadcasted_iota(jnp.int32, (8 * PAIR, TOK), 0)
+    pick = jnp.where(slot == place_t, 1.0, 0.0).astype(BF16)
+    slots = jnp.dot(pick, normed, preferred_element_type=F32).astype(BF16)
+    for k, out in enumerate(outs):
+        out[...] = slots[k * PAIR : (k + 1) * PAIR]
 
 
 def route_call(*args):
-    shapes = [((TOK, DIM), BF16), ((SLOTS, DIM), BF16), ((SLOTS, DIM), BF16)]
-    shapes += [((TOK, 1), F32), ((TOK, 1), jnp.int32)]
+    shapes = [((TOK, DIM), BF16), ((TOK, 1), F32), ((TOK, 1), jnp.int32)]
+    shapes += [((PAIR, DIM), BF16)] * 8
     return pl.pallas_call(
         route_kernel,
-        in_specs=[VMEM] * 5,
-        out_specs=[VMEM] * 5,
+        in_specs=[SMEM] + [VMEM] * 5,
+        out_specs=[VMEM] * 11,
         out_shape=[jax.ShapeDtypeStruct(*shape) for shape in shapes],
         compiler_params=params(16),
         cost_estimate=cost(3),
@@ -294,48 +283,58 @@
     )(*args)
 
 
-def expert_kernel(rows, up, down, out, hidden):
-    for at in range(0, FF, 512):
-        part = pl.ds(at, 512)
-        z = jnp.dot(rows[...], up[:, part], preferred_element_type=F32)
-        act = 0.5 * z * (1.0 + jnp.tanh(0.7978845608028654 * (z + 0.044715 * (z * z * z))))
-        hidden[:, part] = act.astype(BF16)
-    out[...] = jnp.dot(hidden[...], down[...], preferred_element_type=F32).astype(BF16)
-
-
-def expert_call(name, rows, up, down):
+def expert_kernel(*refs):
+    count = (len(refs) - 5) // 2
+    arrays, weights, outs, hidden = refs[:count], refs[count : count + 4], refs[count + 4 : -1], refs[-1]
+    for e in range(2):
+        up, down = weights[e], weights[2 + e]
+        rows = jnp.concatenate([a[e * CAP : (e + 1) * CAP] for a in arrays], axis=0)
+        for at in range(0, FF, 512):
+            part = pl.ds(at, 512)
+            z = jnp.dot(rows, up[:, part], preferred_element_type=F32)
+            act = 0.5 * z * (1.0 + jnp.tanh(0.7978845608028654 * (z + 0.044715 * (z * z * z))))
+            hidden[:, part] = act.astype(BF16)
+        result = jnp.dot(hidden[...], down[...], preferred_element_type=F32).astype(BF16)
+        for n, out in enumerate(outs):
+            out[e * CAP : (e + 1) * CAP] = result[n * CAP : (n + 1) * CAP]
+
+
+def expert_call(name, arrays, weights):
+    count = len(arrays)
     return pl.pallas_call(
         expert_kernel,
-        in_specs=[VMEM] * 3,
-        out_specs=VMEM,
-        out_shape=jax.ShapeDtypeStruct((SLOTS, DIM), BF16),
-        scratch_shapes=[pltpu.VMEM((SLOTS, FF), BF16)],
+        in_specs=[VMEM] * (count + 4),
+        out_specs=[VMEM] * count,
+        out_shape=[jax.ShapeDtypeStruct((PAIR, DIM), BF16)] * count,
+        scratch_shapes=[pltpu.VMEM((count * CAP, FF), BF16)],
         compiler_params=params(12),
         cost_estimate=cost(5),
         name=name,
-    )(rows, up, down)
-
-
-def mix_kernel(embedded, gate, place, back0, back1, out):
-    slot = lax.broadcasted_iota(jnp.int32, (TOK, SLOTS), 1)
-    result = None
-    for n, back in enumerate((back0, back1)):
-        pick = jnp.where(slot + n * SLOTS == place[...], 1.0, 0.0).astype(BF16)
-        part = jnp.dot(pick, back[...], preferred_element_type=F32)
-        result = part if result is None else result + part
-    out[...] = (embedded[...].astype(F32) + gate[...] * result).astype(BF16)
-
-
-def mix_call(*args):
+    )(*arrays, *[in_vmem(a) for a in weights])
+
+
+def mix_kernel(steps, *refs):
+    base, gate, place, *arrays, out = refs
+    slots = jnp.concatenate([a[...] for a in arrays], axis=0)
+    lane = lax.broadcasted_iota(jnp.int32, (TOK, len(steps) * PAIR), 1)
+    slot = lane
+    for n, k in enumerate(steps):
+        slot = jnp.where(lane >= n * PAIR, lane + (k - n) * PAIR, slot)
+    pick = jnp.where(slot == place[...], 1.0, 0.0).astype(BF16)
+    result = jnp.dot(pick, slots, preferred_element_type=F32)
+    out[...] = (base[...].astype(F32) + gate[...] * result).astype(out.dtype)
+
+
+def mix_call(name, steps, base, gate, place, arrays, dtype, micros):
     return pl.pallas_call(
-        mix_kernel,
-        in_specs=[VMEM] * 5,
+        functools.partial(mix_kernel, steps),
+        in_specs=[VMEM] * (3 + len(arrays)),
         out_specs=VMEM,
-        out_shape=jax.ShapeDtypeStruct((TOK, DIM), BF16),
+        out_shape=jax.ShapeDtypeStruct((TOK, DIM), dtype),
         compiler_params=params(12),
-        cost_estimate=cost(2),
-        name="mix",
-    )(*args)
+        cost_estimate=cost(micros),
+        name=name,
+    )(base, gate, place, *arrays)
 
 
 def neighbours(value, axis, ahead):
@@ -348,9 +347,8 @@
     return jnp.concatenate([a[:, first : first + 2] for a in (top, scene, bottom)], axis=0)
 
 
-def exchange(value):
-    value = value.reshape(8, CAP, DIM)
-    return lax.all_to_all(value, "col", 0, 0, tiled=True).reshape(SLOTS, DIM)
+def exchange(arrays, steps):
+    return [lax.ppermute(arrays[k], "col", [(i, i ^ k) for i in range(8)]) for k in steps]
 
 
 def local(
@@ -396,13 +394,21 @@
     partner = embed_call("embed_partner_last", order, came, [(7, last)], [partner], BF16)
     came = send(partner, dc=1)
     own = embed_call("embed_own_last", order, keep, [(7, last)], [own])
-    embedded, out0, out1, gate, slots = route_call(
-        own, came, router_weight, expert_ids.reshape(1, TOK), expert_ids.reshape(TOK, 1)
-    )
-    in0, in1 = exchange(out0), exchange(out1)
-    back0 = exchange(expert_call("expert_0", in0, in_vmem(up0), in_vmem(down0)))
-    back1 = exchange(expert_call("expert_1", in1, in_vmem(up1), in_vmem(down1)))
-    return mix_call(embedded, gate, slots, back0, back1).reshape(1, 1, TOK, DIM)
+    embedded, gate, slots, *outs = route_call(
+        place, own, came, router_weight.T, expert_ids.reshape(1, TOK), expert_ids.reshape(TOK, 1)
+    )
+    first, second, weights = (4, 1, 3), (2, 6, 5, 7), (up0, up1, down0, down1)
+    in_first, outs = lax.optimization_barrier((exchange(outs, first), outs))
+    in_second = exchange(outs, second)
+    back_first = expert_call("experts_first", [outs[0], *in_first], weights)
+    in_second, back_first = lax.optimization_barrier((in_second, back_first))
+    back = dict(zip((0, *first), back_first))
+    back_first = [back[0], *exchange(back, first)]
+    back = dict(zip(second, expert_call("experts_second", in_second, weights)))
+    back_second = exchange(back, second)
+    mixed = mix_call("mix_first", (0, *first), embedded, gate, slots, back_first, F32, 20)
+    mixed = mix_call("mix_second", second, mixed, gate, slots, back_second, BF16, 2)
+    return mixed.reshape(1, 1, TOK, DIM)
 
 
 def solution(mesh):

time: 146 us -> 130 us (0.89)
  blocking collectives: 28.2 us -> 0 us
  waiting for transfers between devices: 8.79 us -> 25 us
  starting transfers between devices: 47.7 us -> 59.9 us
  local copies, waits for them, and re-layouts: 14.4 us -> 4.94 us
  Pallas kernels: 45.2 us -> 38.9 us
    all_to_all x2 -> x0, blocking collectives: 28.2 us -> none  [exchange(): return lax.all_to_all(value, 'col', 0, 0, tiled=True).reshape(SLOTS, DIM)]
    ppermute x0 -> x14, starting transfers between devices: none -> 20.5 us  [exchange(): lax.ppermute(arrays[k], 'col', [(i, i ^ k) for i in range(8)])]
    ppermute x0 -> x14, waiting for transfers between devices: none -> 16.9 us  [exchange(): lax.ppermute(arrays[k], 'col', [(i, i ^ k) for i in range(8)])]
    unnamed x31 -> x38, local copies, waits for them, and re-layouts: 12.1 us -> 2.56 us
    all_to_all x2 -> x0, starting transfers between devices: 8.31 us -> none  [exchange(): return lax.all_to_all(value, 'col', 0, 0, tiled=True).reshape(SLOTS, DIM)]
    pallas_call x8 -> x9, Pallas kernels: 23.1 us -> 17.2 us  [the longest x2 8.24 us: expert_call(): pl.pallas_call(expert_kernel, in_specs=[VMEM] * (count + 4), out_specs=[V...]
    all_to_all x2 -> x0, waiting for transfers between devices: 2.07 us -> none  [exchange(): return lax.all_to_all(value, 'col', 0, 0, tiled=True).reshape(SLOTS, DIM)]
  transfers between devices with their start and end apart: 17 -> 29, of which waited for: 5 -> 15; matrix products, arithmetic and copies ran while one was open for 2% -> 2% of each run, Pallas kernels for 28% -> 27%
where the time goes in v5:
time: 130 us; the launch traced here: 129 us
  starting transfers between devices  59.9 us (46%)
  Pallas kernels  38.9 us (30%)
  waiting for transfers between devices  25 us (19%)
  local copies, waits for them, and re-layouts  4.94 us (4%)
    ppermute x11, starting transfers between devices, send(): return lax.ppermute(value, ('row', 'col'), hop(**step))  31 us
    pallas_call x2, Pallas kernels, conv_call(): pl.pallas_call(functools.partial(conv_kernel, start, len(fetch)), grid=(S...  21.7 us
    ppermute x14, starting transfers between devices, exchange(): lax.ppermute(arrays[k], 'col', [(i, i ^ k) for i in range(8)])  20.5 us
    ppermute x14, waiting for transfers between devices, exchange(): lax.ppermute(arrays[k], 'col', [(i, i ^ k) for i in range(8)])  16.9 us
    ppermute x4, starting transfers between devices, neighbours(): lax.ppermute(value, axis, pairs if ahead else [(j, i) for i, j in pairs])  8.43 us
    pallas_call x2, Pallas kernels, expert_call(): pl.pallas_call(expert_kernel, in_specs=[VMEM] * (count + 4), out_specs=[V...  8.24 us
    pallas_call x4, Pallas kernels, embed_call(): pl.pallas_call(functools.partial(embed_kernel, layout), in_specs=[SMEM] +...  6.08 us
    ppermute x11, waiting for transfers between devices, send(): return lax.ppermute(value, ('row', 'col'), hop(**step))  5.62 us
  transfers between devices with their start and end apart: 29, of which 15 were waited for; matrix products, arithmetic and copies ran while one was open for 2% of the time, Pallas kernels for 27%

profile of v5, /device:TPU:0, one launch (start us, length us, event | category | flops | bytes accessed | tf_op | source)
XLA Modules:
  0.0 129.5 jit_solution(11675563902591283925)
XLA Ops:
  0.0 1.6 %collective-permute-start.4 = (bf16[512,768]{1,0:T(8,128)(2,1)}, bf16[512,768]{1,0:T(8,128)(2,1)S(1)}, u32[]{:S(2)}, u32[]{:S(2)}) collective-permute-start(bf16[512,768]{1,0:T(8,128)(2,1)} %refs_0_.5), channel_id=1, source_target_pairs={{0,32},{1,33},{2,34},{3,35},{4,36},{5,37},{6,38},{7,39},{8,40},{9,... | collective-permute-start | bytes 2359304 | tf_op jit(solution)/shard_map/ppermute | solution.py:56
  1.6 1.7 %collective-permute-start.5 = (bf16[512,768]{1,0:T(8,128)(2,1)}, bf16[512,768]{1,0:T(8,128)(2,1)S(1)}, u32[]{:S(2)}, u32[]{:S(2)}) collective-permute-start(bf16[512,768]{1,0:T(8,128)(2,1)} %refs_0_.5), channel_id=1, source_target_pairs={{0,96},{1,97},{2,98},{3,99},{4,100},{5,101},{6,102},{7,103},{8,104... | collective-permute-start | bytes 2359304 | tf_op jit(solution)/shard_map/ppermute | solution.py:56
  3.2 4.1 %collective-permute-start.6 = (bf16[512,768]{1,0:T(8,128)(2,1)}, bf16[512,768]{1,0:T(8,128)(2,1)S(1)}, u32[]{:S(2)}, u32[]{:S(2)}) collective-permute-start(bf16[512,768]{1,0:T(8,128)(2,1)} %refs_0_.5), channel_id=1, source_target_pairs={{0,20},{1,21},{2,22},{3,23},{4,16},{5,17},{6,18},{7,19},{8,28},{9,... | collective-permute-start | bytes 2359304 | tf_op jit(solution)/shard_map/ppermute | solution.py:56
  7.4 1.0 fusion.1
  8.3 1.3 %collective-permute-start = (bf16[2,256,128]{2,1,0:T(8,128)(2,1)S(1)}, bf16[2,256,128]{2,1,0:T(8,128)(2,1)S(1)}, u32[]{:S(2)}, u32[]{:S(2)}) collective-permute-start(bf16[2,256,128]{2,1,0:T(8,128)(2,1)S(1)} %get-tuple-element.116), channel_id=1, source_target_pairs={{0,8},{8,16},{16,24},{24,32},{32,40},{40,48},{48,56},{56,64},{64,7... | collective-permute-start | bytes 393224 | tf_op jit(solution)/shard_map/ppermute | solution.py:343
  9.7 1.3 collective-permute-start.1
  11.0 1.0 fusion
  12.0 1.1 collective-permute-done.1.bottom
  13.1 1.3 collective-permute-start.2
  14.5 4.5 %collective-permute-start.3 = (bf16[68,2,128]{2,1,0:T(2,128)(2,1)S(1)}, bf16[68,2,128]{2,1,0:T(2,128)(2,1)S(1)}, u32[]{:S(2)}, u32[]{:S(2)}) collective-permute-start(bf16[68,2,128]{2,1,0:T(2,128)(2,1)S(1)} %pad_maximum_fusion.2), channel_id=1, source_target_pairs={{0,1},{1,2},{2,3},{3,4},{4,5},{5,6},{6,7},{8,9},{9,10},{10,11},{11... | collective-permute-start | bytes 104456 | tf_op jit(solution)/shard_map/ppermute | solution.py:343
  19.3 1.3 %collective-permute-done.3 = bf16[68,2,128]{2,1,0:T(2,128)(2,1)S(1)} collective-permute-done((bf16[68,2,128]{2,1,0:T(2,128)(2,1)S(1)}, bf16[68,2,128]{2,1,0:T(2,128)(2,1)S(1)}, u32[]{:S(2)}, u32[]{:S(2)}) %collective-permute-start.3) | collective-permute-done | bytes 34848 | tf_op jit(solution)/shard_map/ppermute | solution.py:343
  20.8 10.6 %convs_0.1 = (bf16[8,256,512]{2,1,0:T(8,128)(2,1)S(1)}, bf16[8,256,512]{2,1,0:T(8,128)(2,1)S(1)}) custom-call(s32[3]{0:T(128)S(1)} %pad_add_fusion.place.where, bf16[64,256,128]{2,1,0:T(8,128)(2,1)} %scene.3, bf16[2,256,128]{2,1,0:T(8,128)(2,1)S(1)} %collective-permute-done.top, bf16[2,256,128]{2,1,0:T(8,128)(2,1)S(1)} %collective-permute-done.1.bottom, ...), custom_call_target="tpu_custom_call" | custom-call | flops 12650000384 | tf_op jit(solution)/shard_map/convs_0/pallas_call | solution.py:182
  31.4 12.9 %collective-permute-start.7 = (bf16[512,768]{1,0:T(8,128)(2,1)S(1)}, bf16[512,768]{1,0:T(8,128)(2,1)S(1)}, u32[]{:S(2)}, u32[]{:S(2)}) collective-permute-start(bf16[512,768]{1,0:T(8,128)(2,1)S(1)} %collective-permute-done.4.refs_1_), channel_id=1, source_target_pairs={{0,32},{1,33},{2,34},{3,35},{4,36},{5,37},{6,38},{7,39},{8,40},{9,... | collective-permute-start | bytes 2359304 | tf_op jit(solution)/shard_map/ppermute | solution.py:56
  44.3 1.5 %collective-permute-start.8 = (bf16[512,768]{1,0:T(8,128)(2,1)S(1)}, bf16[512,768]{1,0:T(8,128)(2,1)S(1)}, u32[]{:S(2)}, u32[]{:S(2)}) collective-permute-start(bf16[512,768]{1,0:T(8,128)(2,1)S(1)} %collective-permute-done.6.refs_4_), channel_id=1, source_target_pairs={{0,96},{1,97},{2,98},{3,99},{4,100},{5,101},{6,102},{7,103},{8,104... | collective-permute-start | bytes 2359304 | tf_op jit(solution)/shard_map/ppermute | solution.py:56
  45.8 11.0 %convs_2.1 = (bf16[8,256,512]{2,1,0:T(8,128)(2,1)S(1)}, bf16[8,256,512]{2,1,0:T(8,128)(2,1)S(1)}, bf16[768,3072]{1,0:T(8,128)(2,1)S(1)}, bf16[768,3072]{1,0:T(8,...) custom-call(s32[3]{0:T(128)S(1)} %pad_add_fusion.place.where, ...), custom_call_target="tpu_custom_call", output_to_operand_aliasing={{0}: (9, {}), {1}: (10, {})} | custom-call | flops 12650000384 | tf_op jit(solution)/shard_map/convs_2/pallas_call | solution.py:182
  56.9 4.2 %collective-permute-start.13 = (bf16[8,256,512]{2,1,0:T(8,128)(2,1)S(1)}, bf16[8,256,512]{2,1,0:T(8,128)(2,1)S(1)}, u32[]{:S(2)}, u32[]{:S(2)}) collective-permute-start(bf16[8,256,512]{2,1,0:T(8,128)(2,1)S(1)} %get-tuple-element.71), channel_id=1, source_target_pairs={{0,8},{1,9},{2,10},{3,11},{4,12},{5,13},{6,14},{7,15},{8,0},{9,1},... | collective-permute-start | bytes 6291464 | tf_op jit(solution)/shard_map/ppermute | solution.py:56
  61.1 4.5 %collective-permute-done.9.refs_5_ = bf16[512,768]{1,0:T(8,128)(2,1)S(1)} collective-permute-done((bf16[512,768]{1,0:T(8,128)(2,1)S(1)}, bf16[512,768]{1,0:T(8,128)(2,1)S(1)}, u32[]{:S(2)}, u32[]{:S(2)}) %collective-permute-start.9) | collective-permute-done | bytes 786464 | tf_op jit(solution)/shard_map/ppermute | solution.py:56
  65.6 1.1 collective-permute-start.10
  66.7 1.3 collective-permute-start.11
  68.0 2.6 %collective-permute-start.12 = (bf16[160,768]{1,0:T(8,128)(2,1)S(1)}, bf16[160,768]{1,0:T(8,128)(2,1)S(1)}, u32[]{:S(2)}, u32[]{:S(2)}) collective-permute-start(bf16[160,768]{1,0:T(8,128)(2,1)S(1)} %slice.43), channel_id=1, source_target_pairs={{0,20},{1,21},{2,22},{3,23},{4,16},{5,17},{6,18},{7,19},{8,28},{9,... | collective-permute-start | bytes 737288 | tf_op jit(solution)/shard_map/ppermute | solution.py:56
  70.6 2.1 %embed_own.1.refs_3_ = f32[256,768]{1,0:T(8,128)S(1)} custom-call(s32[8]{0:T(128)S(1)} %stack.51.order, bf16[8,256,512]{2,1,0:T(8,128)(2,1)S(1)} %get-tuple-element.66.tokens, bf16[512,768]{1,0:T(8,128)(2,1)S(1)} %copy-done.1, bf16[512,768]{1,0:T(8,128)(2,1)S(1)} %collective-permute-done.4.refs_1_, bf16[512,768]{1,0:T(8,128)(2,1)S(1)} %collective-permute-done.5.refs_2_, ...), custom_call_target="tpu_custom_call" | custom-call | flops 46000001024 | tf_op jit(solution)/shard_map/embed_own/pallas_call | solution.py:230
  72.8 0.9 copy-done.9
  73.7 2.1 %embed_partner.1.refs_3_ = f32[256,768]{1,0:T(8,128)S(1)} custom-call(s32[8]{0:T(128)S(1)} %stack.51.order, bf16[8,256,512]{2,1,0:T(8,128)(2,1)S(1)} %collective-permute-done.13.tokens, bf16[512,768]{1,0:T(8,128)(2,1)S(1)} %copy-done.1, bf16[512,768]{1,0:T(8,128)(2,1)S(1)} %collective-permute-done.4.refs_1_, ...), custom_call_target="tpu_custom_call" | custom-call | flops 3449999872 | tf_op jit(solution)/shard_map/embed_partner/pallas_call | solution.py:230
  75.9 0.9 collective-permute-done.12.refs_2_
  77.0 0.9 embed_partner_last.1
  78.2 1.6 %copy-done.8 = bf16[8,256,512]{2,1,0:T(8,128)(2,1)S(1)} copy-done((bf16[8,256,512]{2,1,0:T(8,128)(2,1)S(1)}, bf16[8,256,512]{2,1,0:T(8,128)(2,1)}, u32[]{:S(2)}) %copy-start.8) | copy-done | bytes 2097176
  79.8 0.9 embed_own_last.1.own
  80.8 1.4 %route.1 = (bf16[256,768]{1,0:T(8,128)(2,1)S(1)}, f32[256,1]{1,0:T(8,128)S(1)}, s32[256,1]{1,0:T(8,128)S(1)}, bf16[96,768]{1,0:T(8,128)(2,1)S(1)}, bf16[96,768]{...) custom-call(s32[3]{0:T(128)S(1)} %pad_add_fusion.place.where, ...), custom_call_target="tpu_custom_call" | custom-call | flops 3449999872 | tf_op jit(solution)/shard_map/route/pallas_call | solution.py:275
  82.2 1.2 collective-permute-start.16
  83.4 1.8 %collective-permute-start.17 = (bf16[96,768]{1,0:T(8,128)(2,1)S(1)}, bf16[96,768]{1,0:T(8,128)(2,1)S(1)}, u32[]{:S(2)}, u32[]{:S(2)}) collective-permute-start(bf16[96,768]{1,0:T(8,128)(2,1)S(1)} %get-tuple-element.79), channel_id=1, source_target_pairs={{0,3},{1,2},{2,1},{3,0},{4,7},{5,6},{6,5},{7,4},{8,11},{9,10},{10,... | collective-permute-start | bytes 442376 | tf_op jit(solution)/shard_map/ppermute | solution.py:351
  85.2 3.3 %collective-permute-done.15.refs_1_ = bf16[96,768]{1,0:T(8,128)(2,1)S(1)} collective-permute-done((bf16[96,768]{1,0:T(8,128)(2,1)S(1)}, bf16[96,768]{1,0:T(8,128)(2,1)S(1)}, u32[]{:S(2)}, u32[]{:S(2)}) %collective-permute-start.15) | collective-permute-done | bytes 147488 | tf_op jit(solution)/shard_map/ppermute | solution.py:351
  88.5 2.0 %collective-permute-done.17.refs_3_ = bf16[96,768]{1,0:T(8,128)(2,1)S(1)} collective-permute-done((bf16[96,768]{1,0:T(8,128)(2,1)S(1)}, bf16[96,768]{1,0:T(8,128)(2,1)S(1)}, u32[]{:S(2)}, u32[]{:S(2)}) %collective-permute-start.17) | collective-permute-done | bytes 147488 | tf_op jit(solution)/shard_map/ppermute | solution.py:351
  90.6 0.7 collective-permute-start.18
  91.3 3.9 %collective-permute-start.19 = (bf16[96,768]{1,0:T(8,128)(2,1)S(1)}, bf16[96,768]{1,0:T(8,128)(2,1)S(1)}, u32[]{:S(2)}, u32[]{:S(2)}) collective-permute-start(bf16[96,768]{1,0:T(8,128)(2,1)S(1)} %get-tuple-element.86), channel_id=1, source_target_pairs={{0,6},{1,7},{2,4},{3,5},{4,2},{5,3},{6,0},{7,1},{8,14},{9,15},{10,... | collective-permute-start | bytes 442376 | tf_op jit(solution)/shard_map/ppermute | solution.py:351
  95.2 2.2 %collective-permute-start.21 = (bf16[96,768]{1,0:T(8,128)(2,1)S(1)}, bf16[96,768]{1,0:T(8,128)(2,1)S(1)}, u32[]{:S(2)}, u32[]{:S(2)}) collective-permute-start(bf16[96,768]{1,0:T(8,128)(2,1)S(1)} %get-tuple-element.88), channel_id=1, source_target_pairs={{0,7},{1,6},{2,5},{3,4},{4,3},{5,2},{6,1},{7,0},{8,15},{9,14},{10,... | collective-permute-start | bytes 442376 | tf_op jit(solution)/shard_map/ppermute | solution.py:351
  97.5 4.1 %experts_first.1 = (bf16[96,768]{1,0:T(8,128)(2,1)S(1)}, bf16[96,768]{1,0:T(8,128)(2,1)S(1)}, bf16[96,768]{1,0:T(8,128)(2,1)S(1)}, bf16[96,768]{1,0:T(8,128)(2,1)S(1)}) custom-call(bf16[96,768]{1,0:T(8,128)(2,1)S(1)} %get-tuple-element.89.refs_0_, bf16[96,768]{1,0:T(8,128)(2,1)S(1)} %collective-permute-done.15.refs_1_, ...), custom_call_target="tpu_custom_call" | custom-call | flops 5750000128 | tf_op jit(solution)/shard_map/experts_first/pallas_call | solution.py:304
  101.6 2.7 %collective-permute-done.19.refs_1_ = bf16[96,768]{1,0:T(8,128)(2,1)S(1)} collective-permute-done((bf16[96,768]{1,0:T(8,128)(2,1)S(1)}, bf16[96,768]{1,0:T(8,128)(2,1)S(1)}, u32[]{:S(2)}, u32[]{:S(2)}) %collective-permute-start.19) | collective-permute-done | bytes 147488 | tf_op jit(solution)/shard_map/ppermute | solution.py:351
  104.3 2.0 %collective-permute-done.20.refs_2_ = bf16[96,768]{1,0:T(8,128)(2,1)S(1)} collective-permute-done((bf16[96,768]{1,0:T(8,128)(2,1)S(1)}, bf16[96,768]{1,0:T(8,128)(2,1)S(1)}, u32[]{:S(2)}, u32[]{:S(2)}) %collective-permute-start.20) | collective-permute-done | bytes 147488 | tf_op jit(solution)/shard_map/ppermute | solution.py:351
  106.6 1.0 collective-permute-start.22
  108.1 1.4 %collective-permute-start.24 = (bf16[96,768]{1,0:T(8,128)(2,1)S(1)}, bf16[96,768]{1,0:T(8,128)(2,1)S(1)}, u32[]{:S(2)}, u32[]{:S(2)}) collective-permute-start(bf16[96,768]{1,0:T(8,128)(2,1)S(1)} %get-tuple-element.104), channel_id=1, source_target_pairs={{0,3},{1,2},{2,1},{3,0},{4,7},{5,6},{6,5},{7,4},{8,11},{9,10},{10,... | collective-permute-start | bytes 442376 | tf_op jit(solution)/shard_map/ppermute | solution.py:351
  109.6 4.1 %experts_second.1 = (bf16[96,768]{1,0:T(8,128)(2,1)S(1)}, bf16[96,768]{1,0:T(8,128)(2,1)S(1)}, bf16[96,768]{1,0:T(8,128)(2,1)S(1)}, bf16[96,768]{1,0:T(8,128)(2,1)S(1)}) custom-call(bf16[96,768]{1,0:T(8,128)(2,1)S(1)} %collective-permute-done.18.refs_0_, bf16[96,768]{1,0:T(8,128)(2,1)S(1)} %collective-permute-done.19.refs_1_, ...), custom_call_target="tpu_custom_call" | custom-call | flops 5750000128 | tf_op jit(solution)/shard_map/experts_second/pallas_call | solution.py:304
  113.7 2.2 %collective-permute-start.25 = (bf16[96,768]{1,0:T(8,128)(2,1)S(1)}, bf16[96,768]{1,0:T(8,128)(2,1)S(1)}, u32[]{:S(2)}, u32[]{:S(2)}) collective-permute-start(bf16[96,768]{1,0:T(8,128)(2,1)S(1)} %get-tuple-element.109), channel_id=1, source_target_pairs={{0,2},{1,3},{2,0},{3,1},{4,6},{5,7},{6,4},{7,5},{8,10},{9,11},{10,... | collective-permute-start | bytes 442376 | tf_op jit(solution)/shard_map/ppermute | solution.py:351
  115.9 2.3 %collective-permute-start.26 = (bf16[96,768]{1,0:T(8,128)(2,1)S(1)}, bf16[96,768]{1,0:T(8,128)(2,1)S(1)}, u32[]{:S(2)}, u32[]{:S(2)}) collective-permute-start(bf16[96,768]{1,0:T(8,128)(2,1)S(1)} %get-tuple-element.110), channel_id=1, source_target_pairs={{0,6},{1,7},{2,4},{3,5},{4,2},{5,3},{6,0},{7,1},{8,14},{9,15},{10,... | collective-permute-start | bytes 442376 | tf_op jit(solution)/shard_map/ppermute | solution.py:351
  118.3 1.0 collective-permute-start.27
  119.3 2.1 %collective-permute-start.28 = (bf16[96,768]{1,0:T(8,128)(2,1)S(1)}, bf16[96,768]{1,0:T(8,128)(2,1)S(1)}, u32[]{:S(2)}, u32[]{:S(2)}) collective-permute-start(bf16[96,768]{1,0:T(8,128)(2,1)S(1)} %get-tuple-element.112), channel_id=1, source_target_pairs={{0,7},{1,6},{2,5},{3,4},{4,3},{5,2},{6,1},{7,0},{8,15},{9,14},{10,... | collective-permute-start | bytes 442376 | tf_op jit(solution)/shard_map/ppermute | solution.py:351
  122.0 3.4 %collective-permute-done.26.refs_4_ = bf16[96,768]{1,0:T(8,128)(2,1)S(1)} collective-permute-done((bf16[96,768]{1,0:T(8,128)(2,1)S(1)}, bf16[96,768]{1,0:T(8,128)(2,1)S(1)}, u32[]{:S(2)}, u32[]{:S(2)}) %collective-permute-start.26) | collective-permute-done | bytes 147488 | tf_op jit(solution)/shard_map/ppermute | solution.py:351
  125.4 2.2 %collective-permute-done.27.refs_5_ = bf16[96,768]{1,0:T(8,128)(2,1)S(1)} collective-permute-done((bf16[96,768]{1,0:T(8,128)(2,1)S(1)}, bf16[96,768]{1,0:T(8,128)(2,1)S(1)}, u32[]{:S(2)}, u32[]{:S(2)}) %collective-permute-start.27) | collective-permute-done | bytes 147488 | tf_op jit(solution)/shard_map/ppermute | solution.py:351
  128.3 1.2 mix_second.1
  (78 shorter events, 3.3 us)
Async XLA Ops:
  0.0 31.4 %collective-permute-start.4 = (bf16[512,768]{1,0:T(8,128)(2,1)}, bf16[512,768]{1,0:T(8,128)(2,1)S(1)}, u32[]{:S(2)}, u32[]{:S(2)}) collective-permute-start(bf16[512,768]{1,0:T(8,128)(2,1)} %refs_0_.5), channel_id=1, source_target_pairs={{0,32},{1,33},{2,34},{3,35},{4,36},{5,37},{6,38},{7,39},{8,40},{9,... | collective-permute-start | bytes 2359304 | tf_op jit(solution)/shard_map/ppermute | solution.py:56
  1.6 29.8 %collective-permute-start.5 = (bf16[512,768]{1,0:T(8,128)(2,1)}, bf16[512,768]{1,0:T(8,128)(2,1)S(1)}, u32[]{:S(2)}, u32[]{:S(2)}) collective-permute-start(bf16[512,768]{1,0:T(8,128)(2,1)} %refs_0_.5), channel_id=1, source_target_pairs={{0,96},{1,97},{2,98},{3,99},{4,100},{5,101},{6,102},{7,103},{8,104... | collective-permute-start | bytes 2359304 | tf_op jit(solution)/shard_map/ppermute | solution.py:56
  3.2 28.2 %collective-permute-start.6 = (bf16[512,768]{1,0:T(8,128)(2,1)}, bf16[512,768]{1,0:T(8,128)(2,1)S(1)}, u32[]{:S(2)}, u32[]{:S(2)}) collective-permute-start(bf16[512,768]{1,0:T(8,128)(2,1)} %refs_0_.5), channel_id=1, source_target_pairs={{0,20},{1,21},{2,22},{3,23},{4,16},{5,17},{6,18},{7,19},{8,28},{9,... | collective-permute-start | bytes 2359304 | tf_op jit(solution)/shard_map/ppermute | solution.py:56
  8.3 3.6 %collective-permute-start = (bf16[2,256,128]{2,1,0:T(8,128)(2,1)S(1)}, bf16[2,256,128]{2,1,0:T(8,128)(2,1)S(1)}, u32[]{:S(2)}, u32[]{:S(2)}) collective-permute-start(bf16[2,256,128]{2,1,0:T(8,128)(2,1)S(1)} %get-tuple-element.116), channel_id=1, source_target_pairs={{0,8},{8,16},{16,24},{24,32},{32,40},{40,48},{48,56},{56,64},{64,7... | collective-permute-start | bytes 393224 | tf_op jit(solution)/shard_map/ppermute | solution.py:343
  9.7 3.4 %collective-permute-start.1 = (bf16[2,256,128]{2,1,0:T(8,128)(2,1)S(1)}, bf16[2,256,128]{2,1,0:T(8,128)(2,1)S(1)}, u32[]{:S(2)}, u32[]{:S(2)}) collective-permute-start(bf16[2,256,128]{2,1,0:T(8,128)(2,1)S(1)} %get-tuple-element.115), channel_id=1, source_target_pairs={{8,0},{16,8},{24,16},{32,24},{40,32},{48,40},{56,48},{64,56},{72,6... | collective-permute-start | bytes 393224 | tf_op jit(solution)/shard_map/ppermute | solution.py:343
  13.1 6.2 %collective-permute-start.2 = (bf16[68,2,128]{2,1,0:T(2,128)(2,1)S(1)}, bf16[68,2,128]{2,1,0:T(2,128)(2,1)S(1)}, u32[]{:S(2)}, u32[]{:S(2)}) collective-permute-start(bf16[68,2,128]{2,1,0:T(2,128)(2,1)S(1)} %pad_maximum_fusion.1), channel_id=1, source_target_pairs={{1,0},{2,1},{3,2},{4,3},{5,4},{6,5},{7,6},{9,8},{10,9},{11,10},{12... | collective-permute-start | bytes 104456 | tf_op jit(solution)/shard_map/ppermute | solution.py:343
  14.5 6.2 %collective-permute-start.3 = (bf16[68,2,128]{2,1,0:T(2,128)(2,1)S(1)}, bf16[68,2,128]{2,1,0:T(2,128)(2,1)S(1)}, u32[]{:S(2)}, u32[]{:S(2)}) collective-permute-start(bf16[68,2,128]{2,1,0:T(2,128)(2,1)S(1)} %pad_maximum_fusion.2), channel_id=1, source_target_pairs={{0,1},{1,2},{2,3},{3,4},{4,5},{5,6},{6,7},{8,9},{9,10},{10,11},{11... | collective-permute-start | bytes 104456 | tf_op jit(solution)/shard_map/ppermute | solution.py:343
  31.4 39.2 %copy-start.1 = (bf16[512,768]{1,0:T(8,128)(2,1)S(1)}, bf16[512,768]{1,0:T(8,128)(2,1)}, u32[]{:S(2)}) copy-start(bf16[512,768]{1,0:T(8,128)(2,1)} %refs_0_.5) | copy-start | bytes 2359300
  31.4 29.6 %collective-permute-start.7 = (bf16[512,768]{1,0:T(8,128)(2,1)S(1)}, bf16[512,768]{1,0:T(8,128)(2,1)S(1)}, u32[]{:S(2)}, u32[]{:S(2)}) collective-permute-start(bf16[512,768]{1,0:T(8,128)(2,1)S(1)} %collective-permute-done.4.refs_1_), channel_id=1, source_target_pairs={{0,32},{1,33},{2,34},{3,35},{4,36},{5,37},{6,38},{7,39},{8,40},{9,... | collective-permute-start | bytes 2359304 | tf_op jit(solution)/shard_map/ppermute | solution.py:56
  44.3 21.2 %collective-permute-start.9 = (bf16[512,768]{1,0:T(8,128)(2,1)S(1)}, bf16[512,768]{1,0:T(8,128)(2,1)S(1)}, u32[]{:S(2)}, u32[]{:S(2)}) collective-permute-start(bf16[512,768]{1,0:T(8,128)(2,1)S(1)} %collective-permute-done.4.refs_1_), channel_id=1, source_target_pairs={{0,20},{1,21},{2,22},{3,23},{4,16},{5,17},{6,18},{7,19},{8,28},{9,... | collective-permute-start | bytes 2359304 | tf_op jit(solution)/shard_map/ppermute | solution.py:56
  44.3 21.2 %collective-permute-start.8 = (bf16[512,768]{1,0:T(8,128)(2,1)S(1)}, bf16[512,768]{1,0:T(8,128)(2,1)S(1)}, u32[]{:S(2)}, u32[]{:S(2)}) collective-permute-start(bf16[512,768]{1,0:T(8,128)(2,1)S(1)} %collective-permute-done.6.refs_4_), channel_id=1, source_target_pairs={{0,96},{1,97},{2,98},{3,99},{4,100},{5,101},{6,102},{7,103},{8,104... | collective-permute-start | bytes 2359304 | tf_op jit(solution)/shard_map/ppermute | solution.py:56
  56.9 15.9 %copy-start.3 = (bf16[768,3072]{1,0:T(8,128)(2,1)}, bf16[768,3072]{1,0:T(8,128)(2,1)S(1)}, u32[]{:S(2)}) copy-start(bf16[768,3072]{1,0:T(8,128)(2,1)S(1)} %get-tuple-element.93.refs_4_) | copy-start | bytes 14155780
  56.9 15.9 %copy-start.4 = (bf16[768,3072]{1,0:T(8,128)(2,1)}, bf16[768,3072]{1,0:T(8,128)(2,1)S(1)}, u32[]{:S(2)}) copy-start(bf16[768,3072]{1,0:T(8,128)(2,1)S(1)} %get-tuple-element.94.refs_5_) | copy-start | bytes 14155780
  56.9 15.9 %copy-start.5 = (bf16[3072,768]{1,0:T(8,128)(2,1)}, bf16[3072,768]{1,0:T(8,128)(2,1)S(1)}, u32[]{:S(2)}) copy-start(bf16[3072,768]{1,0:T(8,128)(2,1)S(1)} %get-tuple-element.95.refs_6_) | copy-start | bytes 14155780
  56.9 15.9 %copy-start.6 = (bf16[3072,768]{1,0:T(8,128)(2,1)}, bf16[3072,768]{1,0:T(8,128)(2,1)S(1)}, u32[]{:S(2)}) copy-start(bf16[3072,768]{1,0:T(8,128)(2,1)S(1)} %get-tuple-element.96.refs_7_) | copy-start | bytes 14155780
  56.9 15.9 %copy-start.7 = (bf16[8,256,512]{2,1,0:T(8,128)(2,1)}, bf16[8,256,512]{2,1,0:T(8,128)(2,1)S(1)}, u32[]{:S(2)}) copy-start(bf16[8,256,512]{2,1,0:T(8,128)(2,1)S(1)} %get-tuple-element.66.tokens) | copy-start | bytes 6291460
  56.9 16.8 %collective-permute-start.13 = (bf16[8,256,512]{2,1,0:T(8,128)(2,1)S(1)}, bf16[8,256,512]{2,1,0:T(8,128)(2,1)S(1)}, u32[]{:S(2)}, u32[]{:S(2)}) collective-permute-start(bf16[8,256,512]{2,1,0:T(8,128)(2,1)S(1)} %get-tuple-element.71), channel_id=1, source_target_pairs={{0,8},{1,9},{2,10},{3,11},{4,12},{5,13},{6,14},{7,15},{8,0},{9,1},... | collective-permute-start | bytes 6291464 | tf_op jit(solution)/shard_map/ppermute | solution.py:56
  65.6 11.2 %collective-permute-start.10 = (bf16[176,768]{1,0:T(8,128)(2,1)S(1)}, bf16[176,768]{1,0:T(8,128)(2,1)S(1)}, u32[]{:S(2)}, u32[]{:S(2)}) collective-permute-start(bf16[176,768]{1,0:T(8,128)(2,1)S(1)} %slice.41), channel_id=1, source_target_pairs={{0,96},{1,97},{2,98},{3,99},{4,100},{5,101},{6,102},{7,103},{8,104... | collective-permute-start | bytes 811016 | tf_op jit(solution)/shard_map/ppermute | solution.py:56
  66.7 10.3 %collective-permute-start.11 = (bf16[176,768]{1,0:T(8,128)(2,1)S(1)}, bf16[176,768]{1,0:T(8,128)(2,1)S(1)}, u32[]{:S(2)}, u32[]{:S(2)}) collective-permute-start(bf16[176,768]{1,0:T(8,128)(2,1)S(1)} %slice.42), channel_id=1, source_target_pairs={{0,32},{1,33},{2,34},{3,35},{4,36},{5,37},{6,38},{7,39},{8,40},{9,... | collective-permute-start | bytes 811016 | tf_op jit(solution)/shard_map/ppermute | solution.py:56
  68.0 8.8 %collective-permute-start.12 = (bf16[160,768]{1,0:T(8,128)(2,1)S(1)}, bf16[160,768]{1,0:T(8,128)(2,1)S(1)}, u32[]{:S(2)}, u32[]{:S(2)}) collective-permute-start(bf16[160,768]{1,0:T(8,128)(2,1)S(1)} %slice.43), channel_id=1, source_target_pairs={{0,20},{1,21},{2,22},{3,23},{4,16},{5,17},{6,18},{7,19},{8,28},{9,... | collective-permute-start | bytes 737288 | tf_op jit(solution)/shard_map/ppermute | solution.py:56
  72.8 0.9 copy-start.9
  75.9 2.1 %copy-start = (s32[1,1,256,1]{2,3,1,0:T(1,128)S(1)}, s32[1,1,256,1]{2,3,1,0:T(1,128)}, u32[]{:S(2)}) copy-start(s32[1,1,256,1]{2,3,1,0:T(1,128)} %param.13) | copy-start | bytes 3076
  75.9 2.3 %copy-start.10 = (f32[256,768]{1,0:T(8,128)S(1)}, f32[256,768]{1,0:T(8,128)}, u32[]{:S(2)}) copy-start(f32[256,768]{1,0:T(8,128)} %copy-done.9) | copy-start | bytes 2359300
  77.9 2.8 %collective-permute-start.14 = (bf16[256,768]{1,0:T(8,128)(2,1)S(1)}, bf16[256,768]{1,0:T(8,128)(2,1)S(1)}, u32[]{:S(2)}, u32[]{:S(2)}) collective-permute-start(bf16[256,768]{1,0:T(8,128)(2,1)S(1)} %embed_partner_last.1), channel_id=1, source_target_pairs={{0,8},{1,9},{2,10},{3,11},{4,12},{5,13},{6,14},{7,15},{8,0},{9,1},... | collective-permute-start | bytes 1179656 | tf_op jit(solution)/shard_map/ppermute | solution.py:56
  78.2 1.6 %copy-start.8 = (bf16[8,256,512]{2,1,0:T(8,128)(2,1)S(1)}, bf16[8,256,512]{2,1,0:T(8,128)(2,1)}, u32[]{:S(2)}) copy-start(bf16[8,256,512]{2,1,0:T(8,128)(2,1)} %copy-done.7) | copy-start | bytes 6291460
  79.8 1.0 copy-start.2
  79.8 17.6 %slice-start = ((s8[4718592]{0:T(1024)(128)(4,1)}), s8[4194304]{0:T(1024)(128)(4,1)S(1)}, s32[]{:S(2)}) async-start(s8[4718592]{0:T(1024)(128)(4,1)} %bitcast.18), calls=%async_computation | async-start | bytes 8388608
  79.8 17.6 %slice-start.2 = ((s8[4718592]{0:T(1024)(128)(4,1)}), s8[4194304]{0:T(1024)(128)(4,1)S(1)}, s32[]{:S(2)}) async-start(s8[4718592]{0:T(1024)(128)(4,1)} %bitcast.20), calls=%async_computation.2 | async-start | bytes 8388608
  79.8 17.6 %slice-start.4 = ((s8[4718592]{0:T(1024)(128)(4,1)}), s8[4194304]{0:T(1024)(128)(4,1)S(1)}, s32[]{:S(2)}) async-start(s8[4718592]{0:T(1024)(128)(4,1)} %bitcast.22), calls=%async_computation.4 | async-start | bytes 8388608
  79.8 17.6 %slice-start.6 = ((s8[4718592]{0:T(1024)(128)(4,1)}), s8[4194304]{0:T(1024)(128)(4,1)S(1)}, s32[]{:S(2)}) async-start(s8[4718592]{0:T(1024)(128)(4,1)} %bitcast.24), calls=%async_computation.6 | async-start | bytes 8388608
  80.7 16.7 %slice-start.1 = ((s8[4718592]{0:T(1024)(128)(4,1)}), s8[524288]{0:T(1024)(128)(4,1)S(1)}, s32[]{:S(2)}) async-start(s8[4718592]{0:T(1024)(128)(4,1)} %bitcast.18), calls=%async_computation.1 | async-start | bytes 1048576
  80.7 16.7 %slice-start.3 = ((s8[4718592]{0:T(1024)(128)(4,1)}), s8[524288]{0:T(1024)(128)(4,1)S(1)}, s32[]{:S(2)}) async-start(s8[4718592]{0:T(1024)(128)(4,1)} %bitcast.20), calls=%async_computation.3 | async-start | bytes 1048576
  80.7 16.7 %slice-start.5 = ((s8[4718592]{0:T(1024)(128)(4,1)}), s8[524288]{0:T(1024)(128)(4,1)S(1)}, s32[]{:S(2)}) async-start(s8[4718592]{0:T(1024)(128)(4,1)} %bitcast.22), calls=%async_computation.5 | async-start | bytes 1048576
  80.8 16.7 %slice-start.7 = ((s8[4718592]{0:T(1024)(128)(4,1)}), s8[524288]{0:T(1024)(128)(4,1)S(1)}, s32[]{:S(2)}) async-start(s8[4718592]{0:T(1024)(128)(4,1)} %bitcast.24), calls=%async_computation.7 | async-start | bytes 1048576
  82.1 6.3 %collective-permute-start.15 = (bf16[96,768]{1,0:T(8,128)(2,1)S(1)}, bf16[96,768]{1,0:T(8,128)(2,1)S(1)}, u32[]{:S(2)}, u32[]{:S(2)}) collective-permute-start(bf16[96,768]{1,0:T(8,128)(2,1)S(1)} %get-tuple-element.77), channel_id=1, source_target_pairs={{0,4},{1,5},{2,6},{3,7},{4,0},{5,1},{6,2},{7,3},{8,12},{9,13},{10,... | collective-permute-start | bytes 442376 | tf_op jit(solution)/shard_map/ppermute | solution.py:351
  82.2 6.3 %collective-permute-start.16 = (bf16[96,768]{1,0:T(8,128)(2,1)S(1)}, bf16[96,768]{1,0:T(8,128)(2,1)S(1)}, u32[]{:S(2)}, u32[]{:S(2)}) collective-permute-start(bf16[96,768]{1,0:T(8,128)(2,1)S(1)} %get-tuple-element.78), channel_id=1, source_target_pairs={{0,1},{1,0},{2,3},{3,2},{4,5},{5,4},{6,7},{7,6},{8,9},{9,8},{10,11... | collective-permute-start | bytes 442376 | tf_op jit(solution)/shard_map/ppermute | solution.py:351
  83.4 7.2 %collective-permute-start.17 = (bf16[96,768]{1,0:T(8,128)(2,1)S(1)}, bf16[96,768]{1,0:T(8,128)(2,1)S(1)}, u32[]{:S(2)}, u32[]{:S(2)}) collective-permute-start(bf16[96,768]{1,0:T(8,128)(2,1)S(1)} %get-tuple-element.79), channel_id=1, source_target_pairs={{0,3},{1,2},{2,1},{3,0},{4,7},{5,6},{6,5},{7,4},{8,11},{9,10},{10,... | collective-permute-start | bytes 442376 | tf_op jit(solution)/shard_map/ppermute | solution.py:351
  90.6 11.0 %collective-permute-start.18 = (bf16[96,768]{1,0:T(8,128)(2,1)S(1)}, bf16[96,768]{1,0:T(8,128)(2,1)S(1)}, u32[]{:S(2)}, u32[]{:S(2)}) collective-permute-start(bf16[96,768]{1,0:T(8,128)(2,1)S(1)} %get-tuple-element.85), channel_id=1, source_target_pairs={{0,2},{1,3},{2,0},{3,1},{4,6},{5,7},{6,4},{7,5},{8,10},{9,11},{10,... | collective-permute-start | bytes 442376 | tf_op jit(solution)/shard_map/ppermute | solution.py:351
  91.3 13.0 %collective-permute-start.19 = (bf16[96,768]{1,0:T(8,128)(2,1)S(1)}, bf16[96,768]{1,0:T(8,128)(2,1)S(1)}, u32[]{:S(2)}, u32[]{:S(2)}) collective-permute-start(bf16[96,768]{1,0:T(8,128)(2,1)S(1)} %get-tuple-element.86), channel_id=1, source_target_pairs={{0,6},{1,7},{2,4},{3,5},{4,2},{5,3},{6,0},{7,1},{8,14},{9,15},{10,... | collective-permute-start | bytes 442376 | tf_op jit(solution)/shard_map/ppermute | solution.py:351
  95.2 11.1 %collective-permute-start.20 = (bf16[96,768]{1,0:T(8,128)(2,1)S(1)}, bf16[96,768]{1,0:T(8,128)(2,1)S(1)}, u32[]{:S(2)}, u32[]{:S(2)}) collective-permute-start(bf16[96,768]{1,0:T(8,128)(2,1)S(1)} %get-tuple-element.87), channel_id=1, source_target_pairs={{0,5},{1,4},{2,7},{3,6},{4,1},{5,0},{6,3},{7,2},{8,13},{9,12},{10,... | collective-permute-start | bytes 442376 | tf_op jit(solution)/shard_map/ppermute | solution.py:351
  95.2 11.4 %collective-permute-start.21 = (bf16[96,768]{1,0:T(8,128)(2,1)S(1)}, bf16[96,768]{1,0:T(8,128)(2,1)S(1)}, u32[]{:S(2)}, u32[]{:S(2)}) collective-permute-start(bf16[96,768]{1,0:T(8,128)(2,1)S(1)} %get-tuple-element.88), channel_id=1, source_target_pairs={{0,7},{1,6},{2,5},{3,4},{4,3},{5,2},{6,1},{7,0},{8,15},{9,14},{10,... | collective-permute-start | bytes 442376 | tf_op jit(solution)/shard_map/ppermute | solution.py:351
  106.6 11.7 %collective-permute-start.22 = (bf16[96,768]{1,0:T(8,128)(2,1)S(1)}, bf16[96,768]{1,0:T(8,128)(2,1)S(1)}, u32[]{:S(2)}, u32[]{:S(2)}) collective-permute-start(bf16[96,768]{1,0:T(8,128)(2,1)S(1)} %get-tuple-element.102), channel_id=1, source_target_pairs={{0,4},{1,5},{2,6},{3,7},{4,0},{5,1},{6,2},{7,3},{8,12},{9,13},{10,... | collective-permute-start | bytes 442376 | tf_op jit(solution)/shard_map/ppermute | solution.py:351
  107.6 11.7 %collective-permute-start.23 = (bf16[96,768]{1,0:T(8,128)(2,1)S(1)}, bf16[96,768]{1,0:T(8,128)(2,1)S(1)}, u32[]{:S(2)}, u32[]{:S(2)}) collective-permute-start(bf16[96,768]{1,0:T(8,128)(2,1)S(1)} %get-tuple-element.103), channel_id=1, source_target_pairs={{0,1},{1,0},{2,3},{3,2},{4,5},{5,4},{6,7},{7,6},{8,9},{9,8},{10,11... | collective-permute-start | bytes 442376 | tf_op jit(solution)/shard_map/ppermute | solution.py:351
  108.1 13.3 %collective-permute-start.24 = (bf16[96,768]{1,0:T(8,128)(2,1)S(1)}, bf16[96,768]{1,0:T(8,128)(2,1)S(1)}, u32[]{:S(2)}, u32[]{:S(2)}) collective-permute-start(bf16[96,768]{1,0:T(8,128)(2,1)S(1)} %get-tuple-element.104), channel_id=1, source_target_pairs={{0,3},{1,2},{2,1},{3,0},{4,7},{5,6},{6,5},{7,4},{8,11},{9,10},{10,... | collective-permute-start | bytes 442376 | tf_op jit(solution)/shard_map/ppermute | solution.py:351
  113.7 8.3 %collective-permute-start.25 = (bf16[96,768]{1,0:T(8,128)(2,1)S(1)}, bf16[96,768]{1,0:T(8,128)(2,1)S(1)}, u32[]{:S(2)}, u32[]{:S(2)}) collective-permute-start(bf16[96,768]{1,0:T(8,128)(2,1)S(1)} %get-tuple-element.109), channel_id=1, source_target_pairs={{0,2},{1,3},{2,0},{3,1},{4,6},{5,7},{6,4},{7,5},{8,10},{9,11},{10,... | collective-permute-start | bytes 442376 | tf_op jit(solution)/shard_map/ppermute | solution.py:351
  115.9 9.5 %collective-permute-start.26 = (bf16[96,768]{1,0:T(8,128)(2,1)S(1)}, bf16[96,768]{1,0:T(8,128)(2,1)S(1)}, u32[]{:S(2)}, u32[]{:S(2)}) collective-permute-start(bf16[96,768]{1,0:T(8,128)(2,1)S(1)} %get-tuple-element.110), channel_id=1, source_target_pairs={{0,6},{1,7},{2,4},{3,5},{4,2},{5,3},{6,0},{7,1},{8,14},{9,15},{10,... | collective-permute-start | bytes 442376 | tf_op jit(solution)/shard_map/ppermute | solution.py:351
  118.3 9.4 %collective-permute-start.27 = (bf16[96,768]{1,0:T(8,128)(2,1)S(1)}, bf16[96,768]{1,0:T(8,128)(2,1)S(1)}, u32[]{:S(2)}, u32[]{:S(2)}) collective-permute-start(bf16[96,768]{1,0:T(8,128)(2,1)S(1)} %get-tuple-element.111), channel_id=1, source_target_pairs={{0,5},{1,4},{2,7},{3,6},{4,1},{5,0},{6,3},{7,2},{8,13},{9,12},{10,... | collective-permute-start | bytes 442376 | tf_op jit(solution)/shard_map/ppermute | solution.py:351
  119.3 9.0 %collective-permute-start.28 = (bf16[96,768]{1,0:T(8,128)(2,1)S(1)}, bf16[96,768]{1,0:T(8,128)(2,1)S(1)}, u32[]{:S(2)}, u32[]{:S(2)}) collective-permute-start(bf16[96,768]{1,0:T(8,128)(2,1)S(1)} %get-tuple-element.112), channel_id=1, source_target_pairs={{0,7},{1,6},{2,5},{3,4},{4,3},{5,2},{6,1},{7,0},{8,15},{9,14},{10,... | collective-permute-start | bytes 442376 | tf_op jit(solution)/shard_map/ppermute | solution.py:351

commit v6 on v5

--- a/solution.py
+++ b/solution.py
@@ -11,7 +11,7 @@
 WIDE = 272
 DIM, FF, CAP, TOK = 768, 3072, 48, 256
 PAIR = 2 * CAP
-STEPS, BAND = 2, 2
+BAND = 2
 F32, BF16 = jnp.float32, jnp.bfloat16
 ANY = pl.BlockSpec(memory_space=pl.ANY)
 VMEM = pl.BlockSpec(memory_space=pltpu.VMEM)
@@ -65,61 +65,59 @@
             target[rows, pl.ds(dx * 256 + CH, CH)] = source[j - 1, dx] if j > 0 else zero
 
 
-def pair_conv(source, weights, pair):
-    taps = jnp.concatenate([source[2 * pair + j] for j in range(4)], axis=1)
+def pair_conv(source, weights, start):
+    taps = jnp.concatenate([source[start + j] for j in range(4)], axis=1)
     parts = jnp.dot(taps, weights[...], preferred_element_type=F32)
     left = pltpu.roll(parts[:, 0:256], 1, 0)
     right = pltpu.roll(parts[:, 512:768], WIDE - 1, 0)
     return left + parts[:, 256:512] + right
 
 
-def conv_kernel(start, fetched, place, scene, top, bottom, strip, first, second, *refs):
-    sources, refs = refs[:fetched], refs[-11 - 2 * fetched :]
-    keep, other, targets, refs = refs[0], refs[1], refs[2 : 2 + 2 * fetched], refs[2 + 2 * fetched :]
+def conv_kernel(outer, fetched, place, scene, strip, *refs):
+    (top, bottom), refs = (refs[:2], refs[2:]) if outer else ((None, None), refs)
+    first, second, *sources = refs[: 2 + fetched]
+    keep, other, *refs = refs[-11 - 2 * fetched :]
+    targets, refs = refs[: 2 * fetched], refs[2 * fetched :]
     block, hidden, rows, w1, w2, first_in, second_in, sems, weight_sems = refs
     step = pl.program_id(0)
-    base = start * 8 * BAND - 2
-    height = 8 * BAND * STEPS + 4
-    chunks = []
-    for k in range(STEPS):
-        hi = 8 * BAND * (k + 1) + 4
-        lo = 0 if k == 0 else hi - 8 * BAND
-        a, b = max(lo + base, 0), min(hi + base, ROWS)
-        copies = [(scene.at[a:b], block.at[a - base : b - base, 0:COLS])]
-        if lo + base < 0:
-            copies.append((top, block.at[0:2, 0:COLS]))
-        if hi + base > ROWS:
-            copies.append((bottom, block.at[height - 2 : height, 0:COLS]))
-        copies.append((strip.at[lo + base + 2 : hi + base + 2], block.at[lo:hi, COLS:WIDE]))
-        chunks.append(
-            [pltpu.make_async_copy(s, d, sems.at[k, n]) for n, (s, d) in enumerate(copies)]
-        )
+
+    def arrive(a, b, at, k):
+        return [
+            pltpu.make_async_copy(scene.at[a:b], block.at[at : at + b - a, 0:COLS], sems.at[k, 0]),
+            pltpu.make_async_copy(
+                strip.at[a:b], block.at[at : at + b - a, COLS:WIDE], sems.at[k, 1]
+            ),
+        ]
+
+    if outer:
+        chunks = [arrive(0, 18, 2, 0), arrive(ROWS - 18, ROWS, 20, 1)]
+        chunks[0].append(pltpu.make_async_copy(top, block.at[0:2], sems.at[0, 2]))
+        chunks[1].append(pltpu.make_async_copy(bottom, block.at[38:40], sems.at[1, 2]))
+    else:
+        chunks = [arrive(14, 34, 0, 0), arrive(34, 50, 20, 1)]
+    weights = [
+        pltpu.make_async_copy(first, first_in, weight_sems.at[0]),
+        pltpu.make_async_copy(second, second_in, weight_sems.at[1]),
+    ]
     fetches = [
         pltpu.make_async_copy(sources[n // 2].at[n % 2], target, weight_sems.at[2 + n])
         for n, target in enumerate(targets)
-    ]
-    weights = [
-        pltpu.make_async_copy(first, first_in, weight_sems.at[0]),
-        pltpu.make_async_copy(second, second_in, weight_sems.at[1]),
     ]
     place_row, place_col, core = place[0], place[1], place[2]
     tail = lax.broadcasted_iota(jnp.int32, (16, 256), 0)
     cut = ((place_col == 0) & (tail >= 8)) | ((place_col == 7) & (tail < 8))
     edge = jnp.where(cut, 0.0, 1.0).astype(F32)
 
-    def conv_first(pair):
-        value = jnp.maximum(pair_conv(block, w1, pair), 0.0)
+    def conv_first(start, target):
+        value = jnp.maximum(pair_conv(block, w1, start), 0.0)
         body, ends = value[0:COLS].astype(BF16), (value[COLS:WIDE] * edge).astype(BF16)
         for i in range(2):
-            hidden[2 * pair + i, 0:COLS] = body[:, i * CH : (i + 1) * CH]
-            hidden[2 * pair + i, COLS:WIDE] = ends[:, i * CH : (i + 1) * CH]
+            hidden[target + i, 0:COLS] = body[:, i * CH : (i + 1) * CH]
+            hidden[target + i, COLS:WIDE] = ends[:, i * CH : (i + 1) * CH]
 
     @pl.when(step == 0)
     def _():
-        for chunk in (chunks[0], weights, chunks[1]):
-            for copy in chunk:
-                copy.start()
-        for copy in fetches:
+        for copy in [*chunks[0], *weights, *chunks[1], *fetches]:
             copy.start()
         for copy in weights:
             copy.wait()
@@ -127,35 +125,31 @@
         pair_weights(second_in, w2)
         for copy in chunks[0]:
             copy.wait()
-        conv_first(0)
-        if start == 0:
-
-            @pl.when(place_row == 0)
-            def _():
-                hidden[0] = jnp.zeros((WIDE, CH), BF16)
-
-    for k in range(1, STEPS):
-
-        @pl.when(step == k)
-        def _(k=k):
-            for copy in chunks[k]:
-                copy.wait()
-            for copy in chunks[k + 1] if k + 1 < STEPS else ():
-                copy.start()
+        if not outer:
+            conv_first(0, 0)
+
+    @pl.when(step == 1)
+    def _():
+        for copy in chunks[1]:
+            copy.wait()
+
+    block_at, hidden_at = (20 * step, 18 * step) if outer else (16 * step, 16 * step)
+    for i in range(0 if outer else 1, 4 * BAND + 1):
+        conv_first(block_at + 2 * i, hidden_at + 2 * i)
+    if outer:
+
+        @pl.when((step == 0) & (place_row == 0))
+        def _():
+            hidden[0] = jnp.zeros((WIDE, CH), BF16)
+
+        @pl.when((step == 1) & (place_row == 15))
+        def _():
+            hidden[35] = jnp.zeros((WIDE, CH), BF16)
 
     for i in range(4 * BAND):
-        conv_first(4 * BAND * step + 1 + i)
-    if base + height > ROWS:
-
-        @pl.when((step == STEPS - 1) & (place_row == 15))
-        def _():
-            hidden[height - 3] = jnp.zeros((WIDE, CH), BF16)
-
-    for i in range(4 * BAND):
-        pair = 4 * BAND * step + i
-        value = pair_conv(hidden, w2, pair)[0:COLS]
+        value = pair_conv(hidden, w2, hidden_at + 2 * i)[0:COLS]
         for n in range(2):
-            cells = block[2 * pair + 2 + n, 0:COLS].astype(F32)
+            cells = block[block_at + 2 * i + 2 + n, 0:COLS].astype(F32)
             rows[pl.ds((2 * i + n) * COLS, COLS), :] = value[:, n * CH : (n + 1) * CH] + cells
     for line in range(8 * BAND):
         dy, at = line % 8, pl.ds(line // 8 * 32, 32)
@@ -165,43 +159,45 @@
             lanes = pl.ds(j * CH, CH)
             keep[dy, at, lanes] = jnp.where(core == 0, low, high).astype(BF16)
             other[dy, at, lanes] = jnp.where(core == 0, high, low).astype(BF16)
-
-
     if fetches:
 
-        @pl.when(step == STEPS - 1)
+        @pl.when(step == 1)
         def _():
             for copy in fetches:
                 copy.wait()
 
 
-def conv_call(start, args, fetch=(), given=()):
+def conv_call(place, scene, strip, halo, weights, fetch=(), given=()):
+    outer = bool(halo)
     shape = jax.ShapeDtypeStruct((8, TOK, 512), BF16)
     halves = [pltpu.VMEM(a.shape[1:], a.dtype) for a in fetch for _ in range(2)]
-    height = 8 * BAND * STEPS
+    bands = pl.BlockSpec((8, 32 * BAND, 512), lambda i: (0, 3 * i if outer else 1 + i, 0))
+    before = 5 + len(halo) + len(fetch)
     return pl.pallas_call(
-        functools.partial(conv_kernel, start, len(fetch)),
-        grid=(STEPS,),
-        in_specs=[SMEM, HBM, ANY, ANY, ANY, HBM, HBM] + [HBM] * len(fetch) + [ANY] * len(given),
-        out_specs=[pl.BlockSpec((8, 32 * BAND, 512), lambda i: (0, start + i, 0))] * 2
-        + [ANY] * len(halves),
+        functools.partial(conv_kernel, outer, len(fetch)),
+        grid=(2,),
+        in_specs=[SMEM, HBM]
+        + [ANY] * (1 + len(halo))
+        + [HBM] * (2 + len(fetch))
+        + [ANY] * len(given),
+        out_specs=[bands, bands] + [ANY] * len(halves),
         out_shape=[shape, shape] + halves,
         scratch_shapes=[
-            pltpu.VMEM((height + 4, WIDE, CH), BF16),
-            pltpu.VMEM((height + 2, WIDE, CH), BF16),
+            pltpu.VMEM((40 if outer else 36, WIDE, CH), BF16),
+            pltpu.VMEM((36 if outer else 34, WIDE, CH), BF16),
             pltpu.VMEM((8 * BAND * COLS, CH), F32),
             pltpu.VMEM((512, 768), BF16),
             pltpu.VMEM((512, 768), BF16),
             pltpu.VMEM((3, 3, CH, CH), BF16),
             pltpu.VMEM((3, 3, CH, CH), BF16),
-            pltpu.SemaphoreType.DMA((STEPS, 4)),
+            pltpu.SemaphoreType.DMA((2, 3)),
             pltpu.SemaphoreType.DMA((6,)),
         ],
-        input_output_aliases={7 + len(fetch) + n: n for n in range(len(given))},
+        input_output_aliases={before + n: n for n in range(len(given))},
         compiler_params=params(28),
         cost_estimate=cost(11),
-        name=f"convs_{start}",
-    )(*args, *fetch, *given)
+        name="convs_outer" if outer else "convs_inner",
+    )(place, scene, strip, *halo, *weights, *fetch, *given)
 
 
 def embed_kernel(layout, order, tokens, *refs):
@@ -239,7 +235,7 @@
     )(order, tokens, *arrays, *sums)
 
 
-def route_kernel(where, own, came, router, ids_row, ids_col, embedded, gate, place, *outs):
+def route_kernel(where, own, came, router, ids_row, embedded, gate, place, *outs):
     value = (own[...] + came[...].astype(F32)).astype(BF16)
     embedded[...] = value
     wide = value.astype(F32)
@@ -250,14 +246,19 @@
     )
     across = lax.broadcasted_iota(jnp.int32, (TOK, TOK), 1)
     down = lax.broadcasted_iota(jnp.int32, (TOK, TOK), 0)
-    col, row, me = ids_col[...], ids_row[...], where[1]
-    hot = jnp.where(col == lax.broadcasted_iota(jnp.int32, (TOK, 16), 1), 1.0, 0.0)
+    row, me = ids_row[...], where[1]
+    expert = lax.broadcasted_iota(jnp.int32, (16, TOK), 0)
+    hot_t = jnp.where(row == expert, 1.0, 0.0)
+    same = jnp.where(across == down, 1.0, 0.0).astype(BF16)
+    turn = (((1,), (1,)), ((), ()))
+    hot = lax.dot_general(same, hot_t.astype(BF16), turn, preferred_element_type=F32)
     gate[...] = jax.nn.sigmoid(jnp.sum(scores * hot, axis=-1, keepdims=True))
     earlier = jnp.where(across < down, 1.0, 0.0).astype(BF16)
     counts = jnp.dot(earlier, hot.astype(BF16), preferred_element_type=F32)
-    rank = jnp.sum(counts * hot, axis=-1, keepdims=True).astype(jnp.int32)
-    place[...] = ((col >> 1) ^ me) * PAIR + (col & 1) * CAP + rank
-    hot_t = jnp.where(row == lax.broadcasted_iota(jnp.int32, (16, TOK), 0), 1.0, 0.0)
+    number = lax.broadcasted_iota(jnp.int32, (TOK, 16), 1)
+    start = ((number >> 1) ^ me) * PAIR + (number & 1) * CAP
+    slots = (counts + start.astype(F32)) * hot
+    place[...] = jnp.sum(slots, axis=-1, keepdims=True).astype(jnp.int32)
     later = jnp.where(down < across, 1.0, 0.0).astype(BF16)
     counts_t = jnp.dot(hot_t.astype(BF16), later, preferred_element_type=F32)
     rank_t = jnp.sum(counts_t * hot_t, axis=0, keepdims=True).astype(jnp.int32)
@@ -274,7 +275,7 @@
     shapes += [((PAIR, DIM), BF16)] * 8
     return pl.pallas_call(
         route_kernel,
-        in_specs=[SMEM] + [VMEM] * 5,
+        in_specs=[SMEM] + [VMEM] * 4,
         out_specs=[VMEM] * 11,
         out_shape=[jax.ShapeDtypeStruct(*shape) for shape in shapes],
         compiler_params=params(16),
@@ -343,10 +344,6 @@
     return lax.ppermute(value, axis, pairs if ahead else [(j, i) for i, j in pairs])
 
 
-def columns(top, scene, bottom, first):
-    return jnp.concatenate([a[:, first : first + 2] for a in (top, scene, bottom)], axis=0)
-
-
 def exchange(arrays, steps):
     return [lax.ppermute(arrays[k], "col", [(i, i ^ k) for i in range(8)]) for k in steps]
 
@@ -358,22 +355,21 @@
     x, high, core = row >> 2, (row >> 1) & 1, row & 1
     place = jnp.stack([row, col, core]).astype(jnp.int32)
 
-    top = neighbours(scene[ROWS - 2 :], "row", True)
-    bottom = neighbours(scene[:2], "row", False)
     w = embed_weight
     w_minus, w_plus, w_high = send(w, dx=1), send(w, dx=-1), send(w, dh=1, dl=1)
-    left = neighbours(columns(top, scene, bottom, COLS - 2), "col", True)
-    right = neighbours(columns(top, scene, bottom, 0), "col", False)
-    strip = jnp.concatenate([right, jnp.zeros((ROWS + 4, 12, CH), BF16), left], axis=1)
-    conv_args = (place, in_hbm(scene), top, bottom, strip, in_hbm(conv_first), in_hbm(conv_second))
-    keep, other = conv_call(0, conv_args)
-    keep, other, w_minus, w_plus, w_high = lax.optimization_barrier(
-        (keep, other, w_minus, w_plus, w_high)
-    )
+    left = neighbours(scene[:, COLS - 2 :], "col", True)
+    right = neighbours(scene[:, :2], "col", False)
+    strip = jnp.concatenate([right, jnp.zeros((ROWS, 12, CH), BF16), left], axis=1)
+    lines = [jnp.concatenate([scene[a:b], strip[a:b]], axis=1) for a, b in ((62, 64), (0, 2))]
+    halo = neighbours(lines[0], "row", True), neighbours(lines[1], "row", False)
+    kernels, cells = (in_hbm(conv_first), in_hbm(conv_second)), in_hbm(scene)
+    given = conv_call(place, cells, strip, (), kernels)
+    *given, w_minus, w_plus, w_high = lax.optimization_barrier((*given, w_minus, w_plus, w_high))
     w_far, w_high_plus = send(w_minus, dx=1), send(w_high, dx=-1)
     w_high_minus = send(w_minus, dh=1, dl=1)
+    fetch = in_hbm(expert_up), in_hbm(expert_down)
     keep, other, up0, up1, down0, down1 = conv_call(
-        STEPS, conv_args, (in_hbm(expert_up), in_hbm(expert_down)), (keep, other)
+        place, cells, strip, halo, kernels, fetch, given
     )
     came = send(other, dc=1)
     keep, w_far, w_high_plus, w_high_minus = lax.optimization_barrier(
@@ -395,11 +391,10 @@
     came = send(partner, dc=1)
     own = embed_call("embed_own_last", order, keep, [(7, last)], [own])
     embedded, gate, slots, *outs = route_call(
-        place, own, came, router_weight.T, expert_ids.reshape(1, TOK), expert_ids.reshape(TOK, 1)
+        place, own, came, router_weight.T, expert_ids.reshape(1, TOK)
     )
     first, second, weights = (4, 1, 3), (2, 6, 5, 7), (up0, up1, down0, down1)
-    in_first, outs = lax.optimization_barrier((exchange(outs, first), outs))
-    in_second = exchange(outs, second)
+    in_first, in_second = exchange(outs, first), exchange(outs, second)
     back_first = expert_call("experts_first", [outs[0], *in_first], weights)
     in_second, back_first = lax.optimization_barrier((in_second, back_first))
     back = dict(zip((0, *first), back_first))

time: 130 us -> 120 us (0.923)
  starting transfers between devices: 59.9 us -> 54.2 us
  local copies, waits for them, and re-layouts: 4.94 us -> 2.26 us
  waiting for transfers between devices: 25 us -> 23.7 us
    ppermute x11, starting transfers between devices: 31 us -> 25.1 us  [send(): return lax.ppermute(value, ('row', 'col'), hop(**step))]
    ppermute x11, waiting for transfers between devices: 5.62 us -> 10.5 us  [send(): return lax.ppermute(value, ('row', 'col'), hop(**step))]
    ppermute x14, waiting for transfers between devices: 16.9 us -> 12.8 us  [exchange(): lax.ppermute(arrays[k], 'col', [(i, i ^ k) for i in range(8)])]
    unnamed x38 -> x6, local copies, waits for them, and re-layouts: 2.56 us -> 0.02 us
    ppermute x4, waiting for transfers between devices: 2.41 us -> 0.34 us  [neighbours(): lax.ppermute(value, axis, pairs if ahead else [(j, i) for i, j in pairs])]
  transfers between devices with their start and end apart: 29 -> 29, of which waited for: 15 -> 14; matrix products, arithmetic and copies ran while one was open for 2% -> 2% of each run, Pallas kernels for 27% -> 30%
where the time goes in v6:
time: 120 us
  starting transfers between devices  54.2 us (45%)
  Pallas kernels  39.1 us (33%)
  waiting for transfers between devices  23.7 us (20%)
  local copies, waits for them, and re-layouts  2.26 us (2%)
    ppermute x11, starting transfers between devices, send(): return lax.ppermute(value, ('row', 'col'), hop(**step))  25.1 us
    pallas_call x2, Pallas kernels, conv_call(): pl.pallas_call(functools.partial(conv_kernel, outer, len(fetch)), grid=(2...  21.7 us
    ppermute x14, starting transfers between devices, exchange(): lax.ppermute(arrays[k], 'col', [(i, i ^ k) for i in range(8)])  20.7 us
    ppermute x14, waiting for transfers between devices, exchange(): lax.ppermute(arrays[k], 'col', [(i, i ^ k) for i in range(8)])  12.8 us
    ppermute x11, waiting for transfers between devices, send(): return lax.ppermute(value, ('row', 'col'), hop(**step))  10.5 us
    ppermute x4, starting transfers between devices, neighbours(): lax.ppermute(value, axis, pairs if ahead else [(j, i) for i, j in pairs])  8.43 us
    pallas_call x2, Pallas kernels, expert_call(): pl.pallas_call(expert_kernel, in_specs=[VMEM] * (count + 4), out_specs=[V...  8.23 us
    pallas_call x4, Pallas kernels, embed_call(): pl.pallas_call(functools.partial(embed_kernel, layout), in_specs=[SMEM] +...  6.12 us
  transfers between devices with their start and end apart: 29, of which 14 were waited for; matrix products, arithmetic and copies ran while one was open for 2% of the time, Pallas kernels for 30%

profile of v6, /device:TPU:0, one launch (start us, length us, event | category | flops | bytes accessed | tf_op | source)
XLA Modules:
  0.0 119.8 jit_solution(3099169627030466486)
XLA Ops:
  0.0 1.6 %collective-permute-start.4 = (bf16[512,768]{1,0:T(8,128)(2,1)}, bf16[512,768]{1,0:T(8,128)(2,1)S(1)}, u32[]{:S(2)}, u32[]{:S(2)}) collective-permute-start(bf16[512,768]{1,0:T(8,128)(2,1)} %refs_0_.5), channel_id=1, source_target_pairs={{0,32},{1,33},{2,34},{3,35},{4,36},{5,37},{6,38},{7,39},{8,40},{9,... | collective-permute-start | bytes 2359304 | tf_op jit(solution)/shard_map/ppermute | solution.py:56
  1.6 1.7 %collective-permute-start.5 = (bf16[512,768]{1,0:T(8,128)(2,1)}, bf16[512,768]{1,0:T(8,128)(2,1)S(1)}, u32[]{:S(2)}, u32[]{:S(2)}) collective-permute-start(bf16[512,768]{1,0:T(8,128)(2,1)} %refs_0_.5), channel_id=1, source_target_pairs={{0,96},{1,97},{2,98},{3,99},{4,100},{5,101},{6,102},{7,103},{8,104... | collective-permute-start | bytes 2359304 | tf_op jit(solution)/shard_map/ppermute | solution.py:56
  3.2 4.1 %collective-permute-start.6 = (bf16[512,768]{1,0:T(8,128)(2,1)}, bf16[512,768]{1,0:T(8,128)(2,1)S(1)}, u32[]{:S(2)}, u32[]{:S(2)}) collective-permute-start(bf16[512,768]{1,0:T(8,128)(2,1)} %refs_0_.5), channel_id=1, source_target_pairs={{0,20},{1,21},{2,22},{3,23},{4,16},{5,17},{6,18},{7,19},{8,28},{9,... | collective-permute-start | bytes 2359304 | tf_op jit(solution)/shard_map/ppermute | solution.py:56
  7.4 1.0 fusion.1
  8.4 1.3 %collective-permute-start = (bf16[64,2,128]{2,1,0:T(2,128)(2,1)S(1)}, bf16[64,2,128]{2,1,0:T(2,128)(2,1)S(1)}, u32[]{:S(2)}, u32[]{:S(2)}) collective-permute-start(bf16[64,2,128]{2,1,0:T(2,128)(2,1)S(1)} %get-tuple-element.99), channel_id=1, source_target_pairs={{1,0},{2,1},{3,2},{4,3},{5,4},{6,5},{7,6},{9,8},{10,9},{11,10},{12... | collective-permute-start | bytes 98312 | tf_op jit(solution)/shard_map/ppermute | solution.py:344
  9.7 4.5 %collective-permute-start.1 = (bf16[64,2,128]{2,1,0:T(2,128)(2,1)S(1)}, bf16[64,2,128]{2,1,0:T(2,128)(2,1)S(1)}, u32[]{:S(2)}, u32[]{:S(2)}) collective-permute-start(bf16[64,2,128]{2,1,0:T(2,128)(2,1)S(1)} %get-tuple-element.100), channel_id=1, source_target_pairs={{0,1},{1,2},{2,3},{3,4},{4,5},{5,6},{6,7},{8,9},{9,10},{10,11},{11... | collective-permute-start | bytes 98312 | tf_op jit(solution)/shard_map/ppermute | solution.py:344
  14.2 1.0 fusion
  15.5 0.3 collective-permute-done.1
  16.0 1.3 %collective-permute-start.2 = (bf16[2,272,128]{2,1,0:T(8,128)(2,1)S(1)}, bf16[2,272,128]{2,1,0:T(8,128)(2,1)S(1)}, u32[]{:S(2)}, u32[]{:S(2)}) collective-permute-start(bf16[2,272,128]{2,1,0:T(8,128)(2,1)S(1)} %pad_maximum_fusion.1), channel_id=1, source_target_pairs={{0,8},{8,16},{16,24},{24,32},{32,40},{40,48},{48,56},{56,64},{64,7... | collective-permute-start | bytes 417800 | tf_op jit(solution)/shard_map/ppermute | solution.py:344
  17.3 1.3 %collective-permute-start.3 = (bf16[2,272,128]{2,1,0:T(8,128)(2,1)S(1)}, bf16[2,272,128]{2,1,0:T(8,128)(2,1)S(1)}, u32[]{:S(2)}, u32[]{:S(2)}) collective-permute-start(bf16[2,272,128]{2,1,0:T(8,128)(2,1)S(1)} %pad_maximum_fusion.2), channel_id=1, source_target_pairs={{8,0},{16,8},{24,16},{32,24},{40,32},{48,40},{56,48},{64,56},{72,6... | collective-permute-start | bytes 417800 | tf_op jit(solution)/shard_map/ppermute | solution.py:344
  18.6 10.6 %convs_inner.1 = (bf16[8,256,512]{2,1,0:T(8,128)(2,1)S(1)}, bf16[8,256,512]{2,1,0:T(8,128)(2,1)S(1)}) custom-call(s32[3]{0:T(128)S(1)} %pad_add_fusion.place.where, bf16[64,256,128]{2,1,0:T(8,128)(2,1)} %scene.3, bf16[64,16,128]{2,1,0:T(8,128)(2,1)S(1)} %pad_maximum_fusion.strip, bf16[3,3,128,128]{3,2,1,0:T(8,128)(2,1)} %refs_2_.1, ...), custom_call_target="tpu_custom_call" | custom-call | flops 12650000384 | tf_op jit(solution)/shard_map/convs_inner/pallas_call | solution.py:176
  29.2 5.7 %collective-permute-start.7 = (bf16[512,768]{1,0:T(8,128)(2,1)S(1)}, bf16[512,768]{1,0:T(8,128)(2,1)S(1)}, u32[]{:S(2)}, u32[]{:S(2)}) collective-permute-start(bf16[512,768]{1,0:T(8,128)(2,1)S(1)} %collective-permute-done.4.refs_1_), channel_id=1, source_target_pairs={{0,32},{1,33},{2,34},{3,35},{4,36},{5,37},{6,38},{7,39},{8,40},{9,... | collective-permute-start | bytes 2359304 | tf_op jit(solution)/shard_map/ppermute | solution.py:56
  35.0 4.5 %collective-permute-start.9 = (bf16[512,768]{1,0:T(8,128)(2,1)S(1)}, bf16[512,768]{1,0:T(8,128)(2,1)S(1)}, u32[]{:S(2)}, u32[]{:S(2)}) collective-permute-start(bf16[512,768]{1,0:T(8,128)(2,1)S(1)} %collective-permute-done.4.refs_1_), channel_id=1, source_target_pairs={{0,20},{1,21},{2,22},{3,23},{4,16},{5,17},{6,18},{7,19},{8,28},{9,... | collective-permute-start | bytes 2359304 | tf_op jit(solution)/shard_map/ppermute | solution.py:56
  39.4 3.0 %collective-permute-start.8 = (bf16[512,768]{1,0:T(8,128)(2,1)S(1)}, bf16[512,768]{1,0:T(8,128)(2,1)S(1)}, u32[]{:S(2)}, u32[]{:S(2)}) collective-permute-start(bf16[512,768]{1,0:T(8,128)(2,1)S(1)} %collective-permute-done.6.refs_4_), channel_id=1, source_target_pairs={{0,96},{1,97},{2,98},{3,99},{4,100},{5,101},{6,102},{7,103},{8,104... | collective-permute-start | bytes 2359304 | tf_op jit(solution)/shard_map/ppermute | solution.py:56
  42.4 11.2 %convs_outer.1 = (bf16[8,256,512]{2,1,0:T(8,128)(2,1)S(1)}, bf16[8,256,512]{2,1,0:T(8,128)(2,1)S(1)}, bf16[768,3072]{1,0:T(8,128)(2,1)S(1)}, bf16[768,3072]{1,0:...) custom-call(s32[3]{0:T(128)S(1)} %pad_add_fusion.place.where, ...), custom_call_target="tpu_custom_call", output_to_operand_aliasing={{0}: (9, {}), {1}: (10, {})} | custom-call | flops 12650000384 | tf_op jit(solution)/shard_map/convs_outer/pallas_call | solution.py:176
  53.7 3.1 %collective-permute-done.9.refs_5_ = bf16[512,768]{1,0:T(8,128)(2,1)S(1)} collective-permute-done((bf16[512,768]{1,0:T(8,128)(2,1)S(1)}, bf16[512,768]{1,0:T(8,128)(2,1)S(1)}, u32[]{:S(2)}, u32[]{:S(2)}) %collective-permute-start.9) | collective-permute-done | bytes 786464 | tf_op jit(solution)/shard_map/ppermute | solution.py:56
  56.8 2.8 %collective-permute-done.8.refs_6_ = bf16[512,768]{1,0:T(8,128)(2,1)S(1)} collective-permute-done((bf16[512,768]{1,0:T(8,128)(2,1)S(1)}, bf16[512,768]{1,0:T(8,128)(2,1)S(1)}, u32[]{:S(2)}, u32[]{:S(2)}) %collective-permute-start.8) | collective-permute-done | bytes 786464 | tf_op jit(solution)/shard_map/ppermute | solution.py:56
  59.6 3.8 %collective-permute-start.10 = (bf16[176,768]{1,0:T(8,128)(2,1)S(1)}, bf16[176,768]{1,0:T(8,128)(2,1)S(1)}, u32[]{:S(2)}, u32[]{:S(2)}) collective-permute-start(bf16[176,768]{1,0:T(8,128)(2,1)S(1)} %slice.33), channel_id=1, source_target_pairs={{0,96},{1,97},{2,98},{3,99},{4,100},{5,101},{6,102},{7,103},{8,104... | collective-permute-start | bytes 811016 | tf_op jit(solution)/shard_map/ppermute | solution.py:56
  63.5 0.5 collective-permute-start.12
  64.0 2.1 %embed_own.1.refs_3_ = f32[256,768]{1,0:T(8,128)S(1)} custom-call(s32[8]{0:T(128)S(1)} %stack.51.order, bf16[8,256,512]{2,1,0:T(8,128)(2,1)S(1)} %get-tuple-element.58.tokens, bf16[512,768]{1,0:T(8,128)(2,1)S(1)} %copy-done, bf16[512,768]{1,0:T(8,128)(2,1)S(1)} %collective-permute-done.4.refs_1_, bf16[512,768]{1,0:T(8,128)(2,1)S(1)} %collective-permute-done.5.refs_2_, ...), custom_call_target="tpu_custom_call" | custom-call | flops 46000001024 | tf_op jit(solution)/shard_map/embed_own/pallas_call | solution.py:226
  66.2 2.1 %embed_partner.1.refs_3_ = f32[256,768]{1,0:T(8,128)S(1)} custom-call(s32[8]{0:T(128)S(1)} %stack.51.order, bf16[8,256,512]{2,1,0:T(8,128)(2,1)S(1)} %collective-permute-done.13.tokens, bf16[512,768]{1,0:T(8,128)(2,1)S(1)} %copy-done, bf16[512,768]{1,0:T(8,128)(2,1)S(1)} %collective-permute-done.4.refs_1_, ...), custom_call_target="tpu_custom_call" | custom-call | flops 3449999872 | tf_op jit(solution)/shard_map/embed_partner/pallas_call | solution.py:226
  68.4 3.6 %collective-permute-done.12.refs_2_ = bf16[160,768]{1,0:T(8,128)(2,1)S(1)} collective-permute-done((bf16[160,768]{1,0:T(8,128)(2,1)S(1)}, bf16[160,768]{1,0:T(8,128)(2,1)S(1)}, u32[]{:S(2)}, u32[]{:S(2)}) %collective-permute-start.12) | collective-permute-done | bytes 245792 | tf_op jit(solution)/shard_map/ppermute | solution.py:56
  72.2 0.9 embed_partner_last.1
  73.2 0.9 embed_own_last.1.own
  74.1 0.8 collective-permute-done.14.came
  74.9 1.5 %route.1 = (bf16[256,768]{1,0:T(8,128)(2,1)S(1)}, f32[256,1]{1,0:T(8,128)S(1)}, s32[256,1]{1,0:T(8,128)S(1)}, bf16[96,768]{1,0:T(8,128)(2,1)S(1)}, bf16[96,768]{...) custom-call(s32[3]{0:T(128)S(1)} %pad_add_fusion.place.where, ...), custom_call_target="tpu_custom_call" | custom-call | flops 3449999872 | tf_op jit(solution)/shard_map/route/pallas_call | solution.py:276
  76.7 4.0 %collective-permute-start.15 = (bf16[96,768]{1,0:T(8,128)(2,1)S(1)}, bf16[96,768]{1,0:T(8,128)(2,1)S(1)}, u32[]{:S(2)}, u32[]{:S(2)}) collective-permute-start(bf16[96,768]{1,0:T(8,128)(2,1)S(1)} %get-tuple-element.69), channel_id=1, source_target_pairs={{0,2},{1,3},{2,0},{3,1},{4,6},{5,7},{6,4},{7,5},{8,10},{9,11},{10,... | collective-permute-start | bytes 442376 | tf_op jit(solution)/shard_map/ppermute | solution.py:348
  80.7 1.4 %collective-permute-start.16 = (bf16[96,768]{1,0:T(8,128)(2,1)S(1)}, bf16[96,768]{1,0:T(8,128)(2,1)S(1)}, u32[]{:S(2)}, u32[]{:S(2)}) collective-permute-start(bf16[96,768]{1,0:T(8,128)(2,1)S(1)} %get-tuple-element.70), channel_id=1, source_target_pairs={{0,6},{1,7},{2,4},{3,5},{4,2},{5,3},{6,0},{7,1},{8,14},{9,15},{10,... | collective-permute-start | bytes 442376 | tf_op jit(solution)/shard_map/ppermute | solution.py:348
  82.0 0.3 collective-permute-done.19.refs_1_
  82.4 0.7 collective-permute-start.17
  83.3 3.8 %collective-permute-start.18 = (bf16[96,768]{1,0:T(8,128)(2,1)S(1)}, bf16[96,768]{1,0:T(8,128)(2,1)S(1)}, u32[]{:S(2)}, u32[]{:S(2)}) collective-permute-start(bf16[96,768]{1,0:T(8,128)(2,1)S(1)} %get-tuple-element.72), channel_id=1, source_target_pairs={{0,7},{1,6},{2,5},{3,4},{4,3},{5,2},{6,1},{7,0},{8,15},{9,14},{10,... | collective-permute-start | bytes 442376 | tf_op jit(solution)/shard_map/ppermute | solution.py:348
  87.0 3.6 %collective-permute-done.21.refs_3_ = bf16[96,768]{1,0:T(8,128)(2,1)S(1)} collective-permute-done((bf16[96,768]{1,0:T(8,128)(2,1)S(1)}, bf16[96,768]{1,0:T(8,128)(2,1)S(1)}, u32[]{:S(2)}, u32[]{:S(2)}) %collective-permute-start.21) | collective-permute-done | bytes 147488 | tf_op jit(solution)/shard_map/ppermute | solution.py:348
  90.6 4.1 %experts_first.1 = (bf16[96,768]{1,0:T(8,128)(2,1)S(1)}, bf16[96,768]{1,0:T(8,128)(2,1)S(1)}, bf16[96,768]{1,0:T(8,128)(2,1)S(1)}, bf16[96,768]{1,0:T(8,128)(2,1)S(1)}) custom-call(bf16[96,768]{1,0:T(8,128)(2,1)S(1)} %get-tuple-element.73.refs_0_, bf16[96,768]{1,0:T(8,128)(2,1)S(1)} %collective-permute-done.19.refs_1_, ...), custom_call_target="tpu_custom_call" | custom-call | flops 5750000128 | tf_op jit(solution)/shard_map/experts_first/pallas_call | solution.py:305
  94.8 0.6 collective-permute-done.17.refs_2_
  95.4 0.5 collective-permute-done.18.refs_3_
  95.9 1.0 collective-permute-start.22
  96.9 0.9 collective-permute-start.23
  97.9 0.8 collective-permute-start.24
  98.7 4.1 %experts_second.1 = (bf16[96,768]{1,0:T(8,128)(2,1)S(1)}, bf16[96,768]{1,0:T(8,128)(2,1)S(1)}, bf16[96,768]{1,0:T(8,128)(2,1)S(1)}, bf16[96,768]{1,0:T(8,128)(2,1)S(1)}) custom-call(bf16[96,768]{1,0:T(8,128)(2,1)S(1)} %collective-permute-done.15.refs_0_, bf16[96,768]{1,0:T(8,128)(2,1)S(1)} %collective-permute-done.16.refs_1_, ...), custom_call_target="tpu_custom_call" | custom-call | flops 5750000128 | tf_op jit(solution)/shard_map/experts_second/pallas_call | solution.py:305
  102.8 2.4 %collective-permute-start.25 = (bf16[96,768]{1,0:T(8,128)(2,1)S(1)}, bf16[96,768]{1,0:T(8,128)(2,1)S(1)}, u32[]{:S(2)}, u32[]{:S(2)}) collective-permute-start(bf16[96,768]{1,0:T(8,128)(2,1)S(1)} %get-tuple-element.93), channel_id=1, source_target_pairs={{0,2},{1,3},{2,0},{3,1},{4,6},{5,7},{6,4},{7,5},{8,10},{9,11},{10,... | collective-permute-start | bytes 442376 | tf_op jit(solution)/shard_map/ppermute | solution.py:348
  105.2 2.2 %collective-permute-start.26 = (bf16[96,768]{1,0:T(8,128)(2,1)S(1)}, bf16[96,768]{1,0:T(8,128)(2,1)S(1)}, u32[]{:S(2)}, u32[]{:S(2)}) collective-permute-start(bf16[96,768]{1,0:T(8,128)(2,1)S(1)} %get-tuple-element.94), channel_id=1, source_target_pairs={{0,6},{1,7},{2,4},{3,5},{4,2},{5,3},{6,0},{7,1},{8,14},{9,15},{10,... | collective-permute-start | bytes 442376 | tf_op jit(solution)/shard_map/ppermute | solution.py:348
  107.4 0.9 collective-permute-start.27
  108.3 2.4 %collective-permute-start.28 = (bf16[96,768]{1,0:T(8,128)(2,1)S(1)}, bf16[96,768]{1,0:T(8,128)(2,1)S(1)}, u32[]{:S(2)}, u32[]{:S(2)}) collective-permute-start(bf16[96,768]{1,0:T(8,128)(2,1)S(1)} %get-tuple-element.96), channel_id=1, source_target_pairs={{0,7},{1,6},{2,5},{3,4},{4,3},{5,2},{6,1},{7,0},{8,15},{9,14},{10,... | collective-permute-start | bytes 442376 | tf_op jit(solution)/shard_map/ppermute | solution.py:348
  110.7 0.4 mix_first.1.refs_0_
  111.1 5.3 %collective-permute-done.26.refs_4_ = bf16[96,768]{1,0:T(8,128)(2,1)S(1)} collective-permute-done((bf16[96,768]{1,0:T(8,128)(2,1)S(1)}, bf16[96,768]{1,0:T(8,128)(2,1)S(1)}, u32[]{:S(2)}, u32[]{:S(2)}) %collective-permute-start.26) | collective-permute-done | bytes 147488 | tf_op jit(solution)/shard_map/ppermute | solution.py:348
  116.4 1.5 %collective-permute-done.27.refs_5_ = bf16[96,768]{1,0:T(8,128)(2,1)S(1)} collective-permute-done((bf16[96,768]{1,0:T(8,128)(2,1)S(1)}, bf16[96,768]{1,0:T(8,128)(2,1)S(1)}, u32[]{:S(2)}, u32[]{:S(2)}) %collective-permute-start.27) | collective-permute-done | bytes 147488 | tf_op jit(solution)/shard_map/ppermute | solution.py:348
  117.9 0.7 collective-permute-done.28.refs_6_
  118.6 1.2 mix_second.1
  (40 shorter events, 1.5 us)
Async XLA Ops:
  0.0 29.2 %collective-permute-start.4 = (bf16[512,768]{1,0:T(8,128)(2,1)}, bf16[512,768]{1,0:T(8,128)(2,1)S(1)}, u32[]{:S(2)}, u32[]{:S(2)}) collective-permute-start(bf16[512,768]{1,0:T(8,128)(2,1)} %refs_0_.5), channel_id=1, source_target_pairs={{0,32},{1,33},{2,34},{3,35},{4,36},{5,37},{6,38},{7,39},{8,40},{9,... | collective-permute-start | bytes 2359304 | tf_op jit(solution)/shard_map/ppermute | solution.py:56
  1.6 27.6 %collective-permute-start.5 = (bf16[512,768]{1,0:T(8,128)(2,1)}, bf16[512,768]{1,0:T(8,128)(2,1)S(1)}, u32[]{:S(2)}, u32[]{:S(2)}) collective-permute-start(bf16[512,768]{1,0:T(8,128)(2,1)} %refs_0_.5), channel_id=1, source_target_pairs={{0,96},{1,97},{2,98},{3,99},{4,100},{5,101},{6,102},{7,103},{8,104... | collective-permute-start | bytes 2359304 | tf_op jit(solution)/shard_map/ppermute | solution.py:56
  3.2 26.0 %collective-permute-start.6 = (bf16[512,768]{1,0:T(8,128)(2,1)}, bf16[512,768]{1,0:T(8,128)(2,1)S(1)}, u32[]{:S(2)}, u32[]{:S(2)}) collective-permute-start(bf16[512,768]{1,0:T(8,128)(2,1)} %refs_0_.5), channel_id=1, source_target_pairs={{0,20},{1,21},{2,22},{3,23},{4,16},{5,17},{6,18},{7,19},{8,28},{9,... | collective-permute-start | bytes 2359304 | tf_op jit(solution)/shard_map/ppermute | solution.py:56
  8.4 7.1 %collective-permute-start = (bf16[64,2,128]{2,1,0:T(2,128)(2,1)S(1)}, bf16[64,2,128]{2,1,0:T(2,128)(2,1)S(1)}, u32[]{:S(2)}, u32[]{:S(2)}) collective-permute-start(bf16[64,2,128]{2,1,0:T(2,128)(2,1)S(1)} %get-tuple-element.99), channel_id=1, source_target_pairs={{1,0},{2,1},{3,2},{4,3},{5,4},{6,5},{7,6},{9,8},{10,9},{11,10},{12... | collective-permute-start | bytes 98312 | tf_op jit(solution)/shard_map/ppermute | solution.py:344
  9.7 6.1 %collective-permute-start.1 = (bf16[64,2,128]{2,1,0:T(2,128)(2,1)S(1)}, bf16[64,2,128]{2,1,0:T(2,128)(2,1)S(1)}, u32[]{:S(2)}, u32[]{:S(2)}) collective-permute-start(bf16[64,2,128]{2,1,0:T(2,128)(2,1)S(1)} %get-tuple-element.100), channel_id=1, source_target_pairs={{0,1},{1,2},{2,3},{3,4},{4,5},{5,6},{6,7},{8,9},{9,10},{10,11},{11... | collective-permute-start | bytes 98312 | tf_op jit(solution)/shard_map/ppermute | solution.py:344
  16.0 26.4 %collective-permute-start.2 = (bf16[2,272,128]{2,1,0:T(8,128)(2,1)S(1)}, bf16[2,272,128]{2,1,0:T(8,128)(2,1)S(1)}, u32[]{:S(2)}, u32[]{:S(2)}) collective-permute-start(bf16[2,272,128]{2,1,0:T(8,128)(2,1)S(1)} %pad_maximum_fusion.1), channel_id=1, source_target_pairs={{0,8},{8,16},{16,24},{24,32},{32,40},{40,48},{48,56},{56,64},{64,7... | collective-permute-start | bytes 417800 | tf_op jit(solution)/shard_map/ppermute | solution.py:344
  17.3 25.1 %collective-permute-start.3 = (bf16[2,272,128]{2,1,0:T(8,128)(2,1)S(1)}, bf16[2,272,128]{2,1,0:T(8,128)(2,1)S(1)}, u32[]{:S(2)}, u32[]{:S(2)}) collective-permute-start(bf16[2,272,128]{2,1,0:T(8,128)(2,1)S(1)} %pad_maximum_fusion.2), channel_id=1, source_target_pairs={{8,0},{16,8},{24,16},{32,24},{40,32},{48,40},{56,48},{64,56},{72,6... | collective-permute-start | bytes 417800 | tf_op jit(solution)/shard_map/ppermute | solution.py:344
  29.2 34.8 %copy-start = (bf16[512,768]{1,0:T(8,128)(2,1)S(1)}, bf16[512,768]{1,0:T(8,128)(2,1)}, u32[]{:S(2)}) copy-start(bf16[512,768]{1,0:T(8,128)(2,1)} %refs_0_.5) | copy-start | bytes 2359300
  29.2 24.5 %collective-permute-start.7 = (bf16[512,768]{1,0:T(8,128)(2,1)S(1)}, bf16[512,768]{1,0:T(8,128)(2,1)S(1)}, u32[]{:S(2)}, u32[]{:S(2)}) collective-permute-start(bf16[512,768]{1,0:T(8,128)(2,1)S(1)} %collective-permute-done.4.refs_1_), channel_id=1, source_target_pairs={{0,32},{1,33},{2,34},{3,35},{4,36},{5,37},{6,38},{7,39},{8,40},{9,... | collective-permute-start | bytes 2359304 | tf_op jit(solution)/shard_map/ppermute | solution.py:56
  35.0 21.8 %collective-permute-start.9 = (bf16[512,768]{1,0:T(8,128)(2,1)S(1)}, bf16[512,768]{1,0:T(8,128)(2,1)S(1)}, u32[]{:S(2)}, u32[]{:S(2)}) collective-permute-start(bf16[512,768]{1,0:T(8,128)(2,1)S(1)} %collective-permute-done.4.refs_1_), channel_id=1, source_target_pairs={{0,20},{1,21},{2,22},{3,23},{4,16},{5,17},{6,18},{7,19},{8,28},{9,... | collective-permute-start | bytes 2359304 | tf_op jit(solution)/shard_map/ppermute | solution.py:56
  39.4 20.1 %collective-permute-start.8 = (bf16[512,768]{1,0:T(8,128)(2,1)S(1)}, bf16[512,768]{1,0:T(8,128)(2,1)S(1)}, u32[]{:S(2)}, u32[]{:S(2)}) collective-permute-start(bf16[512,768]{1,0:T(8,128)(2,1)S(1)} %collective-permute-done.6.refs_4_), channel_id=1, source_target_pairs={{0,96},{1,97},{2,98},{3,99},{4,100},{5,101},{6,102},{7,103},{8,104... | collective-permute-start | bytes 2359304 | tf_op jit(solution)/shard_map/ppermute | solution.py:56
  53.6 12.6 %collective-permute-start.13 = (bf16[8,256,512]{2,1,0:T(8,128)(2,1)S(1)}, bf16[8,256,512]{2,1,0:T(8,128)(2,1)S(1)}, u32[]{:S(2)}, u32[]{:S(2)}) collective-permute-start(bf16[8,256,512]{2,1,0:T(8,128)(2,1)S(1)} %get-tuple-element.63), channel_id=1, source_target_pairs={{0,8},{1,9},{2,10},{3,11},{4,12},{5,13},{6,14},{7,15},{8,0},{9,1},... | collective-permute-start | bytes 6291464 | tf_op jit(solution)/shard_map/ppermute | solution.py:56
  59.6 12.3 %collective-permute-start.10 = (bf16[176,768]{1,0:T(8,128)(2,1)S(1)}, bf16[176,768]{1,0:T(8,128)(2,1)S(1)}, u32[]{:S(2)}, u32[]{:S(2)}) collective-permute-start(bf16[176,768]{1,0:T(8,128)(2,1)S(1)} %slice.33), channel_id=1, source_target_pairs={{0,96},{1,97},{2,98},{3,99},{4,100},{5,101},{6,102},{7,103},{8,104... | collective-permute-start | bytes 811016 | tf_op jit(solution)/shard_map/ppermute | solution.py:56
  63.4 8.8 %collective-permute-start.11 = (bf16[176,768]{1,0:T(8,128)(2,1)S(1)}, bf16[176,768]{1,0:T(8,128)(2,1)S(1)}, u32[]{:S(2)}, u32[]{:S(2)}) collective-permute-start(bf16[176,768]{1,0:T(8,128)(2,1)S(1)} %slice.34), channel_id=1, source_target_pairs={{0,32},{1,33},{2,34},{3,35},{4,36},{5,37},{6,38},{7,39},{8,40},{9,... | collective-permute-start | bytes 811016 | tf_op jit(solution)/shard_map/ppermute | solution.py:56
  63.5 8.4 %collective-permute-start.12 = (bf16[160,768]{1,0:T(8,128)(2,1)S(1)}, bf16[160,768]{1,0:T(8,128)(2,1)S(1)}, u32[]{:S(2)}, u32[]{:S(2)}) collective-permute-start(bf16[160,768]{1,0:T(8,128)(2,1)S(1)} %slice.35), channel_id=1, source_target_pairs={{0,20},{1,21},{2,22},{3,23},{4,16},{5,17},{6,18},{7,19},{8,28},{9,... | collective-permute-start | bytes 737288 | tf_op jit(solution)/shard_map/ppermute | solution.py:56
  73.1 1.8 %copy-start.1 = (bf16[768,16]{0,1:T(8,128)(2,1)S(1)}, bf16[768,16]{0,1:T(8,128)(2,1)}, u32[]{:S(2)}) copy-start(bf16[768,16]{0,1:T(8,128)(2,1)} %param.12) | copy-start | bytes 73732
  73.1 1.8 %copy-start.2 = (s32[1,1,256,1]{2,3,1,0:T(1,128)S(1)}, s32[1,1,256,1]{2,3,1,0:T(1,128)}, u32[]{:S(2)}) copy-start(s32[1,1,256,1]{2,3,1,0:T(1,128)} %param.13) | copy-start | bytes 3076
  73.1 1.8 %collective-permute-start.14 = (bf16[256,768]{1,0:T(8,128)(2,1)S(1)}, bf16[256,768]{1,0:T(8,128)(2,1)S(1)}, u32[]{:S(2)}, u32[]{:S(2)}) collective-permute-start(bf16[256,768]{1,0:T(8,128)(2,1)S(1)} %embed_partner_last.1), channel_id=1, source_target_pairs={{0,8},{1,9},{2,10},{3,11},{4,12},{5,13},{6,14},{7,15},{8,0},{9,1},... | collective-permute-start | bytes 1179656 | tf_op jit(solution)/shard_map/ppermute | solution.py:56
  76.4 6.0 %collective-permute-start.19 = (bf16[96,768]{1,0:T(8,128)(2,1)S(1)}, bf16[96,768]{1,0:T(8,128)(2,1)S(1)}, u32[]{:S(2)}, u32[]{:S(2)}) collective-permute-start(bf16[96,768]{1,0:T(8,128)(2,1)S(1)} %get-tuple-element.74), channel_id=1, source_target_pairs={{0,4},{1,5},{2,6},{3,7},{4,0},{5,1},{6,2},{7,3},{8,12},{9,13},{10,... | collective-permute-start | bytes 442376 | tf_op jit(solution)/shard_map/ppermute | solution.py:348
  76.5 6.8 %collective-permute-start.20 = (bf16[96,768]{1,0:T(8,128)(2,1)S(1)}, bf16[96,768]{1,0:T(8,128)(2,1)S(1)}, u32[]{:S(2)}, u32[]{:S(2)}) collective-permute-start(bf16[96,768]{1,0:T(8,128)(2,1)S(1)} %get-tuple-element.75), channel_id=1, source_target_pairs={{0,1},{1,0},{2,3},{3,2},{4,5},{5,4},{6,7},{7,6},{8,9},{9,8},{10,11... | collective-permute-start | bytes 442376 | tf_op jit(solution)/shard_map/ppermute | solution.py:348
  76.6 14.1 %collective-permute-start.21 = (bf16[96,768]{1,0:T(8,128)(2,1)S(1)}, bf16[96,768]{1,0:T(8,128)(2,1)S(1)}, u32[]{:S(2)}, u32[]{:S(2)}) collective-permute-start(bf16[96,768]{1,0:T(8,128)(2,1)S(1)} %get-tuple-element.76), channel_id=1, source_target_pairs={{0,3},{1,2},{2,1},{3,0},{4,7},{5,6},{6,5},{7,4},{8,11},{9,10},{10,... | collective-permute-start | bytes 442376 | tf_op jit(solution)/shard_map/ppermute | solution.py:348
  76.7 18.1 %collective-permute-start.15 = (bf16[96,768]{1,0:T(8,128)(2,1)S(1)}, bf16[96,768]{1,0:T(8,128)(2,1)S(1)}, u32[]{:S(2)}, u32[]{:S(2)}) collective-permute-start(bf16[96,768]{1,0:T(8,128)(2,1)S(1)} %get-tuple-element.69), channel_id=1, source_target_pairs={{0,2},{1,3},{2,0},{3,1},{4,6},{5,7},{6,4},{7,5},{8,10},{9,11},{10,... | collective-permute-start | bytes 442376 | tf_op jit(solution)/shard_map/ppermute | solution.py:348
  80.7 14.1 %collective-permute-start.16 = (bf16[96,768]{1,0:T(8,128)(2,1)S(1)}, bf16[96,768]{1,0:T(8,128)(2,1)S(1)}, u32[]{:S(2)}, u32[]{:S(2)}) collective-permute-start(bf16[96,768]{1,0:T(8,128)(2,1)S(1)} %get-tuple-element.70), channel_id=1, source_target_pairs={{0,6},{1,7},{2,4},{3,5},{4,2},{5,3},{6,0},{7,1},{8,14},{9,15},{10,... | collective-permute-start | bytes 442376 | tf_op jit(solution)/shard_map/ppermute | solution.py:348
  82.4 13.0 %collective-permute-start.17 = (bf16[96,768]{1,0:T(8,128)(2,1)S(1)}, bf16[96,768]{1,0:T(8,128)(2,1)S(1)}, u32[]{:S(2)}, u32[]{:S(2)}) collective-permute-start(bf16[96,768]{1,0:T(8,128)(2,1)S(1)} %get-tuple-element.71), channel_id=1, source_target_pairs={{0,5},{1,4},{2,7},{3,6},{4,1},{5,0},{6,3},{7,2},{8,13},{9,12},{10,... | collective-permute-start | bytes 442376 | tf_op jit(solution)/shard_map/ppermute | solution.py:348
  83.3 12.7 %collective-permute-start.18 = (bf16[96,768]{1,0:T(8,128)(2,1)S(1)}, bf16[96,768]{1,0:T(8,128)(2,1)S(1)}, u32[]{:S(2)}, u32[]{:S(2)}) collective-permute-start(bf16[96,768]{1,0:T(8,128)(2,1)S(1)} %get-tuple-element.72), channel_id=1, source_target_pairs={{0,7},{1,6},{2,5},{3,4},{4,3},{5,2},{6,1},{7,0},{8,15},{9,14},{10,... | collective-permute-start | bytes 442376 | tf_op jit(solution)/shard_map/ppermute | solution.py:348
  95.9 11.5 %collective-permute-start.22 = (bf16[96,768]{1,0:T(8,128)(2,1)S(1)}, bf16[96,768]{1,0:T(8,128)(2,1)S(1)}, u32[]{:S(2)}, u32[]{:S(2)}) collective-permute-start(bf16[96,768]{1,0:T(8,128)(2,1)S(1)} %get-tuple-element.86), channel_id=1, source_target_pairs={{0,4},{1,5},{2,6},{3,7},{4,0},{5,1},{6,2},{7,3},{8,12},{9,13},{10,... | collective-permute-start | bytes 442376 | tf_op jit(solution)/shard_map/ppermute | solution.py:348
  96.9 11.4 %collective-permute-start.23 = (bf16[96,768]{1,0:T(8,128)(2,1)S(1)}, bf16[96,768]{1,0:T(8,128)(2,1)S(1)}, u32[]{:S(2)}, u32[]{:S(2)}) collective-permute-start(bf16[96,768]{1,0:T(8,128)(2,1)S(1)} %get-tuple-element.87), channel_id=1, source_target_pairs={{0,1},{1,0},{2,3},{3,2},{4,5},{5,4},{6,7},{7,6},{8,9},{9,8},{10,11... | collective-permute-start | bytes 442376 | tf_op jit(solution)/shard_map/ppermute | solution.py:348
  97.9 12.8 %collective-permute-start.24 = (bf16[96,768]{1,0:T(8,128)(2,1)S(1)}, bf16[96,768]{1,0:T(8,128)(2,1)S(1)}, u32[]{:S(2)}, u32[]{:S(2)}) collective-permute-start(bf16[96,768]{1,0:T(8,128)(2,1)S(1)} %get-tuple-element.88), channel_id=1, source_target_pairs={{0,3},{1,2},{2,1},{3,0},{4,7},{5,6},{6,5},{7,4},{8,11},{9,10},{10,... | collective-permute-start | bytes 442376 | tf_op jit(solution)/shard_map/ppermute | solution.py:348
  102.8 8.3 %collective-permute-start.25 = (bf16[96,768]{1,0:T(8,128)(2,1)S(1)}, bf16[96,768]{1,0:T(8,128)(2,1)S(1)}, u32[]{:S(2)}, u32[]{:S(2)}) collective-permute-start(bf16[96,768]{1,0:T(8,128)(2,1)S(1)} %get-tuple-element.93), channel_id=1, source_target_pairs={{0,2},{1,3},{2,0},{3,1},{4,6},{5,7},{6,4},{7,5},{8,10},{9,11},{10,... | collective-permute-start | bytes 442376 | tf_op jit(solution)/shard_map/ppermute | solution.py:348
  105.2 11.2 %collective-permute-start.26 = (bf16[96,768]{1,0:T(8,128)(2,1)S(1)}, bf16[96,768]{1,0:T(8,128)(2,1)S(1)}, u32[]{:S(2)}, u32[]{:S(2)}) collective-permute-start(bf16[96,768]{1,0:T(8,128)(2,1)S(1)} %get-tuple-element.94), channel_id=1, source_target_pairs={{0,6},{1,7},{2,4},{3,5},{4,2},{5,3},{6,0},{7,1},{8,14},{9,15},{10,... | collective-permute-start | bytes 442376 | tf_op jit(solution)/shard_map/ppermute | solution.py:348
  107.4 10.5 %collective-permute-start.27 = (bf16[96,768]{1,0:T(8,128)(2,1)S(1)}, bf16[96,768]{1,0:T(8,128)(2,1)S(1)}, u32[]{:S(2)}, u32[]{:S(2)}) collective-permute-start(bf16[96,768]{1,0:T(8,128)(2,1)S(1)} %get-tuple-element.95), channel_id=1, source_target_pairs={{0,5},{1,4},{2,7},{3,6},{4,1},{5,0},{6,3},{7,2},{8,13},{9,12},{10,... | collective-permute-start | bytes 442376 | tf_op jit(solution)/shard_map/ppermute | solution.py:348
  108.3 10.3 %collective-permute-start.28 = (bf16[96,768]{1,0:T(8,128)(2,1)S(1)}, bf16[96,768]{1,0:T(8,128)(2,1)S(1)}, u32[]{:S(2)}, u32[]{:S(2)}) collective-permute-start(bf16[96,768]{1,0:T(8,128)(2,1)S(1)} %get-tuple-element.96), channel_id=1, source_target_pairs={{0,7},{1,6},{2,5},{3,4},{4,3},{5,2},{6,1},{7,0},{8,15},{9,14},{10,... | collective-permute-start | bytes 442376 | tf_op jit(solution)/shard_map/ppermute | solution.py:348

commit v7 on v6

--- a/solution.py
+++ b/solution.py
@@ -11,7 +11,7 @@
 WIDE = 272
 DIM, FF, CAP, TOK = 768, 3072, 48, 256
 PAIR = 2 * CAP
-BAND = 2
+STEPS, BAND = 4, 2
 F32, BF16 = jnp.float32, jnp.bfloat16
 ANY = pl.BlockSpec(memory_space=pl.ANY)
 VMEM = pl.BlockSpec(memory_space=pltpu.VMEM)
@@ -65,36 +65,35 @@
             target[rows, pl.ds(dx * 256 + CH, CH)] = source[j - 1, dx] if j > 0 else zero
 
 
-def pair_conv(source, weights, start):
-    taps = jnp.concatenate([source[start + j] for j in range(4)], axis=1)
+def pair_conv(source, weights, pair):
+    taps = jnp.concatenate([source[2 * pair + j] for j in range(4)], axis=1)
     parts = jnp.dot(taps, weights[...], preferred_element_type=F32)
     left = pltpu.roll(parts[:, 0:256], 1, 0)
     right = pltpu.roll(parts[:, 512:768], WIDE - 1, 0)
     return left + parts[:, 256:512] + right
 
 
-def conv_kernel(outer, fetched, place, scene, strip, *refs):
-    (top, bottom), refs = (refs[:2], refs[2:]) if outer else ((None, None), refs)
-    first, second, *sources = refs[: 2 + fetched]
-    keep, other, *refs = refs[-11 - 2 * fetched :]
+def conv_kernel(fetched, place, scene, strip, top, bottom, first, second, *refs):
+    sources, (keep, other, *refs) = refs[:fetched], refs[fetched:]
     targets, refs = refs[: 2 * fetched], refs[2 * fetched :]
     block, hidden, rows, w1, w2, first_in, second_in, sems, weight_sems = refs
     step = pl.program_id(0)
-
-    def arrive(a, b, at, k):
-        return [
-            pltpu.make_async_copy(scene.at[a:b], block.at[at : at + b - a, 0:COLS], sems.at[k, 0]),
-            pltpu.make_async_copy(
-                strip.at[a:b], block.at[at : at + b - a, COLS:WIDE], sems.at[k, 1]
-            ),
+    chunks = []
+    for k in range(STEPS):
+        hi = 8 * BAND * (k + 1) + 4
+        lo = 0 if k == 0 else hi - 8 * BAND
+        a, b = max(lo - 2, 0), min(hi - 2, ROWS)
+        part = pl.ds(a + 2, b - a)
+        copies = [
+            pltpu.make_async_copy(scene.at[a:b], block.at[part, 0:COLS], sems.at[k, 0]),
+            pltpu.make_async_copy(strip.at[a:b], block.at[part, COLS:WIDE], sems.at[k, 1]),
         ]
-
-    if outer:
-        chunks = [arrive(0, 18, 2, 0), arrive(ROWS - 18, ROWS, 20, 1)]
-        chunks[0].append(pltpu.make_async_copy(top, block.at[0:2], sems.at[0, 2]))
-        chunks[1].append(pltpu.make_async_copy(bottom, block.at[38:40], sems.at[1, 2]))
-    else:
-        chunks = [arrive(14, 34, 0, 0), arrive(34, 50, 20, 1)]
+        if k == 0:
+            copies.append(pltpu.make_async_copy(top, block.at[0:2], sems.at[k, 2]))
+        if k == STEPS - 1:
+            end = block.at[ROWS + 2 : ROWS + 4]
+            copies.append(pltpu.make_async_copy(bottom, end, sems.at[k, 2]))
+        chunks.append(copies)
     weights = [
         pltpu.make_async_copy(first, first_in, weight_sems.at[0]),
         pltpu.make_async_copy(second, second_in, weight_sems.at[1]),
@@ -108,16 +107,16 @@
     cut = ((place_col == 0) & (tail >= 8)) | ((place_col == 7) & (tail < 8))
     edge = jnp.where(cut, 0.0, 1.0).astype(F32)
 
-    def conv_first(start, target):
-        value = jnp.maximum(pair_conv(block, w1, start), 0.0)
+    def conv_first(pair):
+        value = jnp.maximum(pair_conv(block, w1, pair), 0.0)
         body, ends = value[0:COLS].astype(BF16), (value[COLS:WIDE] * edge).astype(BF16)
         for i in range(2):
-            hidden[target + i, 0:COLS] = body[:, i * CH : (i + 1) * CH]
-            hidden[target + i, COLS:WIDE] = ends[:, i * CH : (i + 1) * CH]
+            hidden[2 * pair + i, 0:COLS] = body[:, i * CH : (i + 1) * CH]
+            hidden[2 * pair + i, COLS:WIDE] = ends[:, i * CH : (i + 1) * CH]
 
     @pl.when(step == 0)
     def _():
-        for copy in [*chunks[0], *weights, *chunks[1], *fetches]:
+        for copy in [*chunks[0], *weights, *chunks[1]]:
             copy.start()
         for copy in weights:
             copy.wait()
@@ -125,31 +124,36 @@
         pair_weights(second_in, w2)
         for copy in chunks[0]:
             copy.wait()
-        if not outer:
-            conv_first(0, 0)
-
-    @pl.when(step == 1)
-    def _():
-        for copy in chunks[1]:
-            copy.wait()
-
-    block_at, hidden_at = (20 * step, 18 * step) if outer else (16 * step, 16 * step)
-    for i in range(0 if outer else 1, 4 * BAND + 1):
-        conv_first(block_at + 2 * i, hidden_at + 2 * i)
-    if outer:
-
-        @pl.when((step == 0) & (place_row == 0))
+        conv_first(0)
+
+        @pl.when(place_row == 0)
         def _():
             hidden[0] = jnp.zeros((WIDE, CH), BF16)
 
-        @pl.when((step == 1) & (place_row == 15))
-        def _():
-            hidden[35] = jnp.zeros((WIDE, CH), BF16)
-
+    for k in range(1, STEPS):
+
+        @pl.when(step == k)
+        def _(k=k):
+            for copy in chunks[k]:
+                copy.wait()
+            for copy in chunks[k + 1] if k + 1 < STEPS else ():
+                copy.start()
+            for copy in fetches if k == 1 else ():
+                copy.start()
+
+    first_pair = 4 * BAND * step
     for i in range(4 * BAND):
-        value = pair_conv(hidden, w2, hidden_at + 2 * i)[0:COLS]
+        conv_first(first_pair + 1 + i)
+
+    @pl.when((step == STEPS - 1) & (place_row == 15))
+    def _():
+        hidden[ROWS + 1] = jnp.zeros((WIDE, CH), BF16)
+
+    for i in range(4 * BAND):
+        pair = first_pair + i
+        value = pair_conv(hidden, w2, pair)[0:COLS]
         for n in range(2):
-            cells = block[block_at + 2 * i + 2 + n, 0:COLS].astype(F32)
+            cells = block[2 * pair + 2 + n, 0:COLS].astype(F32)
             rows[pl.ds((2 * i + n) * COLS, COLS), :] = value[:, n * CH : (n + 1) * CH] + cells
     for line in range(8 * BAND):
         dy, at = line % 8, pl.ds(line // 8 * 32, 32)
@@ -161,43 +165,37 @@
             other[dy, at, lanes] = jnp.where(core == 0, high, low).astype(BF16)
     if fetches:
 
-        @pl.when(step == 1)
+        @pl.when(step == STEPS - 1)
         def _():
             for copy in fetches:
                 copy.wait()
 
 
-def conv_call(place, scene, strip, halo, weights, fetch=(), given=()):
-    outer = bool(halo)
+def conv_call(place, scene, strip, top, bottom, first, second, fetch):
     shape = jax.ShapeDtypeStruct((8, TOK, 512), BF16)
     halves = [pltpu.VMEM(a.shape[1:], a.dtype) for a in fetch for _ in range(2)]
-    bands = pl.BlockSpec((8, 32 * BAND, 512), lambda i: (0, 3 * i if outer else 1 + i, 0))
-    before = 5 + len(halo) + len(fetch)
+    band = pl.BlockSpec((8, 32 * BAND, 512), lambda i: (0, i, 0))
     return pl.pallas_call(
-        functools.partial(conv_kernel, outer, len(fetch)),
-        grid=(2,),
-        in_specs=[SMEM, HBM]
-        + [ANY] * (1 + len(halo))
-        + [HBM] * (2 + len(fetch))
-        + [ANY] * len(given),
-        out_specs=[bands, bands] + [ANY] * len(halves),
+        functools.partial(conv_kernel, len(fetch)),
+        grid=(STEPS,),
+        in_specs=[SMEM, HBM, ANY, ANY, ANY, HBM, HBM] + [HBM] * len(fetch),
+        out_specs=[band, band] + [ANY] * len(halves),
         out_shape=[shape, shape] + halves,
         scratch_shapes=[
-            pltpu.VMEM((40 if outer else 36, WIDE, CH), BF16),
-            pltpu.VMEM((36 if outer else 34, WIDE, CH), BF16),
+            pltpu.VMEM((ROWS + 4, WIDE, CH), BF16),
+            pltpu.VMEM((ROWS + 2, WIDE, CH), BF16),
             pltpu.VMEM((8 * BAND * COLS, CH), F32),
             pltpu.VMEM((512, 768), BF16),
             pltpu.VMEM((512, 768), BF16),
             pltpu.VMEM((3, 3, CH, CH), BF16),
             pltpu.VMEM((3, 3, CH, CH), BF16),
-            pltpu.SemaphoreType.DMA((2, 3)),
+            pltpu.SemaphoreType.DMA((STEPS, 3)),
             pltpu.SemaphoreType.DMA((6,)),
         ],
-        input_output_aliases={before + n: n for n in range(len(given))},
         compiler_params=params(28),
-        cost_estimate=cost(11),
-        name="convs_outer" if outer else "convs_inner",
-    )(place, scene, strip, *halo, *weights, *fetch, *given)
+        cost_estimate=cost(20),
+        name="convs",
+    )(place, scene, strip, top, bottom, first, second, *fetch)
 
 
 def embed_kernel(layout, order, tokens, *refs):
@@ -361,15 +359,19 @@
     right = neighbours(scene[:, :2], "col", False)
     strip = jnp.concatenate([right, jnp.zeros((ROWS, 12, CH), BF16), left], axis=1)
     lines = [jnp.concatenate([scene[a:b], strip[a:b]], axis=1) for a, b in ((62, 64), (0, 2))]
-    halo = neighbours(lines[0], "row", True), neighbours(lines[1], "row", False)
-    kernels, cells = (in_hbm(conv_first), in_hbm(conv_second)), in_hbm(scene)
-    given = conv_call(place, cells, strip, (), kernels)
-    *given, w_minus, w_plus, w_high = lax.optimization_barrier((*given, w_minus, w_plus, w_high))
+    top, bottom = neighbours(lines[0], "row", True), neighbours(lines[1], "row", False)
+    strip, w_minus, w_plus, w_high = lax.optimization_barrier((strip, w_minus, w_plus, w_high))
     w_far, w_high_plus = send(w_minus, dx=1), send(w_high, dx=-1)
     w_high_minus = send(w_minus, dh=1, dl=1)
-    fetch = in_hbm(expert_up), in_hbm(expert_down)
     keep, other, up0, up1, down0, down1 = conv_call(
-        place, cells, strip, halo, kernels, fetch, given
+        place,
+        in_hbm(scene),
+        strip,
+        top,
+        bottom,
+        in_hbm(conv_first),
+        in_hbm(conv_second),
+        (in_hbm(expert_up), in_hbm(expert_down)),
     )
     came = send(other, dc=1)
     keep, w_far, w_high_plus, w_high_minus = lax.optimization_barrier(

time: 120 us -> 115 us (0.958)
  Pallas kernels: 39.1 us -> 37.3 us
  starting transfers between devices: 54.2 us -> 52.6 us
  waiting for transfers between devices: 23.7 us -> 22.2 us
    ppermute x11, waiting for transfers between devices: 10.5 us -> 7.92 us  [send(): return lax.ppermute(value, ('row', 'col'), hop(**step))]
    ppermute x11, starting transfers between devices: 25.1 us -> 22.9 us  [send(): return lax.ppermute(value, ('row', 'col'), hop(**step))]
    pallas_call x2 -> x1, Pallas kernels: 21.7 us -> 19.6 us  [conv_call(): pl.pallas_call(functools.partial(conv_kernel, len(fetch)), grid=(STEPS,),...]
  transfers between devices with their start and end apart: 29 -> 29, of which waited for: 14 -> 12; matrix products, arithmetic and copies ran while one was open for 2% -> 2% of each run, Pallas kernels for 30% -> 29%
where the time goes in v7:
time: 115 us
  starting transfers between devices  52.6 us (46%)
  Pallas kernels  37.3 us (32%)
  waiting for transfers between devices  22.2 us (19%)
  local copies, waits for them, and re-layouts  2.25 us (2%)
    ppermute x11, starting transfers between devices, send(): return lax.ppermute(value, ('row', 'col'), hop(**step))  22.9 us
    ppermute x14, starting transfers between devices, exchange(): lax.ppermute(arrays[k], 'col', [(i, i ^ k) for i in range(8)])  21.3 us
    pallas_call x1, Pallas kernels, conv_call(): pl.pallas_call(functools.partial(conv_kernel, len(fetch)), grid=(STEPS,),...  19.6 us
    ppermute x14, waiting for transfers between devices, exchange(): lax.ppermute(arrays[k], 'col', [(i, i ^ k) for i in range(8)])  13.7 us
    pallas_call x2, Pallas kernels, expert_call(): pl.pallas_call(expert_kernel, in_specs=[VMEM] * (count + 4), out_specs=[V...  8.58 us
    ppermute x4, starting transfers between devices, neighbours(): lax.ppermute(value, axis, pairs if ahead else [(j, i) for i, j in pairs])  8.43 us
    ppermute x11, waiting for transfers between devices, send(): return lax.ppermute(value, ('row', 'col'), hop(**step))  7.92 us
    pallas_call x4, Pallas kernels, embed_call(): pl.pallas_call(functools.partial(embed_kernel, layout), in_specs=[SMEM] +...  6.09 us
  transfers between devices with their start and end apart: 29, of which 12 were waited for; matrix products, arithmetic and copies ran while one was open for 2% of the time, Pallas kernels for 29%

profile of v7, /device:TPU:0, one launch (start us, length us, event | category | flops | bytes accessed | tf_op | source)
XLA Modules:
  0.0 114.9 jit_solution(9445513724228889856)
XLA Ops:
  0.0 1.6 %collective-permute-start.2 = (bf16[512,768]{1,0:T(8,128)(2,1)}, bf16[512,768]{1,0:T(8,128)(2,1)S(1)}, u32[]{:S(2)}, u32[]{:S(2)}) collective-permute-start(bf16[512,768]{1,0:T(8,128)(2,1)} %refs_0_.5), channel_id=1, source_target_pairs={{0,32},{1,33},{2,34},{3,35},{4,36},{5,37},{6,38},{7,39},{8,40},{9,... | collective-permute-start | bytes 2359304 | tf_op jit(solution)/shard_map/ppermute | solution.py:56
  1.6 1.7 %collective-permute-start.3 = (bf16[512,768]{1,0:T(8,128)(2,1)}, bf16[512,768]{1,0:T(8,128)(2,1)S(1)}, u32[]{:S(2)}, u32[]{:S(2)}) collective-permute-start(bf16[512,768]{1,0:T(8,128)(2,1)} %refs_0_.5), channel_id=1, source_target_pairs={{0,96},{1,97},{2,98},{3,99},{4,100},{5,101},{6,102},{7,103},{8,104... | collective-permute-start | bytes 2359304 | tf_op jit(solution)/shard_map/ppermute | solution.py:56
  3.2 4.1 %collective-permute-start.4 = (bf16[512,768]{1,0:T(8,128)(2,1)}, bf16[512,768]{1,0:T(8,128)(2,1)S(1)}, u32[]{:S(2)}, u32[]{:S(2)}) collective-permute-start(bf16[512,768]{1,0:T(8,128)(2,1)} %refs_0_.5), channel_id=1, source_target_pairs={{0,20},{1,21},{2,22},{3,23},{4,16},{5,17},{6,18},{7,19},{8,28},{9,... | collective-permute-start | bytes 2359304 | tf_op jit(solution)/shard_map/ppermute | solution.py:56
  7.4 1.0 fusion.1
  8.4 1.3 %collective-permute-start = (bf16[64,2,128]{2,1,0:T(2,128)(2,1)S(1)}, bf16[64,2,128]{2,1,0:T(2,128)(2,1)S(1)}, u32[]{:S(2)}, u32[]{:S(2)}) collective-permute-start(bf16[64,2,128]{2,1,0:T(2,128)(2,1)S(1)} %get-tuple-element.93), channel_id=1, source_target_pairs={{1,0},{2,1},{3,2},{4,3},{5,4},{6,5},{7,6},{9,8},{10,9},{11,10},{12... | collective-permute-start | bytes 98312 | tf_op jit(solution)/shard_map/ppermute | solution.py:342
  9.7 4.5 %collective-permute-start.1 = (bf16[64,2,128]{2,1,0:T(2,128)(2,1)S(1)}, bf16[64,2,128]{2,1,0:T(2,128)(2,1)S(1)}, u32[]{:S(2)}, u32[]{:S(2)}) collective-permute-start(bf16[64,2,128]{2,1,0:T(2,128)(2,1)S(1)} %get-tuple-element.94), channel_id=1, source_target_pairs={{0,1},{1,2},{2,3},{3,4},{4,5},{5,6},{6,7},{8,9},{9,10},{10,11},{11... | collective-permute-start | bytes 98312 | tf_op jit(solution)/shard_map/ppermute | solution.py:342
  14.2 1.0 fusion
  15.3 0.5 collective-permute-done.1
  16.0 1.3 %collective-permute-start.5 = (bf16[2,272,128]{2,1,0:T(8,128)(2,1)S(1)}, bf16[2,272,128]{2,1,0:T(8,128)(2,1)S(1)}, u32[]{:S(2)}, u32[]{:S(2)}) collective-permute-start(bf16[2,272,128]{2,1,0:T(8,128)(2,1)S(1)} %pad_maximum_fusion.1), channel_id=1, source_target_pairs={{0,8},{8,16},{16,24},{24,32},{32,40},{40,48},{48,56},{56,64},{64,7... | collective-permute-start | bytes 417800 | tf_op jit(solution)/shard_map/ppermute | solution.py:342
  17.3 1.3 %collective-permute-start.6 = (bf16[2,272,128]{2,1,0:T(8,128)(2,1)S(1)}, bf16[2,272,128]{2,1,0:T(8,128)(2,1)S(1)}, u32[]{:S(2)}, u32[]{:S(2)}) collective-permute-start(bf16[2,272,128]{2,1,0:T(8,128)(2,1)S(1)} %pad_maximum_fusion.2), channel_id=1, source_target_pairs={{8,0},{16,8},{24,16},{32,24},{40,32},{48,40},{56,48},{64,56},{72,6... | collective-permute-start | bytes 417800 | tf_op jit(solution)/shard_map/ppermute | solution.py:342
  18.8 1.8 %collective-permute-done.2.refs_1_ = bf16[512,768]{1,0:T(8,128)(2,1)S(1)} collective-permute-done((bf16[512,768]{1,0:T(8,128)(2,1)}, bf16[512,768]{1,0:T(8,128)(2,1)S(1)}, u32[]{:S(2)}, u32[]{:S(2)}) %collective-permute-start.2) | collective-permute-done | bytes 786464 | tf_op jit(solution)/shard_map/ppermute | solution.py:56
  20.8 3.8 %collective-permute-done.4.refs_4_ = bf16[512,768]{1,0:T(8,128)(2,1)S(1)} collective-permute-done((bf16[512,768]{1,0:T(8,128)(2,1)}, bf16[512,768]{1,0:T(8,128)(2,1)S(1)}, u32[]{:S(2)}, u32[]{:S(2)}) %collective-permute-start.4) | collective-permute-done | bytes 786464 | tf_op jit(solution)/shard_map/ppermute | solution.py:56
  24.6 3.3 %collective-permute-start.7 = (bf16[512,768]{1,0:T(8,128)(2,1)S(1)}, bf16[512,768]{1,0:T(8,128)(2,1)S(1)}, u32[]{:S(2)}, u32[]{:S(2)}) collective-permute-start(bf16[512,768]{1,0:T(8,128)(2,1)S(1)} %collective-permute-done.2.refs_1_), channel_id=1, source_target_pairs={{0,32},{1,33},{2,34},{3,35},{4,36},{5,37},{6,38},{7,39},{8,40},{9,... | collective-permute-start | bytes 2359304 | tf_op jit(solution)/shard_map/ppermute | solution.py:56
  27.8 1.1 collective-permute-start.9
  29.0 3.0 %collective-permute-start.8 = (bf16[512,768]{1,0:T(8,128)(2,1)S(1)}, bf16[512,768]{1,0:T(8,128)(2,1)S(1)}, u32[]{:S(2)}, u32[]{:S(2)}) collective-permute-start(bf16[512,768]{1,0:T(8,128)(2,1)S(1)} %collective-permute-done.4.refs_4_), channel_id=1, source_target_pairs={{0,96},{1,97},{2,98},{3,99},{4,100},{5,101},{6,102},{7,103},{8,104... | collective-permute-start | bytes 2359304 | tf_op jit(solution)/shard_map/ppermute | solution.py:56
  32.0 19.6 %convs.1 = (bf16[8,256,512]{2,1,0:T(8,128)(2,1)S(1)}, bf16[8,256,512]{2,1,0:T(8,128)(2,1)S(1)}, bf16[768,3072]{1,0:T(8,128)(2,1)S(1)}, bf16[768,3072]{1,0:T(8,12...) custom-call(s32[3]{0:T(128)S(1)} %pad_add_fusion.place.where, bf16[64,256,128]{2,1,0:T(8,128)(2,1)} %scene.1, ...), custom_call_target="tpu_custom_call" | custom-call | flops 23000000512 | tf_op jit(solution)/shard_map/convs/pallas_call | solution.py:178
  51.8 1.2 %collective-permute-start.10 = (bf16[176,768]{1,0:T(8,128)(2,1)S(1)}, bf16[176,768]{1,0:T(8,128)(2,1)S(1)}, u32[]{:S(2)}, u32[]{:S(2)}) collective-permute-start(bf16[176,768]{1,0:T(8,128)(2,1)S(1)} %slice.33), channel_id=1, source_target_pairs={{0,96},{1,97},{2,98},{3,99},{4,100},{5,101},{6,102},{7,103},{8,104... | collective-permute-start | bytes 811016 | tf_op jit(solution)/shard_map/ppermute | solution.py:56
  52.9 1.0 collective-permute-start.11
  54.0 5.7 %collective-permute-start.12 = (bf16[160,768]{1,0:T(8,128)(2,1)S(1)}, bf16[160,768]{1,0:T(8,128)(2,1)S(1)}, u32[]{:S(2)}, u32[]{:S(2)}) collective-permute-start(bf16[160,768]{1,0:T(8,128)(2,1)S(1)} %slice.35), channel_id=1, source_target_pairs={{0,20},{1,21},{2,22},{3,23},{4,16},{5,17},{6,18},{7,19},{8,28},{9,... | collective-permute-start | bytes 737288 | tf_op jit(solution)/shard_map/ppermute | solution.py:56
  59.7 2.1 %embed_own.1.refs_3_ = f32[256,768]{1,0:T(8,128)S(1)} custom-call(s32[8]{0:T(128)S(1)} %stack.51.order, bf16[8,256,512]{2,1,0:T(8,128)(2,1)S(1)} %get-tuple-element.52.tokens, bf16[512,768]{1,0:T(8,128)(2,1)S(1)} %copy-done, bf16[512,768]{1,0:T(8,128)(2,1)S(1)} %collective-permute-done.2.refs_1_, bf16[512,768]{1,0:T(8,128)(2,1)S(1)} %collective-permute-done.3.refs_2_, ...), custom_call_target="tpu_custom_call" | custom-call | flops 46000001024 | tf_op jit(solution)/shard_map/embed_own/pallas_call | solution.py:224
  61.8 2.1 %embed_partner.1.refs_3_ = f32[256,768]{1,0:T(8,128)S(1)} custom-call(s32[8]{0:T(128)S(1)} %stack.51.order, bf16[8,256,512]{2,1,0:T(8,128)(2,1)S(1)} %collective-permute-done.13.tokens, bf16[512,768]{1,0:T(8,128)(2,1)S(1)} %copy-done, bf16[512,768]{1,0:T(8,128)(2,1)S(1)} %collective-permute-done.2.refs_1_, ...), custom_call_target="tpu_custom_call" | custom-call | flops 3449999872 | tf_op jit(solution)/shard_map/embed_partner/pallas_call | solution.py:224
  64.0 1.3 %collective-permute-done.12.refs_2_ = bf16[160,768]{1,0:T(8,128)(2,1)S(1)} collective-permute-done((bf16[160,768]{1,0:T(8,128)(2,1)S(1)}, bf16[160,768]{1,0:T(8,128)(2,1)S(1)}, u32[]{:S(2)}, u32[]{:S(2)}) %collective-permute-start.12) | collective-permute-done | bytes 245792 | tf_op jit(solution)/shard_map/ppermute | solution.py:56
  65.3 0.9 embed_partner_last.1
  66.2 0.3 collective-permute-start.14
  66.5 0.9 embed_own_last.1.own
  67.4 0.8 collective-permute-done.14.came
  68.2 1.5 %route.1 = (bf16[256,768]{1,0:T(8,128)(2,1)S(1)}, f32[256,1]{1,0:T(8,128)S(1)}, s32[256,1]{1,0:T(8,128)S(1)}, bf16[96,768]{1,0:T(8,128)(2,1)S(1)}, bf16[96,768]{...) custom-call(s32[3]{0:T(128)S(1)} %pad_add_fusion.place.where, ...), custom_call_target="tpu_custom_call" | custom-call | flops 3449999872 | tf_op jit(solution)/shard_map/route/pallas_call | solution.py:274
  69.7 1.0 collective-permute-start.19
  70.7 2.4 %collective-permute-start.21 = (bf16[96,768]{1,0:T(8,128)(2,1)S(1)}, bf16[96,768]{1,0:T(8,128)(2,1)S(1)}, u32[]{:S(2)}, u32[]{:S(2)}) collective-permute-start(bf16[96,768]{1,0:T(8,128)(2,1)S(1)} %get-tuple-element.70), channel_id=1, source_target_pairs={{0,3},{1,2},{2,1},{3,0},{4,7},{5,6},{6,5},{7,4},{8,11},{9,10},{10,... | collective-permute-start | bytes 442376 | tf_op jit(solution)/shard_map/ppermute | solution.py:346
  73.2 1.7 %collective-permute-start.15 = (bf16[96,768]{1,0:T(8,128)(2,1)S(1)}, bf16[96,768]{1,0:T(8,128)(2,1)S(1)}, u32[]{:S(2)}, u32[]{:S(2)}) collective-permute-start(bf16[96,768]{1,0:T(8,128)(2,1)S(1)} %get-tuple-element.63), channel_id=1, source_target_pairs={{0,2},{1,3},{2,0},{3,1},{4,6},{5,7},{6,4},{7,5},{8,10},{9,11},{10,... | collective-permute-start | bytes 442376 | tf_op jit(solution)/shard_map/ppermute | solution.py:346
  74.8 3.2 %collective-permute-start.16 = (bf16[96,768]{1,0:T(8,128)(2,1)S(1)}, bf16[96,768]{1,0:T(8,128)(2,1)S(1)}, u32[]{:S(2)}, u32[]{:S(2)}) collective-permute-start(bf16[96,768]{1,0:T(8,128)(2,1)S(1)} %get-tuple-element.64), channel_id=1, source_target_pairs={{0,6},{1,7},{2,4},{3,5},{4,2},{5,3},{6,0},{7,1},{8,14},{9,15},{10,... | collective-permute-start | bytes 442376 | tf_op jit(solution)/shard_map/ppermute | solution.py:346
  78.3 2.1 %collective-permute-start.18 = (bf16[96,768]{1,0:T(8,128)(2,1)S(1)}, bf16[96,768]{1,0:T(8,128)(2,1)S(1)}, u32[]{:S(2)}, u32[]{:S(2)}) collective-permute-start(bf16[96,768]{1,0:T(8,128)(2,1)S(1)} %get-tuple-element.66), channel_id=1, source_target_pairs={{0,7},{1,6},{2,5},{3,4},{4,3},{5,2},{6,1},{7,0},{8,15},{9,14},{10,... | collective-permute-start | bytes 442376 | tf_op jit(solution)/shard_map/ppermute | solution.py:346
  80.3 2.9 %collective-permute-done.21.refs_3_ = bf16[96,768]{1,0:T(8,128)(2,1)S(1)} collective-permute-done((bf16[96,768]{1,0:T(8,128)(2,1)S(1)}, bf16[96,768]{1,0:T(8,128)(2,1)S(1)}, u32[]{:S(2)}, u32[]{:S(2)}) %collective-permute-start.21) | collective-permute-done | bytes 147488 | tf_op jit(solution)/shard_map/ppermute | solution.py:346
  83.3 4.3 %experts_first.1 = (bf16[96,768]{1,0:T(8,128)(2,1)S(1)}, bf16[96,768]{1,0:T(8,128)(2,1)S(1)}, bf16[96,768]{1,0:T(8,128)(2,1)S(1)}, bf16[96,768]{1,0:T(8,128)(2,1)S(1)}) custom-call(bf16[96,768]{1,0:T(8,128)(2,1)S(1)} %get-tuple-element.67.refs_0_, bf16[96,768]{1,0:T(8,128)(2,1)S(1)} %collective-permute-done.19.refs_1_, ...), custom_call_target="tpu_custom_call" | custom-call | flops 5750000128 | tf_op jit(solution)/shard_map/experts_first/pallas_call | solution.py:303
  87.6 2.4 %collective-permute-done.17.refs_2_ = bf16[96,768]{1,0:T(8,128)(2,1)S(1)} collective-permute-done((bf16[96,768]{1,0:T(8,128)(2,1)S(1)}, bf16[96,768]{1,0:T(8,128)(2,1)S(1)}, u32[]{:S(2)}, u32[]{:S(2)}) %collective-permute-start.17) | collective-permute-done | bytes 147488 | tf_op jit(solution)/shard_map/ppermute | solution.py:346
  90.0 1.1 collective-permute-done.18.refs_3_
  91.1 0.7 collective-permute-start.22
  91.8 2.1 %collective-permute-start.24 = (bf16[96,768]{1,0:T(8,128)(2,1)S(1)}, bf16[96,768]{1,0:T(8,128)(2,1)S(1)}, u32[]{:S(2)}, u32[]{:S(2)}) collective-permute-start(bf16[96,768]{1,0:T(8,128)(2,1)S(1)} %get-tuple-element.82), channel_id=1, source_target_pairs={{0,3},{1,2},{2,1},{3,0},{4,7},{5,6},{6,5},{7,4},{8,11},{9,10},{10,... | collective-permute-start | bytes 442376 | tf_op jit(solution)/shard_map/ppermute | solution.py:346
  93.9 4.3 %experts_second.1 = (bf16[96,768]{1,0:T(8,128)(2,1)S(1)}, bf16[96,768]{1,0:T(8,128)(2,1)S(1)}, bf16[96,768]{1,0:T(8,128)(2,1)S(1)}, bf16[96,768]{1,0:T(8,128)(2,1)S(1)}) custom-call(bf16[96,768]{1,0:T(8,128)(2,1)S(1)} %collective-permute-done.15.refs_0_, bf16[96,768]{1,0:T(8,128)(2,1)S(1)} %collective-permute-done.16.refs_1_, ...), custom_call_target="tpu_custom_call" | custom-call | flops 5750000128 | tf_op jit(solution)/shard_map/experts_second/pallas_call | solution.py:303
  98.2 2.1 %collective-permute-start.25 = (bf16[96,768]{1,0:T(8,128)(2,1)S(1)}, bf16[96,768]{1,0:T(8,128)(2,1)S(1)}, u32[]{:S(2)}, u32[]{:S(2)}) collective-permute-start(bf16[96,768]{1,0:T(8,128)(2,1)S(1)} %get-tuple-element.87), channel_id=1, source_target_pairs={{0,2},{1,3},{2,0},{3,1},{4,6},{5,7},{6,4},{7,5},{8,10},{9,11},{10,... | collective-permute-start | bytes 442376 | tf_op jit(solution)/shard_map/ppermute | solution.py:346
  100.3 1.5 %collective-permute-start.26 = (bf16[96,768]{1,0:T(8,128)(2,1)S(1)}, bf16[96,768]{1,0:T(8,128)(2,1)S(1)}, u32[]{:S(2)}, u32[]{:S(2)}) collective-permute-start(bf16[96,768]{1,0:T(8,128)(2,1)S(1)} %get-tuple-element.88), channel_id=1, source_target_pairs={{0,6},{1,7},{2,4},{3,5},{4,2},{5,3},{6,0},{7,1},{8,14},{9,15},{10,... | collective-permute-start | bytes 442376 | tf_op jit(solution)/shard_map/ppermute | solution.py:346
  101.8 1.9 %collective-permute-start.27 = (bf16[96,768]{1,0:T(8,128)(2,1)S(1)}, bf16[96,768]{1,0:T(8,128)(2,1)S(1)}, u32[]{:S(2)}, u32[]{:S(2)}) collective-permute-start(bf16[96,768]{1,0:T(8,128)(2,1)S(1)} %get-tuple-element.89), channel_id=1, source_target_pairs={{0,5},{1,4},{2,7},{3,6},{4,1},{5,0},{6,3},{7,2},{8,13},{9,12},{10,... | collective-permute-start | bytes 442376 | tf_op jit(solution)/shard_map/ppermute | solution.py:346
  103.6 2.4 %collective-permute-start.28 = (bf16[96,768]{1,0:T(8,128)(2,1)S(1)}, bf16[96,768]{1,0:T(8,128)(2,1)S(1)}, u32[]{:S(2)}, u32[]{:S(2)}) collective-permute-start(bf16[96,768]{1,0:T(8,128)(2,1)S(1)} %get-tuple-element.90), channel_id=1, source_target_pairs={{0,7},{1,6},{2,5},{3,4},{4,3},{5,2},{6,1},{7,0},{8,15},{9,14},{10,... | collective-permute-start | bytes 442376 | tf_op jit(solution)/shard_map/ppermute | solution.py:346
  106.0 0.4 mix_first.1.refs_0_
  106.4 4.5 %collective-permute-done.26.refs_4_ = bf16[96,768]{1,0:T(8,128)(2,1)S(1)} collective-permute-done((bf16[96,768]{1,0:T(8,128)(2,1)S(1)}, bf16[96,768]{1,0:T(8,128)(2,1)S(1)}, u32[]{:S(2)}, u32[]{:S(2)}) %collective-permute-start.26) | collective-permute-done | bytes 147488 | tf_op jit(solution)/shard_map/ppermute | solution.py:346
  110.9 2.3 %collective-permute-done.27.refs_5_ = bf16[96,768]{1,0:T(8,128)(2,1)S(1)} collective-permute-done((bf16[96,768]{1,0:T(8,128)(2,1)S(1)}, bf16[96,768]{1,0:T(8,128)(2,1)S(1)}, u32[]{:S(2)}, u32[]{:S(2)}) %collective-permute-start.27) | collective-permute-done | bytes 147488 | tf_op jit(solution)/shard_map/ppermute | solution.py:346
  113.2 0.6 collective-permute-done.28.refs_6_
  113.7 1.2 %mix_second.1 = bf16[256,768]{1,0:T(8,128)(2,1)} custom-call(f32[256,768]{1,0:T(8,128)S(1)} %mix_first.1.refs_0_, f32[256,1]{1,0:T(8,128)S(1)} %get-tuple-element.61.refs_1_, s32[256,1]{1,0:T(8,128)S(1)} %get-tuple-element.62.refs_2_, bf16[96,768]{1,0:T(8,128)(2,1)S(1)} %collective-permute-done.25.refs_3_, ...), custom_call_target="tpu_custom_call" | custom-call | flops 2300000000 | tf_op jit(solution)/shard_map/mix_second/pallas_call | solution.py:328
  (39 shorter events, 1.0 us)
Async XLA Ops:
  0.0 20.6 %collective-permute-start.2 = (bf16[512,768]{1,0:T(8,128)(2,1)}, bf16[512,768]{1,0:T(8,128)(2,1)S(1)}, u32[]{:S(2)}, u32[]{:S(2)}) collective-permute-start(bf16[512,768]{1,0:T(8,128)(2,1)} %refs_0_.5), channel_id=1, source_target_pairs={{0,32},{1,33},{2,34},{3,35},{4,36},{5,37},{6,38},{7,39},{8,40},{9,... | collective-permute-start | bytes 2359304 | tf_op jit(solution)/shard_map/ppermute | solution.py:56
  1.6 19.2 %collective-permute-start.3 = (bf16[512,768]{1,0:T(8,128)(2,1)}, bf16[512,768]{1,0:T(8,128)(2,1)S(1)}, u32[]{:S(2)}, u32[]{:S(2)}) collective-permute-start(bf16[512,768]{1,0:T(8,128)(2,1)} %refs_0_.5), channel_id=1, source_target_pairs={{0,96},{1,97},{2,98},{3,99},{4,100},{5,101},{6,102},{7,103},{8,104... | collective-permute-start | bytes 2359304 | tf_op jit(solution)/shard_map/ppermute | solution.py:56
  3.2 21.4 %collective-permute-start.4 = (bf16[512,768]{1,0:T(8,128)(2,1)}, bf16[512,768]{1,0:T(8,128)(2,1)S(1)}, u32[]{:S(2)}, u32[]{:S(2)}) collective-permute-start(bf16[512,768]{1,0:T(8,128)(2,1)} %refs_0_.5), channel_id=1, source_target_pairs={{0,20},{1,21},{2,22},{3,23},{4,16},{5,17},{6,18},{7,19},{8,28},{9,... | collective-permute-start | bytes 2359304 | tf_op jit(solution)/shard_map/ppermute | solution.py:56
  8.4 6.9 %collective-permute-start = (bf16[64,2,128]{2,1,0:T(2,128)(2,1)S(1)}, bf16[64,2,128]{2,1,0:T(2,128)(2,1)S(1)}, u32[]{:S(2)}, u32[]{:S(2)}) collective-permute-start(bf16[64,2,128]{2,1,0:T(2,128)(2,1)S(1)} %get-tuple-element.93), channel_id=1, source_target_pairs={{1,0},{2,1},{3,2},{4,3},{5,4},{6,5},{7,6},{9,8},{10,9},{11,10},{12... | collective-permute-start | bytes 98312 | tf_op jit(solution)/shard_map/ppermute | solution.py:342
  9.7 6.1 %collective-permute-start.1 = (bf16[64,2,128]{2,1,0:T(2,128)(2,1)S(1)}, bf16[64,2,128]{2,1,0:T(2,128)(2,1)S(1)}, u32[]{:S(2)}, u32[]{:S(2)}) collective-permute-start(bf16[64,2,128]{2,1,0:T(2,128)(2,1)S(1)} %get-tuple-element.94), channel_id=1, source_target_pairs={{0,1},{1,2},{2,3},{3,4},{4,5},{5,6},{6,7},{8,9},{9,10},{10,11},{11... | collective-permute-start | bytes 98312 | tf_op jit(solution)/shard_map/ppermute | solution.py:342
  16.0 16.0 %collective-permute-start.5 = (bf16[2,272,128]{2,1,0:T(8,128)(2,1)S(1)}, bf16[2,272,128]{2,1,0:T(8,128)(2,1)S(1)}, u32[]{:S(2)}, u32[]{:S(2)}) collective-permute-start(bf16[2,272,128]{2,1,0:T(8,128)(2,1)S(1)} %pad_maximum_fusion.1), channel_id=1, source_target_pairs={{0,8},{8,16},{16,24},{24,32},{32,40},{40,48},{48,56},{56,64},{64,7... | collective-permute-start | bytes 417800 | tf_op jit(solution)/shard_map/ppermute | solution.py:342
  17.3 14.7 %collective-permute-start.6 = (bf16[2,272,128]{2,1,0:T(8,128)(2,1)S(1)}, bf16[2,272,128]{2,1,0:T(8,128)(2,1)S(1)}, u32[]{:S(2)}, u32[]{:S(2)}) collective-permute-start(bf16[2,272,128]{2,1,0:T(8,128)(2,1)S(1)} %pad_maximum_fusion.2), channel_id=1, source_target_pairs={{8,0},{16,8},{24,16},{32,24},{40,32},{48,40},{56,48},{64,56},{72,6... | collective-permute-start | bytes 417800 | tf_op jit(solution)/shard_map/ppermute | solution.py:342
  18.8 40.9 %copy-start = (bf16[512,768]{1,0:T(8,128)(2,1)S(1)}, bf16[512,768]{1,0:T(8,128)(2,1)}, u32[]{:S(2)}) copy-start(bf16[512,768]{1,0:T(8,128)(2,1)} %refs_0_.5) | copy-start | bytes 2359300
  24.6 27.1 %collective-permute-start.7 = (bf16[512,768]{1,0:T(8,128)(2,1)S(1)}, bf16[512,768]{1,0:T(8,128)(2,1)S(1)}, u32[]{:S(2)}, u32[]{:S(2)}) collective-permute-start(bf16[512,768]{1,0:T(8,128)(2,1)S(1)} %collective-permute-done.2.refs_1_), channel_id=1, source_target_pairs={{0,32},{1,33},{2,34},{3,35},{4,36},{5,37},{6,38},{7,39},{8,40},{9,... | collective-permute-start | bytes 2359304 | tf_op jit(solution)/shard_map/ppermute | solution.py:56
  27.8 23.9 %collective-permute-start.9 = (bf16[512,768]{1,0:T(8,128)(2,1)S(1)}, bf16[512,768]{1,0:T(8,128)(2,1)S(1)}, u32[]{:S(2)}, u32[]{:S(2)}) collective-permute-start(bf16[512,768]{1,0:T(8,128)(2,1)S(1)} %collective-permute-done.2.refs_1_), channel_id=1, source_target_pairs={{0,20},{1,21},{2,22},{3,23},{4,16},{5,17},{6,18},{7,19},{8,28},{9,... | collective-permute-start | bytes 2359304 | tf_op jit(solution)/shard_map/ppermute | solution.py:56
  29.0 22.7 %collective-permute-start.8 = (bf16[512,768]{1,0:T(8,128)(2,1)S(1)}, bf16[512,768]{1,0:T(8,128)(2,1)S(1)}, u32[]{:S(2)}, u32[]{:S(2)}) collective-permute-start(bf16[512,768]{1,0:T(8,128)(2,1)S(1)} %collective-permute-done.4.refs_4_), channel_id=1, source_target_pairs={{0,96},{1,97},{2,98},{3,99},{4,100},{5,101},{6,102},{7,103},{8,104... | collective-permute-start | bytes 2359304 | tf_op jit(solution)/shard_map/ppermute | solution.py:56
  51.6 10.2 %collective-permute-start.13 = (bf16[8,256,512]{2,1,0:T(8,128)(2,1)S(1)}, bf16[8,256,512]{2,1,0:T(8,128)(2,1)S(1)}, u32[]{:S(2)}, u32[]{:S(2)}) collective-permute-start(bf16[8,256,512]{2,1,0:T(8,128)(2,1)S(1)} %get-tuple-element.57), channel_id=1, source_target_pairs={{0,8},{1,9},{2,10},{3,11},{4,12},{5,13},{6,14},{7,15},{8,0},{9,1},... | collective-permute-start | bytes 6291464 | tf_op jit(solution)/shard_map/ppermute | solution.py:56
  51.8 13.5 %collective-permute-start.10 = (bf16[176,768]{1,0:T(8,128)(2,1)S(1)}, bf16[176,768]{1,0:T(8,128)(2,1)S(1)}, u32[]{:S(2)}, u32[]{:S(2)}) collective-permute-start(bf16[176,768]{1,0:T(8,128)(2,1)S(1)} %slice.33), channel_id=1, source_target_pairs={{0,96},{1,97},{2,98},{3,99},{4,100},{5,101},{6,102},{7,103},{8,104... | collective-permute-start | bytes 811016 | tf_op jit(solution)/shard_map/ppermute | solution.py:56
  52.9 12.3 %collective-permute-start.11 = (bf16[176,768]{1,0:T(8,128)(2,1)S(1)}, bf16[176,768]{1,0:T(8,128)(2,1)S(1)}, u32[]{:S(2)}, u32[]{:S(2)}) collective-permute-start(bf16[176,768]{1,0:T(8,128)(2,1)S(1)} %slice.34), channel_id=1, source_target_pairs={{0,32},{1,33},{2,34},{3,35},{4,36},{5,37},{6,38},{7,39},{8,40},{9,... | collective-permute-start | bytes 811016 | tf_op jit(solution)/shard_map/ppermute | solution.py:56
  54.0 11.3 %collective-permute-start.12 = (bf16[160,768]{1,0:T(8,128)(2,1)S(1)}, bf16[160,768]{1,0:T(8,128)(2,1)S(1)}, u32[]{:S(2)}, u32[]{:S(2)}) collective-permute-start(bf16[160,768]{1,0:T(8,128)(2,1)S(1)} %slice.35), channel_id=1, source_target_pairs={{0,20},{1,21},{2,22},{3,23},{4,16},{5,17},{6,18},{7,19},{8,28},{9,... | collective-permute-start | bytes 737288 | tf_op jit(solution)/shard_map/ppermute | solution.py:56
  66.2 2.0 %copy-start.1 = (bf16[768,16]{0,1:T(8,128)(2,1)S(1)}, bf16[768,16]{0,1:T(8,128)(2,1)}, u32[]{:S(2)}) copy-start(bf16[768,16]{0,1:T(8,128)(2,1)} %param.12) | copy-start | bytes 73732
  66.2 2.0 %copy-start.2 = (s32[1,1,256,1]{2,3,1,0:T(1,128)S(1)}, s32[1,1,256,1]{2,3,1,0:T(1,128)}, u32[]{:S(2)}) copy-start(s32[1,1,256,1]{2,3,1,0:T(1,128)} %param.13) | copy-start | bytes 3076
  66.2 2.0 %collective-permute-start.14 = (bf16[256,768]{1,0:T(8,128)(2,1)S(1)}, bf16[256,768]{1,0:T(8,128)(2,1)S(1)}, u32[]{:S(2)}, u32[]{:S(2)}) collective-permute-start(bf16[256,768]{1,0:T(8,128)(2,1)S(1)} %embed_partner_last.1), channel_id=1, source_target_pairs={{0,8},{1,9},{2,10},{3,11},{4,12},{5,13},{6,14},{7,15},{8,0},{9,1},... | collective-permute-start | bytes 1179656 | tf_op jit(solution)/shard_map/ppermute | solution.py:56
  69.7 8.4 %collective-permute-start.19 = (bf16[96,768]{1,0:T(8,128)(2,1)S(1)}, bf16[96,768]{1,0:T(8,128)(2,1)S(1)}, u32[]{:S(2)}, u32[]{:S(2)}) collective-permute-start(bf16[96,768]{1,0:T(8,128)(2,1)S(1)} %get-tuple-element.68), channel_id=1, source_target_pairs={{0,4},{1,5},{2,6},{3,7},{4,0},{5,1},{6,2},{7,3},{8,12},{9,13},{10,... | collective-permute-start | bytes 442376 | tf_op jit(solution)/shard_map/ppermute | solution.py:346
  70.7 7.5 %collective-permute-start.20 = (bf16[96,768]{1,0:T(8,128)(2,1)S(1)}, bf16[96,768]{1,0:T(8,128)(2,1)S(1)}, u32[]{:S(2)}, u32[]{:S(2)}) collective-permute-start(bf16[96,768]{1,0:T(8,128)(2,1)S(1)} %get-tuple-element.69), channel_id=1, source_target_pairs={{0,1},{1,0},{2,3},{3,2},{4,5},{5,4},{6,7},{7,6},{8,9},{9,8},{10,11... | collective-permute-start | bytes 442376 | tf_op jit(solution)/shard_map/ppermute | solution.py:346
  70.7 12.5 %collective-permute-start.21 = (bf16[96,768]{1,0:T(8,128)(2,1)S(1)}, bf16[96,768]{1,0:T(8,128)(2,1)S(1)}, u32[]{:S(2)}, u32[]{:S(2)}) collective-permute-start(bf16[96,768]{1,0:T(8,128)(2,1)S(1)} %get-tuple-element.70), channel_id=1, source_target_pairs={{0,3},{1,2},{2,1},{3,0},{4,7},{5,6},{6,5},{7,4},{8,11},{9,10},{10,... | collective-permute-start | bytes 442376 | tf_op jit(solution)/shard_map/ppermute | solution.py:346
  73.2 14.4 %collective-permute-start.15 = (bf16[96,768]{1,0:T(8,128)(2,1)S(1)}, bf16[96,768]{1,0:T(8,128)(2,1)S(1)}, u32[]{:S(2)}, u32[]{:S(2)}) collective-permute-start(bf16[96,768]{1,0:T(8,128)(2,1)S(1)} %get-tuple-element.63), channel_id=1, source_target_pairs={{0,2},{1,3},{2,0},{3,1},{4,6},{5,7},{6,4},{7,5},{8,10},{9,11},{10,... | collective-permute-start | bytes 442376 | tf_op jit(solution)/shard_map/ppermute | solution.py:346
  74.8 12.7 %collective-permute-start.16 = (bf16[96,768]{1,0:T(8,128)(2,1)S(1)}, bf16[96,768]{1,0:T(8,128)(2,1)S(1)}, u32[]{:S(2)}, u32[]{:S(2)}) collective-permute-start(bf16[96,768]{1,0:T(8,128)(2,1)S(1)} %get-tuple-element.64), channel_id=1, source_target_pairs={{0,6},{1,7},{2,4},{3,5},{4,2},{5,3},{6,0},{7,1},{8,14},{9,15},{10,... | collective-permute-start | bytes 442376 | tf_op jit(solution)/shard_map/ppermute | solution.py:346
  78.1 11.9 %collective-permute-start.17 = (bf16[96,768]{1,0:T(8,128)(2,1)S(1)}, bf16[96,768]{1,0:T(8,128)(2,1)S(1)}, u32[]{:S(2)}, u32[]{:S(2)}) collective-permute-start(bf16[96,768]{1,0:T(8,128)(2,1)S(1)} %get-tuple-element.65), channel_id=1, source_target_pairs={{0,5},{1,4},{2,7},{3,6},{4,1},{5,0},{6,3},{7,2},{8,13},{9,12},{10,... | collective-permute-start | bytes 442376 | tf_op jit(solution)/shard_map/ppermute | solution.py:346
  78.3 12.8 %collective-permute-start.18 = (bf16[96,768]{1,0:T(8,128)(2,1)S(1)}, bf16[96,768]{1,0:T(8,128)(2,1)S(1)}, u32[]{:S(2)}, u32[]{:S(2)}) collective-permute-start(bf16[96,768]{1,0:T(8,128)(2,1)S(1)} %get-tuple-element.66), channel_id=1, source_target_pairs={{0,7},{1,6},{2,5},{3,4},{4,3},{5,2},{6,1},{7,0},{8,15},{9,14},{10,... | collective-permute-start | bytes 442376 | tf_op jit(solution)/shard_map/ppermute | solution.py:346
  91.1 10.7 %collective-permute-start.22 = (bf16[96,768]{1,0:T(8,128)(2,1)S(1)}, bf16[96,768]{1,0:T(8,128)(2,1)S(1)}, u32[]{:S(2)}, u32[]{:S(2)}) collective-permute-start(bf16[96,768]{1,0:T(8,128)(2,1)S(1)} %get-tuple-element.80), channel_id=1, source_target_pairs={{0,4},{1,5},{2,6},{3,7},{4,0},{5,1},{6,2},{7,3},{8,12},{9,13},{10,... | collective-permute-start | bytes 442376 | tf_op jit(solution)/shard_map/ppermute | solution.py:346
  91.8 11.8 %collective-permute-start.23 = (bf16[96,768]{1,0:T(8,128)(2,1)S(1)}, bf16[96,768]{1,0:T(8,128)(2,1)S(1)}, u32[]{:S(2)}, u32[]{:S(2)}) collective-permute-start(bf16[96,768]{1,0:T(8,128)(2,1)S(1)} %get-tuple-element.81), channel_id=1, source_target_pairs={{0,1},{1,0},{2,3},{3,2},{4,5},{5,4},{6,7},{7,6},{8,9},{9,8},{10,11... | collective-permute-start | bytes 442376 | tf_op jit(solution)/shard_map/ppermute | solution.py:346
  91.8 14.2 %collective-permute-start.24 = (bf16[96,768]{1,0:T(8,128)(2,1)S(1)}, bf16[96,768]{1,0:T(8,128)(2,1)S(1)}, u32[]{:S(2)}, u32[]{:S(2)}) collective-permute-start(bf16[96,768]{1,0:T(8,128)(2,1)S(1)} %get-tuple-element.82), channel_id=1, source_target_pairs={{0,3},{1,2},{2,1},{3,0},{4,7},{5,6},{6,5},{7,4},{8,11},{9,10},{10,... | collective-permute-start | bytes 442376 | tf_op jit(solution)/shard_map/ppermute | solution.py:346
  98.2 8.2 %collective-permute-start.25 = (bf16[96,768]{1,0:T(8,128)(2,1)S(1)}, bf16[96,768]{1,0:T(8,128)(2,1)S(1)}, u32[]{:S(2)}, u32[]{:S(2)}) collective-permute-start(bf16[96,768]{1,0:T(8,128)(2,1)S(1)} %get-tuple-element.87), channel_id=1, source_target_pairs={{0,2},{1,3},{2,0},{3,1},{4,6},{5,7},{6,4},{7,5},{8,10},{9,11},{10,... | collective-permute-start | bytes 442376 | tf_op jit(solution)/shard_map/ppermute | solution.py:346
  100.3 10.6 %collective-permute-start.26 = (bf16[96,768]{1,0:T(8,128)(2,1)S(1)}, bf16[96,768]{1,0:T(8,128)(2,1)S(1)}, u32[]{:S(2)}, u32[]{:S(2)}) collective-permute-start(bf16[96,768]{1,0:T(8,128)(2,1)S(1)} %get-tuple-element.88), channel_id=1, source_target_pairs={{0,6},{1,7},{2,4},{3,5},{4,2},{5,3},{6,0},{7,1},{8,14},{9,15},{10,... | collective-permute-start | bytes 442376 | tf_op jit(solution)/shard_map/ppermute | solution.py:346
  101.8 11.4 %collective-permute-start.27 = (bf16[96,768]{1,0:T(8,128)(2,1)S(1)}, bf16[96,768]{1,0:T(8,128)(2,1)S(1)}, u32[]{:S(2)}, u32[]{:S(2)}) collective-permute-start(bf16[96,768]{1,0:T(8,128)(2,1)S(1)} %get-tuple-element.89), channel_id=1, source_target_pairs={{0,5},{1,4},{2,7},{3,6},{4,1},{5,0},{6,3},{7,2},{8,13},{9,12},{10,... | collective-permute-start | bytes 442376 | tf_op jit(solution)/shard_map/ppermute | solution.py:346
  103.6 10.1 %collective-permute-start.28 = (bf16[96,768]{1,0:T(8,128)(2,1)S(1)}, bf16[96,768]{1,0:T(8,128)(2,1)S(1)}, u32[]{:S(2)}, u32[]{:S(2)}) collective-permute-start(bf16[96,768]{1,0:T(8,128)(2,1)S(1)} %get-tuple-element.90), channel_id=1, source_target_pairs={{0,7},{1,6},{2,5},{3,4},{4,3},{5,2},{6,1},{7,0},{8,15},{9,14},{10,... | collective-permute-start | bytes 442376 | tf_op jit(solution)/shard_map/ppermute | solution.py:346

commit v8 on v7

--- a/solution.py
+++ b/solution.py
@@ -233,8 +233,14 @@
     )(order, tokens, *arrays, *sums)
 
 
-def route_kernel(where, own, came, router, ids_row, embedded, gate, place, *outs):
-    value = (own[...] + came[...].astype(F32)).astype(BF16)
+def route_kernel(where, order, keep, own, came, router, ids_row, *refs):
+    pieces, (embedded, gate, place, *outs), whole = refs[:-12], refs[-12:-1], refs[-1]
+    at = 0
+    for piece in pieces:
+        whole[pl.ds(at, piece.shape[0])] = piece[...]
+        at += piece.shape[0]
+    part = jnp.dot(keep[order[7]], whole[...], preferred_element_type=F32)
+    value = (own[...] + part + came[...].astype(F32)).astype(BF16)
     embedded[...] = value
     wide = value.astype(F32)
     scale = lax.rsqrt(jnp.mean(wide * wide, axis=-1, keepdims=True) + 1e-06)
@@ -273,9 +279,10 @@
     shapes += [((PAIR, DIM), BF16)] * 8
     return pl.pallas_call(
         route_kernel,
-        in_specs=[SMEM] + [VMEM] * 4,
+        in_specs=[SMEM] * 2 + [VMEM] * (len(args) - 2),
         out_specs=[VMEM] * 11,
         out_shape=[jax.ShapeDtypeStruct(*shape) for shape in shapes],
+        scratch_shapes=[pltpu.VMEM((512, DIM), BF16)],
         compiler_params=params(16),
         cost_estimate=cost(3),
         name="route",
@@ -373,15 +380,13 @@
         in_hbm(conv_second),
         (in_hbm(expert_up), in_hbm(expert_down)),
     )
-    came = send(other, dc=1)
     keep, w_far, w_high_plus, w_high_minus = lax.optimization_barrier(
         (keep, w_far, w_high_plus, w_high_minus)
     )
-    last = [
-        send(w_high_plus[:176], dx=-1),
-        send(w_high_minus[176:352], dx=1),
-        send(w_far[352:], dh=1, dl=1),
-    ]
+    last = (w_high_plus[:176], w_high_minus[176:352], w_far[352:])
+    *last, other = lax.optimization_barrier((*last, other))
+    last = [send(last[0], dx=-1), send(last[1], dx=1), send(last[2], dh=1, dl=1)]
+    came = send(other, dc=1)
     order = [(a & 3) * 2 + (b & 1) for b in (high, high + 1) for a in (x, x - 1, x + 1, x + 2)]
     order = jnp.stack(order).astype(jnp.int32)
     shards = [w, w_minus, w_plus, w_far, w_high, w_high_minus, w_high_plus]
@@ -391,9 +396,8 @@
     partner = embed_call("embed_partner", order, came, shards)
     partner = embed_call("embed_partner_last", order, came, [(7, last)], [partner], BF16)
     came = send(partner, dc=1)
-    own = embed_call("embed_own_last", order, keep, [(7, last)], [own])
     embedded, gate, slots, *outs = route_call(
-        place, own, came, router_weight.T, expert_ids.reshape(1, TOK)
+        place, order, keep, own, came, router_weight.T, expert_ids.reshape(1, TOK), *last
     )
     first, second, weights = (4, 1, 3), (2, 6, 5, 7), (up0, up1, down0, down1)
     in_first, in_second = exchange(outs, first), exchange(outs, second)

time: 115 us -> 115 us (level)
    pallas_call x4 -> x3, Pallas kernels: 6.09 us -> 5.17 us  [embed_call(): pl.pallas_call(functools.partial(embed_kernel, layout), in_specs=[SMEM] +...]
  transfers between devices with their start and end apart: 29 -> 29, of which waited for: 12 -> 13; matrix products, arithmetic and copies ran while one was open for 2% -> 2% of each run, Pallas kernels for 29% -> 28%
where the time goes in v8:
time: 115 us
  starting transfers between devices  52.4 us (46%)
  Pallas kernels  36.6 us (32%)
  waiting for transfers between devices  23.2 us (20%)
  local copies, waits for them, and re-layouts  2.26 us (2%)
    ppermute x11, starting transfers between devices, send(): return lax.ppermute(value, ('row', 'col'), hop(**step))  22.8 us
    ppermute x14, starting transfers between devices, exchange(): lax.ppermute(arrays[k], 'col', [(i, i ^ k) for i in range(8)])  21.3 us
    pallas_call x1, Pallas kernels, conv_call(): pl.pallas_call(functools.partial(conv_kernel, len(fetch)), grid=(STEPS,),...  19.6 us
    ppermute x14, waiting for transfers between devices, exchange(): lax.ppermute(arrays[k], 'col', [(i, i ^ k) for i in range(8)])  13.9 us
    ppermute x11, waiting for transfers between devices, send(): return lax.ppermute(value, ('row', 'col'), hop(**step))  8.87 us
    ppermute x4, starting transfers between devices, neighbours(): lax.ppermute(value, axis, pairs if ahead else [(j, i) for i, j in pairs])  8.43 us
    pallas_call x2, Pallas kernels, expert_call(): pl.pallas_call(expert_kernel, in_specs=[VMEM] * (count + 4), out_specs=[V...  8.3 us
    pallas_call x3, Pallas kernels, embed_call(): pl.pallas_call(functools.partial(embed_kernel, layout), in_specs=[SMEM] +...  5.17 us
  transfers between devices with their start and end apart: 29, of which 13 were waited for; matrix products, arithmetic and copies ran while one was open for 2% of the time, Pallas kernels for 28%

profile of v8, /device:TPU:0, one launch (start us, length us, event | category | flops | bytes accessed | tf_op | source)
XLA Modules:
  0.0 115.0 jit_solution(9682658919504120435)
XLA Ops:
  0.0 1.6 %collective-permute-start.2 = (bf16[512,768]{1,0:T(8,128)(2,1)}, bf16[512,768]{1,0:T(8,128)(2,1)S(1)}, u32[]{:S(2)}, u32[]{:S(2)}) collective-permute-start(bf16[512,768]{1,0:T(8,128)(2,1)} %refs_0_.5), channel_id=1, source_target_pairs={{0,32},{1,33},{2,34},{3,35},{4,36},{5,37},{6,38},{7,39},{8,40},{9,... | collective-permute-start | bytes 2359304 | tf_op jit(solution)/shard_map/ppermute | solution.py:56
  1.6 1.7 %collective-permute-start.3 = (bf16[512,768]{1,0:T(8,128)(2,1)}, bf16[512,768]{1,0:T(8,128)(2,1)S(1)}, u32[]{:S(2)}, u32[]{:S(2)}) collective-permute-start(bf16[512,768]{1,0:T(8,128)(2,1)} %refs_0_.5), channel_id=1, source_target_pairs={{0,96},{1,97},{2,98},{3,99},{4,100},{5,101},{6,102},{7,103},{8,104... | collective-permute-start | bytes 2359304 | tf_op jit(solution)/shard_map/ppermute | solution.py:56
  3.2 4.1 %collective-permute-start.4 = (bf16[512,768]{1,0:T(8,128)(2,1)}, bf16[512,768]{1,0:T(8,128)(2,1)S(1)}, u32[]{:S(2)}, u32[]{:S(2)}) collective-permute-start(bf16[512,768]{1,0:T(8,128)(2,1)} %refs_0_.5), channel_id=1, source_target_pairs={{0,20},{1,21},{2,22},{3,23},{4,16},{5,17},{6,18},{7,19},{8,28},{9,... | collective-permute-start | bytes 2359304 | tf_op jit(solution)/shard_map/ppermute | solution.py:56
  7.4 1.0 fusion.1
  8.4 1.3 %collective-permute-start = (bf16[64,2,128]{2,1,0:T(2,128)(2,1)S(1)}, bf16[64,2,128]{2,1,0:T(2,128)(2,1)S(1)}, u32[]{:S(2)}, u32[]{:S(2)}) collective-permute-start(bf16[64,2,128]{2,1,0:T(2,128)(2,1)S(1)} %get-tuple-element.101), channel_id=1, source_target_pairs={{1,0},{2,1},{3,2},{4,3},{5,4},{6,5},{7,6},{9,8},{10,9},{11,10},{12... | collective-permute-start | bytes 98312 | tf_op jit(solution)/shard_map/ppermute | solution.py:349
  9.7 4.5 %collective-permute-start.1 = (bf16[64,2,128]{2,1,0:T(2,128)(2,1)S(1)}, bf16[64,2,128]{2,1,0:T(2,128)(2,1)S(1)}, u32[]{:S(2)}, u32[]{:S(2)}) collective-permute-start(bf16[64,2,128]{2,1,0:T(2,128)(2,1)S(1)} %get-tuple-element.102), channel_id=1, source_target_pairs={{0,1},{1,2},{2,3},{3,4},{4,5},{5,6},{6,7},{8,9},{9,10},{10,11},{11... | collective-permute-start | bytes 98312 | tf_op jit(solution)/shard_map/ppermute | solution.py:349
  14.2 1.0 fusion
  15.3 0.5 collective-permute-done.1
  16.0 1.3 %collective-permute-start.5 = (bf16[2,272,128]{2,1,0:T(8,128)(2,1)S(1)}, bf16[2,272,128]{2,1,0:T(8,128)(2,1)S(1)}, u32[]{:S(2)}, u32[]{:S(2)}) collective-permute-start(bf16[2,272,128]{2,1,0:T(8,128)(2,1)S(1)} %pad_maximum_fusion.1), channel_id=1, source_target_pairs={{0,8},{8,16},{16,24},{24,32},{32,40},{40,48},{48,56},{56,64},{64,7... | collective-permute-start | bytes 417800 | tf_op jit(solution)/shard_map/ppermute | solution.py:349
  17.3 1.3 %collective-permute-start.6 = (bf16[2,272,128]{2,1,0:T(8,128)(2,1)S(1)}, bf16[2,272,128]{2,1,0:T(8,128)(2,1)S(1)}, u32[]{:S(2)}, u32[]{:S(2)}) collective-permute-start(bf16[2,272,128]{2,1,0:T(8,128)(2,1)S(1)} %pad_maximum_fusion.2), channel_id=1, source_target_pairs={{8,0},{16,8},{24,16},{32,24},{40,32},{48,40},{56,48},{64,56},{72,6... | collective-permute-start | bytes 417800 | tf_op jit(solution)/shard_map/ppermute | solution.py:349
  18.8 1.8 %collective-permute-done.2.refs_1_ = bf16[512,768]{1,0:T(8,128)(2,1)S(1)} collective-permute-done((bf16[512,768]{1,0:T(8,128)(2,1)}, bf16[512,768]{1,0:T(8,128)(2,1)S(1)}, u32[]{:S(2)}, u32[]{:S(2)}) %collective-permute-start.2) | collective-permute-done | bytes 786464 | tf_op jit(solution)/shard_map/ppermute | solution.py:56
  20.8 3.8 %collective-permute-done.4.refs_4_ = bf16[512,768]{1,0:T(8,128)(2,1)S(1)} collective-permute-done((bf16[512,768]{1,0:T(8,128)(2,1)}, bf16[512,768]{1,0:T(8,128)(2,1)S(1)}, u32[]{:S(2)}, u32[]{:S(2)}) %collective-permute-start.4) | collective-permute-done | bytes 786464 | tf_op jit(solution)/shard_map/ppermute | solution.py:56
  24.6 3.3 %collective-permute-start.7 = (bf16[512,768]{1,0:T(8,128)(2,1)S(1)}, bf16[512,768]{1,0:T(8,128)(2,1)S(1)}, u32[]{:S(2)}, u32[]{:S(2)}) collective-permute-start(bf16[512,768]{1,0:T(8,128)(2,1)S(1)} %collective-permute-done.2.refs_1_), channel_id=1, source_target_pairs={{0,32},{1,33},{2,34},{3,35},{4,36},{5,37},{6,38},{7,39},{8,40},{9,... | collective-permute-start | bytes 2359304 | tf_op jit(solution)/shard_map/ppermute | solution.py:56
  27.8 1.1 collective-permute-start.9
  29.0 3.0 %collective-permute-start.8 = (bf16[512,768]{1,0:T(8,128)(2,1)S(1)}, bf16[512,768]{1,0:T(8,128)(2,1)S(1)}, u32[]{:S(2)}, u32[]{:S(2)}) collective-permute-start(bf16[512,768]{1,0:T(8,128)(2,1)S(1)} %collective-permute-done.4.refs_4_), channel_id=1, source_target_pairs={{0,96},{1,97},{2,98},{3,99},{4,100},{5,101},{6,102},{7,103},{8,104... | collective-permute-start | bytes 2359304 | tf_op jit(solution)/shard_map/ppermute | solution.py:56
  32.0 19.6 %convs.1 = (bf16[8,256,512]{2,1,0:T(8,128)(2,1)S(1)}, bf16[8,256,512]{2,1,0:T(8,128)(2,1)S(1)}, bf16[768,3072]{1,0:T(8,128)(2,1)S(1)}, bf16[768,3072]{1,0:T(8,12...) custom-call(s32[3]{0:T(128)S(1)} %pad_add_fusion.place.where, bf16[64,256,128]{2,1,0:T(8,128)(2,1)} %scene.1, ...), custom_call_target="tpu_custom_call" | custom-call | flops 23000000512 | tf_op jit(solution)/shard_map/convs/pallas_call | solution.py:178
  51.8 1.3 %collective-permute-start.11 = (bf16[176,768]{1,0:T(8,128)(2,1)S(1)}, bf16[176,768]{1,0:T(8,128)(2,1)S(1)}, u32[]{:S(2)}, u32[]{:S(2)}) collective-permute-start(bf16[176,768]{1,0:T(8,128)(2,1)S(1)} %slice.33), channel_id=1, source_target_pairs={{0,96},{1,97},{2,98},{3,99},{4,100},{5,101},{6,102},{7,103},{8,104... | collective-permute-start | bytes 811016 | tf_op jit(solution)/shard_map/ppermute | solution.py:56
  53.1 0.8 collective-permute-start.12
  53.9 5.6 %collective-permute-start.13 = (bf16[160,768]{1,0:T(8,128)(2,1)S(1)}, bf16[160,768]{1,0:T(8,128)(2,1)S(1)}, u32[]{:S(2)}, u32[]{:S(2)}) collective-permute-start(bf16[160,768]{1,0:T(8,128)(2,1)S(1)} %slice.35), channel_id=1, source_target_pairs={{0,20},{1,21},{2,22},{3,23},{4,16},{5,17},{6,18},{7,19},{8,28},{9,... | collective-permute-start | bytes 737288 | tf_op jit(solution)/shard_map/ppermute | solution.py:56
  59.5 2.1 %embed_own.1.own = f32[256,768]{1,0:T(8,128)S(1)} custom-call(s32[8]{0:T(128)S(1)} %stack.51.order, bf16[8,256,512]{2,1,0:T(8,128)(2,1)S(1)} %get-tuple-element.56.tokens.keep, bf16[512,768]{1,0:T(8,128)(2,1)S(1)} %copy-done, bf16[512,768]{1,0:T(8,128)(2,1)S(1)} %collective-permute-done.2.refs_1_, bf16[512,768]{1,0:T(8,128)(2,1)S(1)} %collective-permute-done.3.refs_2_, ...), custom_call_target="tpu_custom_call" | custom-call | flops 46000001024 | tf_op jit(solution)/shard_map/embed_own/pallas_call | solution.py:224
  61.6 2.1 %embed_partner.1.refs_3_ = f32[256,768]{1,0:T(8,128)S(1)} custom-call(s32[8]{0:T(128)S(1)} %stack.51.order, bf16[8,256,512]{2,1,0:T(8,128)(2,1)S(1)} %collective-permute-done.10.tokens, bf16[512,768]{1,0:T(8,128)(2,1)S(1)} %copy-done, bf16[512,768]{1,0:T(8,128)(2,1)S(1)} %collective-permute-done.2.refs_1_, ...), custom_call_target="tpu_custom_call" | custom-call | flops 3449999872 | tf_op jit(solution)/shard_map/embed_partner/pallas_call | solution.py:224
  63.8 1.3 %collective-permute-done.13.refs_2_ = bf16[160,768]{1,0:T(8,128)(2,1)S(1)} collective-permute-done((bf16[160,768]{1,0:T(8,128)(2,1)S(1)}, bf16[160,768]{1,0:T(8,128)(2,1)S(1)}, u32[]{:S(2)}, u32[]{:S(2)}) %collective-permute-start.13) | collective-permute-done | bytes 245792 | tf_op jit(solution)/shard_map/ppermute | solution.py:56
  65.1 0.9 embed_partner_last.1
  66.1 0.3 collective-permute-start.14
  66.3 1.7 %collective-permute-done.14.came = bf16[256,768]{1,0:T(8,128)(2,1)S(1)} collective-permute-done((bf16[256,768]{1,0:T(8,128)(2,1)S(1)}, bf16[256,768]{1,0:T(8,128)(2,1)S(1)}, u32[]{:S(2)}, u32[]{:S(2)}) %collective-permute-start.14) | collective-permute-done | bytes 393248 | tf_op jit(solution)/shard_map/ppermute | solution.py:56
  68.1 1.9 %route.1 = (bf16[256,768]{1,0:T(8,128)(2,1)S(1)}, f32[256,1]{1,0:T(8,128)S(1)}, s32[256,1]{1,0:T(8,128)S(1)}, bf16[96,768]{1,0:T(8,128)(2,1)S(1)}, bf16[96,768]{...) custom-call(s32[3]{0:T(128)S(1)} %pad_add_fusion.place.where, ...), custom_call_target="tpu_custom_call" | custom-call | flops 3449999872 | tf_op jit(solution)/shard_map/route/pallas_call | solution.py:280
  70.0 1.1 collective-permute-start.19
  71.1 2.3 %collective-permute-start.21 = (bf16[96,768]{1,0:T(8,128)(2,1)S(1)}, bf16[96,768]{1,0:T(8,128)(2,1)S(1)}, u32[]{:S(2)}, u32[]{:S(2)}) collective-permute-start(bf16[96,768]{1,0:T(8,128)(2,1)S(1)} %get-tuple-element.78), channel_id=1, source_target_pairs={{0,3},{1,2},{2,1},{3,0},{4,7},{5,6},{6,5},{7,4},{8,11},{9,10},{10,... | collective-permute-start | bytes 442376 | tf_op jit(solution)/shard_map/ppermute | solution.py:353
  73.4 1.8 %collective-permute-start.15 = (bf16[96,768]{1,0:T(8,128)(2,1)S(1)}, bf16[96,768]{1,0:T(8,128)(2,1)S(1)}, u32[]{:S(2)}, u32[]{:S(2)}) collective-permute-start(bf16[96,768]{1,0:T(8,128)(2,1)S(1)} %get-tuple-element.71), channel_id=1, source_target_pairs={{0,2},{1,3},{2,0},{3,1},{4,6},{5,7},{6,4},{7,5},{8,10},{9,11},{10,... | collective-permute-start | bytes 442376 | tf_op jit(solution)/shard_map/ppermute | solution.py:353
  75.2 3.1 %collective-permute-start.16 = (bf16[96,768]{1,0:T(8,128)(2,1)S(1)}, bf16[96,768]{1,0:T(8,128)(2,1)S(1)}, u32[]{:S(2)}, u32[]{:S(2)}) collective-permute-start(bf16[96,768]{1,0:T(8,128)(2,1)S(1)} %get-tuple-element.72), channel_id=1, source_target_pairs={{0,6},{1,7},{2,4},{3,5},{4,2},{5,3},{6,0},{7,1},{8,14},{9,15},{10,... | collective-permute-start | bytes 442376 | tf_op jit(solution)/shard_map/ppermute | solution.py:353
  78.3 0.2 collective-permute-start.17
  78.5 2.1 %collective-permute-start.18 = (bf16[96,768]{1,0:T(8,128)(2,1)S(1)}, bf16[96,768]{1,0:T(8,128)(2,1)S(1)}, u32[]{:S(2)}, u32[]{:S(2)}) collective-permute-start(bf16[96,768]{1,0:T(8,128)(2,1)S(1)} %get-tuple-element.74), channel_id=1, source_target_pairs={{0,7},{1,6},{2,5},{3,4},{4,3},{5,2},{6,1},{7,0},{8,15},{9,14},{10,... | collective-permute-start | bytes 442376 | tf_op jit(solution)/shard_map/ppermute | solution.py:353
  80.6 2.8 %collective-permute-done.21.refs_3_ = bf16[96,768]{1,0:T(8,128)(2,1)S(1)} collective-permute-done((bf16[96,768]{1,0:T(8,128)(2,1)S(1)}, bf16[96,768]{1,0:T(8,128)(2,1)S(1)}, u32[]{:S(2)}, u32[]{:S(2)}) %collective-permute-start.21) | collective-permute-done | bytes 147488 | tf_op jit(solution)/shard_map/ppermute | solution.py:353
  83.4 4.2 %experts_first.1 = (bf16[96,768]{1,0:T(8,128)(2,1)S(1)}, bf16[96,768]{1,0:T(8,128)(2,1)S(1)}, bf16[96,768]{1,0:T(8,128)(2,1)S(1)}, bf16[96,768]{1,0:T(8,128)(2,1)S(1)}) custom-call(bf16[96,768]{1,0:T(8,128)(2,1)S(1)} %get-tuple-element.75.refs_0_, bf16[96,768]{1,0:T(8,128)(2,1)S(1)} %collective-permute-done.19.refs_1_, ...), custom_call_target="tpu_custom_call" | custom-call | flops 5750000128 | tf_op jit(solution)/shard_map/experts_first/pallas_call | solution.py:310
  87.8 2.5 %collective-permute-done.17.refs_2_ = bf16[96,768]{1,0:T(8,128)(2,1)S(1)} collective-permute-done((bf16[96,768]{1,0:T(8,128)(2,1)S(1)}, bf16[96,768]{1,0:T(8,128)(2,1)S(1)}, u32[]{:S(2)}, u32[]{:S(2)}) %collective-permute-start.17) | collective-permute-done | bytes 147488 | tf_op jit(solution)/shard_map/ppermute | solution.py:353
  90.3 1.0 collective-permute-done.18.refs_3_
  91.3 0.8 collective-permute-start.22
  92.1 1.9 %collective-permute-start.24 = (bf16[96,768]{1,0:T(8,128)(2,1)S(1)}, bf16[96,768]{1,0:T(8,128)(2,1)S(1)}, u32[]{:S(2)}, u32[]{:S(2)}) collective-permute-start(bf16[96,768]{1,0:T(8,128)(2,1)S(1)} %get-tuple-element.90), channel_id=1, source_target_pairs={{0,3},{1,2},{2,1},{3,0},{4,7},{5,6},{6,5},{7,4},{8,11},{9,10},{10,... | collective-permute-start | bytes 442376 | tf_op jit(solution)/shard_map/ppermute | solution.py:353
  94.0 4.1 %experts_second.1 = (bf16[96,768]{1,0:T(8,128)(2,1)S(1)}, bf16[96,768]{1,0:T(8,128)(2,1)S(1)}, bf16[96,768]{1,0:T(8,128)(2,1)S(1)}, bf16[96,768]{1,0:T(8,128)(2,1)S(1)}) custom-call(bf16[96,768]{1,0:T(8,128)(2,1)S(1)} %collective-permute-done.15.refs_0_, bf16[96,768]{1,0:T(8,128)(2,1)S(1)} %collective-permute-done.16.refs_1_, ...), custom_call_target="tpu_custom_call" | custom-call | flops 5750000128 | tf_op jit(solution)/shard_map/experts_second/pallas_call | solution.py:310
  98.1 2.3 %collective-permute-start.25 = (bf16[96,768]{1,0:T(8,128)(2,1)S(1)}, bf16[96,768]{1,0:T(8,128)(2,1)S(1)}, u32[]{:S(2)}, u32[]{:S(2)}) collective-permute-start(bf16[96,768]{1,0:T(8,128)(2,1)S(1)} %get-tuple-element.95), channel_id=1, source_target_pairs={{0,2},{1,3},{2,0},{3,1},{4,6},{5,7},{6,4},{7,5},{8,10},{9,11},{10,... | collective-permute-start | bytes 442376 | tf_op jit(solution)/shard_map/ppermute | solution.py:353
  100.4 1.4 %collective-permute-start.26 = (bf16[96,768]{1,0:T(8,128)(2,1)S(1)}, bf16[96,768]{1,0:T(8,128)(2,1)S(1)}, u32[]{:S(2)}, u32[]{:S(2)}) collective-permute-start(bf16[96,768]{1,0:T(8,128)(2,1)S(1)} %get-tuple-element.96), channel_id=1, source_target_pairs={{0,6},{1,7},{2,4},{3,5},{4,2},{5,3},{6,0},{7,1},{8,14},{9,15},{10,... | collective-permute-start | bytes 442376 | tf_op jit(solution)/shard_map/ppermute | solution.py:353
  101.9 1.8 %collective-permute-start.27 = (bf16[96,768]{1,0:T(8,128)(2,1)S(1)}, bf16[96,768]{1,0:T(8,128)(2,1)S(1)}, u32[]{:S(2)}, u32[]{:S(2)}) collective-permute-start(bf16[96,768]{1,0:T(8,128)(2,1)S(1)} %get-tuple-element.97), channel_id=1, source_target_pairs={{0,5},{1,4},{2,7},{3,6},{4,1},{5,0},{6,3},{7,2},{8,13},{9,12},{10,... | collective-permute-start | bytes 442376 | tf_op jit(solution)/shard_map/ppermute | solution.py:353
  103.7 2.4 %collective-permute-start.28 = (bf16[96,768]{1,0:T(8,128)(2,1)S(1)}, bf16[96,768]{1,0:T(8,128)(2,1)S(1)}, u32[]{:S(2)}, u32[]{:S(2)}) collective-permute-start(bf16[96,768]{1,0:T(8,128)(2,1)S(1)} %get-tuple-element.98), channel_id=1, source_target_pairs={{0,7},{1,6},{2,5},{3,4},{4,3},{5,2},{6,1},{7,0},{8,15},{9,14},{10,... | collective-permute-start | bytes 442376 | tf_op jit(solution)/shard_map/ppermute | solution.py:353
  106.1 0.4 mix_first.1.refs_0_
  106.5 4.5 %collective-permute-done.26.refs_4_ = bf16[96,768]{1,0:T(8,128)(2,1)S(1)} collective-permute-done((bf16[96,768]{1,0:T(8,128)(2,1)S(1)}, bf16[96,768]{1,0:T(8,128)(2,1)S(1)}, u32[]{:S(2)}, u32[]{:S(2)}) %collective-permute-start.26) | collective-permute-done | bytes 147488 | tf_op jit(solution)/shard_map/ppermute | solution.py:353
  111.0 2.3 %collective-permute-done.27.refs_5_ = bf16[96,768]{1,0:T(8,128)(2,1)S(1)} collective-permute-done((bf16[96,768]{1,0:T(8,128)(2,1)S(1)}, bf16[96,768]{1,0:T(8,128)(2,1)S(1)}, u32[]{:S(2)}, u32[]{:S(2)}) %collective-permute-start.27) | collective-permute-done | bytes 147488 | tf_op jit(solution)/shard_map/ppermute | solution.py:353
  113.3 0.6 collective-permute-done.28.refs_6_
  113.9 1.2 %mix_second.1 = bf16[256,768]{1,0:T(8,128)(2,1)} custom-call(f32[256,768]{1,0:T(8,128)S(1)} %mix_first.1.refs_0_, f32[256,1]{1,0:T(8,128)S(1)} %get-tuple-element.69.refs_1_, s32[256,1]{1,0:T(8,128)S(1)} %get-tuple-element.70.refs_2_, bf16[96,768]{1,0:T(8,128)(2,1)S(1)} %collective-permute-done.25.refs_3_, ...), custom_call_target="tpu_custom_call" | custom-call | flops 2300000000 | tf_op jit(solution)/shard_map/mix_second/pallas_call | solution.py:335
  (38 shorter events, 1.0 us)
Async XLA Ops:
  0.0 20.6 %collective-permute-start.2 = (bf16[512,768]{1,0:T(8,128)(2,1)}, bf16[512,768]{1,0:T(8,128)(2,1)S(1)}, u32[]{:S(2)}, u32[]{:S(2)}) collective-permute-start(bf16[512,768]{1,0:T(8,128)(2,1)} %refs_0_.5), channel_id=1, source_target_pairs={{0,32},{1,33},{2,34},{3,35},{4,36},{5,37},{6,38},{7,39},{8,40},{9,... | collective-permute-start | bytes 2359304 | tf_op jit(solution)/shard_map/ppermute | solution.py:56
  1.6 19.2 %collective-permute-start.3 = (bf16[512,768]{1,0:T(8,128)(2,1)}, bf16[512,768]{1,0:T(8,128)(2,1)S(1)}, u32[]{:S(2)}, u32[]{:S(2)}) collective-permute-start(bf16[512,768]{1,0:T(8,128)(2,1)} %refs_0_.5), channel_id=1, source_target_pairs={{0,96},{1,97},{2,98},{3,99},{4,100},{5,101},{6,102},{7,103},{8,104... | collective-permute-start | bytes 2359304 | tf_op jit(solution)/shard_map/ppermute | solution.py:56
  3.2 21.4 %collective-permute-start.4 = (bf16[512,768]{1,0:T(8,128)(2,1)}, bf16[512,768]{1,0:T(8,128)(2,1)S(1)}, u32[]{:S(2)}, u32[]{:S(2)}) collective-permute-start(bf16[512,768]{1,0:T(8,128)(2,1)} %refs_0_.5), channel_id=1, source_target_pairs={{0,20},{1,21},{2,22},{3,23},{4,16},{5,17},{6,18},{7,19},{8,28},{9,... | collective-permute-start | bytes 2359304 | tf_op jit(solution)/shard_map/ppermute | solution.py:56
  8.4 6.9 %collective-permute-start = (bf16[64,2,128]{2,1,0:T(2,128)(2,1)S(1)}, bf16[64,2,128]{2,1,0:T(2,128)(2,1)S(1)}, u32[]{:S(2)}, u32[]{:S(2)}) collective-permute-start(bf16[64,2,128]{2,1,0:T(2,128)(2,1)S(1)} %get-tuple-element.101), channel_id=1, source_target_pairs={{1,0},{2,1},{3,2},{4,3},{5,4},{6,5},{7,6},{9,8},{10,9},{11,10},{12... | collective-permute-start | bytes 98312 | tf_op jit(solution)/shard_map/ppermute | solution.py:349
  9.7 6.1 %collective-permute-start.1 = (bf16[64,2,128]{2,1,0:T(2,128)(2,1)S(1)}, bf16[64,2,128]{2,1,0:T(2,128)(2,1)S(1)}, u32[]{:S(2)}, u32[]{:S(2)}) collective-permute-start(bf16[64,2,128]{2,1,0:T(2,128)(2,1)S(1)} %get-tuple-element.102), channel_id=1, source_target_pairs={{0,1},{1,2},{2,3},{3,4},{4,5},{5,6},{6,7},{8,9},{9,10},{10,11},{11... | collective-permute-start | bytes 98312 | tf_op jit(solution)/shard_map/ppermute | solution.py:349
  16.0 16.0 %collective-permute-start.5 = (bf16[2,272,128]{2,1,0:T(8,128)(2,1)S(1)}, bf16[2,272,128]{2,1,0:T(8,128)(2,1)S(1)}, u32[]{:S(2)}, u32[]{:S(2)}) collective-permute-start(bf16[2,272,128]{2,1,0:T(8,128)(2,1)S(1)} %pad_maximum_fusion.1), channel_id=1, source_target_pairs={{0,8},{8,16},{16,24},{24,32},{32,40},{40,48},{48,56},{56,64},{64,7... | collective-permute-start | bytes 417800 | tf_op jit(solution)/shard_map/ppermute | solution.py:349
  17.3 14.7 %collective-permute-start.6 = (bf16[2,272,128]{2,1,0:T(8,128)(2,1)S(1)}, bf16[2,272,128]{2,1,0:T(8,128)(2,1)S(1)}, u32[]{:S(2)}, u32[]{:S(2)}) collective-permute-start(bf16[2,272,128]{2,1,0:T(8,128)(2,1)S(1)} %pad_maximum_fusion.2), channel_id=1, source_target_pairs={{8,0},{16,8},{24,16},{32,24},{40,32},{48,40},{56,48},{64,56},{72,6... | collective-permute-start | bytes 417800 | tf_op jit(solution)/shard_map/ppermute | solution.py:349
  18.8 40.7 %copy-start = (bf16[512,768]{1,0:T(8,128)(2,1)S(1)}, bf16[512,768]{1,0:T(8,128)(2,1)}, u32[]{:S(2)}) copy-start(bf16[512,768]{1,0:T(8,128)(2,1)} %refs_0_.5) | copy-start | bytes 2359300
  24.6 27.0 %collective-permute-start.7 = (bf16[512,768]{1,0:T(8,128)(2,1)S(1)}, bf16[512,768]{1,0:T(8,128)(2,1)S(1)}, u32[]{:S(2)}, u32[]{:S(2)}) collective-permute-start(bf16[512,768]{1,0:T(8,128)(2,1)S(1)} %collective-permute-done.2.refs_1_), channel_id=1, source_target_pairs={{0,32},{1,33},{2,34},{3,35},{4,36},{5,37},{6,38},{7,39},{8,40},{9,... | collective-permute-start | bytes 2359304 | tf_op jit(solution)/shard_map/ppermute | solution.py:56
  27.8 23.8 %collective-permute-start.9 = (bf16[512,768]{1,0:T(8,128)(2,1)S(1)}, bf16[512,768]{1,0:T(8,128)(2,1)S(1)}, u32[]{:S(2)}, u32[]{:S(2)}) collective-permute-start(bf16[512,768]{1,0:T(8,128)(2,1)S(1)} %collective-permute-done.2.refs_1_), channel_id=1, source_target_pairs={{0,20},{1,21},{2,22},{3,23},{4,16},{5,17},{6,18},{7,19},{8,28},{9,... | collective-permute-start | bytes 2359304 | tf_op jit(solution)/shard_map/ppermute | solution.py:56
  29.0 22.6 %collective-permute-start.8 = (bf16[512,768]{1,0:T(8,128)(2,1)S(1)}, bf16[512,768]{1,0:T(8,128)(2,1)S(1)}, u32[]{:S(2)}, u32[]{:S(2)}) collective-permute-start(bf16[512,768]{1,0:T(8,128)(2,1)S(1)} %collective-permute-done.4.refs_4_), channel_id=1, source_target_pairs={{0,96},{1,97},{2,98},{3,99},{4,100},{5,101},{6,102},{7,103},{8,104... | collective-permute-start | bytes 2359304 | tf_op jit(solution)/shard_map/ppermute | solution.py:56
  51.7 9.9 %collective-permute-start.10 = (bf16[8,256,512]{2,1,0:T(8,128)(2,1)S(1)}, bf16[8,256,512]{2,1,0:T(8,128)(2,1)S(1)}, u32[]{:S(2)}, u32[]{:S(2)}) collective-permute-start(bf16[8,256,512]{2,1,0:T(8,128)(2,1)S(1)} %get-tuple-element.62), channel_id=1, source_target_pairs={{0,8},{1,9},{2,10},{3,11},{4,12},{5,13},{6,14},{7,15},{8,0},{9,1},... | collective-permute-start | bytes 6291464 | tf_op jit(solution)/shard_map/ppermute | solution.py:56
  51.8 13.3 %collective-permute-start.11 = (bf16[176,768]{1,0:T(8,128)(2,1)S(1)}, bf16[176,768]{1,0:T(8,128)(2,1)S(1)}, u32[]{:S(2)}, u32[]{:S(2)}) collective-permute-start(bf16[176,768]{1,0:T(8,128)(2,1)S(1)} %slice.33), channel_id=1, source_target_pairs={{0,96},{1,97},{2,98},{3,99},{4,100},{5,101},{6,102},{7,103},{8,104... | collective-permute-start | bytes 811016 | tf_op jit(solution)/shard_map/ppermute | solution.py:56
  53.1 12.1 %collective-permute-start.12 = (bf16[176,768]{1,0:T(8,128)(2,1)S(1)}, bf16[176,768]{1,0:T(8,128)(2,1)S(1)}, u32[]{:S(2)}, u32[]{:S(2)}) collective-permute-start(bf16[176,768]{1,0:T(8,128)(2,1)S(1)} %slice.34), channel_id=1, source_target_pairs={{0,32},{1,33},{2,34},{3,35},{4,36},{5,37},{6,38},{7,39},{8,40},{9,... | collective-permute-start | bytes 811016 | tf_op jit(solution)/shard_map/ppermute | solution.py:56
  53.9 11.2 %collective-permute-start.13 = (bf16[160,768]{1,0:T(8,128)(2,1)S(1)}, bf16[160,768]{1,0:T(8,128)(2,1)S(1)}, u32[]{:S(2)}, u32[]{:S(2)}) collective-permute-start(bf16[160,768]{1,0:T(8,128)(2,1)S(1)} %slice.35), channel_id=1, source_target_pairs={{0,20},{1,21},{2,22},{3,23},{4,16},{5,17},{6,18},{7,19},{8,28},{9,... | collective-permute-start | bytes 737288 | tf_op jit(solution)/shard_map/ppermute | solution.py:56
  63.8 4.3 %copy-start.1 = (bf16[768,16]{0,1:T(8,128)(2,1)S(1)}, bf16[768,16]{0,1:T(8,128)(2,1)}, u32[]{:S(2)}) copy-start(bf16[768,16]{0,1:T(8,128)(2,1)} %param.12) | copy-start | bytes 73732
  63.8 4.3 %copy-start.2 = (s32[1,1,256,1]{2,3,1,0:T(1,128)S(1)}, s32[1,1,256,1]{2,3,1,0:T(1,128)}, u32[]{:S(2)}) copy-start(s32[1,1,256,1]{2,3,1,0:T(1,128)} %param.13) | copy-start | bytes 3076
  66.1 2.0 %collective-permute-start.14 = (bf16[256,768]{1,0:T(8,128)(2,1)S(1)}, bf16[256,768]{1,0:T(8,128)(2,1)S(1)}, u32[]{:S(2)}, u32[]{:S(2)}) collective-permute-start(bf16[256,768]{1,0:T(8,128)(2,1)S(1)} %embed_partner_last.1), channel_id=1, source_target_pairs={{0,8},{1,9},{2,10},{3,11},{4,12},{5,13},{6,14},{7,15},{8,0},{9,1},... | collective-permute-start | bytes 1179656 | tf_op jit(solution)/shard_map/ppermute | solution.py:56
  70.0 8.3 %collective-permute-start.19 = (bf16[96,768]{1,0:T(8,128)(2,1)S(1)}, bf16[96,768]{1,0:T(8,128)(2,1)S(1)}, u32[]{:S(2)}, u32[]{:S(2)}) collective-permute-start(bf16[96,768]{1,0:T(8,128)(2,1)S(1)} %get-tuple-element.76), channel_id=1, source_target_pairs={{0,4},{1,5},{2,6},{3,7},{4,0},{5,1},{6,2},{7,3},{8,12},{9,13},{10,... | collective-permute-start | bytes 442376 | tf_op jit(solution)/shard_map/ppermute | solution.py:353
  71.1 7.4 %collective-permute-start.20 = (bf16[96,768]{1,0:T(8,128)(2,1)S(1)}, bf16[96,768]{1,0:T(8,128)(2,1)S(1)}, u32[]{:S(2)}, u32[]{:S(2)}) collective-permute-start(bf16[96,768]{1,0:T(8,128)(2,1)S(1)} %get-tuple-element.77), channel_id=1, source_target_pairs={{0,1},{1,0},{2,3},{3,2},{4,5},{5,4},{6,7},{7,6},{8,9},{9,8},{10,11... | collective-permute-start | bytes 442376 | tf_op jit(solution)/shard_map/ppermute | solution.py:353
  71.1 12.3 %collective-permute-start.21 = (bf16[96,768]{1,0:T(8,128)(2,1)S(1)}, bf16[96,768]{1,0:T(8,128)(2,1)S(1)}, u32[]{:S(2)}, u32[]{:S(2)}) collective-permute-start(bf16[96,768]{1,0:T(8,128)(2,1)S(1)} %get-tuple-element.78), channel_id=1, source_target_pairs={{0,3},{1,2},{2,1},{3,0},{4,7},{5,6},{6,5},{7,4},{8,11},{9,10},{10,... | collective-permute-start | bytes 442376 | tf_op jit(solution)/shard_map/ppermute | solution.py:353
  73.4 14.2 %collective-permute-start.15 = (bf16[96,768]{1,0:T(8,128)(2,1)S(1)}, bf16[96,768]{1,0:T(8,128)(2,1)S(1)}, u32[]{:S(2)}, u32[]{:S(2)}) collective-permute-start(bf16[96,768]{1,0:T(8,128)(2,1)S(1)} %get-tuple-element.71), channel_id=1, source_target_pairs={{0,2},{1,3},{2,0},{3,1},{4,6},{5,7},{6,4},{7,5},{8,10},{9,11},{10,... | collective-permute-start | bytes 442376 | tf_op jit(solution)/shard_map/ppermute | solution.py:353
  75.2 12.6 %collective-permute-start.16 = (bf16[96,768]{1,0:T(8,128)(2,1)S(1)}, bf16[96,768]{1,0:T(8,128)(2,1)S(1)}, u32[]{:S(2)}, u32[]{:S(2)}) collective-permute-start(bf16[96,768]{1,0:T(8,128)(2,1)S(1)} %get-tuple-element.72), channel_id=1, source_target_pairs={{0,6},{1,7},{2,4},{3,5},{4,2},{5,3},{6,0},{7,1},{8,14},{9,15},{10,... | collective-permute-start | bytes 442376 | tf_op jit(solution)/shard_map/ppermute | solution.py:353
  78.3 12.0 %collective-permute-start.17 = (bf16[96,768]{1,0:T(8,128)(2,1)S(1)}, bf16[96,768]{1,0:T(8,128)(2,1)S(1)}, u32[]{:S(2)}, u32[]{:S(2)}) collective-permute-start(bf16[96,768]{1,0:T(8,128)(2,1)S(1)} %get-tuple-element.73), channel_id=1, source_target_pairs={{0,5},{1,4},{2,7},{3,6},{4,1},{5,0},{6,3},{7,2},{8,13},{9,12},{10,... | collective-permute-start | bytes 442376 | tf_op jit(solution)/shard_map/ppermute | solution.py:353
  78.5 12.8 %collective-permute-start.18 = (bf16[96,768]{1,0:T(8,128)(2,1)S(1)}, bf16[96,768]{1,0:T(8,128)(2,1)S(1)}, u32[]{:S(2)}, u32[]{:S(2)}) collective-permute-start(bf16[96,768]{1,0:T(8,128)(2,1)S(1)} %get-tuple-element.74), channel_id=1, source_target_pairs={{0,7},{1,6},{2,5},{3,4},{4,3},{5,2},{6,1},{7,0},{8,15},{9,14},{10,... | collective-permute-start | bytes 442376 | tf_op jit(solution)/shard_map/ppermute | solution.py:353
  91.3 10.5 %collective-permute-start.22 = (bf16[96,768]{1,0:T(8,128)(2,1)S(1)}, bf16[96,768]{1,0:T(8,128)(2,1)S(1)}, u32[]{:S(2)}, u32[]{:S(2)}) collective-permute-start(bf16[96,768]{1,0:T(8,128)(2,1)S(1)} %get-tuple-element.88), channel_id=1, source_target_pairs={{0,4},{1,5},{2,6},{3,7},{4,0},{5,1},{6,2},{7,3},{8,12},{9,13},{10,... | collective-permute-start | bytes 442376 | tf_op jit(solution)/shard_map/ppermute | solution.py:353
  92.1 11.6 %collective-permute-start.23 = (bf16[96,768]{1,0:T(8,128)(2,1)S(1)}, bf16[96,768]{1,0:T(8,128)(2,1)S(1)}, u32[]{:S(2)}, u32[]{:S(2)}) collective-permute-start(bf16[96,768]{1,0:T(8,128)(2,1)S(1)} %get-tuple-element.89), channel_id=1, source_target_pairs={{0,1},{1,0},{2,3},{3,2},{4,5},{5,4},{6,7},{7,6},{8,9},{9,8},{10,11... | collective-permute-start | bytes 442376 | tf_op jit(solution)/shard_map/ppermute | solution.py:353
  92.1 14.0 %collective-permute-start.24 = (bf16[96,768]{1,0:T(8,128)(2,1)S(1)}, bf16[96,768]{1,0:T(8,128)(2,1)S(1)}, u32[]{:S(2)}, u32[]{:S(2)}) collective-permute-start(bf16[96,768]{1,0:T(8,128)(2,1)S(1)} %get-tuple-element.90), channel_id=1, source_target_pairs={{0,3},{1,2},{2,1},{3,0},{4,7},{5,6},{6,5},{7,4},{8,11},{9,10},{10,... | collective-permute-start | bytes 442376 | tf_op jit(solution)/shard_map/ppermute | solution.py:353
  98.1 8.4 %collective-permute-start.25 = (bf16[96,768]{1,0:T(8,128)(2,1)S(1)}, bf16[96,768]{1,0:T(8,128)(2,1)S(1)}, u32[]{:S(2)}, u32[]{:S(2)}) collective-permute-start(bf16[96,768]{1,0:T(8,128)(2,1)S(1)} %get-tuple-element.95), channel_id=1, source_target_pairs={{0,2},{1,3},{2,0},{3,1},{4,6},{5,7},{6,4},{7,5},{8,10},{9,11},{10,... | collective-permute-start | bytes 442376 | tf_op jit(solution)/shard_map/ppermute | solution.py:353
  100.4 10.6 %collective-permute-start.26 = (bf16[96,768]{1,0:T(8,128)(2,1)S(1)}, bf16[96,768]{1,0:T(8,128)(2,1)S(1)}, u32[]{:S(2)}, u32[]{:S(2)}) collective-permute-start(bf16[96,768]{1,0:T(8,128)(2,1)S(1)} %get-tuple-element.96), channel_id=1, source_target_pairs={{0,6},{1,7},{2,4},{3,5},{4,2},{5,3},{6,0},{7,1},{8,14},{9,15},{10,... | collective-permute-start | bytes 442376 | tf_op jit(solution)/shard_map/ppermute | solution.py:353
  101.9 11.4 %collective-permute-start.27 = (bf16[96,768]{1,0:T(8,128)(2,1)S(1)}, bf16[96,768]{1,0:T(8,128)(2,1)S(1)}, u32[]{:S(2)}, u32[]{:S(2)}) collective-permute-start(bf16[96,768]{1,0:T(8,128)(2,1)S(1)} %get-tuple-element.97), channel_id=1, source_target_pairs={{0,5},{1,4},{2,7},{3,6},{4,1},{5,0},{6,3},{7,2},{8,13},{9,12},{10,... | collective-permute-start | bytes 442376 | tf_op jit(solution)/shard_map/ppermute | solution.py:353
  103.7 10.2 %collective-permute-start.28 = (bf16[96,768]{1,0:T(8,128)(2,1)S(1)}, bf16[96,768]{1,0:T(8,128)(2,1)S(1)}, u32[]{:S(2)}, u32[]{:S(2)}) collective-permute-start(bf16[96,768]{1,0:T(8,128)(2,1)S(1)} %get-tuple-element.98), channel_id=1, source_target_pairs={{0,7},{1,6},{2,5},{3,4},{4,3},{5,2},{6,1},{7,0},{8,15},{9,14},{10,... | collective-permute-start | bytes 442376 | tf_op jit(solution)/shard_map/ppermute | solution.py:353

commit v9 on v8

--- a/solution.py
+++ b/solution.py
@@ -116,7 +116,7 @@
 
     @pl.when(step == 0)
     def _():
-        for copy in [*chunks[0], *weights, *chunks[1]]:
+        for copy in [*weights, *chunks[0]]:
             copy.start()
         for copy in weights:
             copy.wait()
@@ -124,6 +124,8 @@
         pair_weights(second_in, w2)
         for copy in chunks[0]:
             copy.wait()
+        for copy in chunks[1]:
+            copy.start()
         conv_first(0)
 
         @pl.when(place_row == 0)
@@ -155,14 +157,14 @@
         for n in range(2):
             cells = block[2 * pair + 2 + n, 0:COLS].astype(F32)
             rows[pl.ds((2 * i + n) * COLS, COLS), :] = value[:, n * CH : (n + 1) * CH] + cells
-    for line in range(8 * BAND):
-        dy, at = line % 8, pl.ds(line // 8 * 32, 32)
-        for j in range(4):
-            low = rows[pl.ds(line * COLS + j, 32, stride=8), :]
-            high = rows[pl.ds(line * COLS + 4 + j, 32, stride=8), :]
-            lanes = pl.ds(j * CH, CH)
-            keep[dy, at, lanes] = jnp.where(core == 0, low, high).astype(BF16)
-            other[dy, at, lanes] = jnp.where(core == 0, high, low).astype(BF16)
+        for line in (2 * i, 2 * i + 1):
+            dy, at = line % 8, pl.ds(line // 8 * 32, 32)
+            for j in range(4):
+                low = rows[pl.ds(line * COLS + j, 32, stride=8), :]
+                high = rows[pl.ds(line * COLS + 4 + j, 32, stride=8), :]
+                lanes = pl.ds(j * CH, CH)
+                keep[dy, at, lanes] = jnp.where(core == 0, low, high).astype(BF16)
+                other[dy, at, lanes] = jnp.where(core == 0, high, low).astype(BF16)
     if fetches:
 
         @pl.when(step == STEPS - 1)
@@ -184,7 +186,7 @@
         scratch_shapes=[
             pltpu.VMEM((ROWS + 4, WIDE, CH), BF16),
             pltpu.VMEM((ROWS + 2, WIDE, CH), BF16),
-            pltpu.VMEM((8 * BAND * COLS, CH), F32),
+            pltpu.VMEM((8 * BAND * COLS + 16, CH), F32),
             pltpu.VMEM((512, 768), BF16),
             pltpu.VMEM((512, 768), BF16),
             pltpu.VMEM((3, 3, CH, CH), BF16),
@@ -380,13 +382,15 @@
         in_hbm(conv_second),
         (in_hbm(expert_up), in_hbm(expert_down)),
     )
+    came = send(other, dc=1)
     keep, w_far, w_high_plus, w_high_minus = lax.optimization_barrier(
         (keep, w_far, w_high_plus, w_high_minus)
     )
-    last = (w_high_plus[:176], w_high_minus[176:352], w_far[352:])
-    *last, other = lax.optimization_barrier((*last, other))
-    last = [send(last[0], dx=-1), send(last[1], dx=1), send(last[2], dh=1, dl=1)]
-    came = send(other, dc=1)
+    last = [
+        send(w_high_plus[:176], dx=-1),
+        send(w_high_minus[176:352], dx=1),
+        send(w_far[352:], dh=1, dl=1),
+    ]
     order = [(a & 3) * 2 + (b & 1) for b in (high, high + 1) for a in (x, x - 1, x + 1, x + 2)]
     order = jnp.stack(order).astype(jnp.int32)
     shards = [w, w_minus, w_plus, w_far, w_high, w_high_minus, w_high_plus]

time: 115 us -> 115 us (level)
  no operation moved by 1% of the time
where the time goes in v9:
time: 115 us
  starting transfers between devices  52.6 us (46%)
  Pallas kernels  36.7 us (32%)
  waiting for transfers between devices  23.2 us (20%)
  local copies, waits for them, and re-layouts  2.25 us (2%)
    ppermute x11, starting transfers between devices, send(): return lax.ppermute(value, ('row', 'col'), hop(**step))  22.9 us
    ppermute x14, starting transfers between devices, exchange(): lax.ppermute(arrays[k], 'col', [(i, i ^ k) for i in range(8)])  21.3 us
    pallas_call x1, Pallas kernels, conv_call(): pl.pallas_call(functools.partial(conv_kernel, len(fetch)), grid=(STEPS,),...  19.7 us
    ppermute x14, waiting for transfers between devices, exchange(): lax.ppermute(arrays[k], 'col', [(i, i ^ k) for i in range(8)])  13.9 us
    ppermute x11, waiting for transfers between devices, send(): return lax.ppermute(value, ('row', 'col'), hop(**step))  8.82 us
    ppermute x4, starting transfers between devices, neighbours(): lax.ppermute(value, axis, pairs if ahead else [(j, i) for i, j in pairs])  8.43 us
    pallas_call x2, Pallas kernels, expert_call(): pl.pallas_call(expert_kernel, in_specs=[VMEM] * (count + 4), out_specs=[V...  8.31 us
    pallas_call x3, Pallas kernels, embed_call(): pl.pallas_call(functools.partial(embed_kernel, layout), in_specs=[SMEM] +...  5.17 us
  transfers between devices with their start and end apart: 29, of which 13 were waited for; matrix products, arithmetic and copies ran while one was open for 2% of the time, Pallas kernels for 28%

profile of v9, /device:TPU:0, one launch (start us, length us, event | category | flops | bytes accessed | tf_op | source)
XLA Modules:
  0.0 115.2 jit_solution(14266329194495952367)
XLA Ops:
  0.0 1.6 %collective-permute-start.2 = (bf16[512,768]{1,0:T(8,128)(2,1)}, bf16[512,768]{1,0:T(8,128)(2,1)S(1)}, u32[]{:S(2)}, u32[]{:S(2)}) collective-permute-start(bf16[512,768]{1,0:T(8,128)(2,1)} %refs_0_.5), channel_id=1, source_target_pairs={{0,32},{1,33},{2,34},{3,35},{4,36},{5,37},{6,38},{7,39},{8,40},{9,... | collective-permute-start | bytes 2359304 | tf_op jit(solution)/shard_map/ppermute | solution.py:56
  1.6 1.7 %collective-permute-start.3 = (bf16[512,768]{1,0:T(8,128)(2,1)}, bf16[512,768]{1,0:T(8,128)(2,1)S(1)}, u32[]{:S(2)}, u32[]{:S(2)}) collective-permute-start(bf16[512,768]{1,0:T(8,128)(2,1)} %refs_0_.5), channel_id=1, source_target_pairs={{0,96},{1,97},{2,98},{3,99},{4,100},{5,101},{6,102},{7,103},{8,104... | collective-permute-start | bytes 2359304 | tf_op jit(solution)/shard_map/ppermute | solution.py:56
  3.2 4.1 %collective-permute-start.4 = (bf16[512,768]{1,0:T(8,128)(2,1)}, bf16[512,768]{1,0:T(8,128)(2,1)S(1)}, u32[]{:S(2)}, u32[]{:S(2)}) collective-permute-start(bf16[512,768]{1,0:T(8,128)(2,1)} %refs_0_.5), channel_id=1, source_target_pairs={{0,20},{1,21},{2,22},{3,23},{4,16},{5,17},{6,18},{7,19},{8,28},{9,... | collective-permute-start | bytes 2359304 | tf_op jit(solution)/shard_map/ppermute | solution.py:56
  7.4 1.0 fusion.1
  8.4 1.3 %collective-permute-start = (bf16[64,2,128]{2,1,0:T(2,128)(2,1)S(1)}, bf16[64,2,128]{2,1,0:T(2,128)(2,1)S(1)}, u32[]{:S(2)}, u32[]{:S(2)}) collective-permute-start(bf16[64,2,128]{2,1,0:T(2,128)(2,1)S(1)} %get-tuple-element.93), channel_id=1, source_target_pairs={{1,0},{2,1},{3,2},{4,3},{5,4},{6,5},{7,6},{9,8},{10,9},{11,10},{12... | collective-permute-start | bytes 98312 | tf_op jit(solution)/shard_map/ppermute | solution.py:351
  9.7 4.5 %collective-permute-start.1 = (bf16[64,2,128]{2,1,0:T(2,128)(2,1)S(1)}, bf16[64,2,128]{2,1,0:T(2,128)(2,1)S(1)}, u32[]{:S(2)}, u32[]{:S(2)}) collective-permute-start(bf16[64,2,128]{2,1,0:T(2,128)(2,1)S(1)} %get-tuple-element.94), channel_id=1, source_target_pairs={{0,1},{1,2},{2,3},{3,4},{4,5},{5,6},{6,7},{8,9},{9,10},{10,11},{11... | collective-permute-start | bytes 98312 | tf_op jit(solution)/shard_map/ppermute | solution.py:351
  14.2 1.0 fusion
  15.3 0.5 collective-permute-done.1
  16.0 1.3 %collective-permute-start.5 = (bf16[2,272,128]{2,1,0:T(8,128)(2,1)S(1)}, bf16[2,272,128]{2,1,0:T(8,128)(2,1)S(1)}, u32[]{:S(2)}, u32[]{:S(2)}) collective-permute-start(bf16[2,272,128]{2,1,0:T(8,128)(2,1)S(1)} %pad_maximum_fusion.1), channel_id=1, source_target_pairs={{0,8},{8,16},{16,24},{24,32},{32,40},{40,48},{48,56},{56,64},{64,7... | collective-permute-start | bytes 417800 | tf_op jit(solution)/shard_map/ppermute | solution.py:351
  17.3 1.3 %collective-permute-start.6 = (bf16[2,272,128]{2,1,0:T(8,128)(2,1)S(1)}, bf16[2,272,128]{2,1,0:T(8,128)(2,1)S(1)}, u32[]{:S(2)}, u32[]{:S(2)}) collective-permute-start(bf16[2,272,128]{2,1,0:T(8,128)(2,1)S(1)} %pad_maximum_fusion.2), channel_id=1, source_target_pairs={{8,0},{16,8},{24,16},{32,24},{40,32},{48,40},{56,48},{64,56},{72,6... | collective-permute-start | bytes 417800 | tf_op jit(solution)/shard_map/ppermute | solution.py:351
  18.8 1.8 %collective-permute-done.2.refs_1_ = bf16[512,768]{1,0:T(8,128)(2,1)S(1)} collective-permute-done((bf16[512,768]{1,0:T(8,128)(2,1)}, bf16[512,768]{1,0:T(8,128)(2,1)S(1)}, u32[]{:S(2)}, u32[]{:S(2)}) %collective-permute-start.2) | collective-permute-done | bytes 786464 | tf_op jit(solution)/shard_map/ppermute | solution.py:56
  20.8 3.8 %collective-permute-done.4.refs_4_ = bf16[512,768]{1,0:T(8,128)(2,1)S(1)} collective-permute-done((bf16[512,768]{1,0:T(8,128)(2,1)}, bf16[512,768]{1,0:T(8,128)(2,1)S(1)}, u32[]{:S(2)}, u32[]{:S(2)}) %collective-permute-start.4) | collective-permute-done | bytes 786464 | tf_op jit(solution)/shard_map/ppermute | solution.py:56
  24.6 3.3 %collective-permute-start.7 = (bf16[512,768]{1,0:T(8,128)(2,1)S(1)}, bf16[512,768]{1,0:T(8,128)(2,1)S(1)}, u32[]{:S(2)}, u32[]{:S(2)}) collective-permute-start(bf16[512,768]{1,0:T(8,128)(2,1)S(1)} %collective-permute-done.2.refs_1_), channel_id=1, source_target_pairs={{0,32},{1,33},{2,34},{3,35},{4,36},{5,37},{6,38},{7,39},{8,40},{9,... | collective-permute-start | bytes 2359304 | tf_op jit(solution)/shard_map/ppermute | solution.py:56
  27.8 1.1 collective-permute-start.9
  29.0 3.0 %collective-permute-start.8 = (bf16[512,768]{1,0:T(8,128)(2,1)S(1)}, bf16[512,768]{1,0:T(8,128)(2,1)S(1)}, u32[]{:S(2)}, u32[]{:S(2)}) collective-permute-start(bf16[512,768]{1,0:T(8,128)(2,1)S(1)} %collective-permute-done.4.refs_4_), channel_id=1, source_target_pairs={{0,96},{1,97},{2,98},{3,99},{4,100},{5,101},{6,102},{7,103},{8,104... | collective-permute-start | bytes 2359304 | tf_op jit(solution)/shard_map/ppermute | solution.py:56
  32.0 19.7 %convs.1 = (bf16[8,256,512]{2,1,0:T(8,128)(2,1)S(1)}, bf16[8,256,512]{2,1,0:T(8,128)(2,1)S(1)}, bf16[768,3072]{1,0:T(8,128)(2,1)S(1)}, bf16[768,3072]{1,0:T(8,12...) custom-call(s32[3]{0:T(128)S(1)} %pad_add_fusion.place.where, bf16[64,256,128]{2,1,0:T(8,128)(2,1)} %scene.1, ...), custom_call_target="tpu_custom_call" | custom-call | flops 23000000512 | tf_op jit(solution)/shard_map/convs/pallas_call | solution.py:180
  51.8 1.1 collective-permute-start.11
  52.9 1.1 collective-permute-start.12
  54.0 5.7 %collective-permute-start.13 = (bf16[160,768]{1,0:T(8,128)(2,1)S(1)}, bf16[160,768]{1,0:T(8,128)(2,1)S(1)}, u32[]{:S(2)}, u32[]{:S(2)}) collective-permute-start(bf16[160,768]{1,0:T(8,128)(2,1)S(1)} %slice.35), channel_id=1, source_target_pairs={{0,20},{1,21},{2,22},{3,23},{4,16},{5,17},{6,18},{7,19},{8,28},{9,... | collective-permute-start | bytes 737288 | tf_op jit(solution)/shard_map/ppermute | solution.py:56
  59.7 2.1 %embed_own.1.own = f32[256,768]{1,0:T(8,128)S(1)} custom-call(s32[8]{0:T(128)S(1)} %stack.51.order, bf16[8,256,512]{2,1,0:T(8,128)(2,1)S(1)} %get-tuple-element.52.tokens.keep, bf16[512,768]{1,0:T(8,128)(2,1)S(1)} %copy-done, bf16[512,768]{1,0:T(8,128)(2,1)S(1)} %collective-permute-done.2.refs_1_, bf16[512,768]{1,0:T(8,128)(2,1)S(1)} %collective-permute-done.3.refs_2_, ...), custom_call_target="tpu_custom_call" | custom-call | flops 46000001024 | tf_op jit(solution)/shard_map/embed_own/pallas_call | solution.py:226
  61.9 2.1 %embed_partner.1.refs_3_ = f32[256,768]{1,0:T(8,128)S(1)} custom-call(s32[8]{0:T(128)S(1)} %stack.51.order, bf16[8,256,512]{2,1,0:T(8,128)(2,1)S(1)} %collective-permute-done.10.tokens, bf16[512,768]{1,0:T(8,128)(2,1)S(1)} %copy-done, bf16[512,768]{1,0:T(8,128)(2,1)S(1)} %collective-permute-done.2.refs_1_, ...), custom_call_target="tpu_custom_call" | custom-call | flops 3449999872 | tf_op jit(solution)/shard_map/embed_partner/pallas_call | solution.py:226
  64.0 1.3 %collective-permute-done.13.refs_2_ = bf16[160,768]{1,0:T(8,128)(2,1)S(1)} collective-permute-done((bf16[160,768]{1,0:T(8,128)(2,1)S(1)}, bf16[160,768]{1,0:T(8,128)(2,1)S(1)}, u32[]{:S(2)}, u32[]{:S(2)}) %collective-permute-start.13) | collective-permute-done | bytes 245792 | tf_op jit(solution)/shard_map/ppermute | solution.py:56
  65.3 0.9 embed_partner_last.1
  66.2 0.3 collective-permute-start.14
  66.5 1.7 %collective-permute-done.14.came = bf16[256,768]{1,0:T(8,128)(2,1)S(1)} collective-permute-done((bf16[256,768]{1,0:T(8,128)(2,1)S(1)}, bf16[256,768]{1,0:T(8,128)(2,1)S(1)}, u32[]{:S(2)}, u32[]{:S(2)}) %collective-permute-start.14) | collective-permute-done | bytes 393248 | tf_op jit(solution)/shard_map/ppermute | solution.py:56
  68.2 1.9 %route.1 = (bf16[256,768]{1,0:T(8,128)(2,1)S(1)}, f32[256,1]{1,0:T(8,128)S(1)}, s32[256,1]{1,0:T(8,128)S(1)}, bf16[96,768]{1,0:T(8,128)(2,1)S(1)}, bf16[96,768]{...) custom-call(s32[3]{0:T(128)S(1)} %pad_add_fusion.place.where, ...), custom_call_target="tpu_custom_call" | custom-call | flops 3449999872 | tf_op jit(solution)/shard_map/route/pallas_call | solution.py:282
  70.2 1.1 collective-permute-start.19
  71.2 2.4 %collective-permute-start.21 = (bf16[96,768]{1,0:T(8,128)(2,1)S(1)}, bf16[96,768]{1,0:T(8,128)(2,1)S(1)}, u32[]{:S(2)}, u32[]{:S(2)}) collective-permute-start(bf16[96,768]{1,0:T(8,128)(2,1)S(1)} %get-tuple-element.70), channel_id=1, source_target_pairs={{0,3},{1,2},{2,1},{3,0},{4,7},{5,6},{6,5},{7,4},{8,11},{9,10},{10,... | collective-permute-start | bytes 442376 | tf_op jit(solution)/shard_map/ppermute | solution.py:355
  73.6 1.7 %collective-permute-start.15 = (bf16[96,768]{1,0:T(8,128)(2,1)S(1)}, bf16[96,768]{1,0:T(8,128)(2,1)S(1)}, u32[]{:S(2)}, u32[]{:S(2)}) collective-permute-start(bf16[96,768]{1,0:T(8,128)(2,1)S(1)} %get-tuple-element.63), channel_id=1, source_target_pairs={{0,2},{1,3},{2,0},{3,1},{4,6},{5,7},{6,4},{7,5},{8,10},{9,11},{10,... | collective-permute-start | bytes 442376 | tf_op jit(solution)/shard_map/ppermute | solution.py:355
  75.3 3.2 %collective-permute-start.16 = (bf16[96,768]{1,0:T(8,128)(2,1)S(1)}, bf16[96,768]{1,0:T(8,128)(2,1)S(1)}, u32[]{:S(2)}, u32[]{:S(2)}) collective-permute-start(bf16[96,768]{1,0:T(8,128)(2,1)S(1)} %get-tuple-element.64), channel_id=1, source_target_pairs={{0,6},{1,7},{2,4},{3,5},{4,2},{5,3},{6,0},{7,1},{8,14},{9,15},{10,... | collective-permute-start | bytes 442376 | tf_op jit(solution)/shard_map/ppermute | solution.py:355
  78.5 0.2 collective-permute-start.17
  78.7 2.1 %collective-permute-start.18 = (bf16[96,768]{1,0:T(8,128)(2,1)S(1)}, bf16[96,768]{1,0:T(8,128)(2,1)S(1)}, u32[]{:S(2)}, u32[]{:S(2)}) collective-permute-start(bf16[96,768]{1,0:T(8,128)(2,1)S(1)} %get-tuple-element.66), channel_id=1, source_target_pairs={{0,7},{1,6},{2,5},{3,4},{4,3},{5,2},{6,1},{7,0},{8,15},{9,14},{10,... | collective-permute-start | bytes 442376 | tf_op jit(solution)/shard_map/ppermute | solution.py:355
  80.8 2.9 %collective-permute-done.21.refs_3_ = bf16[96,768]{1,0:T(8,128)(2,1)S(1)} collective-permute-done((bf16[96,768]{1,0:T(8,128)(2,1)S(1)}, bf16[96,768]{1,0:T(8,128)(2,1)S(1)}, u32[]{:S(2)}, u32[]{:S(2)}) %collective-permute-start.21) | collective-permute-done | bytes 147488 | tf_op jit(solution)/shard_map/ppermute | solution.py:355
  83.7 4.2 %experts_first.1 = (bf16[96,768]{1,0:T(8,128)(2,1)S(1)}, bf16[96,768]{1,0:T(8,128)(2,1)S(1)}, bf16[96,768]{1,0:T(8,128)(2,1)S(1)}, bf16[96,768]{1,0:T(8,128)(2,1)S(1)}) custom-call(bf16[96,768]{1,0:T(8,128)(2,1)S(1)} %get-tuple-element.67.refs_0_, bf16[96,768]{1,0:T(8,128)(2,1)S(1)} %collective-permute-done.19.refs_1_, ...), custom_call_target="tpu_custom_call" | custom-call | flops 5750000128 | tf_op jit(solution)/shard_map/experts_first/pallas_call | solution.py:312
  88.0 2.5 %collective-permute-done.17.refs_2_ = bf16[96,768]{1,0:T(8,128)(2,1)S(1)} collective-permute-done((bf16[96,768]{1,0:T(8,128)(2,1)S(1)}, bf16[96,768]{1,0:T(8,128)(2,1)S(1)}, u32[]{:S(2)}, u32[]{:S(2)}) %collective-permute-start.17) | collective-permute-done | bytes 147488 | tf_op jit(solution)/shard_map/ppermute | solution.py:355
  90.5 1.1 collective-permute-done.18.refs_3_
  91.5 0.7 collective-permute-start.22
  92.3 2.0 %collective-permute-start.24 = (bf16[96,768]{1,0:T(8,128)(2,1)S(1)}, bf16[96,768]{1,0:T(8,128)(2,1)S(1)}, u32[]{:S(2)}, u32[]{:S(2)}) collective-permute-start(bf16[96,768]{1,0:T(8,128)(2,1)S(1)} %get-tuple-element.82), channel_id=1, source_target_pairs={{0,3},{1,2},{2,1},{3,0},{4,7},{5,6},{6,5},{7,4},{8,11},{9,10},{10,... | collective-permute-start | bytes 442376 | tf_op jit(solution)/shard_map/ppermute | solution.py:355
  94.2 4.2 %experts_second.1 = (bf16[96,768]{1,0:T(8,128)(2,1)S(1)}, bf16[96,768]{1,0:T(8,128)(2,1)S(1)}, bf16[96,768]{1,0:T(8,128)(2,1)S(1)}, bf16[96,768]{1,0:T(8,128)(2,1)S(1)}) custom-call(bf16[96,768]{1,0:T(8,128)(2,1)S(1)} %collective-permute-done.15.refs_0_, bf16[96,768]{1,0:T(8,128)(2,1)S(1)} %collective-permute-done.16.refs_1_, ...), custom_call_target="tpu_custom_call" | custom-call | flops 5750000128 | tf_op jit(solution)/shard_map/experts_second/pallas_call | solution.py:312
  98.4 2.2 %collective-permute-start.25 = (bf16[96,768]{1,0:T(8,128)(2,1)S(1)}, bf16[96,768]{1,0:T(8,128)(2,1)S(1)}, u32[]{:S(2)}, u32[]{:S(2)}) collective-permute-start(bf16[96,768]{1,0:T(8,128)(2,1)S(1)} %get-tuple-element.87), channel_id=1, source_target_pairs={{0,2},{1,3},{2,0},{3,1},{4,6},{5,7},{6,4},{7,5},{8,10},{9,11},{10,... | collective-permute-start | bytes 442376 | tf_op jit(solution)/shard_map/ppermute | solution.py:355
  100.6 1.5 %collective-permute-start.26 = (bf16[96,768]{1,0:T(8,128)(2,1)S(1)}, bf16[96,768]{1,0:T(8,128)(2,1)S(1)}, u32[]{:S(2)}, u32[]{:S(2)}) collective-permute-start(bf16[96,768]{1,0:T(8,128)(2,1)S(1)} %get-tuple-element.88), channel_id=1, source_target_pairs={{0,6},{1,7},{2,4},{3,5},{4,2},{5,3},{6,0},{7,1},{8,14},{9,15},{10,... | collective-permute-start | bytes 442376 | tf_op jit(solution)/shard_map/ppermute | solution.py:355
  102.1 1.7 %collective-permute-start.27 = (bf16[96,768]{1,0:T(8,128)(2,1)S(1)}, bf16[96,768]{1,0:T(8,128)(2,1)S(1)}, u32[]{:S(2)}, u32[]{:S(2)}) collective-permute-start(bf16[96,768]{1,0:T(8,128)(2,1)S(1)} %get-tuple-element.89), channel_id=1, source_target_pairs={{0,5},{1,4},{2,7},{3,6},{4,1},{5,0},{6,3},{7,2},{8,13},{9,12},{10,... | collective-permute-start | bytes 442376 | tf_op jit(solution)/shard_map/ppermute | solution.py:355
  103.8 2.5 %collective-permute-start.28 = (bf16[96,768]{1,0:T(8,128)(2,1)S(1)}, bf16[96,768]{1,0:T(8,128)(2,1)S(1)}, u32[]{:S(2)}, u32[]{:S(2)}) collective-permute-start(bf16[96,768]{1,0:T(8,128)(2,1)S(1)} %get-tuple-element.90), channel_id=1, source_target_pairs={{0,7},{1,6},{2,5},{3,4},{4,3},{5,2},{6,1},{7,0},{8,15},{9,14},{10,... | collective-permute-start | bytes 442376 | tf_op jit(solution)/shard_map/ppermute | solution.py:355
  106.3 0.4 mix_first.1.refs_0_
  106.7 4.5 %collective-permute-done.26.refs_4_ = bf16[96,768]{1,0:T(8,128)(2,1)S(1)} collective-permute-done((bf16[96,768]{1,0:T(8,128)(2,1)S(1)}, bf16[96,768]{1,0:T(8,128)(2,1)S(1)}, u32[]{:S(2)}, u32[]{:S(2)}) %collective-permute-start.26) | collective-permute-done | bytes 147488 | tf_op jit(solution)/shard_map/ppermute | solution.py:355
  111.2 2.3 %collective-permute-done.27.refs_5_ = bf16[96,768]{1,0:T(8,128)(2,1)S(1)} collective-permute-done((bf16[96,768]{1,0:T(8,128)(2,1)S(1)}, bf16[96,768]{1,0:T(8,128)(2,1)S(1)}, u32[]{:S(2)}, u32[]{:S(2)}) %collective-permute-start.27) | collective-permute-done | bytes 147488 | tf_op jit(solution)/shard_map/ppermute | solution.py:355
  113.5 0.6 collective-permute-done.28.refs_6_
  114.1 1.2 %mix_second.1 = bf16[256,768]{1,0:T(8,128)(2,1)} custom-call(f32[256,768]{1,0:T(8,128)S(1)} %mix_first.1.refs_0_, f32[256,1]{1,0:T(8,128)S(1)} %get-tuple-element.61.refs_1_, s32[256,1]{1,0:T(8,128)S(1)} %get-tuple-element.62.refs_2_, bf16[96,768]{1,0:T(8,128)(2,1)S(1)} %collective-permute-done.25.refs_3_, ...), custom_call_target="tpu_custom_call" | custom-call | flops 2300000000 | tf_op jit(solution)/shard_map/mix_second/pallas_call | solution.py:337
  (38 shorter events, 0.9 us)
Async XLA Ops:
  0.0 20.6 %collective-permute-start.2 = (bf16[512,768]{1,0:T(8,128)(2,1)}, bf16[512,768]{1,0:T(8,128)(2,1)S(1)}, u32[]{:S(2)}, u32[]{:S(2)}) collective-permute-start(bf16[512,768]{1,0:T(8,128)(2,1)} %refs_0_.5), channel_id=1, source_target_pairs={{0,32},{1,33},{2,34},{3,35},{4,36},{5,37},{6,38},{7,39},{8,40},{9,... | collective-permute-start | bytes 2359304 | tf_op jit(solution)/shard_map/ppermute | solution.py:56
  1.6 19.2 %collective-permute-start.3 = (bf16[512,768]{1,0:T(8,128)(2,1)}, bf16[512,768]{1,0:T(8,128)(2,1)S(1)}, u32[]{:S(2)}, u32[]{:S(2)}) collective-permute-start(bf16[512,768]{1,0:T(8,128)(2,1)} %refs_0_.5), channel_id=1, source_target_pairs={{0,96},{1,97},{2,98},{3,99},{4,100},{5,101},{6,102},{7,103},{8,104... | collective-permute-start | bytes 2359304 | tf_op jit(solution)/shard_map/ppermute | solution.py:56
  3.2 21.4 %collective-permute-start.4 = (bf16[512,768]{1,0:T(8,128)(2,1)}, bf16[512,768]{1,0:T(8,128)(2,1)S(1)}, u32[]{:S(2)}, u32[]{:S(2)}) collective-permute-start(bf16[512,768]{1,0:T(8,128)(2,1)} %refs_0_.5), channel_id=1, source_target_pairs={{0,20},{1,21},{2,22},{3,23},{4,16},{5,17},{6,18},{7,19},{8,28},{9,... | collective-permute-start | bytes 2359304 | tf_op jit(solution)/shard_map/ppermute | solution.py:56
  8.4 6.9 %collective-permute-start = (bf16[64,2,128]{2,1,0:T(2,128)(2,1)S(1)}, bf16[64,2,128]{2,1,0:T(2,128)(2,1)S(1)}, u32[]{:S(2)}, u32[]{:S(2)}) collective-permute-start(bf16[64,2,128]{2,1,0:T(2,128)(2,1)S(1)} %get-tuple-element.93), channel_id=1, source_target_pairs={{1,0},{2,1},{3,2},{4,3},{5,4},{6,5},{7,6},{9,8},{10,9},{11,10},{12... | collective-permute-start | bytes 98312 | tf_op jit(solution)/shard_map/ppermute | solution.py:351
  9.7 6.1 %collective-permute-start.1 = (bf16[64,2,128]{2,1,0:T(2,128)(2,1)S(1)}, bf16[64,2,128]{2,1,0:T(2,128)(2,1)S(1)}, u32[]{:S(2)}, u32[]{:S(2)}) collective-permute-start(bf16[64,2,128]{2,1,0:T(2,128)(2,1)S(1)} %get-tuple-element.94), channel_id=1, source_target_pairs={{0,1},{1,2},{2,3},{3,4},{4,5},{5,6},{6,7},{8,9},{9,10},{10,11},{11... | collective-permute-start | bytes 98312 | tf_op jit(solution)/shard_map/ppermute | solution.py:351
  16.0 16.0 %collective-permute-start.5 = (bf16[2,272,128]{2,1,0:T(8,128)(2,1)S(1)}, bf16[2,272,128]{2,1,0:T(8,128)(2,1)S(1)}, u32[]{:S(2)}, u32[]{:S(2)}) collective-permute-start(bf16[2,272,128]{2,1,0:T(8,128)(2,1)S(1)} %pad_maximum_fusion.1), channel_id=1, source_target_pairs={{0,8},{8,16},{16,24},{24,32},{32,40},{40,48},{48,56},{56,64},{64,7... | collective-permute-start | bytes 417800 | tf_op jit(solution)/shard_map/ppermute | solution.py:351
  17.3 14.7 %collective-permute-start.6 = (bf16[2,272,128]{2,1,0:T(8,128)(2,1)S(1)}, bf16[2,272,128]{2,1,0:T(8,128)(2,1)S(1)}, u32[]{:S(2)}, u32[]{:S(2)}) collective-permute-start(bf16[2,272,128]{2,1,0:T(8,128)(2,1)S(1)} %pad_maximum_fusion.2), channel_id=1, source_target_pairs={{8,0},{16,8},{24,16},{32,24},{40,32},{48,40},{56,48},{64,56},{72,6... | collective-permute-start | bytes 417800 | tf_op jit(solution)/shard_map/ppermute | solution.py:351
  18.8 40.9 %copy-start = (bf16[512,768]{1,0:T(8,128)(2,1)S(1)}, bf16[512,768]{1,0:T(8,128)(2,1)}, u32[]{:S(2)}) copy-start(bf16[512,768]{1,0:T(8,128)(2,1)} %refs_0_.5) | copy-start | bytes 2359300
  24.6 27.2 %collective-permute-start.7 = (bf16[512,768]{1,0:T(8,128)(2,1)S(1)}, bf16[512,768]{1,0:T(8,128)(2,1)S(1)}, u32[]{:S(2)}, u32[]{:S(2)}) collective-permute-start(bf16[512,768]{1,0:T(8,128)(2,1)S(1)} %collective-permute-done.2.refs_1_), channel_id=1, source_target_pairs={{0,32},{1,33},{2,34},{3,35},{4,36},{5,37},{6,38},{7,39},{8,40},{9,... | collective-permute-start | bytes 2359304 | tf_op jit(solution)/shard_map/ppermute | solution.py:56
  27.8 23.9 %collective-permute-start.9 = (bf16[512,768]{1,0:T(8,128)(2,1)S(1)}, bf16[512,768]{1,0:T(8,128)(2,1)S(1)}, u32[]{:S(2)}, u32[]{:S(2)}) collective-permute-start(bf16[512,768]{1,0:T(8,128)(2,1)S(1)} %collective-permute-done.2.refs_1_), channel_id=1, source_target_pairs={{0,20},{1,21},{2,22},{3,23},{4,16},{5,17},{6,18},{7,19},{8,28},{9,... | collective-permute-start | bytes 2359304 | tf_op jit(solution)/shard_map/ppermute | solution.py:56
  29.0 22.8 %collective-permute-start.8 = (bf16[512,768]{1,0:T(8,128)(2,1)S(1)}, bf16[512,768]{1,0:T(8,128)(2,1)S(1)}, u32[]{:S(2)}, u32[]{:S(2)}) collective-permute-start(bf16[512,768]{1,0:T(8,128)(2,1)S(1)} %collective-permute-done.4.refs_4_), channel_id=1, source_target_pairs={{0,96},{1,97},{2,98},{3,99},{4,100},{5,101},{6,102},{7,103},{8,104... | collective-permute-start | bytes 2359304 | tf_op jit(solution)/shard_map/ppermute | solution.py:56
  51.7 10.2 %collective-permute-start.10 = (bf16[8,256,512]{2,1,0:T(8,128)(2,1)S(1)}, bf16[8,256,512]{2,1,0:T(8,128)(2,1)S(1)}, u32[]{:S(2)}, u32[]{:S(2)}) collective-permute-start(bf16[8,256,512]{2,1,0:T(8,128)(2,1)S(1)} %get-tuple-element.57), channel_id=1, source_target_pairs={{0,8},{1,9},{2,10},{3,11},{4,12},{5,13},{6,14},{7,15},{8,0},{9,1},... | collective-permute-start | bytes 6291464 | tf_op jit(solution)/shard_map/ppermute | solution.py:56
  51.8 13.5 %collective-permute-start.11 = (bf16[176,768]{1,0:T(8,128)(2,1)S(1)}, bf16[176,768]{1,0:T(8,128)(2,1)S(1)}, u32[]{:S(2)}, u32[]{:S(2)}) collective-permute-start(bf16[176,768]{1,0:T(8,128)(2,1)S(1)} %slice.33), channel_id=1, source_target_pairs={{0,96},{1,97},{2,98},{3,99},{4,100},{5,101},{6,102},{7,103},{8,104... | collective-permute-start | bytes 811016 | tf_op jit(solution)/shard_map/ppermute | solution.py:56
  52.9 12.4 %collective-permute-start.12 = (bf16[176,768]{1,0:T(8,128)(2,1)S(1)}, bf16[176,768]{1,0:T(8,128)(2,1)S(1)}, u32[]{:S(2)}, u32[]{:S(2)}) collective-permute-start(bf16[176,768]{1,0:T(8,128)(2,1)S(1)} %slice.34), channel_id=1, source_target_pairs={{0,32},{1,33},{2,34},{3,35},{4,36},{5,37},{6,38},{7,39},{8,40},{9,... | collective-permute-start | bytes 811016 | tf_op jit(solution)/shard_map/ppermute | solution.py:56
  54.0 11.3 %collective-permute-start.13 = (bf16[160,768]{1,0:T(8,128)(2,1)S(1)}, bf16[160,768]{1,0:T(8,128)(2,1)S(1)}, u32[]{:S(2)}, u32[]{:S(2)}) collective-permute-start(bf16[160,768]{1,0:T(8,128)(2,1)S(1)} %slice.35), channel_id=1, source_target_pairs={{0,20},{1,21},{2,22},{3,23},{4,16},{5,17},{6,18},{7,19},{8,28},{9,... | collective-permute-start | bytes 737288 | tf_op jit(solution)/shard_map/ppermute | solution.py:56
  64.0 4.2 %copy-start.1 = (bf16[768,16]{0,1:T(8,128)(2,1)S(1)}, bf16[768,16]{0,1:T(8,128)(2,1)}, u32[]{:S(2)}) copy-start(bf16[768,16]{0,1:T(8,128)(2,1)} %param.12) | copy-start | bytes 73732
  64.0 4.2 %copy-start.2 = (s32[1,1,256,1]{2,3,1,0:T(1,128)S(1)}, s32[1,1,256,1]{2,3,1,0:T(1,128)}, u32[]{:S(2)}) copy-start(s32[1,1,256,1]{2,3,1,0:T(1,128)} %param.13) | copy-start | bytes 3076
  66.2 2.0 %collective-permute-start.14 = (bf16[256,768]{1,0:T(8,128)(2,1)S(1)}, bf16[256,768]{1,0:T(8,128)(2,1)S(1)}, u32[]{:S(2)}, u32[]{:S(2)}) collective-permute-start(bf16[256,768]{1,0:T(8,128)(2,1)S(1)} %embed_partner_last.1), channel_id=1, source_target_pairs={{0,8},{1,9},{2,10},{3,11},{4,12},{5,13},{6,14},{7,15},{8,0},{9,1},... | collective-permute-start | bytes 1179656 | tf_op jit(solution)/shard_map/ppermute | solution.py:56
  70.2 8.4 %collective-permute-start.19 = (bf16[96,768]{1,0:T(8,128)(2,1)S(1)}, bf16[96,768]{1,0:T(8,128)(2,1)S(1)}, u32[]{:S(2)}, u32[]{:S(2)}) collective-permute-start(bf16[96,768]{1,0:T(8,128)(2,1)S(1)} %get-tuple-element.68), channel_id=1, source_target_pairs={{0,4},{1,5},{2,6},{3,7},{4,0},{5,1},{6,2},{7,3},{8,12},{9,13},{10,... | collective-permute-start | bytes 442376 | tf_op jit(solution)/shard_map/ppermute | solution.py:355
  71.2 7.5 %collective-permute-start.20 = (bf16[96,768]{1,0:T(8,128)(2,1)S(1)}, bf16[96,768]{1,0:T(8,128)(2,1)S(1)}, u32[]{:S(2)}, u32[]{:S(2)}) collective-permute-start(bf16[96,768]{1,0:T(8,128)(2,1)S(1)} %get-tuple-element.69), channel_id=1, source_target_pairs={{0,1},{1,0},{2,3},{3,2},{4,5},{5,4},{6,7},{7,6},{8,9},{9,8},{10,11... | collective-permute-start | bytes 442376 | tf_op jit(solution)/shard_map/ppermute | solution.py:355
  71.2 12.5 %collective-permute-start.21 = (bf16[96,768]{1,0:T(8,128)(2,1)S(1)}, bf16[96,768]{1,0:T(8,128)(2,1)S(1)}, u32[]{:S(2)}, u32[]{:S(2)}) collective-permute-start(bf16[96,768]{1,0:T(8,128)(2,1)S(1)} %get-tuple-element.70), channel_id=1, source_target_pairs={{0,3},{1,2},{2,1},{3,0},{4,7},{5,6},{6,5},{7,4},{8,11},{9,10},{10,... | collective-permute-start | bytes 442376 | tf_op jit(solution)/shard_map/ppermute | solution.py:355
  73.6 14.2 %collective-permute-start.15 = (bf16[96,768]{1,0:T(8,128)(2,1)S(1)}, bf16[96,768]{1,0:T(8,128)(2,1)S(1)}, u32[]{:S(2)}, u32[]{:S(2)}) collective-permute-start(bf16[96,768]{1,0:T(8,128)(2,1)S(1)} %get-tuple-element.63), channel_id=1, source_target_pairs={{0,2},{1,3},{2,0},{3,1},{4,6},{5,7},{6,4},{7,5},{8,10},{9,11},{10,... | collective-permute-start | bytes 442376 | tf_op jit(solution)/shard_map/ppermute | solution.py:355
  75.3 12.7 %collective-permute-start.16 = (bf16[96,768]{1,0:T(8,128)(2,1)S(1)}, bf16[96,768]{1,0:T(8,128)(2,1)S(1)}, u32[]{:S(2)}, u32[]{:S(2)}) collective-permute-start(bf16[96,768]{1,0:T(8,128)(2,1)S(1)} %get-tuple-element.64), channel_id=1, source_target_pairs={{0,6},{1,7},{2,4},{3,5},{4,2},{5,3},{6,0},{7,1},{8,14},{9,15},{10,... | collective-permute-start | bytes 442376 | tf_op jit(solution)/shard_map/ppermute | solution.py:355
  78.5 11.9 %collective-permute-start.17 = (bf16[96,768]{1,0:T(8,128)(2,1)S(1)}, bf16[96,768]{1,0:T(8,128)(2,1)S(1)}, u32[]{:S(2)}, u32[]{:S(2)}) collective-permute-start(bf16[96,768]{1,0:T(8,128)(2,1)S(1)} %get-tuple-element.65), channel_id=1, source_target_pairs={{0,5},{1,4},{2,7},{3,6},{4,1},{5,0},{6,3},{7,2},{8,13},{9,12},{10,... | collective-permute-start | bytes 442376 | tf_op jit(solution)/shard_map/ppermute | solution.py:355
  78.7 12.8 %collective-permute-start.18 = (bf16[96,768]{1,0:T(8,128)(2,1)S(1)}, bf16[96,768]{1,0:T(8,128)(2,1)S(1)}, u32[]{:S(2)}, u32[]{:S(2)}) collective-permute-start(bf16[96,768]{1,0:T(8,128)(2,1)S(1)} %get-tuple-element.66), channel_id=1, source_target_pairs={{0,7},{1,6},{2,5},{3,4},{4,3},{5,2},{6,1},{7,0},{8,15},{9,14},{10,... | collective-permute-start | bytes 442376 | tf_op jit(solution)/shard_map/ppermute | solution.py:355
  91.5 10.6 %collective-permute-start.22 = (bf16[96,768]{1,0:T(8,128)(2,1)S(1)}, bf16[96,768]{1,0:T(8,128)(2,1)S(1)}, u32[]{:S(2)}, u32[]{:S(2)}) collective-permute-start(bf16[96,768]{1,0:T(8,128)(2,1)S(1)} %get-tuple-element.80), channel_id=1, source_target_pairs={{0,4},{1,5},{2,6},{3,7},{4,0},{5,1},{6,2},{7,3},{8,12},{9,13},{10,... | collective-permute-start | bytes 442376 | tf_op jit(solution)/shard_map/ppermute | solution.py:355
  92.2 11.6 %collective-permute-start.23 = (bf16[96,768]{1,0:T(8,128)(2,1)S(1)}, bf16[96,768]{1,0:T(8,128)(2,1)S(1)}, u32[]{:S(2)}, u32[]{:S(2)}) collective-permute-start(bf16[96,768]{1,0:T(8,128)(2,1)S(1)} %get-tuple-element.81), channel_id=1, source_target_pairs={{0,1},{1,0},{2,3},{3,2},{4,5},{5,4},{6,7},{7,6},{8,9},{9,8},{10,11... | collective-permute-start | bytes 442376 | tf_op jit(solution)/shard_map/ppermute | solution.py:355
  92.3 14.1 %collective-permute-start.24 = (bf16[96,768]{1,0:T(8,128)(2,1)S(1)}, bf16[96,768]{1,0:T(8,128)(2,1)S(1)}, u32[]{:S(2)}, u32[]{:S(2)}) collective-permute-start(bf16[96,768]{1,0:T(8,128)(2,1)S(1)} %get-tuple-element.82), channel_id=1, source_target_pairs={{0,3},{1,2},{2,1},{3,0},{4,7},{5,6},{6,5},{7,4},{8,11},{9,10},{10,... | collective-permute-start | bytes 442376 | tf_op jit(solution)/shard_map/ppermute | solution.py:355
  98.4 8.4 %collective-permute-start.25 = (bf16[96,768]{1,0:T(8,128)(2,1)S(1)}, bf16[96,768]{1,0:T(8,128)(2,1)S(1)}, u32[]{:S(2)}, u32[]{:S(2)}) collective-permute-start(bf16[96,768]{1,0:T(8,128)(2,1)S(1)} %get-tuple-element.87), channel_id=1, source_target_pairs={{0,2},{1,3},{2,0},{3,1},{4,6},{5,7},{6,4},{7,5},{8,10},{9,11},{10,... | collective-permute-start | bytes 442376 | tf_op jit(solution)/shard_map/ppermute | solution.py:355
  100.6 10.6 %collective-permute-start.26 = (bf16[96,768]{1,0:T(8,128)(2,1)S(1)}, bf16[96,768]{1,0:T(8,128)(2,1)S(1)}, u32[]{:S(2)}, u32[]{:S(2)}) collective-permute-start(bf16[96,768]{1,0:T(8,128)(2,1)S(1)} %get-tuple-element.88), channel_id=1, source_target_pairs={{0,6},{1,7},{2,4},{3,5},{4,2},{5,3},{6,0},{7,1},{8,14},{9,15},{10,... | collective-permute-start | bytes 442376 | tf_op jit(solution)/shard_map/ppermute | solution.py:355
  102.1 11.4 %collective-permute-start.27 = (bf16[96,768]{1,0:T(8,128)(2,1)S(1)}, bf16[96,768]{1,0:T(8,128)(2,1)S(1)}, u32[]{:S(2)}, u32[]{:S(2)}) collective-permute-start(bf16[96,768]{1,0:T(8,128)(2,1)S(1)} %get-tuple-element.89), channel_id=1, source_target_pairs={{0,5},{1,4},{2,7},{3,6},{4,1},{5,0},{6,3},{7,2},{8,13},{9,12},{10,... | collective-permute-start | bytes 442376 | tf_op jit(solution)/shard_map/ppermute | solution.py:355
  103.8 10.3 %collective-permute-start.28 = (bf16[96,768]{1,0:T(8,128)(2,1)S(1)}, bf16[96,768]{1,0:T(8,128)(2,1)S(1)}, u32[]{:S(2)}, u32[]{:S(2)}) collective-permute-start(bf16[96,768]{1,0:T(8,128)(2,1)S(1)} %get-tuple-element.90), channel_id=1, source_target_pairs={{0,7},{1,6},{2,5},{3,4},{4,3},{5,2},{6,1},{7,0},{8,15},{9,14},{10,... | collective-permute-start | bytes 442376 | tf_op jit(solution)/shard_map/ppermute | solution.py:355

commit v10 on v9

--- a/solution.py
+++ b/solution.py
@@ -235,14 +235,8 @@
     )(order, tokens, *arrays, *sums)
 
 
-def route_kernel(where, order, keep, own, came, router, ids_row, *refs):
-    pieces, (embedded, gate, place, *outs), whole = refs[:-12], refs[-12:-1], refs[-1]
-    at = 0
-    for piece in pieces:
-        whole[pl.ds(at, piece.shape[0])] = piece[...]
-        at += piece.shape[0]
-    part = jnp.dot(keep[order[7]], whole[...], preferred_element_type=F32)
-    value = (own[...] + part + came[...].astype(F32)).astype(BF16)
+def route_kernel(where, own, came, router, ids_row, embedded, gate, place, *outs):
+    value = (own[...] + came[...].astype(F32)).astype(BF16)
     embedded[...] = value
     wide = value.astype(F32)
     scale = lax.rsqrt(jnp.mean(wide * wide, axis=-1, keepdims=True) + 1e-06)
@@ -281,10 +275,9 @@
     shapes += [((PAIR, DIM), BF16)] * 8
     return pl.pallas_call(
         route_kernel,
-        in_specs=[SMEM] * 2 + [VMEM] * (len(args) - 2),
+        in_specs=[SMEM] + [VMEM] * 4,
         out_specs=[VMEM] * 11,
         out_shape=[jax.ShapeDtypeStruct(*shape) for shape in shapes],
-        scratch_shapes=[pltpu.VMEM((512, DIM), BF16)],
         compiler_params=params(16),
         cost_estimate=cost(3),
         name="route",
@@ -400,8 +393,9 @@
     partner = embed_call("embed_partner", order, came, shards)
     partner = embed_call("embed_partner_last", order, came, [(7, last)], [partner], BF16)
     came = send(partner, dc=1)
+    own = embed_call("embed_own_last", order, keep, [(7, last)], [own])
     embedded, gate, slots, *outs = route_call(
-        place, order, keep, own, came, router_weight.T, expert_ids.reshape(1, TOK), *last
+        place, own, came, router_weight.T, expert_ids.reshape(1, TOK)
     )
     first, second, weights = (4, 1, 3), (2, 6, 5, 7), (up0, up1, down0, down1)
     in_first, in_second = exchange(outs, first), exchange(outs, second)

time: 115 us -> 115 us (level)
    pallas_call x3 -> x4, Pallas kernels: 5.17 us -> 6.08 us  [embed_call(): pl.pallas_call(functools.partial(embed_kernel, layout), in_specs=[SMEM] +...]
  transfers between devices with their start and end apart: 29 -> 29, of which waited for: 13 -> 12; matrix products, arithmetic and copies ran while one was open for 2% -> 2% of each run, Pallas kernels for 28% -> 29%
where the time goes in v10:
time: 115 us
  starting transfers between devices  52.6 us (46%)
  Pallas kernels  37.4 us (33%)
  waiting for transfers between devices  22.2 us (19%)
  local copies, waits for them, and re-layouts  2.25 us (2%)
    ppermute x11, starting transfers between devices, send(): return lax.ppermute(value, ('row', 'col'), hop(**step))  22.9 us
    ppermute x14, starting transfers between devices, exchange(): lax.ppermute(arrays[k], 'col', [(i, i ^ k) for i in range(8)])  21.3 us
    pallas_call x1, Pallas kernels, conv_call(): pl.pallas_call(functools.partial(conv_kernel, len(fetch)), grid=(STEPS,),...  19.7 us
    ppermute x14, waiting for transfers between devices, exchange(): lax.ppermute(arrays[k], 'col', [(i, i ^ k) for i in range(8)])  13.7 us
    pallas_call x2, Pallas kernels, expert_call(): pl.pallas_call(expert_kernel, in_specs=[VMEM] * (count + 4), out_specs=[V...  8.59 us
    ppermute x4, starting transfers between devices, neighbours(): lax.ppermute(value, axis, pairs if ahead else [(j, i) for i, j in pairs])  8.43 us
    ppermute x11, waiting for transfers between devices, send(): return lax.ppermute(value, ('row', 'col'), hop(**step))  7.92 us
    pallas_call x4, Pallas kernels, embed_call(): pl.pallas_call(functools.partial(embed_kernel, layout), in_specs=[SMEM] +...  6.08 us
  transfers between devices with their start and end apart: 29, of which 12 were waited for; matrix products, arithmetic and copies ran while one was open for 2% of the time, Pallas kernels for 29%

profile of v10, /device:TPU:0, one launch (start us, length us, event | category | flops | bytes accessed | tf_op | source)
XLA Modules:
  0.0 114.9 jit_solution(18204901553314325074)
XLA Ops:
  0.0 1.6 %collective-permute-start.2 = (bf16[512,768]{1,0:T(8,128)(2,1)}, bf16[512,768]{1,0:T(8,128)(2,1)S(1)}, u32[]{:S(2)}, u32[]{:S(2)}) collective-permute-start(bf16[512,768]{1,0:T(8,128)(2,1)} %refs_0_.5), channel_id=1, source_target_pairs={{0,32},{1,33},{2,34},{3,35},{4,36},{5,37},{6,38},{7,39},{8,40},{9,... | collective-permute-start | bytes 2359304 | tf_op jit(solution)/shard_map/ppermute | solution.py:56
  1.6 1.7 %collective-permute-start.3 = (bf16[512,768]{1,0:T(8,128)(2,1)}, bf16[512,768]{1,0:T(8,128)(2,1)S(1)}, u32[]{:S(2)}, u32[]{:S(2)}) collective-permute-start(bf16[512,768]{1,0:T(8,128)(2,1)} %refs_0_.5), channel_id=1, source_target_pairs={{0,96},{1,97},{2,98},{3,99},{4,100},{5,101},{6,102},{7,103},{8,104... | collective-permute-start | bytes 2359304 | tf_op jit(solution)/shard_map/ppermute | solution.py:56
  3.2 4.1 %collective-permute-start.4 = (bf16[512,768]{1,0:T(8,128)(2,1)}, bf16[512,768]{1,0:T(8,128)(2,1)S(1)}, u32[]{:S(2)}, u32[]{:S(2)}) collective-permute-start(bf16[512,768]{1,0:T(8,128)(2,1)} %refs_0_.5), channel_id=1, source_target_pairs={{0,20},{1,21},{2,22},{3,23},{4,16},{5,17},{6,18},{7,19},{8,28},{9,... | collective-permute-start | bytes 2359304 | tf_op jit(solution)/shard_map/ppermute | solution.py:56
  7.4 1.0 fusion.1
  8.4 1.3 %collective-permute-start = (bf16[64,2,128]{2,1,0:T(2,128)(2,1)S(1)}, bf16[64,2,128]{2,1,0:T(2,128)(2,1)S(1)}, u32[]{:S(2)}, u32[]{:S(2)}) collective-permute-start(bf16[64,2,128]{2,1,0:T(2,128)(2,1)S(1)} %get-tuple-element.93), channel_id=1, source_target_pairs={{1,0},{2,1},{3,2},{4,3},{5,4},{6,5},{7,6},{9,8},{10,9},{11,10},{12... | collective-permute-start | bytes 98312 | tf_op jit(solution)/shard_map/ppermute | solution.py:344
  9.7 4.5 %collective-permute-start.1 = (bf16[64,2,128]{2,1,0:T(2,128)(2,1)S(1)}, bf16[64,2,128]{2,1,0:T(2,128)(2,1)S(1)}, u32[]{:S(2)}, u32[]{:S(2)}) collective-permute-start(bf16[64,2,128]{2,1,0:T(2,128)(2,1)S(1)} %get-tuple-element.94), channel_id=1, source_target_pairs={{0,1},{1,2},{2,3},{3,4},{4,5},{5,6},{6,7},{8,9},{9,10},{10,11},{11... | collective-permute-start | bytes 98312 | tf_op jit(solution)/shard_map/ppermute | solution.py:344
  14.2 1.0 fusion
  15.3 0.5 collective-permute-done.1
  16.0 1.3 %collective-permute-start.5 = (bf16[2,272,128]{2,1,0:T(8,128)(2,1)S(1)}, bf16[2,272,128]{2,1,0:T(8,128)(2,1)S(1)}, u32[]{:S(2)}, u32[]{:S(2)}) collective-permute-start(bf16[2,272,128]{2,1,0:T(8,128)(2,1)S(1)} %pad_maximum_fusion.1), channel_id=1, source_target_pairs={{0,8},{8,16},{16,24},{24,32},{32,40},{40,48},{48,56},{56,64},{64,7... | collective-permute-start | bytes 417800 | tf_op jit(solution)/shard_map/ppermute | solution.py:344
  17.3 1.3 %collective-permute-start.6 = (bf16[2,272,128]{2,1,0:T(8,128)(2,1)S(1)}, bf16[2,272,128]{2,1,0:T(8,128)(2,1)S(1)}, u32[]{:S(2)}, u32[]{:S(2)}) collective-permute-start(bf16[2,272,128]{2,1,0:T(8,128)(2,1)S(1)} %pad_maximum_fusion.2), channel_id=1, source_target_pairs={{8,0},{16,8},{24,16},{32,24},{40,32},{48,40},{56,48},{64,56},{72,6... | collective-permute-start | bytes 417800 | tf_op jit(solution)/shard_map/ppermute | solution.py:344
  18.8 1.8 %collective-permute-done.2.refs_1_ = bf16[512,768]{1,0:T(8,128)(2,1)S(1)} collective-permute-done((bf16[512,768]{1,0:T(8,128)(2,1)}, bf16[512,768]{1,0:T(8,128)(2,1)S(1)}, u32[]{:S(2)}, u32[]{:S(2)}) %collective-permute-start.2) | collective-permute-done | bytes 786464 | tf_op jit(solution)/shard_map/ppermute | solution.py:56
  20.8 3.8 %collective-permute-done.4.refs_4_ = bf16[512,768]{1,0:T(8,128)(2,1)S(1)} collective-permute-done((bf16[512,768]{1,0:T(8,128)(2,1)}, bf16[512,768]{1,0:T(8,128)(2,1)S(1)}, u32[]{:S(2)}, u32[]{:S(2)}) %collective-permute-start.4) | collective-permute-done | bytes 786464 | tf_op jit(solution)/shard_map/ppermute | solution.py:56
  24.6 3.3 %collective-permute-start.7 = (bf16[512,768]{1,0:T(8,128)(2,1)S(1)}, bf16[512,768]{1,0:T(8,128)(2,1)S(1)}, u32[]{:S(2)}, u32[]{:S(2)}) collective-permute-start(bf16[512,768]{1,0:T(8,128)(2,1)S(1)} %collective-permute-done.2.refs_1_), channel_id=1, source_target_pairs={{0,32},{1,33},{2,34},{3,35},{4,36},{5,37},{6,38},{7,39},{8,40},{9,... | collective-permute-start | bytes 2359304 | tf_op jit(solution)/shard_map/ppermute | solution.py:56
  27.8 1.1 collective-permute-start.9
  29.0 3.0 %collective-permute-start.8 = (bf16[512,768]{1,0:T(8,128)(2,1)S(1)}, bf16[512,768]{1,0:T(8,128)(2,1)S(1)}, u32[]{:S(2)}, u32[]{:S(2)}) collective-permute-start(bf16[512,768]{1,0:T(8,128)(2,1)S(1)} %collective-permute-done.4.refs_4_), channel_id=1, source_target_pairs={{0,96},{1,97},{2,98},{3,99},{4,100},{5,101},{6,102},{7,103},{8,104... | collective-permute-start | bytes 2359304 | tf_op jit(solution)/shard_map/ppermute | solution.py:56
  32.0 19.7 %convs.1 = (bf16[8,256,512]{2,1,0:T(8,128)(2,1)S(1)}, bf16[8,256,512]{2,1,0:T(8,128)(2,1)S(1)}, bf16[768,3072]{1,0:T(8,128)(2,1)S(1)}, bf16[768,3072]{1,0:T(8,12...) custom-call(s32[3]{0:T(128)S(1)} %pad_add_fusion.place.where, bf16[64,256,128]{2,1,0:T(8,128)(2,1)} %scene.1, ...), custom_call_target="tpu_custom_call" | custom-call | flops 23000000512 | tf_op jit(solution)/shard_map/convs/pallas_call | solution.py:180
  51.8 1.1 collective-permute-start.10
  52.9 1.1 collective-permute-start.11
  54.0 5.7 %collective-permute-start.12 = (bf16[160,768]{1,0:T(8,128)(2,1)S(1)}, bf16[160,768]{1,0:T(8,128)(2,1)S(1)}, u32[]{:S(2)}, u32[]{:S(2)}) collective-permute-start(bf16[160,768]{1,0:T(8,128)(2,1)S(1)} %slice.35), channel_id=1, source_target_pairs={{0,20},{1,21},{2,22},{3,23},{4,16},{5,17},{6,18},{7,19},{8,28},{9,... | collective-permute-start | bytes 737288 | tf_op jit(solution)/shard_map/ppermute | solution.py:56
  59.7 2.1 %embed_own.1.refs_3_ = f32[256,768]{1,0:T(8,128)S(1)} custom-call(s32[8]{0:T(128)S(1)} %stack.51.order, bf16[8,256,512]{2,1,0:T(8,128)(2,1)S(1)} %get-tuple-element.52.tokens, bf16[512,768]{1,0:T(8,128)(2,1)S(1)} %copy-done, bf16[512,768]{1,0:T(8,128)(2,1)S(1)} %collective-permute-done.2.refs_1_, bf16[512,768]{1,0:T(8,128)(2,1)S(1)} %collective-permute-done.3.refs_2_, ...), custom_call_target="tpu_custom_call" | custom-call | flops 46000001024 | tf_op jit(solution)/shard_map/embed_own/pallas_call | solution.py:226
  61.9 2.1 %embed_partner.1.refs_3_ = f32[256,768]{1,0:T(8,128)S(1)} custom-call(s32[8]{0:T(128)S(1)} %stack.51.order, bf16[8,256,512]{2,1,0:T(8,128)(2,1)S(1)} %collective-permute-done.13.tokens, bf16[512,768]{1,0:T(8,128)(2,1)S(1)} %copy-done, bf16[512,768]{1,0:T(8,128)(2,1)S(1)} %collective-permute-done.2.refs_1_, ...), custom_call_target="tpu_custom_call" | custom-call | flops 3449999872 | tf_op jit(solution)/shard_map/embed_partner/pallas_call | solution.py:226
  64.0 1.3 %collective-permute-done.12.refs_2_ = bf16[160,768]{1,0:T(8,128)(2,1)S(1)} collective-permute-done((bf16[160,768]{1,0:T(8,128)(2,1)S(1)}, bf16[160,768]{1,0:T(8,128)(2,1)S(1)}, u32[]{:S(2)}, u32[]{:S(2)}) %collective-permute-start.12) | collective-permute-done | bytes 245792 | tf_op jit(solution)/shard_map/ppermute | solution.py:56
  65.3 0.9 embed_partner_last.1
  66.3 0.3 collective-permute-start.14
  66.5 0.9 embed_own_last.1.own
  67.5 0.8 collective-permute-done.14.came
  68.3 1.5 %route.1 = (bf16[256,768]{1,0:T(8,128)(2,1)S(1)}, f32[256,1]{1,0:T(8,128)S(1)}, s32[256,1]{1,0:T(8,128)S(1)}, bf16[96,768]{1,0:T(8,128)(2,1)S(1)}, bf16[96,768]{...) custom-call(s32[3]{0:T(128)S(1)} %pad_add_fusion.place.where, ...), custom_call_target="tpu_custom_call" | custom-call | flops 3449999872 | tf_op jit(solution)/shard_map/route/pallas_call | solution.py:276
  69.7 1.1 collective-permute-start.19
  70.8 2.4 %collective-permute-start.21 = (bf16[96,768]{1,0:T(8,128)(2,1)S(1)}, bf16[96,768]{1,0:T(8,128)(2,1)S(1)}, u32[]{:S(2)}, u32[]{:S(2)}) collective-permute-start(bf16[96,768]{1,0:T(8,128)(2,1)S(1)} %get-tuple-element.70), channel_id=1, source_target_pairs={{0,3},{1,2},{2,1},{3,0},{4,7},{5,6},{6,5},{7,4},{8,11},{9,10},{10,... | collective-permute-start | bytes 442376 | tf_op jit(solution)/shard_map/ppermute | solution.py:348
  73.2 1.7 %collective-permute-start.15 = (bf16[96,768]{1,0:T(8,128)(2,1)S(1)}, bf16[96,768]{1,0:T(8,128)(2,1)S(1)}, u32[]{:S(2)}, u32[]{:S(2)}) collective-permute-start(bf16[96,768]{1,0:T(8,128)(2,1)S(1)} %get-tuple-element.63), channel_id=1, source_target_pairs={{0,2},{1,3},{2,0},{3,1},{4,6},{5,7},{6,4},{7,5},{8,10},{9,11},{10,... | collective-permute-start | bytes 442376 | tf_op jit(solution)/shard_map/ppermute | solution.py:348
  74.9 3.2 %collective-permute-start.16 = (bf16[96,768]{1,0:T(8,128)(2,1)S(1)}, bf16[96,768]{1,0:T(8,128)(2,1)S(1)}, u32[]{:S(2)}, u32[]{:S(2)}) collective-permute-start(bf16[96,768]{1,0:T(8,128)(2,1)S(1)} %get-tuple-element.64), channel_id=1, source_target_pairs={{0,6},{1,7},{2,4},{3,5},{4,2},{5,3},{6,0},{7,1},{8,14},{9,15},{10,... | collective-permute-start | bytes 442376 | tf_op jit(solution)/shard_map/ppermute | solution.py:348
  78.3 2.1 %collective-permute-start.18 = (bf16[96,768]{1,0:T(8,128)(2,1)S(1)}, bf16[96,768]{1,0:T(8,128)(2,1)S(1)}, u32[]{:S(2)}, u32[]{:S(2)}) collective-permute-start(bf16[96,768]{1,0:T(8,128)(2,1)S(1)} %get-tuple-element.66), channel_id=1, source_target_pairs={{0,7},{1,6},{2,5},{3,4},{4,3},{5,2},{6,1},{7,0},{8,15},{9,14},{10,... | collective-permute-start | bytes 442376 | tf_op jit(solution)/shard_map/ppermute | solution.py:348
  80.4 2.9 %collective-permute-done.21.refs_3_ = bf16[96,768]{1,0:T(8,128)(2,1)S(1)} collective-permute-done((bf16[96,768]{1,0:T(8,128)(2,1)S(1)}, bf16[96,768]{1,0:T(8,128)(2,1)S(1)}, u32[]{:S(2)}, u32[]{:S(2)}) %collective-permute-start.21) | collective-permute-done | bytes 147488 | tf_op jit(solution)/shard_map/ppermute | solution.py:348
  83.2 4.3 %experts_first.1 = (bf16[96,768]{1,0:T(8,128)(2,1)S(1)}, bf16[96,768]{1,0:T(8,128)(2,1)S(1)}, bf16[96,768]{1,0:T(8,128)(2,1)S(1)}, bf16[96,768]{1,0:T(8,128)(2,1)S(1)}) custom-call(bf16[96,768]{1,0:T(8,128)(2,1)S(1)} %get-tuple-element.67.refs_0_, bf16[96,768]{1,0:T(8,128)(2,1)S(1)} %collective-permute-done.19.refs_1_, ...), custom_call_target="tpu_custom_call" | custom-call | flops 5750000128 | tf_op jit(solution)/shard_map/experts_first/pallas_call | solution.py:305
  87.6 2.5 %collective-permute-done.17.refs_2_ = bf16[96,768]{1,0:T(8,128)(2,1)S(1)} collective-permute-done((bf16[96,768]{1,0:T(8,128)(2,1)S(1)}, bf16[96,768]{1,0:T(8,128)(2,1)S(1)}, u32[]{:S(2)}, u32[]{:S(2)}) %collective-permute-start.17) | collective-permute-done | bytes 147488 | tf_op jit(solution)/shard_map/ppermute | solution.py:348
  90.0 1.0 collective-permute-done.18.refs_3_
  91.1 0.7 collective-permute-start.22
  91.8 2.1 %collective-permute-start.24 = (bf16[96,768]{1,0:T(8,128)(2,1)S(1)}, bf16[96,768]{1,0:T(8,128)(2,1)S(1)}, u32[]{:S(2)}, u32[]{:S(2)}) collective-permute-start(bf16[96,768]{1,0:T(8,128)(2,1)S(1)} %get-tuple-element.82), channel_id=1, source_target_pairs={{0,3},{1,2},{2,1},{3,0},{4,7},{5,6},{6,5},{7,4},{8,11},{9,10},{10,... | collective-permute-start | bytes 442376 | tf_op jit(solution)/shard_map/ppermute | solution.py:348
  93.9 4.3 %experts_second.1 = (bf16[96,768]{1,0:T(8,128)(2,1)S(1)}, bf16[96,768]{1,0:T(8,128)(2,1)S(1)}, bf16[96,768]{1,0:T(8,128)(2,1)S(1)}, bf16[96,768]{1,0:T(8,128)(2,1)S(1)}) custom-call(bf16[96,768]{1,0:T(8,128)(2,1)S(1)} %collective-permute-done.15.refs_0_, bf16[96,768]{1,0:T(8,128)(2,1)S(1)} %collective-permute-done.16.refs_1_, ...), custom_call_target="tpu_custom_call" | custom-call | flops 5750000128 | tf_op jit(solution)/shard_map/experts_second/pallas_call | solution.py:305
  98.2 2.1 %collective-permute-start.25 = (bf16[96,768]{1,0:T(8,128)(2,1)S(1)}, bf16[96,768]{1,0:T(8,128)(2,1)S(1)}, u32[]{:S(2)}, u32[]{:S(2)}) collective-permute-start(bf16[96,768]{1,0:T(8,128)(2,1)S(1)} %get-tuple-element.87), channel_id=1, source_target_pairs={{0,2},{1,3},{2,0},{3,1},{4,6},{5,7},{6,4},{7,5},{8,10},{9,11},{10,... | collective-permute-start | bytes 442376 | tf_op jit(solution)/shard_map/ppermute | solution.py:348
  100.3 1.5 %collective-permute-start.26 = (bf16[96,768]{1,0:T(8,128)(2,1)S(1)}, bf16[96,768]{1,0:T(8,128)(2,1)S(1)}, u32[]{:S(2)}, u32[]{:S(2)}) collective-permute-start(bf16[96,768]{1,0:T(8,128)(2,1)S(1)} %get-tuple-element.88), channel_id=1, source_target_pairs={{0,6},{1,7},{2,4},{3,5},{4,2},{5,3},{6,0},{7,1},{8,14},{9,15},{10,... | collective-permute-start | bytes 442376 | tf_op jit(solution)/shard_map/ppermute | solution.py:348
  101.8 1.9 %collective-permute-start.27 = (bf16[96,768]{1,0:T(8,128)(2,1)S(1)}, bf16[96,768]{1,0:T(8,128)(2,1)S(1)}, u32[]{:S(2)}, u32[]{:S(2)}) collective-permute-start(bf16[96,768]{1,0:T(8,128)(2,1)S(1)} %get-tuple-element.89), channel_id=1, source_target_pairs={{0,5},{1,4},{2,7},{3,6},{4,1},{5,0},{6,3},{7,2},{8,13},{9,12},{10,... | collective-permute-start | bytes 442376 | tf_op jit(solution)/shard_map/ppermute | solution.py:348
  103.6 2.4 %collective-permute-start.28 = (bf16[96,768]{1,0:T(8,128)(2,1)S(1)}, bf16[96,768]{1,0:T(8,128)(2,1)S(1)}, u32[]{:S(2)}, u32[]{:S(2)}) collective-permute-start(bf16[96,768]{1,0:T(8,128)(2,1)S(1)} %get-tuple-element.90), channel_id=1, source_target_pairs={{0,7},{1,6},{2,5},{3,4},{4,3},{5,2},{6,1},{7,0},{8,15},{9,14},{10,... | collective-permute-start | bytes 442376 | tf_op jit(solution)/shard_map/ppermute | solution.py:348
  106.0 0.4 mix_first.1.refs_0_
  106.5 4.4 %collective-permute-done.26.refs_4_ = bf16[96,768]{1,0:T(8,128)(2,1)S(1)} collective-permute-done((bf16[96,768]{1,0:T(8,128)(2,1)S(1)}, bf16[96,768]{1,0:T(8,128)(2,1)S(1)}, u32[]{:S(2)}, u32[]{:S(2)}) %collective-permute-start.26) | collective-permute-done | bytes 147488 | tf_op jit(solution)/shard_map/ppermute | solution.py:348
  110.9 2.3 %collective-permute-done.27.refs_5_ = bf16[96,768]{1,0:T(8,128)(2,1)S(1)} collective-permute-done((bf16[96,768]{1,0:T(8,128)(2,1)S(1)}, bf16[96,768]{1,0:T(8,128)(2,1)S(1)}, u32[]{:S(2)}, u32[]{:S(2)}) %collective-permute-start.27) | collective-permute-done | bytes 147488 | tf_op jit(solution)/shard_map/ppermute | solution.py:348
  113.2 0.6 collective-permute-done.28.refs_6_
  113.8 1.2 %mix_second.1 = bf16[256,768]{1,0:T(8,128)(2,1)} custom-call(f32[256,768]{1,0:T(8,128)S(1)} %mix_first.1.refs_0_, f32[256,1]{1,0:T(8,128)S(1)} %get-tuple-element.61.refs_1_, s32[256,1]{1,0:T(8,128)S(1)} %get-tuple-element.62.refs_2_, bf16[96,768]{1,0:T(8,128)(2,1)S(1)} %collective-permute-done.25.refs_3_, ...), custom_call_target="tpu_custom_call" | custom-call | flops 2300000000 | tf_op jit(solution)/shard_map/mix_second/pallas_call | solution.py:330
  (39 shorter events, 1.0 us)
Async XLA Ops:
  0.0 20.6 %collective-permute-start.2 = (bf16[512,768]{1,0:T(8,128)(2,1)}, bf16[512,768]{1,0:T(8,128)(2,1)S(1)}, u32[]{:S(2)}, u32[]{:S(2)}) collective-permute-start(bf16[512,768]{1,0:T(8,128)(2,1)} %refs_0_.5), channel_id=1, source_target_pairs={{0,32},{1,33},{2,34},{3,35},{4,36},{5,37},{6,38},{7,39},{8,40},{9,... | collective-permute-start | bytes 2359304 | tf_op jit(solution)/shard_map/ppermute | solution.py:56
  1.6 19.2 %collective-permute-start.3 = (bf16[512,768]{1,0:T(8,128)(2,1)}, bf16[512,768]{1,0:T(8,128)(2,1)S(1)}, u32[]{:S(2)}, u32[]{:S(2)}) collective-permute-start(bf16[512,768]{1,0:T(8,128)(2,1)} %refs_0_.5), channel_id=1, source_target_pairs={{0,96},{1,97},{2,98},{3,99},{4,100},{5,101},{6,102},{7,103},{8,104... | collective-permute-start | bytes 2359304 | tf_op jit(solution)/shard_map/ppermute | solution.py:56
  3.2 21.4 %collective-permute-start.4 = (bf16[512,768]{1,0:T(8,128)(2,1)}, bf16[512,768]{1,0:T(8,128)(2,1)S(1)}, u32[]{:S(2)}, u32[]{:S(2)}) collective-permute-start(bf16[512,768]{1,0:T(8,128)(2,1)} %refs_0_.5), channel_id=1, source_target_pairs={{0,20},{1,21},{2,22},{3,23},{4,16},{5,17},{6,18},{7,19},{8,28},{9,... | collective-permute-start | bytes 2359304 | tf_op jit(solution)/shard_map/ppermute | solution.py:56
  8.4 6.9 %collective-permute-start = (bf16[64,2,128]{2,1,0:T(2,128)(2,1)S(1)}, bf16[64,2,128]{2,1,0:T(2,128)(2,1)S(1)}, u32[]{:S(2)}, u32[]{:S(2)}) collective-permute-start(bf16[64,2,128]{2,1,0:T(2,128)(2,1)S(1)} %get-tuple-element.93), channel_id=1, source_target_pairs={{1,0},{2,1},{3,2},{4,3},{5,4},{6,5},{7,6},{9,8},{10,9},{11,10},{12... | collective-permute-start | bytes 98312 | tf_op jit(solution)/shard_map/ppermute | solution.py:344
  9.7 6.1 %collective-permute-start.1 = (bf16[64,2,128]{2,1,0:T(2,128)(2,1)S(1)}, bf16[64,2,128]{2,1,0:T(2,128)(2,1)S(1)}, u32[]{:S(2)}, u32[]{:S(2)}) collective-permute-start(bf16[64,2,128]{2,1,0:T(2,128)(2,1)S(1)} %get-tuple-element.94), channel_id=1, source_target_pairs={{0,1},{1,2},{2,3},{3,4},{4,5},{5,6},{6,7},{8,9},{9,10},{10,11},{11... | collective-permute-start | bytes 98312 | tf_op jit(solution)/shard_map/ppermute | solution.py:344
  16.0 16.0 %collective-permute-start.5 = (bf16[2,272,128]{2,1,0:T(8,128)(2,1)S(1)}, bf16[2,272,128]{2,1,0:T(8,128)(2,1)S(1)}, u32[]{:S(2)}, u32[]{:S(2)}) collective-permute-start(bf16[2,272,128]{2,1,0:T(8,128)(2,1)S(1)} %pad_maximum_fusion.1), channel_id=1, source_target_pairs={{0,8},{8,16},{16,24},{24,32},{32,40},{40,48},{48,56},{56,64},{64,7... | collective-permute-start | bytes 417800 | tf_op jit(solution)/shard_map/ppermute | solution.py:344
  17.3 14.7 %collective-permute-start.6 = (bf16[2,272,128]{2,1,0:T(8,128)(2,1)S(1)}, bf16[2,272,128]{2,1,0:T(8,128)(2,1)S(1)}, u32[]{:S(2)}, u32[]{:S(2)}) collective-permute-start(bf16[2,272,128]{2,1,0:T(8,128)(2,1)S(1)} %pad_maximum_fusion.2), channel_id=1, source_target_pairs={{8,0},{16,8},{24,16},{32,24},{40,32},{48,40},{56,48},{64,56},{72,6... | collective-permute-start | bytes 417800 | tf_op jit(solution)/shard_map/ppermute | solution.py:344
  18.8 40.9 %copy-start = (bf16[512,768]{1,0:T(8,128)(2,1)S(1)}, bf16[512,768]{1,0:T(8,128)(2,1)}, u32[]{:S(2)}) copy-start(bf16[512,768]{1,0:T(8,128)(2,1)} %refs_0_.5) | copy-start | bytes 2359300
  24.6 27.2 %collective-permute-start.7 = (bf16[512,768]{1,0:T(8,128)(2,1)S(1)}, bf16[512,768]{1,0:T(8,128)(2,1)S(1)}, u32[]{:S(2)}, u32[]{:S(2)}) collective-permute-start(bf16[512,768]{1,0:T(8,128)(2,1)S(1)} %collective-permute-done.2.refs_1_), channel_id=1, source_target_pairs={{0,32},{1,33},{2,34},{3,35},{4,36},{5,37},{6,38},{7,39},{8,40},{9,... | collective-permute-start | bytes 2359304 | tf_op jit(solution)/shard_map/ppermute | solution.py:56
  27.8 23.9 %collective-permute-start.9 = (bf16[512,768]{1,0:T(8,128)(2,1)S(1)}, bf16[512,768]{1,0:T(8,128)(2,1)S(1)}, u32[]{:S(2)}, u32[]{:S(2)}) collective-permute-start(bf16[512,768]{1,0:T(8,128)(2,1)S(1)} %collective-permute-done.2.refs_1_), channel_id=1, source_target_pairs={{0,20},{1,21},{2,22},{3,23},{4,16},{5,17},{6,18},{7,19},{8,28},{9,... | collective-permute-start | bytes 2359304 | tf_op jit(solution)/shard_map/ppermute | solution.py:56
  29.0 22.8 %collective-permute-start.8 = (bf16[512,768]{1,0:T(8,128)(2,1)S(1)}, bf16[512,768]{1,0:T(8,128)(2,1)S(1)}, u32[]{:S(2)}, u32[]{:S(2)}) collective-permute-start(bf16[512,768]{1,0:T(8,128)(2,1)S(1)} %collective-permute-done.4.refs_4_), channel_id=1, source_target_pairs={{0,96},{1,97},{2,98},{3,99},{4,100},{5,101},{6,102},{7,103},{8,104... | collective-permute-start | bytes 2359304 | tf_op jit(solution)/shard_map/ppermute | solution.py:56
  51.7 10.2 %collective-permute-start.13 = (bf16[8,256,512]{2,1,0:T(8,128)(2,1)S(1)}, bf16[8,256,512]{2,1,0:T(8,128)(2,1)S(1)}, u32[]{:S(2)}, u32[]{:S(2)}) collective-permute-start(bf16[8,256,512]{2,1,0:T(8,128)(2,1)S(1)} %get-tuple-element.57), channel_id=1, source_target_pairs={{0,8},{1,9},{2,10},{3,11},{4,12},{5,13},{6,14},{7,15},{8,0},{9,1},... | collective-permute-start | bytes 6291464 | tf_op jit(solution)/shard_map/ppermute | solution.py:56
  51.8 13.5 %collective-permute-start.10 = (bf16[176,768]{1,0:T(8,128)(2,1)S(1)}, bf16[176,768]{1,0:T(8,128)(2,1)S(1)}, u32[]{:S(2)}, u32[]{:S(2)}) collective-permute-start(bf16[176,768]{1,0:T(8,128)(2,1)S(1)} %slice.33), channel_id=1, source_target_pairs={{0,96},{1,97},{2,98},{3,99},{4,100},{5,101},{6,102},{7,103},{8,104... | collective-permute-start | bytes 811016 | tf_op jit(solution)/shard_map/ppermute | solution.py:56
  52.9 12.4 %collective-permute-start.11 = (bf16[176,768]{1,0:T(8,128)(2,1)S(1)}, bf16[176,768]{1,0:T(8,128)(2,1)S(1)}, u32[]{:S(2)}, u32[]{:S(2)}) collective-permute-start(bf16[176,768]{1,0:T(8,128)(2,1)S(1)} %slice.34), channel_id=1, source_target_pairs={{0,32},{1,33},{2,34},{3,35},{4,36},{5,37},{6,38},{7,39},{8,40},{9,... | collective-permute-start | bytes 811016 | tf_op jit(solution)/shard_map/ppermute | solution.py:56
  54.0 11.3 %collective-permute-start.12 = (bf16[160,768]{1,0:T(8,128)(2,1)S(1)}, bf16[160,768]{1,0:T(8,128)(2,1)S(1)}, u32[]{:S(2)}, u32[]{:S(2)}) collective-permute-start(bf16[160,768]{1,0:T(8,128)(2,1)S(1)} %slice.35), channel_id=1, source_target_pairs={{0,20},{1,21},{2,22},{3,23},{4,16},{5,17},{6,18},{7,19},{8,28},{9,... | collective-permute-start | bytes 737288 | tf_op jit(solution)/shard_map/ppermute | solution.py:56
  66.2 2.0 %copy-start.1 = (bf16[768,16]{0,1:T(8,128)(2,1)S(1)}, bf16[768,16]{0,1:T(8,128)(2,1)}, u32[]{:S(2)}) copy-start(bf16[768,16]{0,1:T(8,128)(2,1)} %param.12) | copy-start | bytes 73732
  66.3 2.0 %copy-start.2 = (s32[1,1,256,1]{2,3,1,0:T(1,128)S(1)}, s32[1,1,256,1]{2,3,1,0:T(1,128)}, u32[]{:S(2)}) copy-start(s32[1,1,256,1]{2,3,1,0:T(1,128)} %param.13) | copy-start | bytes 3076
  66.3 2.0 %collective-permute-start.14 = (bf16[256,768]{1,0:T(8,128)(2,1)S(1)}, bf16[256,768]{1,0:T(8,128)(2,1)S(1)}, u32[]{:S(2)}, u32[]{:S(2)}) collective-permute-start(bf16[256,768]{1,0:T(8,128)(2,1)S(1)} %embed_partner_last.1), channel_id=1, source_target_pairs={{0,8},{1,9},{2,10},{3,11},{4,12},{5,13},{6,14},{7,15},{8,0},{9,1},... | collective-permute-start | bytes 1179656 | tf_op jit(solution)/shard_map/ppermute | solution.py:56
  69.7 8.4 %collective-permute-start.19 = (bf16[96,768]{1,0:T(8,128)(2,1)S(1)}, bf16[96,768]{1,0:T(8,128)(2,1)S(1)}, u32[]{:S(2)}, u32[]{:S(2)}) collective-permute-start(bf16[96,768]{1,0:T(8,128)(2,1)S(1)} %get-tuple-element.68), channel_id=1, source_target_pairs={{0,4},{1,5},{2,6},{3,7},{4,0},{5,1},{6,2},{7,3},{8,12},{9,13},{10,... | collective-permute-start | bytes 442376 | tf_op jit(solution)/shard_map/ppermute | solution.py:348
  70.8 7.5 %collective-permute-start.20 = (bf16[96,768]{1,0:T(8,128)(2,1)S(1)}, bf16[96,768]{1,0:T(8,128)(2,1)S(1)}, u32[]{:S(2)}, u32[]{:S(2)}) collective-permute-start(bf16[96,768]{1,0:T(8,128)(2,1)S(1)} %get-tuple-element.69), channel_id=1, source_target_pairs={{0,1},{1,0},{2,3},{3,2},{4,5},{5,4},{6,7},{7,6},{8,9},{9,8},{10,11... | collective-permute-start | bytes 442376 | tf_op jit(solution)/shard_map/ppermute | solution.py:348
  70.8 12.5 %collective-permute-start.21 = (bf16[96,768]{1,0:T(8,128)(2,1)S(1)}, bf16[96,768]{1,0:T(8,128)(2,1)S(1)}, u32[]{:S(2)}, u32[]{:S(2)}) collective-permute-start(bf16[96,768]{1,0:T(8,128)(2,1)S(1)} %get-tuple-element.70), channel_id=1, source_target_pairs={{0,3},{1,2},{2,1},{3,0},{4,7},{5,6},{6,5},{7,4},{8,11},{9,10},{10,... | collective-permute-start | bytes 442376 | tf_op jit(solution)/shard_map/ppermute | solution.py:348
  73.2 14.4 %collective-permute-start.15 = (bf16[96,768]{1,0:T(8,128)(2,1)S(1)}, bf16[96,768]{1,0:T(8,128)(2,1)S(1)}, u32[]{:S(2)}, u32[]{:S(2)}) collective-permute-start(bf16[96,768]{1,0:T(8,128)(2,1)S(1)} %get-tuple-element.63), channel_id=1, source_target_pairs={{0,2},{1,3},{2,0},{3,1},{4,6},{5,7},{6,4},{7,5},{8,10},{9,11},{10,... | collective-permute-start | bytes 442376 | tf_op jit(solution)/shard_map/ppermute | solution.py:348
  74.9 12.7 %collective-permute-start.16 = (bf16[96,768]{1,0:T(8,128)(2,1)S(1)}, bf16[96,768]{1,0:T(8,128)(2,1)S(1)}, u32[]{:S(2)}, u32[]{:S(2)}) collective-permute-start(bf16[96,768]{1,0:T(8,128)(2,1)S(1)} %get-tuple-element.64), channel_id=1, source_target_pairs={{0,6},{1,7},{2,4},{3,5},{4,2},{5,3},{6,0},{7,1},{8,14},{9,15},{10,... | collective-permute-start | bytes 442376 | tf_op jit(solution)/shard_map/ppermute | solution.py:348
  78.1 12.0 %collective-permute-start.17 = (bf16[96,768]{1,0:T(8,128)(2,1)S(1)}, bf16[96,768]{1,0:T(8,128)(2,1)S(1)}, u32[]{:S(2)}, u32[]{:S(2)}) collective-permute-start(bf16[96,768]{1,0:T(8,128)(2,1)S(1)} %get-tuple-element.65), channel_id=1, source_target_pairs={{0,5},{1,4},{2,7},{3,6},{4,1},{5,0},{6,3},{7,2},{8,13},{9,12},{10,... | collective-permute-start | bytes 442376 | tf_op jit(solution)/shard_map/ppermute | solution.py:348
  78.3 12.8 %collective-permute-start.18 = (bf16[96,768]{1,0:T(8,128)(2,1)S(1)}, bf16[96,768]{1,0:T(8,128)(2,1)S(1)}, u32[]{:S(2)}, u32[]{:S(2)}) collective-permute-start(bf16[96,768]{1,0:T(8,128)(2,1)S(1)} %get-tuple-element.66), channel_id=1, source_target_pairs={{0,7},{1,6},{2,5},{3,4},{4,3},{5,2},{6,1},{7,0},{8,15},{9,14},{10,... | collective-permute-start | bytes 442376 | tf_op jit(solution)/shard_map/ppermute | solution.py:348
  91.1 10.7 %collective-permute-start.22 = (bf16[96,768]{1,0:T(8,128)(2,1)S(1)}, bf16[96,768]{1,0:T(8,128)(2,1)S(1)}, u32[]{:S(2)}, u32[]{:S(2)}) collective-permute-start(bf16[96,768]{1,0:T(8,128)(2,1)S(1)} %get-tuple-element.80), channel_id=1, source_target_pairs={{0,4},{1,5},{2,6},{3,7},{4,0},{5,1},{6,2},{7,3},{8,12},{9,13},{10,... | collective-permute-start | bytes 442376 | tf_op jit(solution)/shard_map/ppermute | solution.py:348
  91.8 11.8 %collective-permute-start.23 = (bf16[96,768]{1,0:T(8,128)(2,1)S(1)}, bf16[96,768]{1,0:T(8,128)(2,1)S(1)}, u32[]{:S(2)}, u32[]{:S(2)}) collective-permute-start(bf16[96,768]{1,0:T(8,128)(2,1)S(1)} %get-tuple-element.81), channel_id=1, source_target_pairs={{0,1},{1,0},{2,3},{3,2},{4,5},{5,4},{6,7},{7,6},{8,9},{9,8},{10,11... | collective-permute-start | bytes 442376 | tf_op jit(solution)/shard_map/ppermute | solution.py:348
  91.8 14.2 %collective-permute-start.24 = (bf16[96,768]{1,0:T(8,128)(2,1)S(1)}, bf16[96,768]{1,0:T(8,128)(2,1)S(1)}, u32[]{:S(2)}, u32[]{:S(2)}) collective-permute-start(bf16[96,768]{1,0:T(8,128)(2,1)S(1)} %get-tuple-element.82), channel_id=1, source_target_pairs={{0,3},{1,2},{2,1},{3,0},{4,7},{5,6},{6,5},{7,4},{8,11},{9,10},{10,... | collective-permute-start | bytes 442376 | tf_op jit(solution)/shard_map/ppermute | solution.py:348
  98.2 8.2 %collective-permute-start.25 = (bf16[96,768]{1,0:T(8,128)(2,1)S(1)}, bf16[96,768]{1,0:T(8,128)(2,1)S(1)}, u32[]{:S(2)}, u32[]{:S(2)}) collective-permute-start(bf16[96,768]{1,0:T(8,128)(2,1)S(1)} %get-tuple-element.87), channel_id=1, source_target_pairs={{0,2},{1,3},{2,0},{3,1},{4,6},{5,7},{6,4},{7,5},{8,10},{9,11},{10,... | collective-permute-start | bytes 442376 | tf_op jit(solution)/shard_map/ppermute | solution.py:348
  100.3 10.6 %collective-permute-start.26 = (bf16[96,768]{1,0:T(8,128)(2,1)S(1)}, bf16[96,768]{1,0:T(8,128)(2,1)S(1)}, u32[]{:S(2)}, u32[]{:S(2)}) collective-permute-start(bf16[96,768]{1,0:T(8,128)(2,1)S(1)} %get-tuple-element.88), channel_id=1, source_target_pairs={{0,6},{1,7},{2,4},{3,5},{4,2},{5,3},{6,0},{7,1},{8,14},{9,15},{10,... | collective-permute-start | bytes 442376 | tf_op jit(solution)/shard_map/ppermute | solution.py:348
  101.8 11.5 %collective-permute-start.27 = (bf16[96,768]{1,0:T(8,128)(2,1)S(1)}, bf16[96,768]{1,0:T(8,128)(2,1)S(1)}, u32[]{:S(2)}, u32[]{:S(2)}) collective-permute-start(bf16[96,768]{1,0:T(8,128)(2,1)S(1)} %get-tuple-element.89), channel_id=1, source_target_pairs={{0,5},{1,4},{2,7},{3,6},{4,1},{5,0},{6,3},{7,2},{8,13},{9,12},{10,... | collective-permute-start | bytes 442376 | tf_op jit(solution)/shard_map/ppermute | solution.py:348
  103.6 10.2 %collective-permute-start.28 = (bf16[96,768]{1,0:T(8,128)(2,1)S(1)}, bf16[96,768]{1,0:T(8,128)(2,1)S(1)}, u32[]{:S(2)}, u32[]{:S(2)}) collective-permute-start(bf16[96,768]{1,0:T(8,128)(2,1)S(1)} %get-tuple-element.90), channel_id=1, source_target_pairs={{0,7},{1,6},{2,5},{3,4},{4,3},{5,2},{6,1},{7,0},{8,15},{9,14},{10,... | collective-permute-start | bytes 442376 | tf_op jit(solution)/shard_map/ppermute | solution.py:348

commit v11 on v7

--- a/solution.py
+++ b/solution.py
@@ -184,7 +184,7 @@
         scratch_shapes=[
             pltpu.VMEM((ROWS + 4, WIDE, CH), BF16),
             pltpu.VMEM((ROWS + 2, WIDE, CH), BF16),
-            pltpu.VMEM((8 * BAND * COLS, CH), F32),
+            pltpu.VMEM((8 * BAND * COLS + 16, CH), F32),
             pltpu.VMEM((512, 768), BF16),
             pltpu.VMEM((512, 768), BF16),
             pltpu.VMEM((3, 3, CH, CH), BF16),

time: 115 us -> 115 us (level)
  no operation moved by 1% of the time
where the time goes in v11:
time: 115 us
  starting transfers between devices  52.6 us (46%)
  Pallas kernels  37.4 us (33%)
  waiting for transfers between devices  22.2 us (19%)
  local copies, waits for them, and re-layouts  2.25 us (2%)
    ppermute x11, starting transfers between devices, send(): return lax.ppermute(value, ('row', 'col'), hop(**step))  23 us
    ppermute x14, starting transfers between devices, exchange(): lax.ppermute(arrays[k], 'col', [(i, i ^ k) for i in range(8)])  21.3 us
    pallas_call x1, Pallas kernels, conv_call(): pl.pallas_call(functools.partial(conv_kernel, len(fetch)), grid=(STEPS,),...  19.7 us
    ppermute x14, waiting for transfers between devices, exchange(): lax.ppermute(arrays[k], 'col', [(i, i ^ k) for i in range(8)])  13.8 us
    pallas_call x2, Pallas kernels, expert_call(): pl.pallas_call(expert_kernel, in_specs=[VMEM] * (count + 4), out_specs=[V...  8.58 us
    ppermute x4, starting transfers between devices, neighbours(): lax.ppermute(value, axis, pairs if ahead else [(j, i) for i, j in pairs])  8.43 us
    ppermute x11, waiting for transfers between devices, send(): return lax.ppermute(value, ('row', 'col'), hop(**step))  7.92 us
    pallas_call x4, Pallas kernels, embed_call(): pl.pallas_call(functools.partial(embed_kernel, layout), in_specs=[SMEM] +...  6.08 us
  transfers between devices with their start and end apart: 29, of which 12 were waited for; matrix products, arithmetic and copies ran while one was open for 2% of the time, Pallas kernels for 29%

profile of v11, /device:TPU:0, one launch (start us, length us, event | category | flops | bytes accessed | tf_op | source)
XLA Modules:
  0.0 115.0 jit_solution(11651480937998635916)
XLA Ops:
  0.0 1.6 %collective-permute-start.2 = (bf16[512,768]{1,0:T(8,128)(2,1)}, bf16[512,768]{1,0:T(8,128)(2,1)S(1)}, u32[]{:S(2)}, u32[]{:S(2)}) collective-permute-start(bf16[512,768]{1,0:T(8,128)(2,1)} %refs_0_.5), channel_id=1, source_target_pairs={{0,32},{1,33},{2,34},{3,35},{4,36},{5,37},{6,38},{7,39},{8,40},{9,... | collective-permute-start | bytes 2359304 | tf_op jit(solution)/shard_map/ppermute | solution.py:56
  1.6 1.7 %collective-permute-start.3 = (bf16[512,768]{1,0:T(8,128)(2,1)}, bf16[512,768]{1,0:T(8,128)(2,1)S(1)}, u32[]{:S(2)}, u32[]{:S(2)}) collective-permute-start(bf16[512,768]{1,0:T(8,128)(2,1)} %refs_0_.5), channel_id=1, source_target_pairs={{0,96},{1,97},{2,98},{3,99},{4,100},{5,101},{6,102},{7,103},{8,104... | collective-permute-start | bytes 2359304 | tf_op jit(solution)/shard_map/ppermute | solution.py:56
  3.2 4.1 %collective-permute-start.4 = (bf16[512,768]{1,0:T(8,128)(2,1)}, bf16[512,768]{1,0:T(8,128)(2,1)S(1)}, u32[]{:S(2)}, u32[]{:S(2)}) collective-permute-start(bf16[512,768]{1,0:T(8,128)(2,1)} %refs_0_.5), channel_id=1, source_target_pairs={{0,20},{1,21},{2,22},{3,23},{4,16},{5,17},{6,18},{7,19},{8,28},{9,... | collective-permute-start | bytes 2359304 | tf_op jit(solution)/shard_map/ppermute | solution.py:56
  7.4 1.0 fusion.1
  8.4 1.3 %collective-permute-start = (bf16[64,2,128]{2,1,0:T(2,128)(2,1)S(1)}, bf16[64,2,128]{2,1,0:T(2,128)(2,1)S(1)}, u32[]{:S(2)}, u32[]{:S(2)}) collective-permute-start(bf16[64,2,128]{2,1,0:T(2,128)(2,1)S(1)} %get-tuple-element.93), channel_id=1, source_target_pairs={{1,0},{2,1},{3,2},{4,3},{5,4},{6,5},{7,6},{9,8},{10,9},{11,10},{12... | collective-permute-start | bytes 98312 | tf_op jit(solution)/shard_map/ppermute | solution.py:342
  9.7 4.5 %collective-permute-start.1 = (bf16[64,2,128]{2,1,0:T(2,128)(2,1)S(1)}, bf16[64,2,128]{2,1,0:T(2,128)(2,1)S(1)}, u32[]{:S(2)}, u32[]{:S(2)}) collective-permute-start(bf16[64,2,128]{2,1,0:T(2,128)(2,1)S(1)} %get-tuple-element.94), channel_id=1, source_target_pairs={{0,1},{1,2},{2,3},{3,4},{4,5},{5,6},{6,7},{8,9},{9,10},{10,11},{11... | collective-permute-start | bytes 98312 | tf_op jit(solution)/shard_map/ppermute | solution.py:342
  14.2 1.0 fusion
  15.3 0.5 collective-permute-done.1
  16.0 1.3 %collective-permute-start.5 = (bf16[2,272,128]{2,1,0:T(8,128)(2,1)S(1)}, bf16[2,272,128]{2,1,0:T(8,128)(2,1)S(1)}, u32[]{:S(2)}, u32[]{:S(2)}) collective-permute-start(bf16[2,272,128]{2,1,0:T(8,128)(2,1)S(1)} %pad_maximum_fusion.1), channel_id=1, source_target_pairs={{0,8},{8,16},{16,24},{24,32},{32,40},{40,48},{48,56},{56,64},{64,7... | collective-permute-start | bytes 417800 | tf_op jit(solution)/shard_map/ppermute | solution.py:342
  17.3 1.3 %collective-permute-start.6 = (bf16[2,272,128]{2,1,0:T(8,128)(2,1)S(1)}, bf16[2,272,128]{2,1,0:T(8,128)(2,1)S(1)}, u32[]{:S(2)}, u32[]{:S(2)}) collective-permute-start(bf16[2,272,128]{2,1,0:T(8,128)(2,1)S(1)} %pad_maximum_fusion.2), channel_id=1, source_target_pairs={{8,0},{16,8},{24,16},{32,24},{40,32},{48,40},{56,48},{64,56},{72,6... | collective-permute-start | bytes 417800 | tf_op jit(solution)/shard_map/ppermute | solution.py:342
  18.8 1.8 %collective-permute-done.2.refs_1_ = bf16[512,768]{1,0:T(8,128)(2,1)S(1)} collective-permute-done((bf16[512,768]{1,0:T(8,128)(2,1)}, bf16[512,768]{1,0:T(8,128)(2,1)S(1)}, u32[]{:S(2)}, u32[]{:S(2)}) %collective-permute-start.2) | collective-permute-done | bytes 786464 | tf_op jit(solution)/shard_map/ppermute | solution.py:56
  20.8 3.8 %collective-permute-done.4.refs_4_ = bf16[512,768]{1,0:T(8,128)(2,1)S(1)} collective-permute-done((bf16[512,768]{1,0:T(8,128)(2,1)}, bf16[512,768]{1,0:T(8,128)(2,1)S(1)}, u32[]{:S(2)}, u32[]{:S(2)}) %collective-permute-start.4) | collective-permute-done | bytes 786464 | tf_op jit(solution)/shard_map/ppermute | solution.py:56
  24.6 3.3 %collective-permute-start.7 = (bf16[512,768]{1,0:T(8,128)(2,1)S(1)}, bf16[512,768]{1,0:T(8,128)(2,1)S(1)}, u32[]{:S(2)}, u32[]{:S(2)}) collective-permute-start(bf16[512,768]{1,0:T(8,128)(2,1)S(1)} %collective-permute-done.2.refs_1_), channel_id=1, source_target_pairs={{0,32},{1,33},{2,34},{3,35},{4,36},{5,37},{6,38},{7,39},{8,40},{9,... | collective-permute-start | bytes 2359304 | tf_op jit(solution)/shard_map/ppermute | solution.py:56
  27.8 1.1 collective-permute-start.9
  29.0 3.0 %collective-permute-start.8 = (bf16[512,768]{1,0:T(8,128)(2,1)S(1)}, bf16[512,768]{1,0:T(8,128)(2,1)S(1)}, u32[]{:S(2)}, u32[]{:S(2)}) collective-permute-start(bf16[512,768]{1,0:T(8,128)(2,1)S(1)} %collective-permute-done.4.refs_4_), channel_id=1, source_target_pairs={{0,96},{1,97},{2,98},{3,99},{4,100},{5,101},{6,102},{7,103},{8,104... | collective-permute-start | bytes 2359304 | tf_op jit(solution)/shard_map/ppermute | solution.py:56
  32.0 19.7 %convs.1 = (bf16[8,256,512]{2,1,0:T(8,128)(2,1)S(1)}, bf16[8,256,512]{2,1,0:T(8,128)(2,1)S(1)}, bf16[768,3072]{1,0:T(8,128)(2,1)S(1)}, bf16[768,3072]{1,0:T(8,12...) custom-call(s32[3]{0:T(128)S(1)} %pad_add_fusion.place.where, bf16[64,256,128]{2,1,0:T(8,128)(2,1)} %scene.1, ...), custom_call_target="tpu_custom_call" | custom-call | flops 23000000512 | tf_op jit(solution)/shard_map/convs/pallas_call | solution.py:178
  51.8 1.1 collective-permute-start.10
  52.9 1.1 collective-permute-start.11
  54.0 5.7 %collective-permute-start.12 = (bf16[160,768]{1,0:T(8,128)(2,1)S(1)}, bf16[160,768]{1,0:T(8,128)(2,1)S(1)}, u32[]{:S(2)}, u32[]{:S(2)}) collective-permute-start(bf16[160,768]{1,0:T(8,128)(2,1)S(1)} %slice.35), channel_id=1, source_target_pairs={{0,20},{1,21},{2,22},{3,23},{4,16},{5,17},{6,18},{7,19},{8,28},{9,... | collective-permute-start | bytes 737288 | tf_op jit(solution)/shard_map/ppermute | solution.py:56
  59.8 2.1 %embed_own.1.refs_3_ = f32[256,768]{1,0:T(8,128)S(1)} custom-call(s32[8]{0:T(128)S(1)} %stack.51.order, bf16[8,256,512]{2,1,0:T(8,128)(2,1)S(1)} %get-tuple-element.52.tokens, bf16[512,768]{1,0:T(8,128)(2,1)S(1)} %copy-done, bf16[512,768]{1,0:T(8,128)(2,1)S(1)} %collective-permute-done.2.refs_1_, bf16[512,768]{1,0:T(8,128)(2,1)S(1)} %collective-permute-done.3.refs_2_, ...), custom_call_target="tpu_custom_call" | custom-call | flops 46000001024 | tf_op jit(solution)/shard_map/embed_own/pallas_call | solution.py:224
  61.9 2.1 %embed_partner.1.refs_3_ = f32[256,768]{1,0:T(8,128)S(1)} custom-call(s32[8]{0:T(128)S(1)} %stack.51.order, bf16[8,256,512]{2,1,0:T(8,128)(2,1)S(1)} %collective-permute-done.13.tokens, bf16[512,768]{1,0:T(8,128)(2,1)S(1)} %copy-done, bf16[512,768]{1,0:T(8,128)(2,1)S(1)} %collective-permute-done.2.refs_1_, ...), custom_call_target="tpu_custom_call" | custom-call | flops 3449999872 | tf_op jit(solution)/shard_map/embed_partner/pallas_call | solution.py:224
  64.0 1.3 %collective-permute-done.12.refs_2_ = bf16[160,768]{1,0:T(8,128)(2,1)S(1)} collective-permute-done((bf16[160,768]{1,0:T(8,128)(2,1)S(1)}, bf16[160,768]{1,0:T(8,128)(2,1)S(1)}, u32[]{:S(2)}, u32[]{:S(2)}) %collective-permute-start.12) | collective-permute-done | bytes 245792 | tf_op jit(solution)/shard_map/ppermute | solution.py:56
  65.4 0.9 embed_partner_last.1
  66.3 0.3 collective-permute-start.14
  66.6 0.9 embed_own_last.1.own
  67.5 0.8 collective-permute-done.14.came
  68.3 1.5 %route.1 = (bf16[256,768]{1,0:T(8,128)(2,1)S(1)}, f32[256,1]{1,0:T(8,128)S(1)}, s32[256,1]{1,0:T(8,128)S(1)}, bf16[96,768]{1,0:T(8,128)(2,1)S(1)}, bf16[96,768]{...) custom-call(s32[3]{0:T(128)S(1)} %pad_add_fusion.place.where, ...), custom_call_target="tpu_custom_call" | custom-call | flops 3449999872 | tf_op jit(solution)/shard_map/route/pallas_call | solution.py:274
  69.8 1.0 collective-permute-start.19
  70.8 2.4 %collective-permute-start.21 = (bf16[96,768]{1,0:T(8,128)(2,1)S(1)}, bf16[96,768]{1,0:T(8,128)(2,1)S(1)}, u32[]{:S(2)}, u32[]{:S(2)}) collective-permute-start(bf16[96,768]{1,0:T(8,128)(2,1)S(1)} %get-tuple-element.70), channel_id=1, source_target_pairs={{0,3},{1,2},{2,1},{3,0},{4,7},{5,6},{6,5},{7,4},{8,11},{9,10},{10,... | collective-permute-start | bytes 442376 | tf_op jit(solution)/shard_map/ppermute | solution.py:346
  73.2 1.7 %collective-permute-start.15 = (bf16[96,768]{1,0:T(8,128)(2,1)S(1)}, bf16[96,768]{1,0:T(8,128)(2,1)S(1)}, u32[]{:S(2)}, u32[]{:S(2)}) collective-permute-start(bf16[96,768]{1,0:T(8,128)(2,1)S(1)} %get-tuple-element.63), channel_id=1, source_target_pairs={{0,2},{1,3},{2,0},{3,1},{4,6},{5,7},{6,4},{7,5},{8,10},{9,11},{10,... | collective-permute-start | bytes 442376 | tf_op jit(solution)/shard_map/ppermute | solution.py:346
  74.9 3.2 %collective-permute-start.16 = (bf16[96,768]{1,0:T(8,128)(2,1)S(1)}, bf16[96,768]{1,0:T(8,128)(2,1)S(1)}, u32[]{:S(2)}, u32[]{:S(2)}) collective-permute-start(bf16[96,768]{1,0:T(8,128)(2,1)S(1)} %get-tuple-element.64), channel_id=1, source_target_pairs={{0,6},{1,7},{2,4},{3,5},{4,2},{5,3},{6,0},{7,1},{8,14},{9,15},{10,... | collective-permute-start | bytes 442376 | tf_op jit(solution)/shard_map/ppermute | solution.py:346
  78.3 2.1 %collective-permute-start.18 = (bf16[96,768]{1,0:T(8,128)(2,1)S(1)}, bf16[96,768]{1,0:T(8,128)(2,1)S(1)}, u32[]{:S(2)}, u32[]{:S(2)}) collective-permute-start(bf16[96,768]{1,0:T(8,128)(2,1)S(1)} %get-tuple-element.66), channel_id=1, source_target_pairs={{0,7},{1,6},{2,5},{3,4},{4,3},{5,2},{6,1},{7,0},{8,15},{9,14},{10,... | collective-permute-start | bytes 442376 | tf_op jit(solution)/shard_map/ppermute | solution.py:346
  80.4 2.9 %collective-permute-done.21.refs_3_ = bf16[96,768]{1,0:T(8,128)(2,1)S(1)} collective-permute-done((bf16[96,768]{1,0:T(8,128)(2,1)S(1)}, bf16[96,768]{1,0:T(8,128)(2,1)S(1)}, u32[]{:S(2)}, u32[]{:S(2)}) %collective-permute-start.21) | collective-permute-done | bytes 147488 | tf_op jit(solution)/shard_map/ppermute | solution.py:346
  83.3 4.3 %experts_first.1 = (bf16[96,768]{1,0:T(8,128)(2,1)S(1)}, bf16[96,768]{1,0:T(8,128)(2,1)S(1)}, bf16[96,768]{1,0:T(8,128)(2,1)S(1)}, bf16[96,768]{1,0:T(8,128)(2,1)S(1)}) custom-call(bf16[96,768]{1,0:T(8,128)(2,1)S(1)} %get-tuple-element.67.refs_0_, bf16[96,768]{1,0:T(8,128)(2,1)S(1)} %collective-permute-done.19.refs_1_, ...), custom_call_target="tpu_custom_call" | custom-call | flops 5750000128 | tf_op jit(solution)/shard_map/experts_first/pallas_call | solution.py:303
  87.6 2.4 %collective-permute-done.17.refs_2_ = bf16[96,768]{1,0:T(8,128)(2,1)S(1)} collective-permute-done((bf16[96,768]{1,0:T(8,128)(2,1)S(1)}, bf16[96,768]{1,0:T(8,128)(2,1)S(1)}, u32[]{:S(2)}, u32[]{:S(2)}) %collective-permute-start.17) | collective-permute-done | bytes 147488 | tf_op jit(solution)/shard_map/ppermute | solution.py:346
  90.1 1.1 collective-permute-done.18.refs_3_
  91.1 0.7 collective-permute-start.22
  91.9 2.1 %collective-permute-start.24 = (bf16[96,768]{1,0:T(8,128)(2,1)S(1)}, bf16[96,768]{1,0:T(8,128)(2,1)S(1)}, u32[]{:S(2)}, u32[]{:S(2)}) collective-permute-start(bf16[96,768]{1,0:T(8,128)(2,1)S(1)} %get-tuple-element.82), channel_id=1, source_target_pairs={{0,3},{1,2},{2,1},{3,0},{4,7},{5,6},{6,5},{7,4},{8,11},{9,10},{10,... | collective-permute-start | bytes 442376 | tf_op jit(solution)/shard_map/ppermute | solution.py:346
  94.0 4.3 %experts_second.1 = (bf16[96,768]{1,0:T(8,128)(2,1)S(1)}, bf16[96,768]{1,0:T(8,128)(2,1)S(1)}, bf16[96,768]{1,0:T(8,128)(2,1)S(1)}, bf16[96,768]{1,0:T(8,128)(2,1)S(1)}) custom-call(bf16[96,768]{1,0:T(8,128)(2,1)S(1)} %collective-permute-done.15.refs_0_, bf16[96,768]{1,0:T(8,128)(2,1)S(1)} %collective-permute-done.16.refs_1_, ...), custom_call_target="tpu_custom_call" | custom-call | flops 5750000128 | tf_op jit(solution)/shard_map/experts_second/pallas_call | solution.py:303
  98.3 2.1 %collective-permute-start.25 = (bf16[96,768]{1,0:T(8,128)(2,1)S(1)}, bf16[96,768]{1,0:T(8,128)(2,1)S(1)}, u32[]{:S(2)}, u32[]{:S(2)}) collective-permute-start(bf16[96,768]{1,0:T(8,128)(2,1)S(1)} %get-tuple-element.87), channel_id=1, source_target_pairs={{0,2},{1,3},{2,0},{3,1},{4,6},{5,7},{6,4},{7,5},{8,10},{9,11},{10,... | collective-permute-start | bytes 442376 | tf_op jit(solution)/shard_map/ppermute | solution.py:346
  100.3 1.5 %collective-permute-start.26 = (bf16[96,768]{1,0:T(8,128)(2,1)S(1)}, bf16[96,768]{1,0:T(8,128)(2,1)S(1)}, u32[]{:S(2)}, u32[]{:S(2)}) collective-permute-start(bf16[96,768]{1,0:T(8,128)(2,1)S(1)} %get-tuple-element.88), channel_id=1, source_target_pairs={{0,6},{1,7},{2,4},{3,5},{4,2},{5,3},{6,0},{7,1},{8,14},{9,15},{10,... | collective-permute-start | bytes 442376 | tf_op jit(solution)/shard_map/ppermute | solution.py:346
  101.8 1.8 %collective-permute-start.27 = (bf16[96,768]{1,0:T(8,128)(2,1)S(1)}, bf16[96,768]{1,0:T(8,128)(2,1)S(1)}, u32[]{:S(2)}, u32[]{:S(2)}) collective-permute-start(bf16[96,768]{1,0:T(8,128)(2,1)S(1)} %get-tuple-element.89), channel_id=1, source_target_pairs={{0,5},{1,4},{2,7},{3,6},{4,1},{5,0},{6,3},{7,2},{8,13},{9,12},{10,... | collective-permute-start | bytes 442376 | tf_op jit(solution)/shard_map/ppermute | solution.py:346
  103.7 2.4 %collective-permute-start.28 = (bf16[96,768]{1,0:T(8,128)(2,1)S(1)}, bf16[96,768]{1,0:T(8,128)(2,1)S(1)}, u32[]{:S(2)}, u32[]{:S(2)}) collective-permute-start(bf16[96,768]{1,0:T(8,128)(2,1)S(1)} %get-tuple-element.90), channel_id=1, source_target_pairs={{0,7},{1,6},{2,5},{3,4},{4,3},{5,2},{6,1},{7,0},{8,15},{9,14},{10,... | collective-permute-start | bytes 442376 | tf_op jit(solution)/shard_map/ppermute | solution.py:346
  106.1 0.4 mix_first.1.refs_0_
  106.5 4.5 %collective-permute-done.26.refs_4_ = bf16[96,768]{1,0:T(8,128)(2,1)S(1)} collective-permute-done((bf16[96,768]{1,0:T(8,128)(2,1)S(1)}, bf16[96,768]{1,0:T(8,128)(2,1)S(1)}, u32[]{:S(2)}, u32[]{:S(2)}) %collective-permute-start.26) | collective-permute-done | bytes 147488 | tf_op jit(solution)/shard_map/ppermute | solution.py:346
  111.0 2.3 %collective-permute-done.27.refs_5_ = bf16[96,768]{1,0:T(8,128)(2,1)S(1)} collective-permute-done((bf16[96,768]{1,0:T(8,128)(2,1)S(1)}, bf16[96,768]{1,0:T(8,128)(2,1)S(1)}, u32[]{:S(2)}, u32[]{:S(2)}) %collective-permute-start.27) | collective-permute-done | bytes 147488 | tf_op jit(solution)/shard_map/ppermute | solution.py:346
  113.2 0.6 collective-permute-done.28.refs_6_
  113.8 1.2 %mix_second.1 = bf16[256,768]{1,0:T(8,128)(2,1)} custom-call(f32[256,768]{1,0:T(8,128)S(1)} %mix_first.1.refs_0_, f32[256,1]{1,0:T(8,128)S(1)} %get-tuple-element.61.refs_1_, s32[256,1]{1,0:T(8,128)S(1)} %get-tuple-element.62.refs_2_, bf16[96,768]{1,0:T(8,128)(2,1)S(1)} %collective-permute-done.25.refs_3_, ...), custom_call_target="tpu_custom_call" | custom-call | flops 2300000000 | tf_op jit(solution)/shard_map/mix_second/pallas_call | solution.py:328
  (39 shorter events, 1.0 us)
Async XLA Ops:
  0.0 20.6 %collective-permute-start.2 = (bf16[512,768]{1,0:T(8,128)(2,1)}, bf16[512,768]{1,0:T(8,128)(2,1)S(1)}, u32[]{:S(2)}, u32[]{:S(2)}) collective-permute-start(bf16[512,768]{1,0:T(8,128)(2,1)} %refs_0_.5), channel_id=1, source_target_pairs={{0,32},{1,33},{2,34},{3,35},{4,36},{5,37},{6,38},{7,39},{8,40},{9,... | collective-permute-start | bytes 2359304 | tf_op jit(solution)/shard_map/ppermute | solution.py:56
  1.6 19.2 %collective-permute-start.3 = (bf16[512,768]{1,0:T(8,128)(2,1)}, bf16[512,768]{1,0:T(8,128)(2,1)S(1)}, u32[]{:S(2)}, u32[]{:S(2)}) collective-permute-start(bf16[512,768]{1,0:T(8,128)(2,1)} %refs_0_.5), channel_id=1, source_target_pairs={{0,96},{1,97},{2,98},{3,99},{4,100},{5,101},{6,102},{7,103},{8,104... | collective-permute-start | bytes 2359304 | tf_op jit(solution)/shard_map/ppermute | solution.py:56
  3.2 21.4 %collective-permute-start.4 = (bf16[512,768]{1,0:T(8,128)(2,1)}, bf16[512,768]{1,0:T(8,128)(2,1)S(1)}, u32[]{:S(2)}, u32[]{:S(2)}) collective-permute-start(bf16[512,768]{1,0:T(8,128)(2,1)} %refs_0_.5), channel_id=1, source_target_pairs={{0,20},{1,21},{2,22},{3,23},{4,16},{5,17},{6,18},{7,19},{8,28},{9,... | collective-permute-start | bytes 2359304 | tf_op jit(solution)/shard_map/ppermute | solution.py:56
  8.4 6.9 %collective-permute-start = (bf16[64,2,128]{2,1,0:T(2,128)(2,1)S(1)}, bf16[64,2,128]{2,1,0:T(2,128)(2,1)S(1)}, u32[]{:S(2)}, u32[]{:S(2)}) collective-permute-start(bf16[64,2,128]{2,1,0:T(2,128)(2,1)S(1)} %get-tuple-element.93), channel_id=1, source_target_pairs={{1,0},{2,1},{3,2},{4,3},{5,4},{6,5},{7,6},{9,8},{10,9},{11,10},{12... | collective-permute-start | bytes 98312 | tf_op jit(solution)/shard_map/ppermute | solution.py:342
  9.7 6.1 %collective-permute-start.1 = (bf16[64,2,128]{2,1,0:T(2,128)(2,1)S(1)}, bf16[64,2,128]{2,1,0:T(2,128)(2,1)S(1)}, u32[]{:S(2)}, u32[]{:S(2)}) collective-permute-start(bf16[64,2,128]{2,1,0:T(2,128)(2,1)S(1)} %get-tuple-element.94), channel_id=1, source_target_pairs={{0,1},{1,2},{2,3},{3,4},{4,5},{5,6},{6,7},{8,9},{9,10},{10,11},{11... | collective-permute-start | bytes 98312 | tf_op jit(solution)/shard_map/ppermute | solution.py:342
  16.0 16.0 %collective-permute-start.5 = (bf16[2,272,128]{2,1,0:T(8,128)(2,1)S(1)}, bf16[2,272,128]{2,1,0:T(8,128)(2,1)S(1)}, u32[]{:S(2)}, u32[]{:S(2)}) collective-permute-start(bf16[2,272,128]{2,1,0:T(8,128)(2,1)S(1)} %pad_maximum_fusion.1), channel_id=1, source_target_pairs={{0,8},{8,16},{16,24},{24,32},{32,40},{40,48},{48,56},{56,64},{64,7... | collective-permute-start | bytes 417800 | tf_op jit(solution)/shard_map/ppermute | solution.py:342
  17.3 14.7 %collective-permute-start.6 = (bf16[2,272,128]{2,1,0:T(8,128)(2,1)S(1)}, bf16[2,272,128]{2,1,0:T(8,128)(2,1)S(1)}, u32[]{:S(2)}, u32[]{:S(2)}) collective-permute-start(bf16[2,272,128]{2,1,0:T(8,128)(2,1)S(1)} %pad_maximum_fusion.2), channel_id=1, source_target_pairs={{8,0},{16,8},{24,16},{32,24},{40,32},{48,40},{56,48},{64,56},{72,6... | collective-permute-start | bytes 417800 | tf_op jit(solution)/shard_map/ppermute | solution.py:342
  18.8 41.0 %copy-start = (bf16[512,768]{1,0:T(8,128)(2,1)S(1)}, bf16[512,768]{1,0:T(8,128)(2,1)}, u32[]{:S(2)}) copy-start(bf16[512,768]{1,0:T(8,128)(2,1)} %refs_0_.5) | copy-start | bytes 2359300
  24.6 27.2 %collective-permute-start.7 = (bf16[512,768]{1,0:T(8,128)(2,1)S(1)}, bf16[512,768]{1,0:T(8,128)(2,1)S(1)}, u32[]{:S(2)}, u32[]{:S(2)}) collective-permute-start(bf16[512,768]{1,0:T(8,128)(2,1)S(1)} %collective-permute-done.2.refs_1_), channel_id=1, source_target_pairs={{0,32},{1,33},{2,34},{3,35},{4,36},{5,37},{6,38},{7,39},{8,40},{9,... | collective-permute-start | bytes 2359304 | tf_op jit(solution)/shard_map/ppermute | solution.py:56
  27.8 23.9 %collective-permute-start.9 = (bf16[512,768]{1,0:T(8,128)(2,1)S(1)}, bf16[512,768]{1,0:T(8,128)(2,1)S(1)}, u32[]{:S(2)}, u32[]{:S(2)}) collective-permute-start(bf16[512,768]{1,0:T(8,128)(2,1)S(1)} %collective-permute-done.2.refs_1_), channel_id=1, source_target_pairs={{0,20},{1,21},{2,22},{3,23},{4,16},{5,17},{6,18},{7,19},{8,28},{9,... | collective-permute-start | bytes 2359304 | tf_op jit(solution)/shard_map/ppermute | solution.py:56
  29.0 22.8 %collective-permute-start.8 = (bf16[512,768]{1,0:T(8,128)(2,1)S(1)}, bf16[512,768]{1,0:T(8,128)(2,1)S(1)}, u32[]{:S(2)}, u32[]{:S(2)}) collective-permute-start(bf16[512,768]{1,0:T(8,128)(2,1)S(1)} %collective-permute-done.4.refs_4_), channel_id=1, source_target_pairs={{0,96},{1,97},{2,98},{3,99},{4,100},{5,101},{6,102},{7,103},{8,104... | collective-permute-start | bytes 2359304 | tf_op jit(solution)/shard_map/ppermute | solution.py:56
  51.7 10.2 %collective-permute-start.13 = (bf16[8,256,512]{2,1,0:T(8,128)(2,1)S(1)}, bf16[8,256,512]{2,1,0:T(8,128)(2,1)S(1)}, u32[]{:S(2)}, u32[]{:S(2)}) collective-permute-start(bf16[8,256,512]{2,1,0:T(8,128)(2,1)S(1)} %get-tuple-element.57), channel_id=1, source_target_pairs={{0,8},{1,9},{2,10},{3,11},{4,12},{5,13},{6,14},{7,15},{8,0},{9,1},... | collective-permute-start | bytes 6291464 | tf_op jit(solution)/shard_map/ppermute | solution.py:56
  51.8 13.5 %collective-permute-start.10 = (bf16[176,768]{1,0:T(8,128)(2,1)S(1)}, bf16[176,768]{1,0:T(8,128)(2,1)S(1)}, u32[]{:S(2)}, u32[]{:S(2)}) collective-permute-start(bf16[176,768]{1,0:T(8,128)(2,1)S(1)} %slice.33), channel_id=1, source_target_pairs={{0,96},{1,97},{2,98},{3,99},{4,100},{5,101},{6,102},{7,103},{8,104... | collective-permute-start | bytes 811016 | tf_op jit(solution)/shard_map/ppermute | solution.py:56
  52.9 12.4 %collective-permute-start.11 = (bf16[176,768]{1,0:T(8,128)(2,1)S(1)}, bf16[176,768]{1,0:T(8,128)(2,1)S(1)}, u32[]{:S(2)}, u32[]{:S(2)}) collective-permute-start(bf16[176,768]{1,0:T(8,128)(2,1)S(1)} %slice.34), channel_id=1, source_target_pairs={{0,32},{1,33},{2,34},{3,35},{4,36},{5,37},{6,38},{7,39},{8,40},{9,... | collective-permute-start | bytes 811016 | tf_op jit(solution)/shard_map/ppermute | solution.py:56
  54.0 11.3 %collective-permute-start.12 = (bf16[160,768]{1,0:T(8,128)(2,1)S(1)}, bf16[160,768]{1,0:T(8,128)(2,1)S(1)}, u32[]{:S(2)}, u32[]{:S(2)}) collective-permute-start(bf16[160,768]{1,0:T(8,128)(2,1)S(1)} %slice.35), channel_id=1, source_target_pairs={{0,20},{1,21},{2,22},{3,23},{4,16},{5,17},{6,18},{7,19},{8,28},{9,... | collective-permute-start | bytes 737288 | tf_op jit(solution)/shard_map/ppermute | solution.py:56
  66.3 2.0 %copy-start.1 = (bf16[768,16]{0,1:T(8,128)(2,1)S(1)}, bf16[768,16]{0,1:T(8,128)(2,1)}, u32[]{:S(2)}) copy-start(bf16[768,16]{0,1:T(8,128)(2,1)} %param.12) | copy-start | bytes 73732
  66.3 2.0 %copy-start.2 = (s32[1,1,256,1]{2,3,1,0:T(1,128)S(1)}, s32[1,1,256,1]{2,3,1,0:T(1,128)}, u32[]{:S(2)}) copy-start(s32[1,1,256,1]{2,3,1,0:T(1,128)} %param.13) | copy-start | bytes 3076
  66.3 2.0 %collective-permute-start.14 = (bf16[256,768]{1,0:T(8,128)(2,1)S(1)}, bf16[256,768]{1,0:T(8,128)(2,1)S(1)}, u32[]{:S(2)}, u32[]{:S(2)}) collective-permute-start(bf16[256,768]{1,0:T(8,128)(2,1)S(1)} %embed_partner_last.1), channel_id=1, source_target_pairs={{0,8},{1,9},{2,10},{3,11},{4,12},{5,13},{6,14},{7,15},{8,0},{9,1},... | collective-permute-start | bytes 1179656 | tf_op jit(solution)/shard_map/ppermute | solution.py:56
  69.8 8.4 %collective-permute-start.19 = (bf16[96,768]{1,0:T(8,128)(2,1)S(1)}, bf16[96,768]{1,0:T(8,128)(2,1)S(1)}, u32[]{:S(2)}, u32[]{:S(2)}) collective-permute-start(bf16[96,768]{1,0:T(8,128)(2,1)S(1)} %get-tuple-element.68), channel_id=1, source_target_pairs={{0,4},{1,5},{2,6},{3,7},{4,0},{5,1},{6,2},{7,3},{8,12},{9,13},{10,... | collective-permute-start | bytes 442376 | tf_op jit(solution)/shard_map/ppermute | solution.py:346
  70.8 7.5 %collective-permute-start.20 = (bf16[96,768]{1,0:T(8,128)(2,1)S(1)}, bf16[96,768]{1,0:T(8,128)(2,1)S(1)}, u32[]{:S(2)}, u32[]{:S(2)}) collective-permute-start(bf16[96,768]{1,0:T(8,128)(2,1)S(1)} %get-tuple-element.69), channel_id=1, source_target_pairs={{0,1},{1,0},{2,3},{3,2},{4,5},{5,4},{6,7},{7,6},{8,9},{9,8},{10,11... | collective-permute-start | bytes 442376 | tf_op jit(solution)/shard_map/ppermute | solution.py:346
  70.8 12.5 %collective-permute-start.21 = (bf16[96,768]{1,0:T(8,128)(2,1)S(1)}, bf16[96,768]{1,0:T(8,128)(2,1)S(1)}, u32[]{:S(2)}, u32[]{:S(2)}) collective-permute-start(bf16[96,768]{1,0:T(8,128)(2,1)S(1)} %get-tuple-element.70), channel_id=1, source_target_pairs={{0,3},{1,2},{2,1},{3,0},{4,7},{5,6},{6,5},{7,4},{8,11},{9,10},{10,... | collective-permute-start | bytes 442376 | tf_op jit(solution)/shard_map/ppermute | solution.py:346
  73.2 14.4 %collective-permute-start.15 = (bf16[96,768]{1,0:T(8,128)(2,1)S(1)}, bf16[96,768]{1,0:T(8,128)(2,1)S(1)}, u32[]{:S(2)}, u32[]{:S(2)}) collective-permute-start(bf16[96,768]{1,0:T(8,128)(2,1)S(1)} %get-tuple-element.63), channel_id=1, source_target_pairs={{0,2},{1,3},{2,0},{3,1},{4,6},{5,7},{6,4},{7,5},{8,10},{9,11},{10,... | collective-permute-start | bytes 442376 | tf_op jit(solution)/shard_map/ppermute | solution.py:346
  74.9 12.7 %collective-permute-start.16 = (bf16[96,768]{1,0:T(8,128)(2,1)S(1)}, bf16[96,768]{1,0:T(8,128)(2,1)S(1)}, u32[]{:S(2)}, u32[]{:S(2)}) collective-permute-start(bf16[96,768]{1,0:T(8,128)(2,1)S(1)} %get-tuple-element.64), channel_id=1, source_target_pairs={{0,6},{1,7},{2,4},{3,5},{4,2},{5,3},{6,0},{7,1},{8,14},{9,15},{10,... | collective-permute-start | bytes 442376 | tf_op jit(solution)/shard_map/ppermute | solution.py:346
  78.1 11.9 %collective-permute-start.17 = (bf16[96,768]{1,0:T(8,128)(2,1)S(1)}, bf16[96,768]{1,0:T(8,128)(2,1)S(1)}, u32[]{:S(2)}, u32[]{:S(2)}) collective-permute-start(bf16[96,768]{1,0:T(8,128)(2,1)S(1)} %get-tuple-element.65), channel_id=1, source_target_pairs={{0,5},{1,4},{2,7},{3,6},{4,1},{5,0},{6,3},{7,2},{8,13},{9,12},{10,... | collective-permute-start | bytes 442376 | tf_op jit(solution)/shard_map/ppermute | solution.py:346
  78.3 12.8 %collective-permute-start.18 = (bf16[96,768]{1,0:T(8,128)(2,1)S(1)}, bf16[96,768]{1,0:T(8,128)(2,1)S(1)}, u32[]{:S(2)}, u32[]{:S(2)}) collective-permute-start(bf16[96,768]{1,0:T(8,128)(2,1)S(1)} %get-tuple-element.66), channel_id=1, source_target_pairs={{0,7},{1,6},{2,5},{3,4},{4,3},{5,2},{6,1},{7,0},{8,15},{9,14},{10,... | collective-permute-start | bytes 442376 | tf_op jit(solution)/shard_map/ppermute | solution.py:346
  91.1 10.7 %collective-permute-start.22 = (bf16[96,768]{1,0:T(8,128)(2,1)S(1)}, bf16[96,768]{1,0:T(8,128)(2,1)S(1)}, u32[]{:S(2)}, u32[]{:S(2)}) collective-permute-start(bf16[96,768]{1,0:T(8,128)(2,1)S(1)} %get-tuple-element.80), channel_id=1, source_target_pairs={{0,4},{1,5},{2,6},{3,7},{4,0},{5,1},{6,2},{7,3},{8,12},{9,13},{10,... | collective-permute-start | bytes 442376 | tf_op jit(solution)/shard_map/ppermute | solution.py:346
  91.9 11.8 %collective-permute-start.23 = (bf16[96,768]{1,0:T(8,128)(2,1)S(1)}, bf16[96,768]{1,0:T(8,128)(2,1)S(1)}, u32[]{:S(2)}, u32[]{:S(2)}) collective-permute-start(bf16[96,768]{1,0:T(8,128)(2,1)S(1)} %get-tuple-element.81), channel_id=1, source_target_pairs={{0,1},{1,0},{2,3},{3,2},{4,5},{5,4},{6,7},{7,6},{8,9},{9,8},{10,11... | collective-permute-start | bytes 442376 | tf_op jit(solution)/shard_map/ppermute | solution.py:346
  91.9 14.2 %collective-permute-start.24 = (bf16[96,768]{1,0:T(8,128)(2,1)S(1)}, bf16[96,768]{1,0:T(8,128)(2,1)S(1)}, u32[]{:S(2)}, u32[]{:S(2)}) collective-permute-start(bf16[96,768]{1,0:T(8,128)(2,1)S(1)} %get-tuple-element.82), channel_id=1, source_target_pairs={{0,3},{1,2},{2,1},{3,0},{4,7},{5,6},{6,5},{7,4},{8,11},{9,10},{10,... | collective-permute-start | bytes 442376 | tf_op jit(solution)/shard_map/ppermute | solution.py:346
  98.3 8.2 %collective-permute-start.25 = (bf16[96,768]{1,0:T(8,128)(2,1)S(1)}, bf16[96,768]{1,0:T(8,128)(2,1)S(1)}, u32[]{:S(2)}, u32[]{:S(2)}) collective-permute-start(bf16[96,768]{1,0:T(8,128)(2,1)S(1)} %get-tuple-element.87), channel_id=1, source_target_pairs={{0,2},{1,3},{2,0},{3,1},{4,6},{5,7},{6,4},{7,5},{8,10},{9,11},{10,... | collective-permute-start | bytes 442376 | tf_op jit(solution)/shard_map/ppermute | solution.py:346
  100.3 10.6 %collective-permute-start.26 = (bf16[96,768]{1,0:T(8,128)(2,1)S(1)}, bf16[96,768]{1,0:T(8,128)(2,1)S(1)}, u32[]{:S(2)}, u32[]{:S(2)}) collective-permute-start(bf16[96,768]{1,0:T(8,128)(2,1)S(1)} %get-tuple-element.88), channel_id=1, source_target_pairs={{0,6},{1,7},{2,4},{3,5},{4,2},{5,3},{6,0},{7,1},{8,14},{9,15},{10,... | collective-permute-start | bytes 442376 | tf_op jit(solution)/shard_map/ppermute | solution.py:346
  101.8 11.4 %collective-permute-start.27 = (bf16[96,768]{1,0:T(8,128)(2,1)S(1)}, bf16[96,768]{1,0:T(8,128)(2,1)S(1)}, u32[]{:S(2)}, u32[]{:S(2)}) collective-permute-start(bf16[96,768]{1,0:T(8,128)(2,1)S(1)} %get-tuple-element.89), channel_id=1, source_target_pairs={{0,5},{1,4},{2,7},{3,6},{4,1},{5,0},{6,3},{7,2},{8,13},{9,12},{10,... | collective-permute-start | bytes 442376 | tf_op jit(solution)/shard_map/ppermute | solution.py:346
  103.7 10.2 %collective-permute-start.28 = (bf16[96,768]{1,0:T(8,128)(2,1)S(1)}, bf16[96,768]{1,0:T(8,128)(2,1)S(1)}, u32[]{:S(2)}, u32[]{:S(2)}) collective-permute-start(bf16[96,768]{1,0:T(8,128)(2,1)S(1)} %get-tuple-element.90), channel_id=1, source_target_pairs={{0,7},{1,6},{2,5},{3,4},{4,3},{5,2},{6,1},{7,0},{8,15},{9,14},{10,... | collective-permute-start | bytes 442376 | tf_op jit(solution)/shard_map/ppermute | solution.py:346
